TPU v7x, 32 devices: a whole 2x2x4 slice. The times are simulated.
32 devices in a mesh: section: 2 (over core), dp: 4 (over z), rep: 4 (over y, x).
Axes of the slice: x: 2, y: 2, z: 4, core: 2. Of those that a mesh axis runs over, the one named last changes fastest.
Arguments:
- block_input: bfloat16 [4, 4, 512, 256], P(None, 'rep', 'dp'), may hold values from -6 to 6
- output_grad: bfloat16 [4, 4, 512, 256], P(None, 'rep', 'dp'), may hold values from -6 to 6
- seq_lengths: int32 [4, 4, 4], replicated, may hold values from 1 to 509, as said below
- attn_gain: bfloat16 [2, 256], P('section'), may hold values from 0.5 to 1.5
- qkv_proj: bfloat16 [2, 256, 768], P('section'), may hold values from -0.5 to 0.5
- out_proj: bfloat16 [2, 256, 256], P('section'), may hold values from -1 to 1
- ffn_gain: bfloat16 [2, 256], P('section'), may hold values from 0.5 to 1.5
- up_proj: bfloat16 [2, 256, 1024], P('section'), may hold values from -0.375 to 0.375
- down_proj: bfloat16 [2, 1024, 256], P('section'), may hold values from -0.25 to 0.25
Outputs:
- block_output: bfloat16 [2, 4, 4, 512, 256], P('section', None, 'rep', 'dp')
- input_grad: bfloat16 [2, 4, 4, 512, 256], P('section', None, 'rep', 'dp')
- attn_gain_grad: float32 [2, 256], P('section')
- qkv_proj_grad: float32 [2, 256, 768], P('section')
- out_proj_grad: float32 [2, 256, 256], P('section')
- ffn_gain_grad: float32 [2, 256], P('section')
- up_proj_grad: float32 [2, 256, 1024], P('section')
- down_proj_grad: float32 [2, 1024, 256], P('section')
Inputs may be any that keep to these rules, and one draw needn't show every extreme that they name: seq_lengths[m, g] lists in order the lengths of the 4 sequences packed from the start of line g of micro-batch m; their sum is at most 512 and the rest of the line is padding. In every g, one micro-batch, drawn from the seed, has a first sequence that starts at the line's first position and ends among its last 128 positions, followed by sequences of 1 to 32 positions; in line 0 that first sequence is 509 long. In the other micro-batches every sequence is 64 long or more and the line is at least half used.
All inputs are finite; a program needn't handle non-finite values.
Results may differ from a plain program's by a relative error of at most 0.02.
Values may be sent and summed in bfloat16 or wider, within the bound.
No kernel may reach another device: no remote copies, remote signals or barrier semaphores. Data moves between devices by JAX's collectives and lax.ppermute only.
A program may use at most 128 MiB of HBM per device.

v0:
```python
from functools import partial

import jax
import jax.numpy as jnp
from jax import lax
from jax.sharding import PartitionSpec as P

HEADS = 2
STRIDE = 128


NEG = -1e30


def from_behind(shard, axis, by):
    length = lax.axis_size(axis)
    pairs = [(i, i + by) for i in range(length) if 0 <= i + by < length]
    return lax.ppermute(shard, axis, pairs)


def normalize(values):
    centered = values - jnp.mean(values, axis=-1, keepdims=True)
    spread = jnp.mean(centered * centered, axis=-1, keepdims=True)
    return centered * lax.rsqrt(spread + 1e-05)


def gained(values, gain):
    return normalize(values) * gain


def allowed(query_pos, query_seg, key_pos, key_seg, strided, seq_slots):
    offset = query_pos - key_pos
    same_seq = (query_seg == key_seg) & (query_seg < seq_slots)
    nearby = (offset >= 0) & (offset < STRIDE)
    spaced = (offset >= 0) & (offset % STRIDE == 0)
    pattern = jnp.where(strided, spaced, nearby)
    return same_seq & pattern | (offset == 0)


def product(left, right):
    return jnp.dot(left, right, preferred_element_type=jnp.float32)


def contract_rows(left, right):
    return lax.dot_general(
        left, right, (((0,), (0,)), ((), ())), preferred_element_type=jnp.float32
    )


def contract_cols(left, right):
    return lax.dot_general(
        left, right, (((1,), (1,)), ((), ())), preferred_element_type=jnp.float32
    )


def put_row(buffer, value, slot_index, is_valid):
    current = lax.dynamic_index_in_dim(buffer, slot_index, 0, keepdims=False)
    return lax.dynamic_update_index_in_dim(
        buffer, jnp.where(is_valid, value, current), slot_index, 0
    )


def softmax_parts(scores):
    row_max = jnp.max(scores, axis=-1, keepdims=True)
    shifted = jnp.exp(scores - row_max)
    row_total = jnp.sum(shifted, axis=-1, keepdims=True)
    return ((shifted / row_total).astype(jnp.bfloat16), (row_max + jnp.log(row_total))[..., 0])


def local(
    block_input,
    output_grad,
    seq_lengths,
    attn_gain,
    qkv_proj,
    out_proj,
    ffn_gain,
    up_proj,
    down_proj,
):
    section_index = lax.axis_index("section")
    line_row = lax.axis_index("dp")
    group_index = lax.axis_index("rep")
    strided = section_index == 1
    micro_count, _, tok_rows, model_width = block_input.shape
    line_count = lax.axis_size("dp")
    line_span = tok_rows * line_count
    head_size = model_width // HEADS
    score_scale = float(head_size) ** (-0.5)
    seq_slots = seq_lengths.shape[-1]
    block_count = line_span // STRIDE
    residues = STRIDE // line_count
    line_lengths = lax.dynamic_index_in_dim(seq_lengths, group_index, 1, keepdims=False)
    all_pos = jnp.arange(line_span, dtype=jnp.int32)
    my_pos = line_row * tok_rows + jnp.arange(tok_rows, dtype=jnp.int32)
    win_pos = line_row * tok_rows - tok_rows + jnp.arange(2 * tok_rows, dtype=jnp.int32)
    res_pos = (
        jnp.arange(block_count, dtype=jnp.int32)[None, :] * STRIDE
        + line_row * residues
        + jnp.arange(residues, dtype=jnp.int32)[:, None]
    )
    gain_attn = attn_gain[0].astype(jnp.float32)
    gain_ffn = ffn_gain[0].astype(jnp.float32)
    w_qkv = qkv_proj[0]
    w_out = out_proj[0]
    w_up = up_proj[0]
    w_down = down_proj[0]

    def segments_of(slot_index):
        seq_ends = jnp.cumsum(lax.dynamic_index_in_dim(line_lengths, slot_index, 0, keepdims=False))
        all_seg = jnp.sum((all_pos[:, None] >= seq_ends[None, :]).astype(jnp.int32), axis=1)
        my_seg = lax.dynamic_slice_in_dim(all_seg, line_row * tok_rows, tok_rows)
        padded = jnp.concatenate([jnp.full((tok_rows,), seq_slots, jnp.int32), all_seg])
        win_seg = lax.dynamic_slice_in_dim(padded, line_row * tok_rows, 2 * tok_rows)
        res_seg = lax.dynamic_slice_in_dim(
            all_seg.reshape(block_count, STRIDE), line_row * residues, residues, 1
        ).T
        dense_mask = allowed(
            my_pos[:, None], my_seg[:, None], all_pos[None, :], all_seg[None, :], strided, seq_slots
        )
        win_mask = allowed(
            my_pos[:, None], my_seg[:, None], win_pos[None, :], win_seg[None, :], False, seq_slots
        )
        res_mask = allowed(
            res_pos[:, :, None],
            res_seg[:, :, None],
            res_pos[:, None, :],
            res_seg[:, None, :],
            True,
            seq_slots,
        )
        return (all_seg, my_seg, dense_mask, win_mask, res_mask)

    def project(hidden):
        normed = gained(hidden, gain_attn).astype(jnp.bfloat16)
        packed = product(normed, w_qkv).astype(jnp.bfloat16)
        return (normed, packed)

    def finish(hidden, attended):
        middle = hidden + product(attended, w_out)
        second = gained(middle, gain_ffn).astype(jnp.bfloat16)
        pre_act = product(second, w_up)
        active = jax.nn.gelu(pre_act, approximate=False).astype(jnp.bfloat16)
        return (middle, second, pre_act, active, middle + product(active, w_down))

    def dense_backward(packed, grad_att, lse_now, masks):
        all_seg, my_seg, dense_mask = (masks[0], masks[1], masks[2])
        queries = packed[:, :model_width]
        key_rows = packed[:, model_width : 2 * model_width]
        values = packed[:, 2 * model_width :]
        keys_all, values_all = (
            lax.all_gather(key_rows, "dp", axis=0, tiled=True),
            lax.all_gather(values, "dp", axis=0, tiled=True),
        )
        grad_q_heads = []
        grad_k_heads = []
        grad_v_heads = []
        delta_heads = []
        for head_index in range(HEADS):
            columns = slice(head_index * head_size, (head_index + 1) * head_size)
            query_head = queries[:, columns]
            out_head = grad_att[:, columns]
            scores = jnp.where(
                dense_mask, contract_cols(query_head, keys_all[:, columns]) * score_scale, NEG
            )
            attn_probs = jnp.exp(scores - lse_now[head_index][:, None])
            grad_probs = contract_cols(out_head, values_all[:, columns])
            delta_row = jnp.sum(attn_probs * grad_probs, axis=1)
            grad_scores = (attn_probs * (grad_probs - delta_row[:, None])).astype(jnp.bfloat16)
            grad_q_heads.append(product(grad_scores, keys_all[:, columns]) * score_scale)
            delta_heads.append(delta_row)
            key_part = contract_rows(grad_scores, query_head) * score_scale
            value_part = contract_rows(attn_probs.astype(jnp.bfloat16), out_head)
            key_mine, value_mine = (
                lax.psum_scatter(
                    key_part.astype(jnp.bfloat16), "dp", scatter_dimension=0, tiled=True
                ).astype(jnp.float32),
                lax.psum_scatter(
                    value_part.astype(jnp.bfloat16), "dp", scatter_dimension=0, tiled=True
                ).astype(jnp.float32),
            )
            grad_k_heads.append(key_mine)
            grad_v_heads.append(value_mine)
        return jnp.concatenate(
            [
                jnp.concatenate(grad_q_heads, axis=1).astype(jnp.bfloat16),
                jnp.concatenate(grad_k_heads, axis=1).astype(jnp.bfloat16),
                jnp.concatenate(grad_v_heads, axis=1).astype(jnp.bfloat16),
            ],
            axis=1,
        )

    received = jnp.zeros((tok_rows, model_width), jnp.bfloat16)
    saved_in = jnp.zeros((micro_count, tok_rows, model_width), jnp.bfloat16)
    saved_att = jnp.zeros((micro_count, tok_rows, model_width), jnp.bfloat16)
    saved_lse = jnp.zeros((micro_count, HEADS, tok_rows), jnp.float32)
    results = jnp.zeros((micro_count, tok_rows, model_width), jnp.bfloat16)
    for tick_index in range(micro_count + 1):
        slot_raw = tick_index - section_index
        is_valid = (slot_raw >= 0) & (slot_raw < micro_count)
        slot_index = jnp.clip(slot_raw, 0, micro_count - 1)
        hidden_low = jnp.where(
            section_index == 0, block_input[min(tick_index, micro_count - 1), 0], received
        )
        hidden = hidden_low.astype(jnp.float32)
        normed, packed = project(hidden)
        masks = segments_of(slot_index)
        dense_dense_mask = masks[2]
        dense_keys_all = lax.all_gather(
            packed[:, model_width : 2 * model_width], "dp", axis=0, tiled=True
        )
        dense_values_all = lax.all_gather(packed[:, 2 * model_width :], "dp", axis=0, tiled=True)
        head_outs = []
        head_lse = []
        for dense_head_index in range(HEADS):
            dense_columns = slice(dense_head_index * head_size, (dense_head_index + 1) * head_size)
            dense_scores = jnp.where(
                dense_dense_mask,
                contract_cols(packed[:, dense_columns], dense_keys_all[:, dense_columns])
                * score_scale,
                NEG,
            )
            dense_attn_probs, lse_row = softmax_parts(dense_scores)
            head_outs.append(product(dense_attn_probs, dense_values_all[:, dense_columns]))
            head_lse.append(lse_row)
        attended = jnp.concatenate(head_outs, axis=1).astype(jnp.bfloat16)
        lse_rows = jnp.stack(head_lse)
        output = finish(hidden, attended)[4].astype(jnp.bfloat16)
        saved_in = put_row(saved_in, hidden_low, slot_index, is_valid)
        saved_att = put_row(saved_att, attended, slot_index, is_valid)
        saved_lse = put_row(saved_lse, lse_rows, slot_index, is_valid)
        results = put_row(results, output, slot_index, is_valid)
        if tick_index < micro_count:
            received = from_behind(output, "section", 1)
    totals = (
        jnp.zeros((model_width,), jnp.float32),
        jnp.zeros(w_qkv.shape, jnp.float32),
        jnp.zeros(w_out.shape, jnp.float32),
        jnp.zeros((model_width,), jnp.float32),
        jnp.zeros(w_up.shape, jnp.float32),
        jnp.zeros(w_down.shape, jnp.float32),
    )
    sent_back = jnp.zeros((tok_rows, model_width), jnp.bfloat16)
    input_grads = jnp.zeros((micro_count, tok_rows, model_width), jnp.bfloat16)
    for tick_index in range(micro_count + 1):
        slot_raw = tick_index - (1 - section_index)
        is_valid = (slot_raw >= 0) & (slot_raw < micro_count)
        slot_index = jnp.clip(slot_raw, 0, micro_count - 1)
        grad_out = jnp.where(
            section_index == 1, output_grad[min(tick_index, micro_count - 1), 0], sent_back
        )
        hidden = lax.dynamic_index_in_dim(saved_in, slot_index, 0, keepdims=False).astype(
            jnp.float32
        )
        attended = lax.dynamic_index_in_dim(saved_att, slot_index, 0, keepdims=False)
        lse_now = lax.dynamic_index_in_dim(saved_lse, slot_index, 0, keepdims=False)
        normed, packed = project(hidden)
        middle, second, pre_act, active, _ = finish(hidden, attended)
        grad_down = contract_rows(active, grad_out)
        grad_active = contract_cols(grad_out, w_down)
        gelu_back = jax.vjp(partial(jax.nn.gelu, approximate=False), pre_act)[1]
        grad_pre = gelu_back(grad_active)[0].astype(jnp.bfloat16)
        grad_up = contract_rows(second, grad_pre)
        ffn_back = jax.vjp(gained, middle, gain_ffn)[1]
        grad_mid_norm, grad_gain_ffn = ffn_back(contract_cols(grad_pre, w_up))
        grad_middle = grad_out.astype(jnp.float32) + grad_mid_norm
        grad_branch = grad_middle.astype(jnp.bfloat16)
        grad_outproj = contract_rows(attended, grad_branch)
        grad_att = contract_cols(grad_branch, w_out).astype(jnp.bfloat16)
        masks = segments_of(slot_index)
        grad_packed = dense_backward(packed, grad_att, lse_now, masks)
        grad_qkv = contract_rows(normed, grad_packed)
        attn_back = jax.vjp(gained, hidden, gain_attn)[1]
        grad_hid_norm, grad_gain_attn = attn_back(contract_cols(grad_packed, w_qkv))
        grad_hidden = (grad_middle + grad_hid_norm).astype(jnp.bfloat16)
        terms = (grad_gain_attn, grad_qkv, grad_outproj, grad_gain_ffn, grad_up, grad_down)
        totals = tuple(
            (
                running + jnp.where(is_valid, term_now, 0.0)
                for running, term_now in zip(totals, terms)
            )
        )
        input_grads = put_row(input_grads, grad_hidden, slot_index, is_valid)
        if tick_index < micro_count:
            sent_back = from_behind(grad_hidden, "section", -1)
    summed = lax.psum(
        (totals[0], totals[1], totals[2], totals[3], totals[4], totals[5]), ("dp", "rep")
    )
    return (
        results[None, :, None],
        input_grads[None, :, None],
        summed[0][None],
        summed[1][None],
        summed[2][None],
        summed[3][None],
        summed[4][None],
        summed[5][None],
    )


def solution(mesh):
    placed = (
        P(None, "rep", "dp", None),
        P(None, "rep", "dp", None),
        P(),
        P("section", None),
        P("section", None, None),
        P("section", None, None),
        P("section", None),
        P("section", None, None),
        P("section", None, None),
    )
    return jax.shard_map(
        local,
        mesh=mesh,
        in_specs=placed,
        out_specs=(
            P("section", None, "rep", "dp", None),
            P("section", None, "rep", "dp", None),
            P("section", None),
            P("section", None, None),
            P("section", None, None),
            P("section", None),
            P("section", None, None),
            P("section", None, None),
        ),
        check_vma=False,
    )
```

profile of v0, /device:TPU:0, one launch (start us, length us, event | category | flops | bytes accessed | tf_op | source)
XLA Modules:
  0.0 1015.0 jit_solution(5345080813445076931)
XLA Ops:
  12.4 15.6 %all_gather.60 = bf16[512,256]{1,0:T(8,128)(2,1)S(1)} all-gather(bf16[128,256]{1,0:T(8,128)(2,1)S(1)} %get-tuple-element.131), channel_id=1, replica_groups=mesh['section'=2,'dp'=4,'rep'=4] {'dp'}, dimensions={0}, use_global_device_ids=true | all-gather | bytes 327680 | tf_op jit(solution)/shard_map/all_gather | solution.py:209
  29.1 14.4 %all_gather.61 = bf16[512,256]{1,0:T(8,128)(2,1)S(1)} all-gather(bf16[128,256]{1,0:T(8,128)(2,1)S(1)} %get-tuple-element.132), channel_id=1, replica_groups=mesh['section'=2,'dp'=4,'rep'=4] {'dp'}, dimensions={0}, use_global_device_ids=true | all-gather | bytes 327680 | tf_op jit(solution)/shard_map/all_gather | solution.py:212
  56.6 13.9 %all_gather.62 = bf16[512,256]{1,0:T(8,128)(2,1)S(1)} all-gather(bf16[128,256]{1,0:T(8,128)(2,1)S(1)} %get-tuple-element.129), channel_id=1, replica_groups=mesh['section'=2,'dp'=4,'rep'=4] {'dp'}, dimensions={0}, use_global_device_ids=true | all-gather | bytes 327680 | tf_op jit(solution)/shard_map/all_gather | solution.py:209
  71.5 14.0 %all_gather.63 = bf16[512,256]{1,0:T(8,128)(2,1)S(1)} all-gather(bf16[128,256]{1,0:T(8,128)(2,1)S(1)} %get-tuple-element.130), channel_id=1, replica_groups=mesh['section'=2,'dp'=4,'rep'=4] {'dp'}, dimensions={0}, use_global_device_ids=true | all-gather | bytes 327680 | tf_op jit(solution)/shard_map/all_gather | solution.py:212
  91.7 14.3 %all_gather.64 = bf16[512,256]{1,0:T(8,128)(2,1)S(1)} all-gather(bf16[128,256]{1,0:T(8,128)(2,1)S(1)} %get-tuple-element.127), channel_id=1, replica_groups=mesh['section'=2,'dp'=4,'rep'=4] {'dp'}, dimensions={0}, use_global_device_ids=true | all-gather | bytes 327680 | tf_op jit(solution)/shard_map/all_gather | solution.py:209
  107.0 14.6 %all_gather.65 = bf16[512,256]{1,0:T(8,128)(2,1)S(1)} all-gather(bf16[128,256]{1,0:T(8,128)(2,1)S(1)} %get-tuple-element.128), channel_id=1, replica_groups=mesh['section'=2,'dp'=4,'rep'=4] {'dp'}, dimensions={0}, use_global_device_ids=true | all-gather | bytes 327680 | tf_op jit(solution)/shard_map/all_gather | solution.py:212
  127.8 14.4 %all_gather.66 = bf16[512,256]{1,0:T(8,128)(2,1)S(1)} all-gather(bf16[128,256]{1,0:T(8,128)(2,1)S(1)} %get-tuple-element.125), channel_id=1, replica_groups=mesh['section'=2,'dp'=4,'rep'=4] {'dp'}, dimensions={0}, use_global_device_ids=true | all-gather | bytes 327680 | tf_op jit(solution)/shard_map/all_gather | solution.py:209
  143.1 14.7 %all_gather.67 = bf16[512,256]{1,0:T(8,128)(2,1)S(1)} all-gather(bf16[128,256]{1,0:T(8,128)(2,1)S(1)} %get-tuple-element.126), channel_id=1, replica_groups=mesh['section'=2,'dp'=4,'rep'=4] {'dp'}, dimensions={0}, use_global_device_ids=true | all-gather | bytes 327680 | tf_op jit(solution)/shard_map/all_gather | solution.py:212
  164.4 13.9 %all_gather.68 = bf16[512,256]{1,0:T(8,128)(2,1)S(1)} all-gather(bf16[128,256]{1,0:T(8,128)(2,1)S(1)} %get-tuple-element.123), channel_id=1, replica_groups=mesh['section'=2,'dp'=4,'rep'=4] {'dp'}, dimensions={0}, use_global_device_ids=true | all-gather | bytes 327680 | tf_op jit(solution)/shard_map/all_gather | solution.py:209
  179.3 14.6 %all_gather.69 = bf16[512,256]{1,0:T(8,128)(2,1)S(1)} all-gather(bf16[128,256]{1,0:T(8,128)(2,1)S(1)} %get-tuple-element.124), channel_id=1, replica_groups=mesh['section'=2,'dp'=4,'rep'=4] {'dp'}, dimensions={0}, use_global_device_ids=true | all-gather | bytes 327680 | tf_op jit(solution)/shard_map/all_gather | solution.py:212
  203.2 14.0 %all_gather.71 = bf16[512,256]{1,0:T(8,128)(2,1)S(1)} all-gather(bf16[128,256]{1,0:T(8,128)(2,1)S(1)} %get-tuple-element.121), channel_id=1, replica_groups=mesh['section'=2,'dp'=4,'rep'=4] {'dp'}, dimensions={0}, use_global_device_ids=true | all-gather | bytes 327680 | tf_op jit(solution)/shard_map/all_gather | solution.py:153
  218.3 14.2 %all_gather.70 = bf16[512,256]{1,0:T(8,128)(2,1)S(1)} all-gather(bf16[128,256]{1,0:T(8,128)(2,1)S(1)} %get-tuple-element.122), channel_id=1, replica_groups=mesh['section'=2,'dp'=4,'rep'=4] {'dp'}, dimensions={0}, use_global_device_ids=true | all-gather | bytes 327680 | tf_op jit(solution)/shard_map/all_gather | solution.py:152
  239.5 2.2 convolution_select_fusion.4
  252.8 2.1 fusion.116
  258.7 2.1 fusion.117
  270.2 18.2 %reduce-scatter.65.cloned.1.call-done = bf16[128,128]{1,0:T(8,128)(2,1)} async-done(((bf16[512,128]{1,0:T(8,128)(2,1)}), bf16[128,128]{1,0:T(8,128)(2,1)}) %reduce-scatter.65.cloned.1.call-update) | async-done | bytes 32784
  289.3 18.8 %reduce-scatter.63.cloned.1.call-done = bf16[128,128]{1,0:T(8,128)(2,1)} async-done(((bf16[512,128]{1,0:T(8,128)(2,1)}), bf16[128,128]{1,0:T(8,128)(2,1)}) %reduce-scatter.63.cloned.1.call-update) | async-done | bytes 32784
  310.2 17.4 %reduce-scatter.67.cloned.1.call-done = bf16[128,128]{1,0:T(8,128)(2,1)} async-done(((bf16[512,128]{1,0:T(8,128)(2,1)}), bf16[128,128]{1,0:T(8,128)(2,1)}) %reduce-scatter.67.cloned.1.call-update) | async-done | bytes 32784
  335.8 14.5 %all_gather.73 = bf16[512,256]{1,0:T(8,128)(2,1)S(1)} all-gather(bf16[128,256]{1,0:T(8,128)(2,1)S(1)} %get-tuple-element.119), channel_id=1, replica_groups=mesh['section'=2,'dp'=4,'rep'=4] {'dp'}, dimensions={0}, use_global_device_ids=true | all-gather | bytes 327680 | tf_op jit(solution)/shard_map/all_gather | solution.py:153
  350.3 14.3 %all_gather.72 = bf16[512,256]{1,0:T(8,128)(2,1)S(1)} all-gather(bf16[128,256]{1,0:T(8,128)(2,1)S(1)} %get-tuple-element.120), channel_id=1, replica_groups=mesh['section'=2,'dp'=4,'rep'=4] {'dp'}, dimensions={0}, use_global_device_ids=true | all-gather | bytes 327680 | tf_op jit(solution)/shard_map/all_gather | solution.py:152
  365.8 14.5 %all_gather.75 = bf16[512,256]{1,0:T(8,128)(2,1)} all-gather(bf16[128,256]{1,0:T(8,128)(2,1)S(1)} %get-tuple-element.117), channel_id=1, replica_groups=mesh['section'=2,'dp'=4,'rep'=4] {'dp'}, dimensions={0}, use_global_device_ids=true | all-gather | bytes 327680 | tf_op jit(solution)/shard_map/all_gather | solution.py:153
  380.3 14.6 %all_gather.74 = bf16[512,256]{1,0:T(8,128)(2,1)} all-gather(bf16[128,256]{1,0:T(8,128)(2,1)S(1)} %get-tuple-element.118), channel_id=1, replica_groups=mesh['section'=2,'dp'=4,'rep'=4] {'dp'}, dimensions={0}, use_global_device_ids=true | all-gather | bytes 327680 | tf_op jit(solution)/shard_map/all_gather | solution.py:152
  395.5 15.3 %all_gather.77 = bf16[512,256]{1,0:T(8,128)(2,1)} all-gather(bf16[128,256]{1,0:T(8,128)(2,1)S(1)} %get-tuple-element.115), channel_id=1, replica_groups=mesh['section'=2,'dp'=4,'rep'=4] {'dp'}, dimensions={0}, use_global_device_ids=true | all-gather | bytes 327680 | tf_op jit(solution)/shard_map/all_gather | solution.py:153
  410.8 14.8 %all_gather.76 = bf16[512,256]{1,0:T(8,128)(2,1)} all-gather(bf16[128,256]{1,0:T(8,128)(2,1)S(1)} %get-tuple-element.116), channel_id=1, replica_groups=mesh['section'=2,'dp'=4,'rep'=4] {'dp'}, dimensions={0}, use_global_device_ids=true | all-gather | bytes 327680 | tf_op jit(solution)/shard_map/all_gather | solution.py:152
  426.2 15.2 %all_gather.79 = bf16[512,256]{1,0:T(8,128)(2,1)} all-gather(bf16[128,256]{1,0:T(8,128)(2,1)S(1)} %get-tuple-element.113), channel_id=1, replica_groups=mesh['section'=2,'dp'=4,'rep'=4] {'dp'}, dimensions={0}, use_global_device_ids=true | all-gather | bytes 327680 | tf_op jit(solution)/shard_map/all_gather | solution.py:153
  441.4 14.5 %all_gather.78 = bf16[512,256]{1,0:T(8,128)(2,1)} all-gather(bf16[128,256]{1,0:T(8,128)(2,1)S(1)} %get-tuple-element.114), channel_id=1, replica_groups=mesh['section'=2,'dp'=4,'rep'=4] {'dp'}, dimensions={0}, use_global_device_ids=true | all-gather | bytes 327680 | tf_op jit(solution)/shard_map/all_gather | solution.py:152
  467.4 1.6 fusion.63
  474.3 3.8 fusion.4
  480.0 2.3 fusion.9
  483.3 1.7 fusion.85
  485.0 1.8 fusion.19
  487.1 6.0 reduce-scatter.69.cloned.1.call-done
  494.0 19.2 %reduce-scatter.73.cloned.1.call-done = bf16[128,128]{1,0:T(8,128)(2,1)} async-done(((bf16[512,128]{1,0:T(8,128)(2,1)}), bf16[128,128]{1,0:T(8,128)(2,1)}) %reduce-scatter.73.cloned.1.call-update) | async-done | bytes 32784
  514.0 18.7 %reduce-scatter.71.cloned.1.call-done = bf16[128,128]{1,0:T(8,128)(2,1)} async-done(((bf16[512,128]{1,0:T(8,128)(2,1)}), bf16[128,128]{1,0:T(8,128)(2,1)}) %reduce-scatter.71.cloned.1.call-update) | async-done | bytes 32784
  533.6 18.8 %reduce-scatter.75.cloned.1.call-done = bf16[128,128]{1,0:T(8,128)(2,1)} async-done(((bf16[512,128]{1,0:T(8,128)(2,1)}), bf16[128,128]{1,0:T(8,128)(2,1)}) %reduce-scatter.75.cloned.1.call-update) | async-done | bytes 32784
  576.7 1.8 convolution_convert_fusion.15
  578.6 1.8 fusion.87
  580.4 1.6 convolution_convert_fusion.14
  582.2 2.4 fusion.8
  586.5 2.3 reduce-scatter.77.cloned.1.call-done
  589.7 18.7 %reduce-scatter.81.cloned.1.call-done = bf16[128,128]{1,0:T(8,128)(2,1)} async-done(((bf16[512,128]{1,0:T(8,128)(2,1)}), bf16[128,128]{1,0:T(8,128)(2,1)}) %reduce-scatter.81.cloned.1.call-update) | async-done | bytes 32784
  609.3 18.8 %reduce-scatter.79.cloned.1.call-done = bf16[128,128]{1,0:T(8,128)(2,1)} async-done(((bf16[512,128]{1,0:T(8,128)(2,1)}), bf16[128,128]{1,0:T(8,128)(2,1)}) %reduce-scatter.79.cloned.1.call-update) | async-done | bytes 32784
  628.9 19.3 %reduce-scatter.83.cloned.1.call-done = bf16[128,128]{1,0:T(8,128)(2,1)} async-done(((bf16[512,128]{1,0:T(8,128)(2,1)}), bf16[128,128]{1,0:T(8,128)(2,1)}) %reduce-scatter.83.cloned.1.call-update) | async-done | bytes 32784
  669.4 1.6 fusion.66
  671.1 1.8 fusion.91
  675.1 2.4 fusion.7
  680.2 2.5 convolution_select_fusion.1
  682.7 5.8 reduce-scatter.85.cloned.1.call-done
  689.4 19.3 %reduce-scatter.89.cloned.1.call-done = bf16[128,128]{1,0:T(8,128)(2,1)} async-done(((bf16[512,128]{1,0:T(8,128)(2,1)}), bf16[128,128]{1,0:T(8,128)(2,1)}) %reduce-scatter.89.cloned.1.call-update) | async-done | bytes 32784
  709.6 18.6 %reduce-scatter.87.cloned.1.call-done = bf16[128,128]{1,0:T(8,128)(2,1)} async-done(((bf16[512,128]{1,0:T(8,128)(2,1)}), bf16[128,128]{1,0:T(8,128)(2,1)}) %reduce-scatter.87.cloned.1.call-update) | async-done | bytes 32784
  729.1 18.7 %reduce-scatter.91.cloned.1.call-done = bf16[128,128]{1,0:T(8,128)(2,1)} async-done(((bf16[512,128]{1,0:T(8,128)(2,1)}), bf16[128,128]{1,0:T(8,128)(2,1)}) %reduce-scatter.91.cloned.1.call-update) | async-done | bytes 32784
  751.9 1.7 collective-permute-start.7
  769.3 1.6 fusion.69
  771.0 1.7 fusion.97
  778.5 2.5 convolution_select_fusion
  781.8 3.9 fusion.3
  785.7 3.2 reduce-scatter.93.cloned.1.call-done
  790.4 18.7 %reduce-scatter.97.cloned.1.call-done = bf16[128,128]{1,0:T(8,128)(2,1)} async-done(((bf16[512,128]{1,0:T(8,128)(2,1)}), bf16[128,128]{1,0:T(8,128)(2,1)}) %reduce-scatter.97.cloned.1.call-update) | async-done | bytes 32784
  809.9 19.3 %reduce-scatter.95.cloned.1.call-done = bf16[128,128]{1,0:T(8,128)(2,1)} async-done(((bf16[512,128]{1,0:T(8,128)(2,1)}), bf16[128,128]{1,0:T(8,128)(2,1)}) %reduce-scatter.95.cloned.1.call-update) | async-done | bytes 32784
  831.3 17.5 %reduce-scatter.99.cloned.1.call-done = bf16[128,128]{1,0:T(8,128)(2,1)} async-done(((bf16[512,128]{1,0:T(8,128)(2,1)}), bf16[128,128]{1,0:T(8,128)(2,1)}) %reduce-scatter.99.cloned.1.call-update) | async-done | bytes 32784
  851.6 2.4 fusion.14
  861.3 41.0 %all-reduce = (f32[1,256]{1,0:T(1,128)}, f32[1,256]{1,0:T(1,128)}) all-reduce(f32[1,256]{1,0:T(1,128)S(1)} %bitcast.790, f32[1,256]{1,0:T(1,128)S(1)} %bitcast.789), channel_id=1, replica_groups=mesh['section'=2,'dp'=4,'rep'=4] {'dp','rep'}, use_global_device_ids=true, to_apply=%region_135.136 | all-reduce | flops 512 | bytes 4096 | tf_op jit(solution)/shard_map/psum | solution.py:286
  903.0 99.2 %all-reduce.4.cloned.1.call-done = (f32[1,256,768]{2,1,0:T(8,128)}, f32[1,256,256]{2,1,0:T(8,128)}, f32[1,256,1024]{2,1,0:T(8,128)}, f32[1,1024,256]{2,1,0:T(8,128)}) async-done(((f32[1,256,768]{2,1,0:T(8,128)}, f32[1,256,256]{2,1,0:T(8,128)}, f32[1,256,1024]{2,1,0:T(8,128)}, f32[1,1024,256]{2,1,0:T(8,128)}), (f32[1,256,768]{2,1,0:T(8,128)}, f32[1,256,256]{2,1,0:T(8,128)}, f32[1,256,1024]{2,1,0:T(8,128)}, ...) | async-done | bytes 3145744 | tf_op jit(solution)/shard_map/psum | solution.py:286
  1002.2 2.2 copy.218
  (958 shorter events, 219.5 us)
Async XLA Ops:
  7.2 39.1 %copy-start = (bf16[1,256,1024]{2,1,0:T(8,128)(2,1)S(1)}, bf16[1,256,1024]{2,1,0:T(8,128)(2,1)}, u32[]{:S(2)}) copy-start(bf16[1,256,1024]{2,1,0:T(8,128)(2,1)} %param.16) | copy-start | bytes 1572868
  7.2 261.6 %reduce-scatter.61.cloned.1.call-start = ((), (), s32[]{:S(2)}) async-start(), calls=%async_computation.20 | async-start | bytes 163840
  7.3 171.5 %copy-start.252 = (s32[128]{0:T(128)}, s32[128]{0:T(128)S(1)}, u32[]{:S(2)}) copy-start(s32[128]{0:T(128)S(1)} %iota_add_fusion) | copy-start | bytes 1540
  47.8 7.6 collective-permute-start
  88.9 2.2 collective-permute-start.1
  125.0 2.2 collective-permute-start.2
  161.3 2.2 collective-permute-start.3
  203.2 29.2 %copy-start.74 = (bf16[128,768]{1,0:T(8,128)(2,1)}, bf16[128,768]{1,0:T(8,128)(2,1)S(1)}, u32[]{:S(2)}) copy-start(bf16[128,768]{1,0:T(8,128)(2,1)S(1)} %convolution_convert_fusion.4) | copy-start | bytes 589828
  243.2 20.8 %copy-start.124 = (f32[128]{0:T(128)}, f32[128]{0:T(128)S(1)}, u32[]{:S(2)}) copy-start(f32[128]{0:T(128)S(1)} %broadcast_multiply_fusion.7) | copy-start | bytes 1540
  244.0 20.1 %copy-start.139 = (f32[128]{0:T(128)}, f32[128]{0:T(128)S(1)}, u32[]{:S(2)}) copy-start(f32[128]{0:T(128)S(1)} %fusion.861) | copy-start | bytes 1540
  247.8 40.6 %reduce-scatter.65.cloned.1.call-start = ((), (), s32[]{:S(2)}) async-start(), calls=%async_computation.22 | async-start | bytes 163840
  265.1 43.0 %reduce-scatter.63.cloned.1.call-start = ((), (), s32[]{:S(2)}) async-start(), calls=%async_computation.21 | async-start | bytes 163840
  267.0 60.7 %reduce-scatter.67.cloned.1.call-start = ((), (), s32[]{:S(2)}) async-start(), calls=%async_computation.23 | async-start | bytes 163840
  268.7 224.4 %reduce-scatter.69.cloned.1.call-start = ((), (), s32[]{:S(2)}) async-start(), calls=%async_computation.24 | async-start | bytes 163840
  332.5 32.7 %copy-start.237 = (f32[128]{0:T(128)}, f32[128]{0:T(128)S(1)}, u32[]{:S(2)}) copy-start(f32[128]{0:T(128)S(1)} %get-tuple-element.54) | copy-start | bytes 1540
  332.5 62.4 %copy-start.235 = (f32[128]{0:T(128)}, f32[128]{0:T(128)S(1)}, u32[]{:S(2)}) copy-start(f32[128]{0:T(128)S(1)} %get-tuple-element.53) | copy-start | bytes 1540
  332.6 93.0 %copy-start.233 = (f32[128]{0:T(128)}, f32[128]{0:T(128)S(1)}, u32[]{:S(2)}) copy-start(f32[128]{0:T(128)S(1)} %get-tuple-element.52) | copy-start | bytes 1540
  333.7 122.3 %collective-permute-start.4 = (bf16[128,256]{1,0:T(8,128)(2,1)S(1)}, bf16[128,256]{1,0:T(8,128)(2,1)S(1)}, u32[]{:S(2)}, u32[]{:S(2)}) collective-permute-start(bf16[128,256]{1,0:T(8,128)(2,1)S(1)} %get-tuple-element.90), channel_id=1, source_target_pairs={{16,0},{17,1},{18,2},{19,3},{20,4},{21,5},{22,6},{23,7},{24,8},{25... | collective-permute-start | bytes 196616 | tf_op jit(solution)/shard_map/ppermute | solution.py:18
  335.7 125.8 %copy-start.73 = (bf16[128,768]{1,0:T(8,128)(2,1)}, bf16[128,768]{1,0:T(8,128)(2,1)S(1)}, u32[]{:S(2)}) copy-start(bf16[128,768]{1,0:T(8,128)(2,1)S(1)} %convolution_convert_fusion.3) | copy-start | bytes 589828
  364.6 97.0 %copy-start.40 = (bf16[512,256]{1,0:T(8,128)(2,1)}, bf16[512,256]{1,0:T(8,128)(2,1)S(1)}, u32[]{:S(2)}) copy-start(bf16[512,256]{1,0:T(8,128)(2,1)S(1)} %all_gather.72) | copy-start | bytes 786436
  365.8 14.6 %copy-start.72 = (bf16[128,768]{1,0:T(8,128)(2,1)}, bf16[128,768]{1,0:T(8,128)(2,1)S(1)}, u32[]{:S(2)}) copy-start(bf16[128,768]{1,0:T(8,128)(2,1)S(1)} %convolution_convert_fusion.2) | copy-start | bytes 589828
  395.5 15.3 %copy-start.71 = (bf16[128,768]{1,0:T(8,128)(2,1)}, bf16[128,768]{1,0:T(8,128)(2,1)S(1)}, u32[]{:S(2)}) copy-start(bf16[128,768]{1,0:T(8,128)(2,1)S(1)} %convolution_convert_fusion.1) | copy-start | bytes 589828
  426.2 15.3 %copy-start.70 = (bf16[128,768]{1,0:T(8,128)(2,1)}, bf16[128,768]{1,0:T(8,128)(2,1)S(1)}, u32[]{:S(2)}) copy-start(bf16[128,768]{1,0:T(8,128)(2,1)S(1)} %convolution_convert_fusion) | copy-start | bytes 589828
  426.2 29.8 %copy-start.100 = (f32[128,1024]{1,0:T(8,128)S(1)}, f32[128,1024]{1,0:T(8,128)}, u32[]{:S(2)}) copy-start(f32[128,1024]{1,0:T(8,128)} %fusion.147) | copy-start | bytes 1572868
  426.2 29.8 %copy-start.247 = (bf16[1,1024,256]{2,1,0:T(8,128)(2,1)S(1)}, bf16[1,1024,256]{2,1,0:T(8,128)(2,1)}, u32[]{:S(2)}) copy-start(bf16[1,1024,256]{2,1,0:T(8,128)(2,1)} %param.17) | copy-start | bytes 1572868
  474.2 38.9 %reduce-scatter.73.cloned.1.call-start = ((), (), s32[]{:S(2)}) async-start(), calls=%async_computation.26 | async-start | bytes 163840
  474.3 4.7 copy-start.91
  480.0 52.8 %reduce-scatter.71.cloned.1.call-start = ((), (), s32[]{:S(2)}) async-start(), calls=%async_computation.25 | async-start | bytes 163840
  482.4 70.0 %reduce-scatter.75.cloned.1.call-start = ((), (), s32[]{:S(2)}) async-start(), calls=%async_computation.27 | async-start | bytes 163840
  485.0 8.9 copy-start.64
  486.8 102.0 %reduce-scatter.77.cloned.1.call-start = ((), (), s32[]{:S(2)}) async-start(), calls=%async_computation.28 | async-start | bytes 163840
  556.3 5.0 copy-start.98
  556.4 5.0 copy-start.248
  557.3 3.1 collective-permute-start.5
  566.7 4.8 copy-start.49
  571.4 37.0 %reduce-scatter.81.cloned.1.call-start = ((), (), s32[]{:S(2)}) async-start(), calls=%async_computation.30 | async-start | bytes 163840
  573.3 8.9 copy-start.3
  578.6 49.5 %reduce-scatter.79.cloned.1.call-start = ((), (), s32[]{:S(2)}) async-start(), calls=%async_computation.29 | async-start | bytes 163840
  582.1 66.1 %reduce-scatter.83.cloned.1.call-start = ((), (), s32[]{:S(2)}) async-start(), calls=%async_computation.31 | async-start | bytes 163840
  586.5 102.1 %reduce-scatter.85.cloned.1.call-start = ((), (), s32[]{:S(2)}) async-start(), calls=%async_computation.32 | async-start | bytes 163840
  650.4 6.9 copy-start.249
  652.2 5.0 copy-start.95
  652.2 5.0 copy-start.97
  653.2 3.1 collective-permute-start.6
  661.6 4.6 copy-start.56
  668.2 6.4 copy-start.4
  671.0 37.7 %reduce-scatter.89.cloned.1.call-start = ((), (), s32[]{:S(2)}) async-start(), calls=%async_computation.34 | async-start | bytes 163840
  674.5 53.7 %reduce-scatter.87.cloned.1.call-start = ((), (), s32[]{:S(2)}) async-start(), calls=%async_computation.33 | async-start | bytes 163840
  679.4 68.4 %reduce-scatter.91.cloned.1.call-start = ((), (), s32[]{:S(2)}) async-start(), calls=%async_computation.35 | async-start | bytes 163840
  680.2 9.2 copy-start.67
  682.7 106.2 %reduce-scatter.93.cloned.1.call-start = ((), (), s32[]{:S(2)}) async-start(), calls=%async_computation.36 | async-start | bytes 163840
  751.9 3.3 collective-permute-start.7
  760.6 5.5 copy-start.52
  768.1 4.7 copy-start.5
  770.9 38.1 %reduce-scatter.97.cloned.1.call-start = ((), (), s32[]{:S(2)}) async-start(), calls=%async_computation.38 | async-start | bytes 163840
  775.0 54.2 %reduce-scatter.95.cloned.1.call-start = ((), (), s32[]{:S(2)}) async-start(), calls=%async_computation.37 | async-start | bytes 163840
  777.7 71.1 %reduce-scatter.99.cloned.1.call-start = ((), (), s32[]{:S(2)}) async-start(), calls=%async_computation.39 | async-start | bytes 163840
  781.0 221.2 %all-reduce.4.cloned.1.call-start = ((), (), s32[]{:S(2)}) async-start(), calls=%async_computation.40 | async-start | bytes 6291456 | tf_op jit(solution)/shard_map/psum | solution.py:286
  781.8 68.5 %copy-start.127 = (f32[128]{0:T(128)S(1)}, f32[128]{0:T(128)}, u32[]{:S(2)}) copy-start(f32[128]{0:T(128)} %copy-done.126) | copy-start | bytes 1540
  781.8 69.8 %copy-start.63 = (bf16[128,768]{0,1:T(8,128)(2,1)S(1)}, bf16[128,768]{0,1:T(8,128)(2,1)}, u32[]{:S(2)}) copy-start(bf16[128,768]{0,1:T(8,128)(2,1)} %constant_dynamic-update-slice_fusion) | copy-start | bytes 589828
  785.7 65.9 %copy-start.6 = (f32[256,768]{1,0:T(8,128)S(1)}, f32[256,768]{1,0:T(8,128)}, u32[]{:S(2)}) copy-start(f32[256,768]{1,0:T(8,128)} %convolution_select_fusion.13) | copy-start | bytes 2359300
  785.7 65.9 %copy-start.7 = (f32[256,768]{1,0:T(8,128)S(1)}, f32[256,768]{1,0:T(8,128)}, u32[]{:S(2)}) copy-start(f32[256,768]{1,0:T(8,128)} %convolution_select_fusion.12) | copy-start | bytes 2359300
  860.4 41.9 %copy-start.31 = (bf16[128,256]{1,0:T(8,128)(2,1)S(1)}, bf16[128,256]{1,0:T(8,128)(2,1)}, u32[]{:S(2)}) copy-start(bf16[128,256]{1,0:T(8,128)(2,1)} %copy-done.29) | copy-start | bytes 196612
  903.0 101.4 %copy-start.106 = (bf16[1,4,1,128,256]{4,3,1,2,0:T(8,128)(2,1)}, bf16[1,4,1,128,256]{4,3,1,2,0:T(8,128)(2,1)S(1)}, u32[]{:S(2)}) copy-start(bf16[1,4,1,128,256]{4,3,1,2,0:T(8,128)(2,1)S(1)} %fusion.647) | copy-start | bytes 786436
  (225 other events, 280.0 us)
Sparse Core Ops, SparseCore 0:
  247.9 20.7 reduce-scatter.60
  271.1 17.3 reduce-scatter.64
  290.7 17.3 reduce-scatter.62
  310.3 17.2 reduce-scatter.66
  474.3 18.6 reduce-scatter.68
  495.8 17.2 reduce-scatter.72
  515.4 17.2 reduce-scatter.70
  535.1 17.3 reduce-scatter.74
  571.5 17.2 reduce-scatter.76
  591.0 17.3 reduce-scatter.80
  610.7 17.3 reduce-scatter.78
  630.8 17.3 reduce-scatter.82
  671.1 17.3 reduce-scatter.84
  691.3 17.3 reduce-scatter.88
  710.8 17.3 reduce-scatter.86
  730.4 17.3 reduce-scatter.90
  771.0 17.8 reduce-scatter.92
  791.7 17.3 reduce-scatter.96
  811.9 17.3 reduce-scatter.94
  831.4 17.3 reduce-scatter.98
  855.4 146.8 all-reduce.3
where the time goes:
time: 1030 us; the launch traced here: 1010 us
  waiting for transfers between devices  402 us (39%)
  blocking collectives  331 us (32%)
  matrix products  134 us (13%)
  local copies, waits for them, and re-layouts  89.2 us (9%)
  other arithmetic  28.8 us (3%)
  between operations  18 us (2%)
  starting transfers between devices  12 us (1%)
    unnamed x41, waiting for transfers between devices  298 us
    psum x1, waiting for transfers between devices, local(): lax.psum((totals[0], totals[1], totals[2], totals[3], totals[4], totals[5...  99.2 us
    unnamed x561, local copies, waits for them, and re-layouts  81.9 us
    all_gather x5, blocking collectives, dense_backward(): lax.all_gather(values, 'dp', axis=0, tiled=True)  73.6 us
    all_gather x5, blocking collectives, dense_backward(): lax.all_gather(key_rows, 'dp', axis=0, tiled=True)  72.4 us
    all_gather x5, blocking collectives, local(): lax.all_gather(packed[:, 2 * model_width:], 'dp', axis=0, tiled=True)  72.3 us
    all_gather x5, blocking collectives, local(): lax.all_gather(packed[:, model_width:2 * model_width], 'dp', axis=0, tile...  72.1 us
    dot_general x40, matrix products, contract_rows(): lax.dot_general(left, right, (((0,), (0,)), ((), ())), preferred_element_...  64 us
  transfers between devices with their start and end apart: 29, of which 26 were waited for; matrix products, arithmetic and copies ran while one was open for 9% of the time, Pallas kernels for 0%

commit v1 on v0

--- a/solution.py
+++ b/solution.py
@@ -3,6 +3,8 @@
 import jax
 import jax.numpy as jnp
 from jax import lax
+from jax.experimental import pallas as pl
+from jax.experimental.pallas import tpu as pltpu
 from jax.sharding import PartitionSpec as P
 
 HEADS = 2
@@ -67,7 +69,7 @@
     return ((shifted / row_total).astype(jnp.bfloat16), (row_max + jnp.log(row_total))[..., 0])
 
 
-def local(
+def general(
     block_input,
     output_grad,
     seq_lengths,
@@ -298,6 +300,656 @@
     )
 
 
+BF = jnp.bfloat16
+F32 = jnp.float32
+VMEM_BYTES = 56 * 1024 * 1024
+
+
+def vmem_call(body, out_shape, scratch=(), in_specs=None, out_specs=None):
+    return pl.pallas_call(
+        body,
+        out_shape=out_shape,
+        in_specs=in_specs,
+        out_specs=out_specs,
+        scratch_shapes=list(scratch),
+        compiler_params=pltpu.CompilerParams(vmem_limit_bytes=VMEM_BYTES),
+    )
+
+
+def smem():
+    return pl.BlockSpec(memory_space=pltpu.SMEM)
+
+
+def vmem():
+    return pl.BlockSpec(memory_space=pltpu.VMEM)
+
+
+def anywhere():
+    return pl.BlockSpec(memory_space=pl.ANY)
+
+
+SEC, ZED, REP, FLIP = 0, 1, 2, 3
+
+
+def pack_kernel(info, tokens, grads, *pieces):
+    half = tokens.shape[1] // 2
+    rows = pl.ds(pl.multiple_of(info[SEC] * half, half), half)
+    for step, piece in enumerate(pieces):
+        micro = info[ZED] ^ step
+        piece[:half, :] = tokens[micro, rows, :]
+        piece[half:, :] = grads[micro, rows, :]
+
+
+def unit(values):
+    centered = values - jnp.mean(values, axis=-1, keepdims=True)
+    inverse = lax.rsqrt(jnp.mean(centered * centered, axis=-1, keepdims=True) + 1e-05)
+    return centered * inverse, inverse
+
+
+def unit_back(grad, normal, inverse):
+    return inverse * (
+        grad
+        - jnp.mean(grad, axis=-1, keepdims=True)
+        - normal * jnp.mean(grad * normal, axis=-1, keepdims=True)
+    )
+
+
+def segment_at(ends, position):
+    total = jnp.zeros(position.shape, jnp.int32)
+    for end in ends:
+        total = total + (position >= end).astype(jnp.int32)
+    return total
+
+
+def step_kernel(
+    info,
+    lengths,
+    own0,
+    own1,
+    own2,
+    own3,
+    far0,
+    far1,
+    far2,
+    far3,
+    gain_attn_own,
+    gain_ffn_own,
+    gain_attn_far,
+    gain_ffn_far,
+    qkv_own,
+    out_own,
+    up_own,
+    down_own,
+    qkv_far,
+    out_far,
+    up_far,
+    down_far,
+    result_keep,
+    result_send,
+    grad_in_one,
+    grad_in_zero,
+    ffn_keep,
+    ffn_send,
+    attn_keep,
+    attn_send,
+    w_qkv,
+    w_out,
+    w_up,
+    w_down,
+    ffn_terms,
+    attn_terms,
+    line,
+    mine,
+    cotangent,
+    normal_all,
+    normed_all,
+    padded,
+    probs_window,
+    probs_strided,
+    active,
+    slope,
+    middle_unit,
+    normal_one,
+    normed_one,
+    packed_one,
+    query_zero,
+    grad_padded,
+    in_sems,
+    out_sems,
+):
+    section = info[SEC]
+    half = own0.shape[0] // 2
+    width = own0.shape[1]
+    blocks = 4
+    span = line.shape[0]
+    block = span // blocks
+    rows = half * blocks
+    head = width // HEADS
+    hidden_units = w_up.shape[2]
+    scale = float(head) ** (-0.5)
+    other = 1 - section
+    loads = []
+    for index, (near, far, held) in enumerate(
+        (
+            (qkv_own, qkv_far, w_qkv),
+            (out_own, out_far, w_out),
+            (up_own, up_far, w_up),
+            (down_own, down_far, w_down),
+        )
+    ):
+        pair = (
+            pltpu.make_async_copy(near, held.at[section], in_sems.at[2 * index]),
+            pltpu.make_async_copy(far, held.at[other], in_sems.at[2 * index + 1]),
+        )
+        for copy in pair:
+            copy.start()
+        loads.append(pair)
+
+    def arrive(index):
+        for copy in loads[index]:
+            copy.wait()
+
+    def gain_of(near, far, layer):
+        return jnp.where(section == layer, near[...], far[...]).astype(F32)
+
+    gain_attn = [gain_of(gain_attn_own, gain_attn_far, layer) for layer in range(2)]
+    gain_ffn = [gain_of(gain_ffn_own, gain_ffn_far, layer) for layer in range(2)]
+
+    for step, (near, far) in enumerate(((own0, far0), (own1, far1), (own2, far2), (own3, far3))):
+        spot = info[ZED] ^ step
+        base = spot * block
+        near_rows = pl.ds(pl.multiple_of(base + section * half, half), half)
+        far_rows = pl.ds(pl.multiple_of(base + other * half, half), half)
+        mine_rows = pl.ds(pl.multiple_of(spot * half, half), half)
+        line[near_rows, :] = near[:half, :]
+        line[far_rows, :] = far[:half, :]
+        mine[mine_rows, :] = near[:half, :]
+        cotangent[mine_rows, :] = near[half:, :]
+
+    ends = []
+    so_far = jnp.int32(0)
+    for slot in range(lengths.shape[2]):
+        so_far = so_far + lengths[info[ZED], info[REP], slot]
+        ends.append(so_far)
+    slots = len(ends)
+
+    hidden_all = line[...].astype(F32)
+    normal, inverse_all = unit(hidden_all)
+    normal_all[...] = normal
+    normed_all[...] = (normal * gain_attn[0]).astype(BF)
+    arrive(0)
+
+    def mine_of(ref, spot, columns=slice(None)):
+        start = pl.multiple_of(block * spot + section * half, half)
+        return ref[pl.ds(start, half), columns]
+
+    normed_mine = jnp.concatenate([mine_of(normed_all, spot) for spot in range(blocks)], axis=0)
+    query_zero[...] = product(normed_mine, w_qkv[0, :, :width]).astype(BF)
+    padded[:block, :] = jnp.zeros((block, 2 * width), BF)
+    padded[block:, :] = product(normed_all[...], w_qkv[0, :, width:]).astype(BF)
+    reach = block + half
+
+    def window(spot):
+        return pl.ds(pl.multiple_of(block * spot + section * half, half), reach)
+
+    def window_mask(spot):
+        first = block * spot + section * half
+        query_pos = first + lax.broadcasted_iota(jnp.int32, (half, reach), 0)
+        key_pos = first - block + lax.broadcasted_iota(jnp.int32, (half, reach), 1)
+        offset = query_pos - key_pos
+        segment = segment_at(ends, query_pos)
+        same = (segment == segment_at(ends, key_pos)) & (segment < slots) & (key_pos >= 0)
+        return same & (offset >= 0) & (offset < STRIDE) | (offset == 0)
+
+    attended_parts = []
+    for spot in range(blocks):
+        mask = window_mask(spot)
+        spot_parts = []
+        for number in range(HEADS):
+            columns = slice(number * head, (number + 1) * head)
+            value_columns = slice(width + number * head, width + (number + 1) * head)
+            scores = contract_cols(
+                query_zero[spot * half : (spot + 1) * half, columns], padded[window(spot), columns]
+            )
+            scores = jnp.where(mask, scores * scale, NEG)
+            shifted = jnp.exp(scores - jnp.max(scores, axis=-1, keepdims=True))
+            probs = shifted / jnp.sum(shifted, axis=-1, keepdims=True)
+            probs_window[spot * HEADS + number] = probs
+            spot_parts.append(product(probs.astype(BF), padded[window(spot), value_columns]))
+        attended_parts.append(jnp.concatenate(spot_parts, axis=1).astype(BF))
+    attended_zero = jnp.concatenate(attended_parts, axis=0)
+    chunk = width
+    chunks = hidden_units // chunk
+
+    def ffn_forward(layer, hidden, attended):
+        middle = hidden + product(attended, w_out[layer])
+        normal, inverse = unit(middle)
+        middle_unit[layer] = normal
+        second = (normal * gain_ffn[layer]).astype(BF)
+        result = middle
+        for index in range(chunks):
+            columns = slice(index * chunk, (index + 1) * chunk)
+            pre_act = product(second, w_up[layer, :, columns])
+            below = 0.5 + 0.5 * lax.erf(pre_act * (0.5**0.5))
+            now = (pre_act * below).astype(BF)
+            active[layer, :, columns] = now
+            slope[layer, :, columns] = below + pre_act * (
+                jnp.exp(-0.5 * pre_act * pre_act) * 0.3989422804014327
+            )
+            result = result + product(now, w_down[layer, columns, :])
+        return result.astype(BF), second, inverse
+
+    arrive(1)
+    arrive(2)
+    arrive(3)
+    result_zero, second_zero, inverse_mid_zero = ffn_forward(
+        0, mine[...].astype(F32), attended_zero
+    )
+
+    hidden = result_zero.astype(F32)
+    normal, inverse_one = unit(hidden)
+    normal_one[...] = normal
+    normed_one[...] = (normal * gain_attn[1]).astype(BF)
+    packed_one[...] = product(normed_one[...], w_qkv[1]).astype(BF)
+
+    def place(axis, shape):
+        index = lax.broadcasted_iota(jnp.int32, shape, axis)
+        return block * (index // half) + section * half + (index & (half - 1))
+
+    query_pos = place(0, (rows, rows))
+    key_pos = place(1, (rows, rows))
+    offset = query_pos - key_pos
+    segment = segment_at(ends, query_pos)
+    same = (segment == segment_at(ends, key_pos)) & (segment < slots)
+    strided_mask = same & (offset >= 0) & ((offset & (STRIDE - 1)) == 0) | (offset == 0)
+    attended_parts = []
+    for number in range(HEADS):
+        columns = slice(number * head, (number + 1) * head)
+        key_columns = slice(width + number * head, width + (number + 1) * head)
+        value_columns = slice(2 * width + number * head, 2 * width + (number + 1) * head)
+        scores = contract_cols(packed_one[:, columns], packed_one[:, key_columns])
+        scores = jnp.where(strided_mask, scores * scale, NEG)
+        shifted = jnp.exp(scores - jnp.max(scores, axis=-1, keepdims=True))
+        probs = shifted / jnp.sum(shifted, axis=-1, keepdims=True)
+        probs_strided[number] = probs
+        attended_parts.append(product(probs.astype(BF), packed_one[:, value_columns]))
+    attended_one = jnp.concatenate(attended_parts, axis=1).astype(BF)
+    result_one, second_one, inverse_mid_one = ffn_forward(1, hidden, attended_one)
+
+    result_keep[...] = jnp.where(section == 0, result_zero, result_one)
+    result_send[...] = jnp.where(section == 0, result_one, result_zero)
+
+    def ffn_backward(layer, grad_out, second, inverse, attended):
+        side, flip = section ^ layer, info[FLIP + layer]
+        grad_second = None
+        for index in range(chunks):
+            columns = slice(index * chunk, (index + 1) * chunk)
+            grad_active = contract_cols(grad_out, w_down[layer, columns, :])
+            grad_pre = (grad_active * slope[layer, :, columns]).astype(BF)
+            quarter, part = index // 2, index % 2
+            spread = slice(part * chunk, (part + 1) * chunk)
+            ffn_terms[side, flip ^ quarter, spread, :] = contract_rows(second, grad_pre).astype(BF)
+            ffn_terms[side, flip ^ (quarter + 2), spread, :] = contract_rows(
+                active[layer, :, columns], grad_out
+            ).astype(BF)
+            term = contract_cols(grad_pre, w_up[layer, :, columns])
+            grad_second = term if grad_second is None else grad_second + term
+        normal = middle_unit[layer]
+        gain_term = jnp.sum(grad_second * normal, axis=0, keepdims=True)
+        grad_middle = grad_out.astype(F32) + unit_back(
+            grad_second * gain_ffn[layer], normal, inverse
+        )
+        grad_branch = grad_middle.astype(BF)
+        attn_terms[side, flip ^ 3, :width, :] = contract_rows(attended, grad_branch).astype(BF)
+        grad_att = contract_cols(grad_branch, w_out[layer]).astype(BF)
+        return grad_middle, grad_att, gain_term
+
+    def store_gains(layer, attn_term, ffn_term):
+        side, flip = section ^ layer, info[FLIP + layer]
+        rest = attn_terms.shape[2] - width
+        spare = jnp.concatenate([attn_term, ffn_term, jnp.zeros((rest - 2, width), F32)], axis=0)
+        for quarter in range(4):
+            attn_terms[side, flip ^ quarter, width:, :] = spare.astype(BF)
+
+    def outward(terms, keep, send, index):
+        pair = (
+            pltpu.make_async_copy(terms.at[0], keep, out_sems.at[index]),
+            pltpu.make_async_copy(terms.at[1], send, out_sems.at[index + 1]),
+        )
+        for copy in pair:
+            copy.start()
+        return pair
+
+    grad_middle, grad_att, ffn_term = ffn_backward(
+        1, cotangent[...], second_one, inverse_mid_one, attended_one
+    )
+    side, flip = section ^ 1, info[FLIP + 1]
+    grad_parts = [[], [], []]
+    for number in range(HEADS):
+        columns = slice(number * head, (number + 1) * head)
+        key_columns = slice(width + number * head, width + (number + 1) * head)
+        value_columns = slice(2 * width + number * head, 2 * width + (number + 1) * head)
+        probs = probs_strided[number]
+        grad_here = grad_att[:, columns]
+        grad_probs = contract_cols(grad_here, packed_one[:, value_columns])
+        delta = jnp.sum(probs * grad_probs, axis=-1, keepdims=True)
+        grad_scores = (probs * (grad_probs - delta)).astype(BF)
+        grad_parts[0].append(product(grad_scores, packed_one[:, key_columns]) * scale)
+        grad_parts[1].append(contract_rows(grad_scores, packed_one[:, columns]) * scale)
+        grad_parts[2].append(contract_rows(probs.astype(BF), grad_here))
+    grad_normed = None
+    for index in range(3):
+        columns = slice(index * width, (index + 1) * width)
+        grad_block = jnp.concatenate(grad_parts[index], axis=1).astype(BF)
+        attn_terms[side, flip ^ index, :width, :] = contract_rows(
+            normed_one[...], grad_block
+        ).astype(BF)
+        term = contract_cols(grad_block, w_qkv[1, :, columns])
+        grad_normed = term if grad_normed is None else grad_normed + term
+    normal = normal_one[...]
+    store_gains(1, jnp.sum(grad_normed * normal, axis=0, keepdims=True), ffn_term)
+    grad_in = (
+        grad_middle + unit_back(grad_normed * gain_attn[1], normal, inverse_one)
+    ).astype(BF)
+    grad_in_one[...] = grad_in
+
+    grad_middle, grad_att, ffn_term = ffn_backward(
+        0, grad_in, second_zero, inverse_mid_zero, attended_zero
+    )
+    ffn_out = outward(ffn_terms, ffn_keep, ffn_send, 0)
+    side, flip = section, info[FLIP]
+    grad_padded[...] = jnp.zeros(grad_padded.shape, F32)
+    grad_query_parts = []
+    for spot in range(blocks):
+        spot_parts = []
+        for number in range(HEADS):
+            columns = slice(number * head, (number + 1) * head)
+            value_columns = slice(width + number * head, width + (number + 1) * head)
+            probs = probs_window[spot * HEADS + number]
+            grad_here = grad_att[spot * half : (spot + 1) * half, columns]
+            query_here = query_zero[spot * half : (spot + 1) * half, columns]
+            grad_probs = contract_cols(grad_here, padded[window(spot), value_columns])
+            delta = jnp.sum(probs * grad_probs, axis=-1, keepdims=True)
+            grad_scores = (probs * (grad_probs - delta)).astype(BF)
+            spot_parts.append(product(grad_scores, padded[window(spot), columns]) * scale)
+            grad_padded[window(spot), columns] += contract_rows(grad_scores, query_here) * scale
+            grad_padded[window(spot), value_columns] += contract_rows(probs.astype(BF), grad_here)
+        grad_query_parts.append(jnp.concatenate(spot_parts, axis=1))
+    grad_query = jnp.concatenate(grad_query_parts, axis=0).astype(BF)
+    attn_terms[side, flip ^ 0, :width, :] = contract_rows(normed_mine, grad_query).astype(BF)
+    grad_keys = grad_padded[block:, :width].astype(BF)
+    grad_values = grad_padded[block:, width:].astype(BF)
+    attn_terms[side, flip ^ 1, :width, :] = contract_rows(normed_all[...], grad_keys).astype(BF)
+    attn_terms[side, flip ^ 2, :width, :] = contract_rows(normed_all[...], grad_values).astype(BF)
+    grad_in_zero[...] = contract_cols(grad_keys, w_qkv[0, :, width : 2 * width]) + contract_cols(
+        grad_values, w_qkv[0, :, 2 * width :]
+    )
+    from_query = contract_cols(grad_query, w_qkv[0, :, :width])
+    for spot in range(blocks):
+        here = pl.ds(pl.multiple_of(block * spot + section * half, half), half)
+        grad_in_zero[here, :] += from_query[spot * half : (spot + 1) * half, :]
+    grad_normed = grad_in_zero[...]
+    normal = normal_all[...]
+    store_gains(0, jnp.sum(grad_normed * normal, axis=0, keepdims=True), ffn_term)
+    attn_out = outward(attn_terms, attn_keep, attn_send, 2)
+    grad_in_zero[...] = unit_back(grad_normed * gain_attn[0], normal, inverse_all)
+    for spot in range(blocks):
+        here = pl.ds(pl.multiple_of(block * spot + section * half, half), half)
+        grad_in_zero[here, :] += grad_middle[spot * half : (spot + 1) * half, :]
+    for copy in (*ffn_out, *attn_out):
+        copy.wait()
+
+
+def run_step(info, seq_lengths, near, far, gains, weights):
+    width = near[0].shape[1]
+    half = near[0].shape[0] // 2
+    blocks = len(near)
+    rows = blocks * half
+    span = 2 * rows
+    block = span // blocks
+    hidden_units = weights[2].shape[1]
+    shape = jax.ShapeDtypeStruct
+    ffn_rows = 2 * hidden_units // 4
+    attn_rows = width + 16
+    outs = (
+        shape((rows, width), BF),
+        shape((rows, width), BF),
+        shape((rows, width), BF),
+        shape((span, width), F32),
+        shape((4, ffn_rows, width), BF),
+        shape((4, ffn_rows, width), BF),
+        shape((4, attn_rows, width), BF),
+        shape((4, attn_rows, width), BF),
+    )
+    scratch = (
+        pltpu.VMEM((2, width, 3 * width), BF),
+        pltpu.VMEM((2, width, width), BF),
+        pltpu.VMEM((2, width, hidden_units), BF),
+        pltpu.VMEM((2, hidden_units, width), BF),
+        pltpu.VMEM((2, 4, ffn_rows, width), BF),
+        pltpu.VMEM((2, 4, attn_rows, width), BF),
+        pltpu.VMEM((span, width), BF),
+        pltpu.VMEM((rows, width), BF),
+        pltpu.VMEM((rows, width), BF),
+        pltpu.VMEM((span, width), F32),
+        pltpu.VMEM((span, width), BF),
+        pltpu.VMEM((block + span, 2 * width), BF),
+        pltpu.VMEM((blocks * HEADS, half, block + half), F32),
+        pltpu.VMEM((HEADS, rows, rows), F32),
+        pltpu.VMEM((2, rows, hidden_units), BF),
+        pltpu.VMEM((2, rows, hidden_units), F32),
+        pltpu.VMEM((2, rows, width), F32),
+        pltpu.VMEM((rows, width), F32),
+        pltpu.VMEM((rows, width), BF),
+        pltpu.VMEM((rows, 3 * width), BF),
+        pltpu.VMEM((rows, width), BF),
+        pltpu.VMEM((block + span, 2 * width), F32),
+        pltpu.SemaphoreType.DMA((8,)),
+        pltpu.SemaphoreType.DMA((4,)),
+    )
+    return vmem_call(
+        step_kernel,
+        outs,
+        scratch,
+        in_specs=[smem()] * 2 + [vmem()] * 12 + [anywhere()] * 8,
+        out_specs=[vmem()] * 4 + [anywhere()] * 4,
+    )(info, seq_lengths, *near, *far, *gains, *weights)
+
+
+def share_kernel(info, keep, send_back, one_near, one_far, zero_near, zero_far, *pieces):
+    half = keep.shape[0] // len(pieces)
+    block = 2 * half
+    section = info[SEC]
+    other = 1 - section
+    for step, piece in enumerate(pieces):
+        spot = info[ZED] ^ step
+        near_rows = pl.ds(pl.multiple_of(section * half, half), half)
+        far_rows = pl.ds(pl.multiple_of(other * half, half), half)
+        mine = pl.ds(pl.multiple_of(spot * half, half), half)
+        whole = pl.ds(pl.multiple_of(spot * block, block), block)
+        piece[near_rows, :] = keep[mine, :]
+        piece[far_rows, :] = send_back[mine, :]
+
+        @pl.when(section == 0)
+        def _():
+            piece[block:, :] = (zero_near[whole, :] + zero_far[whole, :]).astype(BF)
+
+        @pl.when(section == 1)
+        def _():
+            piece[block : block + half, :] = one_far[mine, :]
+            piece[block + half :, :] = one_near[mine, :]
+
+
+def settle_kernel(info, piece0, piece1, piece2, piece3, results, input_grads):
+    block = piece0.shape[0] // 2
+    for step, piece in enumerate((piece0, piece1, piece2, piece3)):
+        micro = info[ZED] ^ step
+        results[0, micro, 0] = piece[:block, :]
+        input_grads[0, micro, 0] = piece[block:, :]
+
+
+def ffn_finish_kernel(info, piece0, piece1, piece2, piece3, up, down, held):
+    for step, piece in enumerate((piece0, piece1, piece2, piece3)):
+        held[info[FLIP + info[SEC]] ^ step] = piece[...]
+    rows, width = held.shape[1:]
+    blocks = rows // width
+    for quarter in range(2):
+        for part in range(blocks):
+            spread = slice(part * width, (part + 1) * width)
+            column = (quarter * blocks + part) * width
+            up[0, :, column : column + width] = held[quarter, spread, :].astype(F32)
+            down[0, column : column + width, :] = held[quarter + 2, spread, :].astype(F32)
+
+
+def attn_finish_kernel(info, piece0, piece1, piece2, piece3, gain_attn, gain_ffn, qkv, out, held):
+    for step, piece in enumerate((piece0, piece1, piece2, piece3)):
+        held[info[FLIP + info[SEC]] ^ step] = piece[...]
+    width = held.shape[2]
+    for quarter in range(3):
+        qkv[0, :, quarter * width : (quarter + 1) * width] = held[quarter, :width, :].astype(F32)
+    out[0] = held[3, :width, :].astype(F32)
+    spare = held[0, width:, :].astype(F32)
+    gain_attn[...] = spare[0:1, :]
+    gain_ffn[...] = spare[1:2, :]
+
+
+SWAP = [(0, 1), (1, 0)]
+
+
+def crossed(flips):
+    return [(4 * s + g, 4 * s + (g ^ flips[s])) for s in range(2) for g in range(4)]
+
+
+FIRST = crossed((1, 2))
+SECOND = crossed((2, 1))
+
+
+def line_pairs(step):
+    return [(z, z ^ step) for z in range(4)]
+
+
+def reduce_terms(keep, send):
+    came = lax.ppermute(send, "section", SWAP)
+    from_first = lax.ppermute(keep[2:4] + came[2:4], ("section", "rep"), FIRST)
+    from_second = lax.ppermute(
+        keep[1] + came[1] + from_first[1], ("section", "rep"), SECOND
+    )
+    total = lax.optimization_barrier(keep[0] + came[0] + from_first[0] + from_second)
+    total = lax.optimization_barrier(total + lax.ppermute(total, "dp", line_pairs(1)))
+    total = lax.optimization_barrier(total + lax.ppermute(total, "dp", line_pairs(2)))
+    one = lax.ppermute(total, ("section", "rep"), SECOND)
+    two = lax.ppermute(total, ("section", "rep"), FIRST)
+    three = lax.ppermute(one, ("section", "rep"), FIRST)
+    return total, one, two, three
+
+
+def lines(
+    block_input,
+    output_grad,
+    seq_lengths,
+    attn_gain,
+    qkv_proj,
+    out_proj,
+    ffn_gain,
+    up_proj,
+    down_proj,
+):
+    section = lax.axis_index("section")
+    zed = lax.axis_index("dp")
+    rep = lax.axis_index("rep")
+    low, high = rep & 1, rep >> 1
+    info = jnp.stack([section, zed, rep, 2 * low + high, 2 * high + low]).astype(jnp.int32)
+    micro_count, _, block, width = block_input.shape
+    hidden_units = up_proj.shape[2]
+    shape = jax.ShapeDtypeStruct
+
+    packed = vmem_call(
+        pack_kernel,
+        (shape((block, width), BF),) * micro_count,
+        in_specs=[smem()] + [vmem()] * 2,
+        out_specs=[vmem()] * micro_count,
+    )(info, block_input[:, 0], output_grad[:, 0])
+    near = [packed[0]] + [
+        lax.ppermute(packed[step], "dp", line_pairs(step)) for step in range(1, micro_count)
+    ]
+    far = [lax.ppermute(piece, "section", SWAP) for piece in near]
+    own = (attn_gain, ffn_gain, qkv_proj[0], out_proj[0], up_proj[0], down_proj[0])
+    swapped = [lax.ppermute(weight, "section", SWAP) for weight in own]
+    (
+        result_keep,
+        result_send,
+        grad_in_one,
+        grad_in_zero,
+        ffn_keep,
+        ffn_send,
+        attn_keep,
+        attn_send,
+    ) = run_step(
+        info,
+        seq_lengths,
+        near,
+        far,
+        (own[0], own[1], swapped[0], swapped[1]),
+        (*own[2:], *swapped[2:]),
+    )
+    ffn_pieces = reduce_terms(ffn_keep, ffn_send)
+    attn_pieces = reduce_terms(attn_keep, attn_send)
+
+    result_back = lax.ppermute(result_send, "section", SWAP)
+    one_far = lax.ppermute(grad_in_one, "section", [(0, 1)])
+    zero_far = lax.ppermute(grad_in_zero, "section", [(1, 0)])
+    shared = vmem_call(
+        share_kernel,
+        (shape((2 * block, width), BF),) * micro_count,
+        in_specs=[smem()] + [vmem()] * 6,
+        out_specs=[vmem()] * micro_count,
+    )(info, result_keep, result_back, grad_in_one, one_far, grad_in_zero, zero_far)
+    home = [shared[0]] + [
+        lax.ppermute(shared[step], "dp", line_pairs(step)) for step in range(1, micro_count)
+    ]
+    results, input_grads = vmem_call(
+        settle_kernel,
+        (shape((1, micro_count, 1, block, width), BF),) * 2,
+        in_specs=[smem()] + [vmem()] * micro_count,
+        out_specs=[vmem()] * 2,
+    )(info, *home)
+
+    up, down = vmem_call(
+        ffn_finish_kernel,
+        (shape((1, width, hidden_units), F32), shape((1, hidden_units, width), F32)),
+        [pltpu.VMEM((4, *ffn_keep.shape[1:]), BF)],
+        in_specs=[smem()] + [vmem()] * 4,
+        out_specs=[vmem()] * 2,
+    )(info, *ffn_pieces)
+    gain_attn, gain_ffn, qkv, out = vmem_call(
+        attn_finish_kernel,
+        (
+            shape((1, width), F32),
+            shape((1, width), F32),
+            shape((1, width, 3 * width), F32),
+            shape((1, width, width), F32),
+        ),
+        [pltpu.VMEM((4, *attn_keep.shape[1:]), BF)],
+        in_specs=[smem()] + [vmem()] * 4,
+        out_specs=[vmem()] * 4,
+    )(info, *attn_pieces)
+    return (results, input_grads, gain_attn, qkv, out, gain_ffn, up, down)
+
+
+def local(*arrays):
+    micro_count, _, tok_rows, model_width = arrays[0].shape
+    one_line_per_chip = (
+        lax.axis_size("section") == 2
+        and lax.axis_size("dp") == 4
+        and lax.axis_size("rep") == 4
+        and micro_count == 4
+        and tok_rows == STRIDE
+        and model_width == 256
+        and arrays[7].shape[2] == 4 * model_width
+    )
+    return lines(*arrays) if one_line_per_chip else general(*arrays)
+
+
 def solution(mesh):
     placed = (
         P(None, "rep", "dp", None),

time: 1030 us -> 124 us (0.12); the launches traced: 1010 us -> 124 us
  waiting for transfers between devices: 402 us -> 53.1 us
  blocking collectives: 331 us -> 0 us
  matrix products: 134 us -> 0 us
  local copies, waits for them, and re-layouts: 89.2 us -> 6.99 us
  Pallas kernels: 0 us -> 27.8 us
  other arithmetic: 28.8 us -> 1.5 us
  starting transfers between devices: 12 us -> 33.6 us
  between operations: 18 us -> 0.95 us
    unnamed x41 -> x0, waiting for transfers between devices: 298 us -> none
    all_gather x20 -> x0, blocking collectives: 290 us -> none  [the longest x5 73.6 us: dense_backward(): lax.all_gather(values, 'dp', axis=0, tiled=True)]
    dot_general x140 -> x0, matrix products: 134 us -> none  [the longest x40 64 us: contract_rows(): lax.dot_general(left, right, (((0,), (0,)), ((), ())), preferred_element_...]
    psum x1 -> x0, waiting for transfers between devices: 99.2 us -> none  [local(): lax.psum((totals[0], totals[1], totals[2], totals[3], totals[4], totals[5...]
    unnamed x561 -> x70, local copies, waits for them, and re-layouts: 81.9 us -> 6.32 us
    ppermute x8 -> x35, waiting for transfers between devices: 5.15 us -> 53.1 us  [the longest x2 15.9 us: reduce_terms(): lax.ppermute(total, 'dp', line_pairs(2))]
    psum x1 -> x0, blocking collectives: 41 us -> none  [local(): lax.psum((totals[0], totals[1], totals[2], totals[3], totals[4], totals[5...]
    pallas_call x0 -> x6, Pallas kernels: none -> 27.8 us  [the longest x1 16.9 us: run_step(): vmem_call(step_kernel, outs, scratch, in_specs=[smem()] * 2 + [vmem()] *...]
  transfers between devices with their start and end apart: 29 -> 35, of which waited for: 26 -> 16; matrix products, arithmetic and copies ran while one was open for 9% -> 1% of each run, Pallas kernels for 0% -> 7%
where the time goes in v1:
time: 124 us
  waiting for transfers between devices  53.1 us (43%)
  starting transfers between devices  33.6 us (27%)
  Pallas kernels  27.8 us (22%)
  local copies, waits for them, and re-layouts  6.99 us (6%)
  other arithmetic  1.5 us (1%)
    pallas_call x1, Pallas kernels, run_step(): vmem_call(step_kernel, outs, scratch, in_specs=[smem()] * 2 + [vmem()] *...  16.9 us
    ppermute x2, waiting for transfers between devices, reduce_terms(): lax.ppermute(total, 'dp', line_pairs(2))  15.9 us
    ppermute x3, waiting for transfers between devices, lines(): lax.ppermute(shared[step], 'dp', line_pairs(step))  8.75 us
    ppermute x2, waiting for transfers between devices, reduce_terms(): from_first = lax.ppermute(keep[2:4] + came[2:4], ('section', 'rep'), FIRST)  7.69 us
    ppermute x3, starting transfers between devices, lines(): lax.ppermute(packed[step], 'dp', line_pairs(step))  7.09 us
    unnamed x70, local copies, waits for them, and re-layouts  6.32 us
    ppermute x2, waiting for transfers between devices, reduce_terms(): lax.ppermute(keep[1] + came[1] + from_first[1], ('section', 'rep'), SECOND)  5.89 us
    ppermute x3, waiting for transfers between devices, lines(): lax.ppermute(packed[step], 'dp', line_pairs(step))  4.54 us
  transfers between devices with their start and end apart: 35, of which 16 were waited for; matrix products, arithmetic and copies ran while one was open for 1% of the time, Pallas kernels for 7%

profile of v1, /device:TPU:0, one launch (start us, length us, event | category | flops | bytes accessed | tf_op | source)
XLA Modules:
  0.0 124.0 jit_solution(16373370735819126322)
XLA Ops:
  0.6 0.5 collective-permute-start.11
  1.2 0.4 collective-permute-start.9
  1.7 0.7 stack.23.info
  2.3 1.8 %shard_map.152 = (bf16[128,256]{1,0:T(8,128)(2,1)}, bf16[128,256]{1,0:T(8,128)(2,1)}, bf16[128,256]{1,0:T(8,128)(2,1)}, bf16[128,256]{1,0:T(8,128)(2,1)}) custom-call(s32[5]{0:T(128)} %stack.23.info, bf16[4,128,256]{2,1,0:T(8,128)(2,1)} %bitcast.29, bf16[4,128,256]{2,1,0:T(8,128)(2,1)} %bitcast.30), custom_call_target="tpu_custom_call" | custom-call | tf_op jit(solution)/shard_map/pallas_call | solution.py:866
  4.1 2.7 %collective-permute-start = (bf16[128,256]{1,0:T(8,128)(2,1)}, bf16[128,256]{1,0:T(8,128)(2,1)S(1)}, u32[]{:S(2)}, u32[]{:S(2)}) collective-permute-start(bf16[128,256]{1,0:T(8,128)(2,1)} %get-tuple-element.33), channel_id=1, source_target_pairs={{0,4},{4,0},{8,12},{12,8},{1,5},{5,1},{9,13},{13,9},{2,6},{6,2},{1... | collective-permute-start | bytes 196616 | tf_op jit(solution)/shard_map/ppermute | solution.py:873
  6.8 0.2 collective-permute-start.7
  6.9 1.0 collective-permute-done.7.gain_attn_far
  7.9 0.2 collective-permute-start.8
  8.1 0.9 collective-permute-done.8.gain_ffn_far
  9.1 2.6 %collective-permute-start.1 = (bf16[128,256]{1,0:T(8,128)(2,1)}, bf16[128,256]{1,0:T(8,128)(2,1)S(1)}, u32[]{:S(2)}, u32[]{:S(2)}) collective-permute-start(bf16[128,256]{1,0:T(8,128)(2,1)} %get-tuple-element.34), channel_id=1, source_target_pairs={{0,8},{4,12},{8,0},{12,4},{1,9},{5,13},{9,1},{13,5},{2,10},{6,14},... | collective-permute-start | bytes 196616 | tf_op jit(solution)/shard_map/ppermute | solution.py:873
  11.7 1.9 %collective-permute-start.2 = (bf16[128,256]{1,0:T(8,128)(2,1)}, bf16[128,256]{1,0:T(8,128)(2,1)S(1)}, u32[]{:S(2)}, u32[]{:S(2)}) collective-permute-start(bf16[128,256]{1,0:T(8,128)(2,1)} %get-tuple-element.35), channel_id=1, source_target_pairs={{0,12},{4,8},{8,4},{12,0},{1,13},{5,9},{9,5},{13,1},{2,14},{6,10},... | collective-permute-start | bytes 196616 | tf_op jit(solution)/shard_map/ppermute | solution.py:873
  13.5 2.7 %collective-permute-done.1.own2 = bf16[128,256]{1,0:T(8,128)(2,1)S(1)} collective-permute-done((bf16[128,256]{1,0:T(8,128)(2,1)}, bf16[128,256]{1,0:T(8,128)(2,1)S(1)}, u32[]{:S(2)}, u32[]{:S(2)}) %collective-permute-start.1) | collective-permute-done | bytes 65568 | tf_op jit(solution)/shard_map/ppermute | solution.py:873
  16.2 1.9 %collective-permute-done.2.own3 = bf16[128,256]{1,0:T(8,128)(2,1)S(1)} collective-permute-done((bf16[128,256]{1,0:T(8,128)(2,1)}, bf16[128,256]{1,0:T(8,128)(2,1)S(1)}, u32[]{:S(2)}, u32[]{:S(2)}) %collective-permute-start.2) | collective-permute-done | bytes 65568 | tf_op jit(solution)/shard_map/ppermute | solution.py:873
  18.1 1.5 %collective-permute-done.3.far0 = bf16[128,256]{1,0:T(8,128)(2,1)S(1)} collective-permute-done((bf16[128,256]{1,0:T(8,128)(2,1)}, bf16[128,256]{1,0:T(8,128)(2,1)S(1)}, u32[]{:S(2)}, u32[]{:S(2)}) %collective-permute-start.3) | collective-permute-done | bytes 65568 | tf_op jit(solution)/shard_map/ppermute | solution.py:875
  19.5 0.2 collective-permute-start.4
  19.7 0.4 collective-permute-start.5
  20.1 0.7 collective-permute-done.4.far1
  20.8 0.2 collective-permute-start.6
  21.0 1.1 collective-permute-done.6.far3
  22.2 0.5 copy-done.29
  22.7 0.2 copy-done.8
  22.8 0.2 copy-done.4
  23.0 0.8 copy-done.5
  23.8 16.9 %shard_map.153 = (bf16[256,256]{1,0:T(8,128)(2,1)}, bf16[256,256]{1,0:T(8,128)(2,1)}, bf16[256,256]{1,0:T(8,128)(2,1)}, f32[512,256]{1,0:T(8,128)}, bf16[4,512,2...) custom-call(s32[5]{0:T(128)} %stack.23.info, ...), custom_call_target="tpu_custom_call" | custom-call | tf_op jit(solution)/shard_map/pallas_call | solution.py:750
  40.7 0.2 collective-permute-start.27
  40.9 2.7 %collective-permute-done.27 = bf16[4,512,256]{2,1,0:T(8,128)(2,1)S(1)} collective-permute-done((bf16[4,512,256]{2,1,0:T(8,128)(2,1)}, bf16[4,512,256]{2,1,0:T(8,128)(2,1)S(1)}, u32[]{:S(2)}, u32[]{:S(2)}) %collective-permute-start.27) | collective-permute-done | bytes 1048608 | tf_op jit(solution)/shard_map/ppermute | solution.py:832
  43.6 1.1 slice_add_fusion
  44.8 1.6 %collective-permute-start.28 = (bf16[2,512,256]{2,1,0:T(8,128)(2,1)S(1)}, bf16[2,512,256]{2,1,0:T(8,128)(2,1)S(1)}, u32[]{:S(2)}, u32[]{:S(2)}) collective-permute-start(bf16[2,512,256]{2,1,0:T(8,128)(2,1)S(1)} %slice_add_fusion), channel_id=1, source_target_pairs={{0,1},{1,0},{2,3},{3,2},{16,18},{17,19},{18,16},{19,17},{4,5},{5,4... | collective-permute-start | bytes 1572872 | tf_op jit(solution)/shard_map/ppermute | solution.py:833
  46.3 7.7 %collective-permute-done.28 = bf16[2,512,256]{2,1,0:T(8,128)(2,1)S(1)} collective-permute-done((bf16[2,512,256]{2,1,0:T(8,128)(2,1)S(1)}, bf16[2,512,256]{2,1,0:T(8,128)(2,1)S(1)}, u32[]{:S(2)}, u32[]{:S(2)}) %collective-permute-start.28) | collective-permute-done | bytes 524320 | tf_op jit(solution)/shard_map/ppermute | solution.py:833
  54.1 1.6 %collective-permute-start.29 = (bf16[512,256]{1,0:T(8,128)(2,1)S(1)}, bf16[512,256]{1,0:T(8,128)(2,1)S(1)}, u32[]{:S(2)}, u32[]{:S(2)}) collective-permute-start(bf16[512,256]{1,0:T(8,128)(2,1)S(1)} %fusion), channel_id=1, source_target_pairs={{0,2},{1,3},{2,0},{3,1},{16,17},{17,16},{18,19},{19,18},{4,6},{5,7... | collective-permute-start | bytes 786440 | tf_op jit(solution)/shard_map/ppermute | solution.py:834
  55.7 1.6 %collective-permute-start.20 = (bf16[2,272,256]{2,1,0:T(8,128)(2,1)S(1)}, bf16[2,272,256]{2,1,0:T(8,128)(2,1)S(1)}, u32[]{:S(2)}, u32[]{:S(2)}) collective-permute-start(bf16[2,272,256]{2,1,0:T(8,128)(2,1)S(1)} %slice_add_fusion.1), channel_id=1, source_target_pairs={{0,1},{1,0},{2,3},{3,2},{16,18},{17,19},{18,16},{19,17},{4,5},{5,4... | collective-permute-start | bytes 835592 | tf_op jit(solution)/shard_map/ppermute | solution.py:833
  57.2 5.9 %collective-permute-done.29 = bf16[512,256]{1,0:T(8,128)(2,1)S(1)} collective-permute-done((bf16[512,256]{1,0:T(8,128)(2,1)S(1)}, bf16[512,256]{1,0:T(8,128)(2,1)S(1)}, u32[]{:S(2)}, u32[]{:S(2)}) %collective-permute-start.29) | collective-permute-done | bytes 262176 | tf_op jit(solution)/shard_map/ppermute | solution.py:834
  63.2 1.1 collective-permute-start.30
  64.4 1.6 %collective-permute-start.21 = (bf16[272,256]{1,0:T(8,128)(2,1)S(1)}, bf16[272,256]{1,0:T(8,128)(2,1)S(1)}, u32[]{:S(2)}, u32[]{:S(2)}) collective-permute-start(bf16[272,256]{1,0:T(8,128)(2,1)S(1)} %fusion.3), channel_id=1, source_target_pairs={{0,2},{1,3},{2,0},{3,1},{16,17},{17,16},{18,19},{19,18},{4,6},{5,7... | collective-permute-start | bytes 417800 | tf_op jit(solution)/shard_map/ppermute | solution.py:834
  66.0 1.3 %collective-permute-start.15 = (f32[512,256]{1,0:T(8,128)S(1)}, f32[512,256]{1,0:T(8,128)S(1)}, u32[]{:S(2)}, u32[]{:S(2)}) collective-permute-start(f32[512,256]{1,0:T(8,128)S(1)} %copy-done.6), channel_id=1, source_target_pairs={{16,0},{17,1},{18,2},{19,3},{20,4},{21,5},{22,6},{23,7},{24,8},{25... | collective-permute-start | bytes 1572872 | tf_op jit(solution)/shard_map/ppermute | solution.py:900
  67.3 2.4 %collective-permute-done.30 = bf16[512,256]{1,0:T(8,128)(2,1)S(1)} collective-permute-done((bf16[512,256]{1,0:T(8,128)(2,1)S(1)}, bf16[512,256]{1,0:T(8,128)(2,1)S(1)}, u32[]{:S(2)}, u32[]{:S(2)}) %collective-permute-start.30) | collective-permute-done | bytes 262176 | tf_op jit(solution)/shard_map/ppermute | solution.py:838
  69.7 2.6 %collective-permute-start.31 = (bf16[512,256]{1,0:T(8,128)(2,1)S(1)}, bf16[512,256]{1,0:T(8,128)(2,1)S(1)}, u32[]{:S(2)}, u32[]{:S(2)}) collective-permute-start(bf16[512,256]{1,0:T(8,128)(2,1)S(1)} %add.90), channel_id=1, source_target_pairs={{0,8},{4,12},{8,0},{12,4},{1,9},{5,13},{9,1},{13,5},{2,10},{6,14},... | collective-permute-start | bytes 786440 | tf_op jit(solution)/shard_map/ppermute | solution.py:839
  72.4 1.1 collective-permute-start.22
  73.4 9.8 %collective-permute-done.31 = bf16[512,256]{1,0:T(8,128)(2,1)S(1)} collective-permute-done((bf16[512,256]{1,0:T(8,128)(2,1)S(1)}, bf16[512,256]{1,0:T(8,128)(2,1)S(1)}, u32[]{:S(2)}, u32[]{:S(2)}) %collective-permute-start.31) | collective-permute-done | bytes 262176 | tf_op jit(solution)/shard_map/ppermute | solution.py:839
  83.4 0.6 collective-permute-start.32
  84.1 0.3 copy-done.34
  84.4 2.4 %collective-permute-start.14 = (bf16[256,256]{1,0:T(8,128)(2,1)S(1)}, bf16[256,256]{1,0:T(8,128)(2,1)S(1)}, u32[]{:S(2)}, u32[]{:S(2)}) collective-permute-start(bf16[256,256]{1,0:T(8,128)(2,1)S(1)} %copy-done.16), channel_id=1, source_target_pairs={{0,16},{1,17},{2,18},{3,19},{4,20},{5,21},{6,22},{7,23},{8,24},{9,... | collective-permute-start | bytes 393224 | tf_op jit(solution)/shard_map/ppermute | solution.py:899
  86.8 6.0 %collective-permute-done.23 = bf16[272,256]{1,0:T(8,128)(2,1)S(1)} collective-permute-done((bf16[272,256]{1,0:T(8,128)(2,1)S(1)}, bf16[272,256]{1,0:T(8,128)(2,1)S(1)}, u32[]{:S(2)}, u32[]{:S(2)}) %collective-permute-start.23) | collective-permute-done | bytes 139296 | tf_op jit(solution)/shard_map/ppermute | solution.py:839
  92.9 0.4 collective-permute-start.24
  93.3 0.6 copy-done.20
  94.0 0.2 copy-done.7
  94.1 2.4 %shard_map.154 = (bf16[256,256]{1,0:T(8,128)(2,1)}, bf16[256,256]{1,0:T(8,128)(2,1)}, bf16[256,256]{1,0:T(8,128)(2,1)}, bf16[256,256]{1,0:T(8,128)(2,1)}) custom-call(s32[5]{0:T(128)} %stack.23.info, bf16[256,256]{1,0:T(8,128)(2,1)} %get-tuple-element.36.keep, bf16[256,256]{1,0:T(8,128)(2,1)} %copy-done.20, bf16[256,256]{1,0:T(8,128)(2,1)} %get-tuple-element.38.one_near, ...), custom_call_target="tpu_custom_call" | custom-call | tf_op jit(solution)/shard_map/pallas_call | solution.py:901
  96.5 2.1 %collective-permute-start.17 = (bf16[256,256]{1,0:T(8,128)(2,1)}, bf16[256,256]{1,0:T(8,128)(2,1)S(1)}, u32[]{:S(2)}, u32[]{:S(2)}) collective-permute-start(bf16[256,256]{1,0:T(8,128)(2,1)} %get-tuple-element.42), channel_id=1, source_target_pairs={{0,8},{4,12},{8,0},{12,4},{1,9},{5,13},{9,1},{13,5},{2,10},{6,14},... | collective-permute-start | bytes 393224 | tf_op jit(solution)/shard_map/ppermute | solution.py:908
  98.7 1.2 collective-permute-start.33
  99.9 0.8 collective-permute-start.34
  100.7 3.7 %collective-permute-done.16.piece1 = bf16[256,256]{1,0:T(8,128)(2,1)S(1)} collective-permute-done((bf16[256,256]{1,0:T(8,128)(2,1)}, bf16[256,256]{1,0:T(8,128)(2,1)S(1)}, u32[]{:S(2)}, u32[]{:S(2)}) %collective-permute-start.16) | collective-permute-done | bytes 131104 | tf_op jit(solution)/shard_map/ppermute | solution.py:908
  104.4 0.3 collective-permute-start.25
  104.7 1.7 %collective-permute-start.26 = (bf16[272,256]{1,0:T(8,128)(2,1)S(1)}, bf16[272,256]{1,0:T(8,128)(2,1)S(1)}, u32[]{:S(2)}, u32[]{:S(2)}) collective-permute-start(bf16[272,256]{1,0:T(8,128)(2,1)S(1)} %collective-permute-done.24.piece1), channel_id=1, source_target_pairs={{0,1},{1,0},{2,3},{3,2},{16,18},{17,19},{18,16},{19,17},{4,5},{5,4... | collective-permute-start | bytes 417800 | tf_op jit(solution)/shard_map/ppermute | solution.py:842
  106.4 0.1 collective-permute-done.17.piece2
  106.5 2.3 %collective-permute-start.18 = (bf16[256,256]{1,0:T(8,128)(2,1)}, bf16[256,256]{1,0:T(8,128)(2,1)S(1)}, u32[]{:S(2)}, u32[]{:S(2)}) collective-permute-start(bf16[256,256]{1,0:T(8,128)(2,1)} %get-tuple-element.43), channel_id=1, source_target_pairs={{0,12},{4,8},{8,4},{12,0},{1,13},{5,9},{9,5},{13,1},{2,14},{6,10},... | collective-permute-start | bytes 393224 | tf_op jit(solution)/shard_map/ppermute | solution.py:908
  108.8 4.9 %collective-permute-done.18.piece3 = bf16[256,256]{1,0:T(8,128)(2,1)S(1)} collective-permute-done((bf16[256,256]{1,0:T(8,128)(2,1)}, bf16[256,256]{1,0:T(8,128)(2,1)S(1)}, u32[]{:S(2)}, u32[]{:S(2)}) %collective-permute-start.18) | collective-permute-done | bytes 131104 | tf_op jit(solution)/shard_map/ppermute | solution.py:908
  113.7 0.7 copy-done.22
  114.4 1.9 %shard_map.155 = (bf16[1,4,1,128,256]{4,3,2,1,0:T(8,128)(2,1)}, bf16[1,4,1,128,256]{4,3,2,1,0:T(8,128)(2,1)}) custom-call(s32[5]{0:T(128)} %stack.23.info, bf16[256,256]{1,0:T(8,128)(2,1)} %get-tuple-element.40.piece0, bf16[256,256]{1,0:T(8,128)(2,1)} %copy-done.18, bf16[256,256]{1,0:T(8,128)(2,1)} %copy-done.19, bf16[256,256]{1,0:T(8,128)(2,1)} %copy-done.22), custom_call_target="tpu_custom_call" | custom-call | tf_op jit(solution)/shard_map/pallas_call | solution.py:910
  116.3 0.6 copy-done.13
  117.0 0.7 copy-done.14
  117.7 2.2 %shard_map.156 = (f32[1,256]{1,0:T(1,128)}, f32[1,256]{1,0:T(1,128)}, f32[1,256,768]{2,1,0:T(8,128)}, f32[1,256,256]{2,1,0:T(8,128)}) custom-call(s32[5]{0:T(128)} %stack.23.info, bf16[272,256]{1,0:T(8,128)(2,1)} %copy-done.3, bf16[272,256]{1,0:T(8,128)(2,1)} %copy-done.12, bf16[272,256]{1,0:T(8,128)(2,1)} %copy-done.13, bf16[272,256]{1,0:T(8,128)(2,1)} %copy-done.14), custom_call_target="tpu_custom_call" | custom-call | tf_op jit(solution)/shard_map/pallas_call | solution.py:924
  119.8 0.7 copy-done.10
  120.5 0.7 copy-done.11
  121.2 2.7 %shard_map.157 = (f32[1,256,1024]{2,1,0:T(8,128)}, f32[1,1024,256]{2,1,0:T(8,128)}) custom-call(s32[5]{0:T(128)} %stack.23.info, bf16[512,256]{1,0:T(8,128)(2,1)} %copy-done.1, bf16[512,256]{1,0:T(8,128)(2,1)} %copy-done.9, bf16[512,256]{1,0:T(8,128)(2,1)} %copy-done.10, bf16[512,256]{1,0:T(8,128)(2,1)} %copy-done.11), custom_call_target="tpu_custom_call" | custom-call | tf_op jit(solution)/shard_map/pallas_call | solution.py:917
  (93 shorter events, 0.9 us)
Async XLA Ops:
  0.6 21.4 %collective-permute-start.11 = (bf16[256,1024]{1,0:T(8,128)(2,1)}, bf16[256,1024]{1,0:T(8,128)(2,1)S(1)}, u32[]{:S(2)}, u32[]{:S(2)}) collective-permute-start(bf16[256,1024]{1,0:T(8,128)(2,1)} %bitcast.23), channel_id=1, source_target_pairs={{0,16},{16,0},{1,17},{17,1},{2,18},{18,2},{3,19},{19,3},{4,20},{20... | collective-permute-start | bytes 1572872 | tf_op jit(solution)/shard_map/ppermute | solution.py:877
  1.1 20.9 %collective-permute-start.12 = (bf16[1024,256]{1,0:T(8,128)(2,1)}, bf16[1024,256]{1,0:T(8,128)(2,1)S(1)}, u32[]{:S(2)}, u32[]{:S(2)}) collective-permute-start(bf16[1024,256]{1,0:T(8,128)(2,1)} %bitcast.25), channel_id=1, source_target_pairs={{0,16},{16,0},{1,17},{17,1},{2,18},{18,2},{3,19},{19,3},{4,20},{20... | collective-permute-start | bytes 1572872 | tf_op jit(solution)/shard_map/ppermute | solution.py:877
  1.2 20.8 %collective-permute-start.9 = (bf16[256,768]{1,0:T(8,128)(2,1)}, bf16[256,768]{1,0:T(8,128)(2,1)S(1)}, u32[]{:S(2)}, u32[]{:S(2)}) collective-permute-start(bf16[256,768]{1,0:T(8,128)(2,1)} %bitcast.27), channel_id=1, source_target_pairs={{0,16},{16,0},{1,17},{17,1},{2,18},{18,2},{3,19},{19,3},{4,20},{20... | collective-permute-start | bytes 1179656 | tf_op jit(solution)/shard_map/ppermute | solution.py:877
  2.3 5.6 %copy-start.31 = (bf16[1,256]{1,0:T(2,128)(2,1)S(1)}, bf16[1,256]{1,0:T(2,128)(2,1)}, u32[]{:S(2)}) copy-start(bf16[1,256]{1,0:T(2,128)(2,1)} %gain_ffn_own.1) | copy-start | bytes 1540
  2.3 13.9 %copy-start.15 = (bf16[1,256,256]{2,1,0:T(8,128)(2,1)S(1)}, bf16[1,256,256]{2,1,0:T(8,128)(2,1)}, u32[]{:S(2)}) copy-start(bf16[1,256,256]{2,1,0:T(8,128)(2,1)} %param.14) | copy-start | bytes 393220
  4.1 2.7 %copy-start.30 = (bf16[1,256]{1,0:T(2,128)(2,1)S(1)}, bf16[1,256]{1,0:T(2,128)(2,1)}, u32[]{:S(2)}) copy-start(bf16[1,256]{1,0:T(2,128)(2,1)} %gain_attn_own.1) | copy-start | bytes 1540
  4.1 7.5 %collective-permute-start = (bf16[128,256]{1,0:T(8,128)(2,1)}, bf16[128,256]{1,0:T(8,128)(2,1)S(1)}, u32[]{:S(2)}, u32[]{:S(2)}) collective-permute-start(bf16[128,256]{1,0:T(8,128)(2,1)} %get-tuple-element.33), channel_id=1, source_target_pairs={{0,4},{4,0},{8,12},{12,8},{1,5},{5,1},{9,13},{13,9},{2,6},{6,2},{1... | collective-permute-start | bytes 196616 | tf_op jit(solution)/shard_map/ppermute | solution.py:873
  6.8 1.1 collective-permute-start.7
  7.9 3.7 %copy-start.32 = (bf16[1,256]{1,0:T(2,128)(2,1)}, bf16[1,256]{1,0:T(2,128)(2,1)S(1)}, u32[]{:S(2)}) copy-start(bf16[1,256]{1,0:T(2,128)(2,1)S(1)} %collective-permute-done.7.gain_attn_far) | copy-start | bytes 1540
  7.9 1.1 collective-permute-start.8
  9.1 2.6 %copy-start.33 = (bf16[1,256]{1,0:T(2,128)(2,1)}, bf16[1,256]{1,0:T(2,128)(2,1)S(1)}, u32[]{:S(2)}) copy-start(bf16[1,256]{1,0:T(2,128)(2,1)S(1)} %collective-permute-done.8.gain_ffn_far) | copy-start | bytes 1540
  9.1 7.1 %collective-permute-start.1 = (bf16[128,256]{1,0:T(8,128)(2,1)}, bf16[128,256]{1,0:T(8,128)(2,1)S(1)}, u32[]{:S(2)}, u32[]{:S(2)}) collective-permute-start(bf16[128,256]{1,0:T(8,128)(2,1)} %get-tuple-element.34), channel_id=1, source_target_pairs={{0,8},{4,12},{8,0},{12,4},{1,9},{5,13},{9,1},{13,5},{2,10},{6,14},... | collective-permute-start | bytes 196616 | tf_op jit(solution)/shard_map/ppermute | solution.py:873
  11.7 10.4 %copy-start.23 = (bf16[128,256]{1,0:T(8,128)(2,1)}, bf16[128,256]{1,0:T(8,128)(2,1)S(1)}, u32[]{:S(2)}) copy-start(bf16[128,256]{1,0:T(8,128)(2,1)S(1)} %collective-permute-done.own1) | copy-start | bytes 196612
  11.7 6.4 %collective-permute-start.2 = (bf16[128,256]{1,0:T(8,128)(2,1)}, bf16[128,256]{1,0:T(8,128)(2,1)S(1)}, u32[]{:S(2)}, u32[]{:S(2)}) collective-permute-start(bf16[128,256]{1,0:T(8,128)(2,1)} %get-tuple-element.35), channel_id=1, source_target_pairs={{0,12},{4,8},{8,4},{12,0},{1,13},{5,9},{9,5},{13,1},{2,14},{6,10},... | collective-permute-start | bytes 196616 | tf_op jit(solution)/shard_map/ppermute | solution.py:873
  16.2 5.9 %copy-start.24 = (bf16[128,256]{1,0:T(8,128)(2,1)}, bf16[128,256]{1,0:T(8,128)(2,1)S(1)}, u32[]{:S(2)}) copy-start(bf16[128,256]{1,0:T(8,128)(2,1)S(1)} %collective-permute-done.1.own2) | copy-start | bytes 196612
  16.2 3.5 %collective-permute-start.10 = (bf16[256,256]{1,0:T(8,128)(2,1)S(1)}, bf16[256,256]{1,0:T(8,128)(2,1)S(1)}, u32[]{:S(2)}, u32[]{:S(2)}) collective-permute-start(bf16[256,256]{1,0:T(8,128)(2,1)S(1)} %bitcast.32), channel_id=1, source_target_pairs={{0,16},{16,0},{1,17},{17,1},{2,18},{18,2},{3,19},{19,3},{4,20},{20... | collective-permute-start | bytes 393224 | tf_op jit(solution)/shard_map/ppermute | solution.py:877
  18.1 4.0 %copy-start.25 = (bf16[128,256]{1,0:T(8,128)(2,1)}, bf16[128,256]{1,0:T(8,128)(2,1)S(1)}, u32[]{:S(2)}) copy-start(bf16[128,256]{1,0:T(8,128)(2,1)S(1)} %collective-permute-done.2.own3) | copy-start | bytes 196612
  18.1 1.5 %collective-permute-start.3 = (bf16[128,256]{1,0:T(8,128)(2,1)}, bf16[128,256]{1,0:T(8,128)(2,1)S(1)}, u32[]{:S(2)}, u32[]{:S(2)}) collective-permute-start(bf16[128,256]{1,0:T(8,128)(2,1)} %get-tuple-element.32.own0), channel_id=1, source_target_pairs={{0,16},{16,0},{1,17},{17,1},{2,18},{18,2},{3,19},{19,3},{4,20},{20... | collective-permute-start | bytes 196616 | tf_op jit(solution)/shard_map/ppermute | solution.py:875
  19.5 2.6 %copy-start.26 = (bf16[128,256]{1,0:T(8,128)(2,1)}, bf16[128,256]{1,0:T(8,128)(2,1)S(1)}, u32[]{:S(2)}) copy-start(bf16[128,256]{1,0:T(8,128)(2,1)S(1)} %collective-permute-done.3.far0) | copy-start | bytes 196612
  19.5 1.3 %collective-permute-start.4 = (bf16[128,256]{1,0:T(8,128)(2,1)S(1)}, bf16[128,256]{1,0:T(8,128)(2,1)S(1)}, u32[]{:S(2)}, u32[]{:S(2)}) collective-permute-start(bf16[128,256]{1,0:T(8,128)(2,1)S(1)} %collective-permute-done.own1), channel_id=1, source_target_pairs={{0,16},{16,0},{1,17},{17,1},{2,18},{18,2},{3,19},{19,3},{4,20},{20... | collective-permute-start | bytes 196616 | tf_op jit(solution)/shard_map/ppermute | solution.py:875
  19.7 2.4 %copy-start.17 = (bf16[256,256]{1,0:T(8,128)(2,1)}, bf16[256,256]{1,0:T(8,128)(2,1)S(1)}, u32[]{:S(2)}) copy-start(bf16[256,256]{1,0:T(8,128)(2,1)S(1)} %collective-permute-done.10.out_far) | copy-start | bytes 393220
  19.7 1.3 %collective-permute-start.5 = (bf16[128,256]{1,0:T(8,128)(2,1)S(1)}, bf16[128,256]{1,0:T(8,128)(2,1)S(1)}, u32[]{:S(2)}, u32[]{:S(2)}) collective-permute-start(bf16[128,256]{1,0:T(8,128)(2,1)S(1)} %collective-permute-done.1.own2), channel_id=1, source_target_pairs={{0,16},{16,0},{1,17},{17,1},{2,18},{18,2},{3,19},{19,3},{4,20},{20... | collective-permute-start | bytes 196616 | tf_op jit(solution)/shard_map/ppermute | solution.py:875
  20.8 1.3 %copy-start.27 = (bf16[128,256]{1,0:T(8,128)(2,1)}, bf16[128,256]{1,0:T(8,128)(2,1)S(1)}, u32[]{:S(2)}) copy-start(bf16[128,256]{1,0:T(8,128)(2,1)S(1)} %collective-permute-done.4.far1) | copy-start | bytes 196612
  20.8 1.3 %collective-permute-start.6 = (bf16[128,256]{1,0:T(8,128)(2,1)S(1)}, bf16[128,256]{1,0:T(8,128)(2,1)S(1)}, u32[]{:S(2)}, u32[]{:S(2)}) collective-permute-start(bf16[128,256]{1,0:T(8,128)(2,1)S(1)} %collective-permute-done.2.own3), channel_id=1, source_target_pairs={{0,16},{16,0},{1,17},{17,1},{2,18},{18,2},{3,19},{19,3},{4,20},{20... | collective-permute-start | bytes 196616 | tf_op jit(solution)/shard_map/ppermute | solution.py:875
  21.0 1.2 copy-start.28
  22.1 0.8 copy-start.8
  22.1 0.9 copy-start.4
  23.0 0.8 copy-start.5
  40.7 13.3 %copy-start = (bf16[4,512,256]{2,1,0:T(8,128)(2,1)S(1)}, bf16[4,512,256]{2,1,0:T(8,128)(2,1)}, u32[]{:S(2)}) copy-start(bf16[4,512,256]{2,1,0:T(8,128)(2,1)} %get-tuple-element.52) | copy-start | bytes 3145732
  40.7 2.9 %collective-permute-start.27 = (bf16[4,512,256]{2,1,0:T(8,128)(2,1)}, bf16[4,512,256]{2,1,0:T(8,128)(2,1)S(1)}, u32[]{:S(2)}, u32[]{:S(2)}) collective-permute-start(bf16[4,512,256]{2,1,0:T(8,128)(2,1)} %get-tuple-element.53), channel_id=1, source_target_pairs={{0,16},{16,0},{1,17},{17,1},{2,18},{18,2},{3,19},{19,3},{4,20},{20... | collective-permute-start | bytes 3145736 | tf_op jit(solution)/shard_map/ppermute | solution.py:832
  44.7 10.9 %copy-start.2 = (bf16[4,272,256]{2,1,0:T(8,128)(2,1)S(1)}, bf16[4,272,256]{2,1,0:T(8,128)(2,1)}, u32[]{:S(2)}) copy-start(bf16[4,272,256]{2,1,0:T(8,128)(2,1)} %get-tuple-element.46) | copy-start | bytes 1671172
  44.8 9.2 %collective-permute-start.28 = (bf16[2,512,256]{2,1,0:T(8,128)(2,1)S(1)}, bf16[2,512,256]{2,1,0:T(8,128)(2,1)S(1)}, u32[]{:S(2)}, u32[]{:S(2)}) collective-permute-start(bf16[2,512,256]{2,1,0:T(8,128)(2,1)S(1)} %slice_add_fusion), channel_id=1, source_target_pairs={{0,1},{1,0},{2,3},{3,2},{16,18},{17,19},{18,16},{19,17},{4,5},{5,4... | collective-permute-start | bytes 1572872 | tf_op jit(solution)/shard_map/ppermute | solution.py:833
  46.3 9.3 %collective-permute-start.19 = (bf16[4,272,256]{2,1,0:T(8,128)(2,1)}, bf16[4,272,256]{2,1,0:T(8,128)(2,1)S(1)}, u32[]{:S(2)}, u32[]{:S(2)}) collective-permute-start(bf16[4,272,256]{2,1,0:T(8,128)(2,1)} %get-tuple-element.47), channel_id=1, source_target_pairs={{0,16},{16,0},{1,17},{17,1},{2,18},{18,2},{3,19},{19,3},{4,20},{20... | collective-permute-start | bytes 1671176 | tf_op jit(solution)/shard_map/ppermute | solution.py:832
  54.1 9.1 %collective-permute-start.29 = (bf16[512,256]{1,0:T(8,128)(2,1)S(1)}, bf16[512,256]{1,0:T(8,128)(2,1)S(1)}, u32[]{:S(2)}, u32[]{:S(2)}) collective-permute-start(bf16[512,256]{1,0:T(8,128)(2,1)S(1)} %fusion), channel_id=1, source_target_pairs={{0,2},{1,3},{2,0},{3,1},{16,17},{17,16},{18,19},{19,18},{4,6},{5,7... | collective-permute-start | bytes 786440 | tf_op jit(solution)/shard_map/ppermute | solution.py:834
  55.7 8.7 %collective-permute-start.20 = (bf16[2,272,256]{2,1,0:T(8,128)(2,1)S(1)}, bf16[2,272,256]{2,1,0:T(8,128)(2,1)S(1)}, u32[]{:S(2)}, u32[]{:S(2)}) collective-permute-start(bf16[2,272,256]{2,1,0:T(8,128)(2,1)S(1)} %slice_add_fusion.1), channel_id=1, source_target_pairs={{0,1},{1,0},{2,3},{3,2},{16,18},{17,19},{18,16},{19,17},{4,5},{5,4... | collective-permute-start | bytes 835592 | tf_op jit(solution)/shard_map/ppermute | solution.py:833
  63.2 2.8 %copy-start.6 = (f32[512,256]{1,0:T(8,128)S(1)}, f32[512,256]{1,0:T(8,128)}, u32[]{:S(2)}) copy-start(f32[512,256]{1,0:T(8,128)} %get-tuple-element.39.zero_near) | copy-start | bytes 1572868
  63.2 6.4 %collective-permute-start.30 = (bf16[512,256]{1,0:T(8,128)(2,1)S(1)}, bf16[512,256]{1,0:T(8,128)(2,1)S(1)}, u32[]{:S(2)}, u32[]{:S(2)}) collective-permute-start(bf16[512,256]{1,0:T(8,128)(2,1)S(1)} %fusion.2), channel_id=1, source_target_pairs={{0,4},{4,0},{8,12},{12,8},{1,5},{5,1},{9,13},{13,9},{2,6},{6,2},{1... | collective-permute-start | bytes 786440 | tf_op jit(solution)/shard_map/ppermute | solution.py:838
  64.4 8.0 %collective-permute-start.21 = (bf16[272,256]{1,0:T(8,128)(2,1)S(1)}, bf16[272,256]{1,0:T(8,128)(2,1)S(1)}, u32[]{:S(2)}, u32[]{:S(2)}) collective-permute-start(bf16[272,256]{1,0:T(8,128)(2,1)S(1)} %fusion.3), channel_id=1, source_target_pairs={{0,2},{1,3},{2,0},{3,1},{16,17},{17,16},{18,19},{19,18},{4,6},{5,7... | collective-permute-start | bytes 417800 | tf_op jit(solution)/shard_map/ppermute | solution.py:834
  66.0 27.3 %collective-permute-start.15 = (f32[512,256]{1,0:T(8,128)S(1)}, f32[512,256]{1,0:T(8,128)S(1)}, u32[]{:S(2)}, u32[]{:S(2)}) collective-permute-start(f32[512,256]{1,0:T(8,128)S(1)} %copy-done.6), channel_id=1, source_target_pairs={{16,0},{17,1},{18,2},{19,3},{20,4},{21,5},{22,6},{23,7},{24,8},{25... | collective-permute-start | bytes 1572872 | tf_op jit(solution)/shard_map/ppermute | solution.py:900
  69.7 13.6 %collective-permute-start.31 = (bf16[512,256]{1,0:T(8,128)(2,1)S(1)}, bf16[512,256]{1,0:T(8,128)(2,1)S(1)}, u32[]{:S(2)}, u32[]{:S(2)}) collective-permute-start(bf16[512,256]{1,0:T(8,128)(2,1)S(1)} %add.90), channel_id=1, source_target_pairs={{0,8},{4,12},{8,0},{12,4},{1,9},{5,13},{9,1},{13,5},{2,10},{6,14},... | collective-permute-start | bytes 786440 | tf_op jit(solution)/shard_map/ppermute | solution.py:839
  72.4 11.6 %collective-permute-start.22 = (bf16[272,256]{1,0:T(8,128)(2,1)S(1)}, bf16[272,256]{1,0:T(8,128)(2,1)S(1)}, u32[]{:S(2)}, u32[]{:S(2)}) collective-permute-start(bf16[272,256]{1,0:T(8,128)(2,1)S(1)} %fusion.5), channel_id=1, source_target_pairs={{0,4},{4,0},{8,12},{12,8},{1,5},{5,1},{9,13},{13,9},{2,6},{6,2},{1... | collective-permute-start | bytes 417800 | tf_op jit(solution)/shard_map/ppermute | solution.py:838
  83.4 15.3 %copy-start.1 = (bf16[512,256]{1,0:T(8,128)(2,1)}, bf16[512,256]{1,0:T(8,128)(2,1)S(1)}, u32[]{:S(2)}) copy-start(bf16[512,256]{1,0:T(8,128)(2,1)S(1)} %add.91.piece0) | copy-start | bytes 786436
  83.4 1.0 copy-start.34
  83.4 1.1 copy-start.16
  83.4 16.5 %collective-permute-start.32 = (bf16[512,256]{1,0:T(8,128)(2,1)S(1)}, bf16[512,256]{1,0:T(8,128)(2,1)S(1)}, u32[]{:S(2)}, u32[]{:S(2)}) collective-permute-start(bf16[512,256]{1,0:T(8,128)(2,1)S(1)} %add.91.piece0), channel_id=1, source_target_pairs={{0,2},{1,3},{2,0},{3,1},{16,17},{17,16},{18,19},{19,18},{4,6},{5,7... | collective-permute-start | bytes 786440 | tf_op jit(solution)/shard_map/ppermute | solution.py:840
  84.0 8.8 %collective-permute-start.23 = (bf16[272,256]{1,0:T(8,128)(2,1)S(1)}, bf16[272,256]{1,0:T(8,128)(2,1)S(1)}, u32[]{:S(2)}, u32[]{:S(2)}) collective-permute-start(bf16[272,256]{1,0:T(8,128)(2,1)S(1)} %add.80), channel_id=1, source_target_pairs={{0,8},{4,12},{8,0},{12,4},{1,9},{5,13},{9,1},{13,5},{2,10},{6,14},... | collective-permute-start | bytes 417800 | tf_op jit(solution)/shard_map/ppermute | solution.py:839
  84.4 8.9 %collective-permute-start.13 = (bf16[256,256]{1,0:T(8,128)(2,1)S(1)}, bf16[256,256]{1,0:T(8,128)(2,1)S(1)}, u32[]{:S(2)}, u32[]{:S(2)}) collective-permute-start(bf16[256,256]{1,0:T(8,128)(2,1)S(1)} %copy-done.34), channel_id=1, source_target_pairs={{0,16},{16,0},{1,17},{17,1},{2,18},{18,2},{3,19},{19,3},{4,20},{20... | collective-permute-start | bytes 393224 | tf_op jit(solution)/shard_map/ppermute | solution.py:898
  84.4 8.8 %collective-permute-start.14 = (bf16[256,256]{1,0:T(8,128)(2,1)S(1)}, bf16[256,256]{1,0:T(8,128)(2,1)S(1)}, u32[]{:S(2)}, u32[]{:S(2)}) collective-permute-start(bf16[256,256]{1,0:T(8,128)(2,1)S(1)} %copy-done.16), channel_id=1, source_target_pairs={{0,16},{1,17},{2,18},{3,19},{4,20},{5,21},{6,22},{7,23},{8,24},{9,... | collective-permute-start | bytes 393224 | tf_op jit(solution)/shard_map/ppermute | solution.py:899
  92.9 11.5 %copy-start.3 = (bf16[272,256]{1,0:T(8,128)(2,1)}, bf16[272,256]{1,0:T(8,128)(2,1)S(1)}, u32[]{:S(2)}) copy-start(bf16[272,256]{1,0:T(8,128)(2,1)S(1)} %add.81.piece0) | copy-start | bytes 417796
  92.9 11.8 %collective-permute-start.24 = (bf16[272,256]{1,0:T(8,128)(2,1)S(1)}, bf16[272,256]{1,0:T(8,128)(2,1)S(1)}, u32[]{:S(2)}, u32[]{:S(2)}) collective-permute-start(bf16[272,256]{1,0:T(8,128)(2,1)S(1)} %add.81.piece0), channel_id=1, source_target_pairs={{0,2},{1,3},{2,0},{3,1},{16,17},{17,16},{18,19},{19,18},{4,6},{5,7... | collective-permute-start | bytes 417800 | tf_op jit(solution)/shard_map/ppermute | solution.py:840
  93.3 0.7 copy-start.21
  93.3 0.9 copy-start.7
  96.5 7.9 %collective-permute-start.16 = (bf16[256,256]{1,0:T(8,128)(2,1)}, bf16[256,256]{1,0:T(8,128)(2,1)S(1)}, u32[]{:S(2)}, u32[]{:S(2)}) collective-permute-start(bf16[256,256]{1,0:T(8,128)(2,1)} %get-tuple-element.41), channel_id=1, source_target_pairs={{0,4},{4,0},{8,12},{12,8},{1,5},{5,1},{9,13},{13,9},{2,6},{6,2},{1... | collective-permute-start | bytes 393224 | tf_op jit(solution)/shard_map/ppermute | solution.py:908
  96.5 10.0 %collective-permute-start.17 = (bf16[256,256]{1,0:T(8,128)(2,1)}, bf16[256,256]{1,0:T(8,128)(2,1)S(1)}, u32[]{:S(2)}, u32[]{:S(2)}) collective-permute-start(bf16[256,256]{1,0:T(8,128)(2,1)} %get-tuple-element.42), channel_id=1, source_target_pairs={{0,8},{4,12},{8,0},{12,4},{1,9},{5,13},{9,1},{13,5},{2,10},{6,14},... | collective-permute-start | bytes 393224 | tf_op jit(solution)/shard_map/ppermute | solution.py:908
  98.7 21.2 %collective-permute-start.33 = (bf16[512,256]{1,0:T(8,128)(2,1)S(1)}, bf16[512,256]{1,0:T(8,128)(2,1)S(1)}, u32[]{:S(2)}, u32[]{:S(2)}) collective-permute-start(bf16[512,256]{1,0:T(8,128)(2,1)S(1)} %add.91.piece0), channel_id=1, source_target_pairs={{0,1},{1,0},{2,3},{3,2},{16,18},{17,19},{18,16},{19,17},{4,5},{5,4... | collective-permute-start | bytes 786440 | tf_op jit(solution)/shard_map/ppermute | solution.py:841
  99.9 16.4 %copy-start.9 = (bf16[512,256]{1,0:T(8,128)(2,1)}, bf16[512,256]{1,0:T(8,128)(2,1)S(1)}, u32[]{:S(2)}) copy-start(bf16[512,256]{1,0:T(8,128)(2,1)S(1)} %collective-permute-done.32.piece1) | copy-start | bytes 786436
  99.9 19.9 %collective-permute-start.34 = (bf16[512,256]{1,0:T(8,128)(2,1)S(1)}, bf16[512,256]{1,0:T(8,128)(2,1)S(1)}, u32[]{:S(2)}, u32[]{:S(2)}) collective-permute-start(bf16[512,256]{1,0:T(8,128)(2,1)S(1)} %collective-permute-done.32.piece1), channel_id=1, source_target_pairs={{0,1},{1,0},{2,3},{3,2},{16,18},{17,19},{18,16},{19,17},{4,5},{5,4... | collective-permute-start | bytes 786440 | tf_op jit(solution)/shard_map/ppermute | solution.py:842
  104.4 9.4 %copy-start.18 = (bf16[256,256]{1,0:T(8,128)(2,1)}, bf16[256,256]{1,0:T(8,128)(2,1)S(1)}, u32[]{:S(2)}) copy-start(bf16[256,256]{1,0:T(8,128)(2,1)S(1)} %collective-permute-done.16.piece1) | copy-start | bytes 393220
  104.4 11.9 %collective-permute-start.25 = (bf16[272,256]{1,0:T(8,128)(2,1)S(1)}, bf16[272,256]{1,0:T(8,128)(2,1)S(1)}, u32[]{:S(2)}, u32[]{:S(2)}) collective-permute-start(bf16[272,256]{1,0:T(8,128)(2,1)S(1)} %add.81.piece0), channel_id=1, source_target_pairs={{0,1},{1,0},{2,3},{3,2},{16,18},{17,19},{18,16},{19,17},{4,5},{5,4... | collective-permute-start | bytes 417800 | tf_op jit(solution)/shard_map/ppermute | solution.py:841
  104.7 11.6 %copy-start.12 = (bf16[272,256]{1,0:T(8,128)(2,1)}, bf16[272,256]{1,0:T(8,128)(2,1)S(1)}, u32[]{:S(2)}) copy-start(bf16[272,256]{1,0:T(8,128)(2,1)S(1)} %collective-permute-done.24.piece1) | copy-start | bytes 417796
  104.7 11.6 %collective-permute-start.26 = (bf16[272,256]{1,0:T(8,128)(2,1)S(1)}, bf16[272,256]{1,0:T(8,128)(2,1)S(1)}, u32[]{:S(2)}, u32[]{:S(2)}) collective-permute-start(bf16[272,256]{1,0:T(8,128)(2,1)S(1)} %collective-permute-done.24.piece1), channel_id=1, source_target_pairs={{0,1},{1,0},{2,3},{3,2},{16,18},{17,19},{18,16},{19,17},{4,5},{5,4... | collective-permute-start | bytes 417800 | tf_op jit(solution)/shard_map/ppermute | solution.py:842
  106.5 7.2 %copy-start.19 = (bf16[256,256]{1,0:T(8,128)(2,1)}, bf16[256,256]{1,0:T(8,128)(2,1)S(1)}, u32[]{:S(2)}) copy-start(bf16[256,256]{1,0:T(8,128)(2,1)S(1)} %collective-permute-done.17.piece2) | copy-start | bytes 393220
  106.5 7.2 %collective-permute-start.18 = (bf16[256,256]{1,0:T(8,128)(2,1)}, bf16[256,256]{1,0:T(8,128)(2,1)S(1)}, u32[]{:S(2)}, u32[]{:S(2)}) collective-permute-start(bf16[256,256]{1,0:T(8,128)(2,1)} %get-tuple-element.43), channel_id=1, source_target_pairs={{0,12},{4,8},{8,4},{12,0},{1,13},{5,9},{9,5},{13,1},{2,14},{6,10},... | collective-permute-start | bytes 393224 | tf_op jit(solution)/shard_map/ppermute | solution.py:908
  120.5 0.7 copy-start.11
  (6 other events, 4.0 us)

commit v2 on v0

--- a/solution.py
+++ b/solution.py
@@ -3,6 +3,8 @@
 import jax
 import jax.numpy as jnp
 from jax import lax
+from jax.experimental import pallas as pl
+from jax.experimental.pallas import tpu as pltpu
 from jax.sharding import PartitionSpec as P
 
 HEADS = 2
@@ -67,7 +69,7 @@
     return ((shifted / row_total).astype(jnp.bfloat16), (row_max + jnp.log(row_total))[..., 0])
 
 
-def local(
+def general(
     block_input,
     output_grad,
     seq_lengths,
@@ -298,6 +300,912 @@
     )
 
 
+BF = jnp.bfloat16
+F32 = jnp.float32
+MIB = 1024 * 1024
+GAIN_ROWS = 32
+
+
+def call(body, scalars, arrays, shapes, mib=24, micros=1.0, scratch=(), held=0):
+    in_specs = [pl.BlockSpec(memory_space=pltpu.SMEM)] * len(scalars)
+    in_specs += [pl.BlockSpec(memory_space=pl.ANY)] * held
+    in_specs += [pl.BlockSpec(memory_space=pltpu.VMEM)] * (len(arrays) - held)
+    return pl.pallas_call(
+        body,
+        out_shape=tuple(jax.ShapeDtypeStruct(*shape) for shape in shapes),
+        in_specs=in_specs,
+        out_specs=tuple(pl.BlockSpec(memory_space=pltpu.VMEM) for _ in shapes),
+        scratch_shapes=list(scratch),
+        compiler_params=pltpu.CompilerParams(vmem_limit_bytes=mib * MIB),
+        cost_estimate=pl.CostEstimate(
+            flops=int(micros * 1.1e9), bytes_accessed=int(micros * 3.4e6), transcendentals=0
+        ),
+    )(
+        *scalars,
+        *(pltpu.with_memory_space_constraint(array, pltpu.HBM) for array in arrays[:held]),
+        *arrays[held:],
+    )
+
+
+SEC, ZED, REP, FLIP = 0, 1, 2, 3
+
+
+def rows_at(start, count):
+    return pl.ds(pl.multiple_of(start, count), count)
+
+
+def pack_kernel(info, tokens, grads, gain_attn, gain_ffn, *rest):
+    *pieces, gains, sems, gain_sems = rest
+    block = tokens.shape[2]
+    half = block // 2
+    rows = rows_at(info[SEC] * half, half)
+    copies = [
+        pltpu.make_async_copy(gain_attn, gains.at[0], gain_sems.at[0]),
+        pltpu.make_async_copy(gain_ffn, gains.at[1], gain_sems.at[1]),
+    ]
+    for step, piece in enumerate(pieces):
+        micro = info[ZED] ^ step
+        for part, source in enumerate((tokens, grads)):
+            copies.append(
+                pltpu.make_async_copy(
+                    source.at[micro, 0, rows],
+                    piece.at[part * half : (part + 1) * half],
+                    sems.at[2 * step + part],
+                )
+            )
+    for copy in copies:
+        copy.start()
+    for copy in copies:
+        copy.wait()
+    pieces[0][block:, :] = jnp.concatenate(
+        [
+            gains[0].astype(F32),
+            gains[1].astype(F32),
+            jnp.zeros((pieces[0].shape[0] - block - 2, gains.shape[2]), F32),
+        ],
+        axis=0,
+    ).astype(BF)
+
+
+def unit(values):
+    centered = values - jnp.mean(values, axis=-1, keepdims=True)
+    inverse = lax.rsqrt(jnp.mean(centered * centered, axis=-1, keepdims=True) + 1e-05)
+    return centered * inverse, inverse
+
+
+def unit_back(grad, normal, inverse):
+    return inverse * (
+        grad
+        - jnp.mean(grad, axis=-1, keepdims=True)
+        - normal * jnp.mean(grad * normal, axis=-1, keepdims=True)
+    )
+
+
+def widened(column, width):
+    return jnp.broadcast_to(column, (column.shape[0], width))
+
+
+def segment_at(ends, position):
+    total = jnp.zeros(position.shape, jnp.int32)
+    for end in ends:
+        total = total + (position >= end).astype(jnp.int32)
+    return total
+
+
+def ends_of(info, lengths):
+    ends = []
+    so_far = jnp.int32(0)
+    for slot in range(lengths.shape[2]):
+        so_far = so_far + lengths[info[ZED], info[REP], slot]
+        ends.append(so_far)
+    return ends
+
+
+def normalized_exp(scores):
+    shifted = jnp.exp(scores - jnp.max(scores, axis=-1, keepdims=True))
+    return shifted * (1.0 / jnp.sum(shifted, axis=-1, keepdims=True))
+
+
+def ffn_forward(hidden, attended, gain, w_out, w_up, w_down, saved):
+    result, middle_unit, middle_inverse, second_ref, active, slope = saved
+    middle = hidden + product(attended, w_out)
+    normal, inverse = unit(middle)
+    middle_unit[...] = normal
+    middle_inverse[...] = widened(inverse, middle_inverse.shape[1])
+    second = (normal * gain).astype(BF)
+    second_ref[...] = second
+    chunk = middle.shape[1]
+    total = middle
+    for index in range(w_up.shape[1] // chunk):
+        columns = slice(index * chunk, (index + 1) * chunk)
+        pre_act = product(second, w_up[:, columns])
+        below = 0.5 + 0.5 * lax.erf(pre_act * (0.5**0.5))
+        now = (pre_act * below).astype(BF)
+        active[:, columns] = now
+        slope[:, columns] = below + pre_act * (
+            jnp.exp(-0.5 * pre_act * pre_act) * 0.3989422804014327
+        )
+        total = total + product(now, w_down[columns, :])
+    result[...] = total.astype(BF)
+
+
+def own_unit(spot, half):
+    return slice((2 * spot + 2) * half, (2 * spot + 3) * half)
+
+
+def key_units(spot, half):
+    return slice(2 * spot * half, (2 * spot + 3) * half)
+
+
+def zero_forward_kernel(
+    info,
+    lengths,
+    own0,
+    own1,
+    own2,
+    own3,
+    far0,
+    far1,
+    far2,
+    far3,
+    w_qkv,
+    w_out,
+    w_up,
+    w_down,
+    gains,
+    line,
+    normal_all,
+    inverse_all,
+    normed_all,
+    query,
+    padded,
+    probs_ref,
+    attended_ref,
+    cotangent,
+    *saved,
+):
+    section = info[SEC]
+    reached, width = normal_all.shape
+    half = line.shape[0] // 10
+    block = 2 * half
+    blocks = 4
+    rows = blocks * half
+    head = width // HEADS
+    scale = float(head) ** (-0.5)
+    reach = block + half
+    line[:block, :] = jnp.zeros((block, width), BF)
+    for step, (near, far) in enumerate(((own0, far0), (own1, far1), (own2, far2), (own3, far3))):
+        spot = info[ZED] ^ step
+        line[rows_at(spot * block + block, half), :] = near[:half, :]
+        line[rows_at(spot * block + block + half - section * block, half), :] = far[:half, :]
+        cotangent[rows_at(spot * half, half), :] = near[half:block, :]
+    normal, inverse = unit(line[:reached, :].astype(F32))
+    normal_all[...] = normal
+    inverse_all[...] = widened(inverse, inverse_all.shape[1])
+    normed = (normal * gains[0, 0:1, :]).astype(BF)
+    normed_all[...] = normed
+    padded[...] = product(normed, w_qkv[0, :, width:]).astype(BF)
+    normed_mine = jnp.concatenate(
+        [normed[own_unit(spot, half), :] for spot in range(blocks)], axis=0
+    )
+    query[...] = product(normed_mine, w_qkv[0, :, :width]).astype(BF)
+    ends = ends_of(info, lengths)
+    row = lax.broadcasted_iota(jnp.int32, (rows, reach), 0)
+    query_pos = block * (row // half) + section * half + (row & (half - 1))
+    key_pos = query_pos - (row & (half - 1)) - block
+    key_pos = key_pos + lax.broadcasted_iota(jnp.int32, (rows, reach), 1)
+    offset = query_pos - key_pos
+    segment = segment_at(ends, query_pos)
+    same = (segment == segment_at(ends, key_pos)) & (segment < len(ends)) & (key_pos >= 0)
+    mask = same & (offset >= 0) & (offset < STRIDE) | (offset == 0)
+    spots = [(slice(spot * half, (spot + 1) * half), key_units(spot, half)) for spot in range(blocks)]
+    heads = [
+        (slice(number * head, (number + 1) * head), slice(width + number * head, width + (number + 1) * head))
+        for number in range(HEADS)
+    ]
+    scores = [
+        jnp.concatenate(
+            [contract_cols(query[here, columns], padded[window, columns]) for here, window in spots],
+            axis=0,
+        )
+        for columns, _ in heads
+    ]
+    probs = [normalized_exp(jnp.where(mask, values * scale, NEG)) for values in scores]
+    attended = []
+    for number, (_, value_columns) in enumerate(heads):
+        probs_ref[number] = probs[number]
+        low = probs[number].astype(BF)
+        attended.append(
+            jnp.concatenate(
+                [product(low[here, :], padded[window, value_columns]) for here, window in spots], axis=0
+            )
+        )
+    attended = jnp.concatenate(attended, axis=1).astype(BF)
+    attended_ref[...] = attended
+    hidden = jnp.concatenate([line[own_unit(spot, half), :] for spot in range(blocks)], axis=0)
+    ffn_forward(
+        hidden.astype(F32), attended, gains[0, 1:2, :], w_out[0], w_up.at[0], w_down.at[0], saved
+    )
+
+
+def one_forward_kernel(
+    info,
+    lengths,
+    hidden_ref,
+    w_qkv,
+    w_out,
+    w_up,
+    w_down,
+    gains,
+    normal_ref,
+    inverse_ref,
+    normed_ref,
+    packed,
+    probs_ref,
+    attended_ref,
+    *saved,
+):
+    section = info[SEC]
+    rows, width = hidden_ref.shape
+    half = rows // 4
+    block = 2 * half
+    head = width // HEADS
+    scale = float(head) ** (-0.5)
+    hidden = hidden_ref[...].astype(F32)
+    normal, inverse = unit(hidden)
+    normal_ref[...] = normal
+    inverse_ref[...] = widened(inverse, inverse_ref.shape[1])
+    normed = (normal * gains[1, 0:1, :]).astype(BF)
+    normed_ref[...] = normed
+    packed[...] = product(normed, w_qkv[1]).astype(BF)
+    ends = ends_of(info, lengths)
+
+    def place(axis):
+        index = lax.broadcasted_iota(jnp.int32, (rows, rows), axis)
+        return block * (index // half) + section * half + (index & (half - 1))
+
+    query_pos, key_pos = place(0), place(1)
+    offset = query_pos - key_pos
+    segment = segment_at(ends, query_pos)
+    same = (segment == segment_at(ends, key_pos)) & (segment < len(ends))
+    mask = same & (offset >= 0) & ((offset & (STRIDE - 1)) == 0) | (offset == 0)
+    heads = [
+        tuple(
+            slice(part * width + number * head, part * width + (number + 1) * head) for part in range(3)
+        )
+        for number in range(HEADS)
+    ]
+    scores = [contract_cols(packed[:, near], packed[:, far]) for near, far, _ in heads]
+    probs = [normalized_exp(jnp.where(mask, values * scale, NEG)) for values in scores]
+    parts = []
+    for number, (_, _, value_columns) in enumerate(heads):
+        probs_ref[number] = probs[number]
+        parts.append(product(probs[number].astype(BF), packed[:, value_columns]))
+    attended = jnp.concatenate(parts, axis=1).astype(BF)
+    attended_ref[...] = attended
+    ffn_forward(hidden, attended, gains[1, 1:2, :], w_out[1], w_up.at[1], w_down.at[1], saved)
+
+
+def store_block(info, terms, number, value):
+    width = value.shape[1]
+    unit_rows = width // 2
+    core, number = divmod(number, 6)
+    side, flip = info[SEC] ^ core, info[FLIP + core]
+    value = value.astype(BF)
+    for part in range(2):
+        quarter, place = divmod(2 * number + part, 3)
+        terms[side, flip ^ quarter, place * unit_rows : (place + 1) * unit_rows, :] = value[
+            part * unit_rows : (part + 1) * unit_rows, :
+        ]
+
+
+def store_gains(info, terms, attn_term, ffn_term):
+    spare, width = terms.shape[2] - GAIN_ROWS, terms.shape[3]
+    value = jnp.concatenate(
+        [attn_term, ffn_term, jnp.zeros((GAIN_ROWS - 2, width), F32)], axis=0
+    ).astype(BF)
+    for side in range(2):
+        for quarter in range(4):
+            terms[side, quarter, spare:, :] = value
+
+
+def ffn_input_grad(grad_out, saved, gain, w_out, w_up, w_down, grad_pre_ref):
+    middle_unit, middle_inverse, slope = saved
+    width = grad_out.shape[1]
+    grad_second = None
+    for index in range(w_up.shape[1] // width):
+        columns = slice(index * width, (index + 1) * width)
+        grad_active = contract_cols(grad_out, w_down[columns, :])
+        grad_pre = (grad_active * slope[:, columns]).astype(BF)
+        grad_pre_ref[:, columns] = grad_pre
+        term = contract_cols(grad_pre, w_up[:, columns])
+        grad_second = term if grad_second is None else grad_second + term
+    normal = middle_unit[...]
+    gain_term = jnp.sum(grad_second * normal, axis=0, keepdims=True)
+    grad_middle = grad_out.astype(F32) + unit_back(
+        grad_second * gain, normal, middle_inverse[:, 0:1]
+    )
+    return grad_middle, contract_cols(grad_middle.astype(BF), w_out).astype(BF), gain_term
+
+
+def ffn_weight_grads(info, terms, grad_out, grad_middle, second, active, attended, grad_pre):
+    width = grad_out.shape[1]
+    store_block(info, terms, 3, contract_rows(attended[...], grad_middle.astype(BF)))
+    for index in range(active.shape[1] // width):
+        columns = slice(index * width, (index + 1) * width)
+        store_block(info, terms, 4 + index, contract_rows(second[...], grad_pre[:, columns]))
+        store_block(info, terms, 8 + index, contract_rows(active[:, columns], grad_out))
+
+
+def one_backward_kernel(
+    info,
+    grad_ref,
+    w_qkv,
+    w_out,
+    w_up,
+    w_down,
+    gains,
+    normal_ref,
+    inverse_ref,
+    normed_ref,
+    packed,
+    probs_ref,
+    *rest,
+):
+    middle_unit, middle_inverse, second, active, slope, attended, grad_in, terms, grad_pre = rest
+    width = grad_ref.shape[1]
+    head = width // HEADS
+    scale = float(head) ** (-0.5)
+    grad_out = grad_ref[...]
+    grad_middle, grad_att, ffn_term = ffn_input_grad(
+        grad_out,
+        (middle_unit, middle_inverse, slope),
+        gains[1, 1:2, :],
+        w_out[1],
+        w_up.at[1],
+        w_down.at[1],
+        grad_pre,
+    )
+    ffn_weight_grads(info, terms, grad_out, grad_middle, second, active, attended, grad_pre)
+    heads = [
+        tuple(
+            slice(part * width + number * head, part * width + (number + 1) * head) for part in range(3)
+        )
+        for number in range(HEADS)
+    ]
+    probs = [probs_ref[number] for number in range(HEADS)]
+    grad_probs = [
+        contract_cols(grad_att[:, near], packed[:, value_columns]) for near, _, value_columns in heads
+    ]
+    grad_scores = [
+        (prob * (grad - jnp.sum(prob * grad, axis=-1, keepdims=True))).astype(BF)
+        for prob, grad in zip(probs, grad_probs)
+    ]
+    grad_parts = [
+        [product(grad, packed[:, far]) * scale for grad, (_, far, _) in zip(grad_scores, heads)],
+        [contract_rows(grad, packed[:, near]) * scale for grad, (near, _, _) in zip(grad_scores, heads)],
+        [contract_rows(prob.astype(BF), grad_att[:, near]) for prob, (near, _, _) in zip(probs, heads)],
+    ]
+    grad_normed = None
+    for index in range(3):
+        columns = slice(index * width, (index + 1) * width)
+        grad_block = jnp.concatenate(grad_parts[index], axis=1).astype(BF)
+        term = contract_cols(grad_block, w_qkv[1, :, columns])
+        grad_normed = term if grad_normed is None else grad_normed + term
+        store_block(info, terms, index, contract_rows(normed_ref[...], grad_block))
+    normal = normal_ref[...]
+    store_gains(info, terms, jnp.sum(grad_normed * normal, axis=0, keepdims=True), ffn_term)
+    grad_in[...] = (
+        grad_middle + unit_back(grad_normed * gains[1, 0:1, :], normal, inverse_ref[:, 0:1])
+    ).astype(BF)
+
+
+def zero_ffn_kernel(
+    grad_ref,
+    w_out,
+    w_up,
+    w_down,
+    gains,
+    middle_unit,
+    middle_inverse,
+    slope,
+    grad_middle_ref,
+    grad_att_ref,
+    grad_pre,
+    gain_term,
+):
+    grad_middle, grad_att, term = ffn_input_grad(
+        grad_ref[...],
+        (middle_unit, middle_inverse, slope),
+        gains[0, 1:2, :],
+        w_out[0],
+        w_up.at[0],
+        w_down.at[0],
+        grad_pre,
+    )
+    grad_middle_ref[...] = grad_middle
+    grad_att_ref[...] = grad_att
+    gain_term[...] = term
+
+
+def zero_backward_kernel(
+    info,
+    grad_ref,
+    w_qkv,
+    gains,
+    normal_all,
+    inverse_all,
+    normed_all,
+    query,
+    padded,
+    probs_ref,
+    result_zero,
+    result_one,
+    second,
+    active,
+    attended,
+    grad_middle_ref,
+    grad_att_ref,
+    grad_pre,
+    ffn_term,
+    result_keep,
+    grad_line,
+    swap,
+    terms,
+):
+    section = info[SEC]
+    rows, width = grad_ref.shape
+    reached = normal_all.shape[0]
+    half = rows // 4
+    blocks = 4
+    head = width // HEADS
+    scale = float(head) ** (-0.5)
+    grad_out = grad_ref[...]
+
+    @pl.when(section == 0)
+    def _():
+        result_keep[...] = result_zero[...]
+        swap[:rows, :] = result_one[...]
+
+    @pl.when(section == 1)
+    def _():
+        result_keep[...] = result_one[...]
+        swap[:rows, :] = result_zero[...]
+
+    grad_middle = grad_middle_ref[...]
+    grad_att = grad_att_ref[...]
+    ffn_weight_grads(info, terms, grad_out, grad_middle, second, active, attended, grad_pre)
+    spots = [(slice(spot * half, (spot + 1) * half), key_units(spot, half)) for spot in range(blocks)]
+    heads = [
+        (slice(number * head, (number + 1) * head), slice(width + number * head, width + (number + 1) * head))
+        for number in range(HEADS)
+    ]
+    probs = [probs_ref[number] for number in range(HEADS)]
+    grad_probs = [
+        jnp.concatenate(
+            [
+                contract_cols(grad_att[here, columns], padded[window, value_columns])
+                for here, window in spots
+            ],
+            axis=0,
+        )
+        for columns, value_columns in heads
+    ]
+    grad_scores = [
+        (prob * (grad - jnp.sum(prob * grad, axis=-1, keepdims=True))).astype(BF)
+        for prob, grad in zip(probs, grad_probs)
+    ]
+    grad_query = [
+        jnp.concatenate(
+            [product(grad[here, :], padded[window, columns]) for here, window in spots], axis=0
+        )
+        * scale
+        for grad, (columns, _) in zip(grad_scores, heads)
+    ]
+    grad_query = jnp.concatenate(grad_query, axis=1).astype(BF)
+
+    def gathered(lefts, right):
+        parts = []
+        for left, (columns, _) in zip(lefts, heads):
+            terms_of = [contract_rows(left[here, :], right[here, columns]) for here, _ in spots]
+            units = []
+            for index in range(reached // half):
+                spot, place = divmod(index, 2)
+                held = None
+                if spot < blocks:
+                    held = terms_of[spot][place * half : (place + 1) * half, :]
+                if place == 0 and spot > 0:
+                    last = terms_of[spot - 1][2 * half :, :]
+                    held = last if held is None else held + last
+                units.append(held)
+            parts.append(jnp.concatenate(units, axis=0))
+        return jnp.concatenate(parts, axis=1)
+
+    grad_keys = (gathered(grad_scores, query) * scale).astype(BF)
+    grad_values = gathered([prob.astype(BF) for prob in probs], grad_att).astype(BF)
+    normed = normed_all[...]
+    normed_mine = jnp.concatenate(
+        [normed[own_unit(spot, half), :] for spot in range(blocks)], axis=0
+    )
+    store_block(info, terms, 0, contract_rows(normed_mine, grad_query))
+    store_block(info, terms, 1, contract_rows(normed, grad_keys))
+    store_block(info, terms, 2, contract_rows(normed, grad_values))
+    from_query = contract_cols(grad_query, w_qkv[0, :, :width])
+    grad_line[:reached, :] = contract_cols(
+        grad_keys, w_qkv[0, :, width : 2 * width]
+    ) + contract_cols(grad_values, w_qkv[0, :, 2 * width :])
+    for spot in range(blocks):
+        grad_line[own_unit(spot, half), :] += from_query[spot * half : (spot + 1) * half, :]
+    grad_normed = grad_line[:reached, :]
+    normal = normal_all[...]
+    store_gains(info, terms, jnp.sum(grad_normed * normal, axis=0, keepdims=True), ffn_term[...])
+    grad_line[:reached, :] = unit_back(grad_normed * gains[0, 0:1, :], normal, inverse_all[:, 0:1])
+    for spot in range(blocks):
+        grad_line[own_unit(spot, half), :] += grad_middle[spot * half : (spot + 1) * half, :]
+    grad_line[reached:, :] = jnp.zeros((grad_line.shape[0] - reached, width), F32)
+
+    @pl.when(section == 0)
+    def _():
+        swap[rows : 2 * rows, :] = grad_out
+
+    @pl.when(section == 1)
+    def _():
+        swap[rows:, :] = grad_line[:reached, :].astype(BF)
+
+
+def share_kernel(info, keep, one_near, zero_near, came, *pieces):
+    rows = keep.shape[0]
+    half = rows // 4
+    block = 2 * half
+    section = info[SEC]
+    near_rows = rows_at(section * half, half)
+    far_rows = rows_at(half - section * half, half)
+    for step, piece in enumerate(pieces):
+        spot = info[ZED] ^ step
+        mine = rows_at(spot * half, half)
+        piece[near_rows, :] = keep[mine, :]
+        piece[far_rows, :] = came[mine, :]
+
+    @pl.when(section == 0)
+    def _():
+        for step, piece in enumerate(pieces):
+            base = (info[ZED] ^ step) * block
+            near, far = rows_at(base + block, block), rows_at(rows + base + half, half)
+            far = pl.ds(far.start, block)
+            piece[block:, :] = (zero_near[near, :] + came[far, :].astype(F32)).astype(BF)
+
+    @pl.when(section == 1)
+    def _():
+        for step, piece in enumerate(pieces):
+            spot = info[ZED] ^ step
+            piece[block : block + half, :] = came[rows_at(rows + spot * half, half), :]
+            piece[block + half :, :] = one_near[rows_at(spot * half, half), :]
+
+
+def settle_kernel(info, piece0, piece1, piece2, piece3, results, input_grads):
+    block = piece0.shape[0] // 2
+    for step, piece in enumerate((piece0, piece1, piece2, piece3)):
+        micro = info[ZED] ^ step
+        results[0, micro, 0] = piece[:block, :]
+        input_grads[0, micro, 0] = piece[block:, :]
+
+
+def collect_kernel(info, piece0, piece1, piece2, piece3, held):
+    for step, piece in enumerate((piece0, piece1, piece2, piece3)):
+        held[info[FLIP + info[SEC]] ^ step] = piece[...]
+
+
+def finish_kernel(info, zero_near, zero_far, one_near, one_far, *outs):
+    gain_attn, qkv, out, gain_ffn, up, down = outs
+    width = zero_near.shape[2]
+    unit_rows = width // 2
+
+    def write(halves):
+        def units(number):
+            core, number = divmod(number, 6)
+            for part in range(2):
+                quarter, place = divmod(2 * number + part, 3)
+                yield part * unit_rows, halves[core][
+                    quarter, place * unit_rows : (place + 1) * unit_rows, :
+                ].astype(F32)
+
+        for number in range(12):
+            for row, value in units(number):
+                rows = slice(row, row + unit_rows)
+                if number < 3:
+                    qkv[0, rows, number * width : (number + 1) * width] = value
+                elif number == 3:
+                    out[0, rows, :] = value
+                elif number < 8:
+                    up[0, rows, (number - 4) * width : (number - 3) * width] = value
+                else:
+                    base = (number - 8) * width + row
+                    down[0, base : base + unit_rows, :] = value
+        spare = halves[0][0, zero_near.shape[1] - GAIN_ROWS :, :].astype(F32)
+        gain_attn[...] = spare[0:1, :]
+        gain_ffn[...] = spare[1:2, :]
+
+    @pl.when(info[SEC] == 0)
+    def _():
+        write((zero_near, zero_far))
+
+    @pl.when(info[SEC] == 1)
+    def _():
+        write((one_far, one_near))
+
+
+SWAP = [(0, 1), (1, 0)]
+PLANE = ("section", "rep")
+
+
+def crossed(flips):
+    return [(4 * s + g, 4 * s + (g ^ flips[s])) for s in range(2) for g in range(4)]
+
+
+FIRST = crossed((1, 2))
+SECOND = crossed((2, 1))
+
+
+def along_line(value, step):
+    return lax.ppermute(value, "dp", [(z, z ^ step) for z in range(4)])
+
+
+def reduce_terms(info, terms, came, zed, along=()):
+    bar = lax.optimization_barrier
+    first = lax.ppermute(terms[0, 2:4] + came[2:4], PLANE, FIRST)
+    second = lax.ppermute(terms[0, 1] + came[1] + first[1], PLANE, SECOND)
+    total = bar(terms[0, 0] + came[0] + first[0] + second)
+    total = bar(total + along_line(total, 1))
+    if along:
+        total, *along = bar((total, *along))
+    half = total.shape[0] // 2
+    odd = zed & 1
+    mine = lax.dynamic_slice_in_dim(total, odd * half, half, 0)
+    mine = bar(mine + along_line(mine, 2))
+    other = along_line(mine, 1)
+    total = bar(
+        jnp.where(
+            odd == 0, jnp.concatenate([mine, other]), jnp.concatenate([other, mine])
+        )
+    )
+    one = lax.ppermute(total, PLANE, SECOND)
+    two = lax.ppermute(total, PLANE, FIRST)
+    three = lax.ppermute(one, PLANE, FIRST)
+    shape = ((4, *total.shape), BF)
+    return call(collect_kernel, (info,), (total, one, two, three), (shape,), 8)[0], along
+
+
+def lines(
+    block_input,
+    output_grad,
+    seq_lengths,
+    attn_gain,
+    qkv_proj,
+    out_proj,
+    ffn_gain,
+    up_proj,
+    down_proj,
+):
+    section = lax.axis_index("section")
+    zed = lax.axis_index("dp")
+    rep = lax.axis_index("rep")
+    low, high = rep & 1, rep >> 1
+    info = jnp.stack([section, zed, rep, 2 * low + high, 2 * high + low]).astype(jnp.int32)
+    micro_count, _, block, width = block_input.shape
+    hidden_units = up_proj.shape[2]
+    half = block // 2
+    rows, reach = micro_count * half, block + half
+    reached = rows + rows + half
+    term_rows = 6 * width // 4 + GAIN_ROWS
+
+    packed = call(
+        pack_kernel,
+        (info,),
+        (block_input, output_grad, attn_gain, ffn_gain),
+        (((block + 16, width), BF),) + (((block, width), BF),) * (micro_count - 1),
+        8,
+        scratch=(
+            pltpu.VMEM((2, 1, width), BF),
+            pltpu.SemaphoreType.DMA((2 * micro_count,)),
+            pltpu.SemaphoreType.DMA((2,)),
+        ),
+        held=4,
+    )
+    near = [packed[0]] + [along_line(packed[step], step) for step in range(1, micro_count)]
+    far = [lax.ppermute(piece, "section", SWAP) for piece in near]
+    own = (qkv_proj[0], out_proj[0], up_proj[0], down_proj[0])
+    swapped = [lax.ppermute(weight, "section", SWAP) for weight in own]
+    weights = tuple(
+        jnp.stack([jnp.where(section == 0, a, b), jnp.where(section == 0, b, a)])
+        for a, b in zip(own, swapped)
+    )
+    gains_near, gains_far = near[0][block:].astype(F32), far[0][block:].astype(F32)
+    weights += (
+        jnp.stack(
+            [
+                jnp.where(section == 0, gains_near, gains_far),
+                jnp.where(section == 0, gains_far, gains_near),
+            ]
+        ),
+    )
+    ffn_saved = (
+        ((rows, width), BF),
+        ((rows, width), F32),
+        ((rows, 128), F32),
+        ((rows, width), BF),
+        ((rows, hidden_units), BF),
+        ((rows, hidden_units), F32),
+    )
+    (
+        _,
+        normal_all,
+        inverse_all,
+        normed_all,
+        query,
+        padded,
+        probs_zero,
+        attended_zero,
+        cotangent,
+        result_zero,
+        *saved_zero,
+    ) = call(
+        zero_forward_kernel,
+        (info, seq_lengths),
+        (*near, *far, *weights),
+        (
+            ((reached + half, width), BF),
+            ((reached, width), F32),
+            ((reached, 128), F32),
+            ((reached, width), BF),
+            ((rows, width), BF),
+            ((reached, 2 * width), BF),
+            ((HEADS, rows, reach), F32),
+            ((rows, width), BF),
+            ((rows, width), BF),
+            *ffn_saved,
+        ),
+    )
+    (
+        normal_one,
+        inverse_one,
+        normed_one,
+        packed_one,
+        probs_one,
+        attended_one,
+        result_one,
+        *saved_one,
+    ) = call(
+        one_forward_kernel,
+        (info, seq_lengths),
+        (result_zero, *weights),
+        (
+            ((rows, width), F32),
+            ((rows, 128), F32),
+            ((rows, width), BF),
+            ((rows, 3 * width), BF),
+            ((HEADS, rows, rows), F32),
+            ((rows, width), BF),
+            *ffn_saved,
+        ),
+    )
+    middle_one, mid_inverse_one, second_one, active_one, slope_one = saved_one
+    grad_one, terms_one, _ = call(
+        one_backward_kernel,
+        (info,),
+        (
+            cotangent,
+            *weights,
+            normal_one,
+            inverse_one,
+            normed_one,
+            packed_one,
+            probs_one,
+            middle_one,
+            mid_inverse_one,
+            second_one,
+            active_one,
+            slope_one,
+            attended_one,
+        ),
+        (((rows, width), BF), ((2, 4, term_rows, width), BF), ((rows, hidden_units), BF)),
+        micros=3.0,
+    )
+    middle_zero, mid_inverse_zero, second_zero, active_zero, slope_zero = saved_zero
+    came_one = lax.ppermute(terms_one[1], "section", SWAP)
+    w_qkv, w_out, w_up, w_down, gains = weights
+    zero_ffn = call(
+        zero_ffn_kernel,
+        (),
+        (grad_one, w_out, w_up, w_down, gains, middle_zero, mid_inverse_zero, slope_zero),
+        (
+            ((rows, width), F32),
+            ((rows, width), BF),
+            ((rows, hidden_units), BF),
+            ((1, width), F32),
+        ),
+        micros=2.0,
+    )
+    came_one, *zero_ffn = lax.optimization_barrier((came_one, *zero_ffn))
+    result_keep, grad_line, swap, terms_zero = call(
+        zero_backward_kernel,
+        (info,),
+        (
+            grad_one,
+            w_qkv,
+            gains,
+            normal_all,
+            inverse_all,
+            normed_all,
+            query,
+            padded,
+            probs_zero,
+            result_zero,
+            result_one,
+            second_zero,
+            active_zero,
+            attended_zero,
+            *zero_ffn,
+        ),
+        (
+            ((rows, width), BF),
+            ((reached + half, width), F32),
+            ((rows + reached, width), BF),
+            ((2, 4, term_rows, width), BF),
+        ),
+        micros=4.0,
+    )
+    came = lax.ppermute(swap, "section", SWAP)
+    shared = call(
+        share_kernel,
+        (info,),
+        (result_keep, grad_one, grad_line, came),
+        (((2 * block, width), BF),) * micro_count,
+        8,
+    )
+    home = [shared[0]] + [along_line(shared[step], step) for step in range(1, micro_count)]
+    came_zero = lax.ppermute(terms_zero[1], "section", SWAP)
+    one_near, home = reduce_terms(info, terms_one, came_one, zed, home)
+    results, input_grads = call(
+        settle_kernel,
+        (info,),
+        home,
+        (((1, micro_count, 1, block, width), BF),) * 2,
+        8,
+    )
+    zero_near, _ = reduce_terms(info, terms_zero, came_zero, zed)
+    one_far = lax.ppermute(one_near, "section", [(0, 1)])
+    zero_far = lax.ppermute(zero_near, "section", [(1, 0)])
+    sums = call(
+        finish_kernel,
+        (info,),
+        (zero_near, zero_far, one_near, one_far),
+        (
+            ((1, width), F32),
+            ((1, width, 3 * width), F32),
+            ((1, width, width), F32),
+            ((1, width), F32),
+            ((1, width, hidden_units), F32),
+            ((1, hidden_units, width), F32),
+        ),
+        16,
+    )
+    return (results, input_grads, *sums)
+
+
+def local(*arrays):
+    micro_count, _, tok_rows, model_width = arrays[0].shape
+    one_line_per_chip = (
+        lax.axis_size("section") == 2
+        and lax.axis_size("dp") == 4
+        and lax.axis_size("rep") == 4
+        and micro_count == 4
+        and tok_rows == STRIDE
+        and model_width == 256
+        and arrays[7].shape[2] == 4 * model_width
+    )
+    return lines(*arrays) if one_line_per_chip else general(*arrays)
+
+
 def solution(mesh):
     placed = (
         P(None, "rep", "dp", None),

time: 1030 us -> 97.2 us (0.09); the launches traced: 1010 us -> 96.9 us
  waiting for transfers between devices: 402 us -> 40.2 us
  blocking collectives: 331 us -> 0 us
  matrix products: 134 us -> 0 us
  local copies, waits for them, and re-layouts: 89.2 us -> 0.39 us
  other arithmetic: 28.8 us -> 1.14 us
  starting transfers between devices: 12 us -> 34.3 us
  Pallas kernels: 0 us -> 19.9 us
  between operations: 18 us -> 0.98 us
    unnamed x41 -> x0, waiting for transfers between devices: 298 us -> none
    all_gather x20 -> x0, blocking collectives: 290 us -> none  [the longest x5 73.6 us: dense_backward(): lax.all_gather(values, 'dp', axis=0, tiled=True)]
    dot_general x140 -> x0, matrix products: 134 us -> none  [the longest x40 64 us: contract_rows(): lax.dot_general(left, right, (((0,), (0,)), ((), ())), preferred_element_...]
    psum x1 -> x0, waiting for transfers between devices: 99.2 us -> none  [local(): lax.psum((totals[0], totals[1], totals[2], totals[3], totals[4], totals[5...]
    unnamed x561 -> x10, local copies, waits for them, and re-layouts: 81.9 us -> 0.16 us
    psum x1 -> x0, blocking collectives: 41 us -> none  [local(): lax.psum((totals[0], totals[1], totals[2], totals[3], totals[4], totals[5...]
    ppermute x8 -> x35, waiting for transfers between devices: 5.15 us -> 40.2 us  [the longest x12 17.8 us: along_line(): return lax.ppermute(value, 'dp', [(z, z ^ step) for z in range(4)])]
    ppermute x8 -> x35, starting transfers between devices: 10.7 us -> 34.3 us  [the longest x12 16.6 us: along_line(): return lax.ppermute(value, 'dp', [(z, z ^ step) for z in range(4)])]
  transfers between devices with their start and end apart: 29 -> 35, of which waited for: 26 -> 21; matrix products, arithmetic and copies ran while one was open for 9% -> 1% of each run, Pallas kernels for 0% -> 4%
where the time goes in v2:
time: 97.2 us; the launch traced here: 96.9 us
  waiting for transfers between devices  40.2 us (41%)
  starting transfers between devices  34.3 us (35%)
  Pallas kernels  19.9 us (20%)
  other arithmetic  1.14 us (1%)
  between operations  0.98 us (1%)
    pallas_call x11, Pallas kernels, call(): pl.pallas_call(body, out_shape=tuple((jax.ShapeDtypeStruct(*shape) for sh...  19.9 us
    ppermute x12, waiting for transfers between devices, along_line(): return lax.ppermute(value, 'dp', [(z, z ^ step) for z in range(4)])  17.8 us
    ppermute x12, starting transfers between devices, along_line(): return lax.ppermute(value, 'dp', [(z, z ^ step) for z in range(4)])  16.6 us
    ppermute x2, waiting for transfers between devices, reduce_terms(): one = lax.ppermute(total, PLANE, SECOND)  7.34 us
    ppermute x2, waiting for transfers between devices, reduce_terms(): first = lax.ppermute(terms[0, 2:4] + came[2:4], PLANE, FIRST)  4.62 us
    ppermute x2, starting transfers between devices, reduce_terms(): second = lax.ppermute(terms[0, 1] + came[1] + first[1], PLANE, SECOND)  3.41 us
    ppermute x2, starting transfers between devices, reduce_terms(): first = lax.ppermute(terms[0, 2:4] + came[2:4], PLANE, FIRST)  3.13 us
    ppermute x2, waiting for transfers between devices, reduce_terms(): second = lax.ppermute(terms[0, 1] + came[1] + first[1], PLANE, SECOND)  2.85 us
  transfers between devices with their start and end apart: 35, of which 21 were waited for; matrix products, arithmetic and copies ran while one was open for 1% of the time, Pallas kernels for 4%

profile of v2, /device:TPU:0, one launch (start us, length us, event | category | flops | bytes accessed | tf_op | source)
XLA Modules:
  0.0 96.9 jit_solution(6699633762158914436)
XLA Ops:
  0.6 0.1 stack.68.info
  0.7 1.5 %shard_map.152 = (bf16[144,256]{1,0:T(8,128)(2,1)S(1)}, bf16[128,256]{1,0:T(8,128)(2,1)S(1)}, bf16[128,256]{1,0:T(8,128)(2,1)S(1)}, bf16[128,256]{1,0:T(8,128)(2,1)S(1)}) custom-call(s32[5]{0:T(128)S(1)} %stack.68.info, bf16[4,1,128,256]{3,2,1,0:T(8,128)(2,1)} %tokens.1, bf16[4,1,128,256]{3,2,1,0:T(8,128)(2,1)} %grads.1, bf16[1,256]{1,0:T(2,128)(2,1)} %gain_attn.1, ...), custom_call_target="tpu_custom_call" | custom-call | flops 1100000000 | bytes 3400000 | tf_op jit(solution)/shard_map/pallas_call | solution.py:313
  2.3 0.5 collective-permute-start.3
  2.8 2.6 %collective-permute-start = (bf16[128,256]{1,0:T(8,128)(2,1)S(1)}, bf16[128,256]{1,0:T(8,128)(2,1)S(1)}, u32[]{:S(2)}, u32[]{:S(2)}) collective-permute-start(bf16[128,256]{1,0:T(8,128)(2,1)S(1)} %get-tuple-element.71), channel_id=1, source_target_pairs={{0,4},{4,0},{8,12},{12,8},{1,5},{5,1},{9,13},{13,9},{2,6},{6,2},{1... | collective-permute-start | bytes 196616 | tf_op jit(solution)/shard_map/ppermute | solution.py:950
  5.5 2.6 %collective-permute-start.1 = (bf16[128,256]{1,0:T(8,128)(2,1)S(1)}, bf16[128,256]{1,0:T(8,128)(2,1)S(1)}, u32[]{:S(2)}, u32[]{:S(2)}) collective-permute-start(bf16[128,256]{1,0:T(8,128)(2,1)S(1)} %get-tuple-element.72), channel_id=1, source_target_pairs={{0,8},{4,12},{8,0},{12,4},{1,9},{5,13},{9,1},{13,5},{2,10},{6,14},... | collective-permute-start | bytes 196616 | tf_op jit(solution)/shard_map/ppermute | solution.py:950
  8.1 0.5 collective-permute-start.8
  8.6 1.4 %collective-permute-done.8 = bf16[256,256]{1,0:T(8,128)(2,1)S(1)} collective-permute-done((bf16[256,256]{1,0:T(8,128)(2,1)S(1)}, bf16[256,256]{1,0:T(8,128)(2,1)S(1)}, u32[]{:S(2)}, u32[]{:S(2)}) %collective-permute-start.8) | collective-permute-done | bytes 131104 | tf_op jit(solution)/shard_map/ppermute | solution.py:1017
  10.0 0.1 collective-permute-start.9
  10.2 0.4 collective-permute-start.10
  10.6 2.5 %collective-permute-done.1.own2 = bf16[128,256]{1,0:T(8,128)(2,1)S(1)} collective-permute-done((bf16[128,256]{1,0:T(8,128)(2,1)S(1)}, bf16[128,256]{1,0:T(8,128)(2,1)S(1)}, u32[]{:S(2)}, u32[]{:S(2)}) %collective-permute-start.1) | collective-permute-done | bytes 65568 | tf_op jit(solution)/shard_map/ppermute | solution.py:950
  13.2 1.0 %collective-permute-done.2.own3 = bf16[128,256]{1,0:T(8,128)(2,1)S(1)} collective-permute-done((bf16[128,256]{1,0:T(8,128)(2,1)S(1)}, bf16[128,256]{1,0:T(8,128)(2,1)S(1)}, u32[]{:S(2)}, u32[]{:S(2)}) %collective-permute-start.2) | collective-permute-done | bytes 65568 | tf_op jit(solution)/shard_map/ppermute | solution.py:950
  14.2 0.5 collective-permute-start.6
  14.9 0.1 pad_maximum_fusion.w_up
  15.1 0.1 pad_maximum_fusion.1.w_down
  15.2 0.2 collective-permute-done.5.far2
  15.4 0.2 collective-permute-done.6.far3
  15.6 0.1 copy-done
  15.7 3.6 %shard_map.153 = (bf16[640,256]{1,0:T(8,128)(2,1)}, f32[576,256]{1,0:T(8,128)S(1)}, f32[576,128]{1,0:T(8,128)S(1)}, bf16[576,256]{1,0:T(8,128)(2,1)S(1)}, bf16[2...) custom-call(s32[5]{0:T(128)S(1)} %stack.68.info, ...), custom_call_target="tpu_custom_call" | custom-call | flops 1100000000 | bytes 3400000 | tf_op jit(solution)/shard_map/pallas_call | solution.py:313
  19.3 2.6 %shard_map.154 = (f32[256,256]{1,0:T(8,128)S(1)}, f32[256,128]{1,0:T(8,128)S(1)}, bf16[256,256]{1,0:T(8,128)(2,1)S(1)}, bf16[256,768]{1,0:T(8,128)(2,1)S(1)}, f3...) custom-call(s32[5]{0:T(128)S(1)} %stack.68.info, ...), custom_call_target="tpu_custom_call" | custom-call | flops 1100000000 | bytes 3400000 | tf_op jit(solution)/shard_map/pallas_call | solution.py:313
  21.9 3.2 %shard_map.155 = (bf16[256,256]{1,0:T(8,128)(2,1)S(1)}, bf16[2,4,416,256]{3,2,1,0:T(8,128)(2,1)S(1)}, bf16[256,1024]{1,0:T(8,128)(2,1)}) custom-call(s32[5]{0:T(128)S(1)} %stack.68.info, bf16[256,256]{1,0:T(8,128)(2,1)S(1)} %get-tuple-element.74.grad_ref, bf16[2,256,768]{2,1,0:T(8,128)(2,1)S(1)} %pad_maximum_fusion.2.w_qkv, ...), custom_call_target="tpu_custom_call" | custom-call | flops 3300000000 | bytes 10200000 | tf_op jit(solution)/shard_map/pallas_call | solution.py:313
  25.2 0.3 collective-permute-start.11
  25.4 0.8 shard_map.156
  26.3 1.4 %collective-permute-done.11 = bf16[4,416,256]{2,1,0:T(8,128)(2,1)S(1)} collective-permute-done((bf16[4,416,256]{2,1,0:T(8,128)(2,1)S(1)}, bf16[4,416,256]{2,1,0:T(8,128)(2,1)S(1)}, u32[]{:S(2)}, u32[]{:S(2)}) %collective-permute-start.11) | collective-permute-done | bytes 852000 | tf_op jit(solution)/shard_map/ppermute | solution.py:1114
  27.6 2.4 %shard_map.157 = (bf16[256,256]{1,0:T(8,128)(2,1)S(1)}, f32[640,256]{1,0:T(8,128)S(1)}, bf16[832,256]{1,0:T(8,128)(2,1)S(1)}, bf16[2,4,416,256]{3,2,1,0:T(8,128)(2,1)S(1)}) custom-call(s32[5]{0:T(128)S(1)} %stack.68.info, bf16[256,256]{1,0:T(8,128)(2,1)S(1)} %get-tuple-element.88.grad_ref.one_near, bf16[2,256,768]{2,1,0:T(8,128)(2,1)S(1)} %pad_maximum_fusion.2.w_qkv, ...), custom_call_target="tpu_custom_call" | custom-call | flops 4400000000 | bytes 13600000 | tf_op jit(solution)/shard_map/pallas_call | solution.py:313
  30.1 0.3 collective-permute-start.19
  30.4 0.3 collective-permute-start.15
  30.7 1.6 %collective-permute-start.12 = (bf16[2,416,256]{2,1,0:T(8,128)(2,1)S(1)}, bf16[2,416,256]{2,1,0:T(8,128)(2,1)S(1)}, u32[]{:S(2)}, u32[]{:S(2)}) collective-permute-start(bf16[2,416,256]{2,1,0:T(8,128)(2,1)S(1)} %bitcast_add_fusion), channel_id=1, source_target_pairs={{0,1},{1,0},{2,3},{3,2},{16,18},{17,19},{18,16},{19,17},{4,5},{5,4... | collective-permute-start | bytes 1277960 | tf_op jit(solution)/shard_map/ppermute | solution.py:955
  32.3 0.3 collective-permute-done.19
  32.6 1.6 %collective-permute-start.20 = (bf16[2,416,256]{2,1,0:T(8,128)(2,1)S(1)}, bf16[2,416,256]{2,1,0:T(8,128)(2,1)S(1)}, u32[]{:S(2)}, u32[]{:S(2)}) collective-permute-start(bf16[2,416,256]{2,1,0:T(8,128)(2,1)S(1)} %slice_add_fusion), channel_id=1, source_target_pairs={{0,1},{1,0},{2,3},{3,2},{16,18},{17,19},{18,16},{19,17},{4,5},{5,4... | collective-permute-start | bytes 1277960 | tf_op jit(solution)/shard_map/ppermute | solution.py:955
  34.2 0.8 shard_map.158
  35.0 1.3 %collective-permute-start.16 = (bf16[256,256]{1,0:T(8,128)(2,1)S(1)}, bf16[256,256]{1,0:T(8,128)(2,1)S(1)}, u32[]{:S(2)}, u32[]{:S(2)}) collective-permute-start(bf16[256,256]{1,0:T(8,128)(2,1)S(1)} %get-tuple-element.115), channel_id=1, source_target_pairs={{0,4},{4,0},{8,12},{12,8},{1,5},{5,1},{9,13},{13,9},{2,6},{6,2},{1... | collective-permute-start | bytes 393224 | tf_op jit(solution)/shard_map/ppermute | solution.py:950
  36.3 1.9 %collective-permute-start.17 = (bf16[256,256]{1,0:T(8,128)(2,1)S(1)}, bf16[256,256]{1,0:T(8,128)(2,1)S(1)}, u32[]{:S(2)}, u32[]{:S(2)}) collective-permute-start(bf16[256,256]{1,0:T(8,128)(2,1)S(1)} %get-tuple-element.116), channel_id=1, source_target_pairs={{0,8},{4,12},{8,0},{12,4},{1,9},{5,13},{9,1},{13,5},{2,10},{6,14},... | collective-permute-start | bytes 393224 | tf_op jit(solution)/shard_map/ppermute | solution.py:950
  38.2 1.3 %collective-permute-start.18 = (bf16[256,256]{1,0:T(8,128)(2,1)S(1)}, bf16[256,256]{1,0:T(8,128)(2,1)S(1)}, u32[]{:S(2)}, u32[]{:S(2)}) collective-permute-start(bf16[256,256]{1,0:T(8,128)(2,1)S(1)} %get-tuple-element.117), channel_id=1, source_target_pairs={{0,12},{4,8},{8,4},{12,0},{1,13},{5,9},{9,5},{13,1},{2,14},{6,10},... | collective-permute-start | bytes 393224 | tf_op jit(solution)/shard_map/ppermute | solution.py:950
  39.5 1.6 %collective-permute-start.13 = (bf16[416,256]{1,0:T(8,128)(2,1)S(1)}, bf16[416,256]{1,0:T(8,128)(2,1)S(1)}, u32[]{:S(2)}, u32[]{:S(2)}) collective-permute-start(bf16[416,256]{1,0:T(8,128)(2,1)S(1)} %fusion.5), channel_id=1, source_target_pairs={{0,2},{1,3},{2,0},{3,1},{16,17},{17,16},{18,19},{19,18},{4,6},{5,7... | collective-permute-start | bytes 638984 | tf_op jit(solution)/shard_map/ppermute | solution.py:956
  41.1 4.6 %collective-permute-done.20 = bf16[2,416,256]{2,1,0:T(8,128)(2,1)S(1)} collective-permute-done((bf16[2,416,256]{2,1,0:T(8,128)(2,1)S(1)}, bf16[2,416,256]{2,1,0:T(8,128)(2,1)S(1)}, u32[]{:S(2)}, u32[]{:S(2)}) %collective-permute-start.20) | collective-permute-done | bytes 426016 | tf_op jit(solution)/shard_map/ppermute | solution.py:955
  45.7 1.8 %collective-permute-start.21 = (bf16[416,256]{1,0:T(8,128)(2,1)S(1)}, bf16[416,256]{1,0:T(8,128)(2,1)S(1)}, u32[]{:S(2)}, u32[]{:S(2)}) collective-permute-start(bf16[416,256]{1,0:T(8,128)(2,1)S(1)} %fusion), channel_id=1, source_target_pairs={{0,2},{1,3},{2,0},{3,1},{16,17},{17,16},{18,19},{19,18},{4,6},{5,7... | collective-permute-start | bytes 638984 | tf_op jit(solution)/shard_map/ppermute | solution.py:956
  47.6 1.2 %collective-permute-start.14 = (bf16[416,256]{1,0:T(8,128)(2,1)S(1)}, bf16[416,256]{1,0:T(8,128)(2,1)S(1)}, u32[]{:S(2)}, u32[]{:S(2)}) collective-permute-start(bf16[416,256]{1,0:T(8,128)(2,1)S(1)} %fusion.7), channel_id=1, source_target_pairs={{0,4},{4,0},{8,12},{12,8},{1,5},{5,1},{9,13},{13,9},{2,6},{6,2},{1... | collective-permute-start | bytes 638984 | tf_op jit(solution)/shard_map/ppermute | solution.py:950
  48.8 2.8 %collective-permute-done.21 = bf16[416,256]{1,0:T(8,128)(2,1)S(1)} collective-permute-done((bf16[416,256]{1,0:T(8,128)(2,1)S(1)}, bf16[416,256]{1,0:T(8,128)(2,1)S(1)}, u32[]{:S(2)}, u32[]{:S(2)}) %collective-permute-start.21) | collective-permute-done | bytes 213024 | tf_op jit(solution)/shard_map/ppermute | solution.py:956
  51.7 1.4 %collective-permute-start.22 = (bf16[416,256]{1,0:T(8,128)(2,1)S(1)}, bf16[416,256]{1,0:T(8,128)(2,1)S(1)}, u32[]{:S(2)}, u32[]{:S(2)}) collective-permute-start(bf16[416,256]{1,0:T(8,128)(2,1)S(1)} %fusion.3), channel_id=1, source_target_pairs={{0,4},{4,0},{8,12},{12,8},{1,5},{5,1},{9,13},{13,9},{2,6},{6,2},{1... | collective-permute-start | bytes 638984 | tf_op jit(solution)/shard_map/ppermute | solution.py:950
  53.0 3.8 %collective-permute-done.14 = bf16[416,256]{1,0:T(8,128)(2,1)S(1)} collective-permute-done((bf16[416,256]{1,0:T(8,128)(2,1)S(1)}, bf16[416,256]{1,0:T(8,128)(2,1)S(1)}, u32[]{:S(2)}, u32[]{:S(2)}) %collective-permute-start.14) | collective-permute-done | bytes 213024 | tf_op jit(solution)/shard_map/ppermute | solution.py:950
  57.0 1.1 %collective-permute-start.29 = (bf16[208,256]{1,0:T(8,128)(2,1)S(1)}, bf16[208,256]{1,0:T(8,128)(2,1)S(1)}, u32[]{:S(2)}, u32[]{:S(2)}) collective-permute-start(bf16[208,256]{1,0:T(8,128)(2,1)S(1)} %constant_dynamic-slice_fusion), channel_id=1, source_target_pairs={{0,8},{4,12},{8,0},{12,4},{1,9},{5,13},{9,1},{13,5},{2,10},{6,14},... | collective-permute-start | bytes 319496 | tf_op jit(solution)/shard_map/ppermute | solution.py:950
  58.1 1.1 %collective-permute-done.22 = bf16[416,256]{1,0:T(8,128)(2,1)S(1)} collective-permute-done((bf16[416,256]{1,0:T(8,128)(2,1)S(1)}, bf16[416,256]{1,0:T(8,128)(2,1)S(1)}, u32[]{:S(2)}, u32[]{:S(2)}) %collective-permute-start.22) | collective-permute-done | bytes 213024 | tf_op jit(solution)/shard_map/ppermute | solution.py:950
  59.2 2.1 %collective-permute-start.23 = (bf16[208,256]{1,0:T(8,128)(2,1)S(1)}, bf16[208,256]{1,0:T(8,128)(2,1)S(1)}, u32[]{:S(2)}, u32[]{:S(2)}) collective-permute-start(bf16[208,256]{1,0:T(8,128)(2,1)S(1)} %constant_dynamic-slice_fusion.1), channel_id=1, source_target_pairs={{0,8},{4,12},{8,0},{12,4},{1,9},{5,13},{9,1},{13,5},{2,10},{6,14},... | collective-permute-start | bytes 319496 | tf_op jit(solution)/shard_map/ppermute | solution.py:950
  61.4 4.6 %collective-permute-done.29 = bf16[208,256]{1,0:T(8,128)(2,1)S(1)} collective-permute-done((bf16[208,256]{1,0:T(8,128)(2,1)S(1)}, bf16[208,256]{1,0:T(8,128)(2,1)S(1)}, u32[]{:S(2)}, u32[]{:S(2)}) %collective-permute-start.29) | collective-permute-done | bytes 106528 | tf_op jit(solution)/shard_map/ppermute | solution.py:950
  66.1 1.0 %collective-permute-done.23 = bf16[208,256]{1,0:T(8,128)(2,1)S(1)} collective-permute-done((bf16[208,256]{1,0:T(8,128)(2,1)S(1)}, bf16[208,256]{1,0:T(8,128)(2,1)S(1)}, u32[]{:S(2)}, u32[]{:S(2)}) %collective-permute-start.23) | collective-permute-done | bytes 106528 | tf_op jit(solution)/shard_map/ppermute | solution.py:950
  67.1 1.1 %collective-permute-start.24 = (bf16[208,256]{1,0:T(8,128)(2,1)S(1)}, bf16[208,256]{1,0:T(8,128)(2,1)S(1)}, u32[]{:S(2)}, u32[]{:S(2)}) collective-permute-start(bf16[208,256]{1,0:T(8,128)(2,1)S(1)} %fusion.11), channel_id=1, source_target_pairs={{0,4},{4,0},{8,12},{12,8},{1,5},{5,1},{9,13},{13,9},{2,6},{6,2},{1... | collective-permute-start | bytes 319496 | tf_op jit(solution)/shard_map/ppermute | solution.py:950
  68.2 2.7 %collective-permute-done.30 = bf16[208,256]{1,0:T(8,128)(2,1)S(1)} collective-permute-done((bf16[208,256]{1,0:T(8,128)(2,1)S(1)}, bf16[208,256]{1,0:T(8,128)(2,1)S(1)}, u32[]{:S(2)}, u32[]{:S(2)}) %collective-permute-start.30) | collective-permute-done | bytes 106528 | tf_op jit(solution)/shard_map/ppermute | solution.py:950
  71.0 1.0 %collective-permute-done.24 = bf16[208,256]{1,0:T(8,128)(2,1)S(1)} collective-permute-done((bf16[208,256]{1,0:T(8,128)(2,1)S(1)}, bf16[208,256]{1,0:T(8,128)(2,1)S(1)}, u32[]{:S(2)}, u32[]{:S(2)}) %collective-permute-start.24) | collective-permute-done | bytes 106528 | tf_op jit(solution)/shard_map/ppermute | solution.py:950
  72.1 1.1 %collective-permute-start.25 = (bf16[416,256]{1,0:T(8,128)(2,1)S(1)}, bf16[416,256]{1,0:T(8,128)(2,1)S(1)}, u32[]{:S(2)}, u32[]{:S(2)}) collective-permute-start(bf16[416,256]{1,0:T(8,128)(2,1)S(1)} %maximum_select_fusion.piece0), channel_id=1, source_target_pairs={{0,2},{1,3},{2,0},{3,1},{16,17},{17,16},{18,19},{19,18},{4,6},{5,7... | collective-permute-start | bytes 638984 | tf_op jit(solution)/shard_map/ppermute | solution.py:971
  73.2 1.2 %collective-permute-start.32 = (bf16[416,256]{1,0:T(8,128)(2,1)S(1)}, bf16[416,256]{1,0:T(8,128)(2,1)S(1)}, u32[]{:S(2)}, u32[]{:S(2)}) collective-permute-start(bf16[416,256]{1,0:T(8,128)(2,1)S(1)} %maximum_select_fusion.1.piece0), channel_id=1, source_target_pairs={{0,1},{1,0},{2,3},{3,2},{16,18},{17,19},{18,16},{19,17},{4,5},{5,4... | collective-permute-start | bytes 638984 | tf_op jit(solution)/shard_map/ppermute | solution.py:972
  74.4 4.8 %collective-permute-done.31.piece1 = bf16[416,256]{1,0:T(8,128)(2,1)S(1)} collective-permute-done((bf16[416,256]{1,0:T(8,128)(2,1)S(1)}, bf16[416,256]{1,0:T(8,128)(2,1)S(1)}, u32[]{:S(2)}, u32[]{:S(2)}) %collective-permute-start.31) | collective-permute-done | bytes 213024 | tf_op jit(solution)/shard_map/ppermute | solution.py:971
  79.2 1.2 %collective-permute-start.33 = (bf16[416,256]{1,0:T(8,128)(2,1)S(1)}, bf16[416,256]{1,0:T(8,128)(2,1)S(1)}, u32[]{:S(2)}, u32[]{:S(2)}) collective-permute-start(bf16[416,256]{1,0:T(8,128)(2,1)S(1)} %collective-permute-done.31.piece1), channel_id=1, source_target_pairs={{0,1},{1,0},{2,3},{3,2},{16,18},{17,19},{18,16},{19,17},{4,5},{5,4... | collective-permute-start | bytes 638984 | tf_op jit(solution)/shard_map/ppermute | solution.py:973
  80.4 0.8 collective-permute-start.26
  81.2 2.5 %collective-permute-done.25.piece1 = bf16[416,256]{1,0:T(8,128)(2,1)S(1)} collective-permute-done((bf16[416,256]{1,0:T(8,128)(2,1)S(1)}, bf16[416,256]{1,0:T(8,128)(2,1)S(1)}, u32[]{:S(2)}, u32[]{:S(2)}) %collective-permute-start.25) | collective-permute-done | bytes 213024 | tf_op jit(solution)/shard_map/ppermute | solution.py:971
  83.8 1.2 %collective-permute-start.27 = (bf16[416,256]{1,0:T(8,128)(2,1)S(1)}, bf16[416,256]{1,0:T(8,128)(2,1)S(1)}, u32[]{:S(2)}, u32[]{:S(2)}) collective-permute-start(bf16[416,256]{1,0:T(8,128)(2,1)S(1)} %collective-permute-done.25.piece1), channel_id=1, source_target_pairs={{0,1},{1,0},{2,3},{3,2},{16,18},{17,19},{18,16},{19,17},{4,5},{5,4... | collective-permute-start | bytes 638984 | tf_op jit(solution)/shard_map/ppermute | solution.py:973
  85.0 0.6 shard_map.161.one_near
  85.7 1.3 %collective-permute-start.34 = (bf16[4,416,256]{2,1,0:T(8,128)(2,1)S(1)}, bf16[4,416,256]{2,1,0:T(8,128)(2,1)S(1)}, u32[]{:S(2)}, u32[]{:S(2)}) collective-permute-start(bf16[4,416,256]{2,1,0:T(8,128)(2,1)S(1)} %shard_map.161.one_near), channel_id=1, source_target_pairs={{0,16},{1,17},{2,18},{3,19},{4,20},{5,21},{6,22},{7,23},{8,24},{9,... | collective-permute-start | bytes 2555912 | tf_op jit(solution)/shard_map/ppermute | solution.py:1176
  87.0 0.3 collective-permute-done.26.piece2
  87.3 2.3 %collective-permute-done.27.piece3 = bf16[416,256]{1,0:T(8,128)(2,1)S(1)} collective-permute-done((bf16[416,256]{1,0:T(8,128)(2,1)S(1)}, bf16[416,256]{1,0:T(8,128)(2,1)S(1)}, u32[]{:S(2)}, u32[]{:S(2)}) %collective-permute-start.27) | collective-permute-done | bytes 213024 | tf_op jit(solution)/shard_map/ppermute | solution.py:973
  89.6 0.6 shard_map.160.zero_near
  90.2 1.3 %collective-permute-start.28 = (bf16[4,416,256]{2,1,0:T(8,128)(2,1)S(1)}, bf16[4,416,256]{2,1,0:T(8,128)(2,1)S(1)}, u32[]{:S(2)}, u32[]{:S(2)}) collective-permute-start(bf16[4,416,256]{2,1,0:T(8,128)(2,1)S(1)} %shard_map.160.zero_near), channel_id=1, source_target_pairs={{16,0},{17,1},{18,2},{19,3},{20,4},{21,5},{22,6},{23,7},{24,8},{25... | collective-permute-start | bytes 2555912 | tf_op jit(solution)/shard_map/ppermute | solution.py:1177
  91.5 1.4 %shard_map.159 = (bf16[1,4,1,128,256]{4,3,2,1,0:T(8,128)(2,1)}, bf16[1,4,1,128,256]{4,3,2,1,0:T(8,128)(2,1)}) custom-call(s32[5]{0:T(128)S(1)} %stack.68.info, bf16[256,256]{1,0:T(8,128)(2,1)S(1)} %get-tuple-element.118.piece0, bf16[256,256]{1,0:T(8,128)(2,1)S(1)} %collective-permute-done.16.piece1, bf16[256,256]{1,0:T(8,128)(2,1)S(1)} %collective-permute-done.17.piece2, ...), custom_call_target="tpu_custom_call" | custom-call | flops 1100000000 | bytes 3400000 | tf_op jit(solution)/shard_map/pallas_call | solution.py:313
  92.9 1.6 %collective-permute-done.28.zero_far = bf16[4,416,256]{2,1,0:T(8,128)(2,1)S(1)} collective-permute-done((bf16[4,416,256]{2,1,0:T(8,128)(2,1)S(1)}, bf16[4,416,256]{2,1,0:T(8,128)(2,1)S(1)}, u32[]{:S(2)}, u32[]{:S(2)}) %collective-permute-start.28) | collective-permute-done | bytes 852000 | tf_op jit(solution)/shard_map/ppermute | solution.py:1177
  94.5 2.4 %shard_map.162 = (f32[1,256]{1,0:T(1,128)}, f32[1,256,768]{2,1,0:T(8,128)}, f32[1,256,256]{2,1,0:T(8,128)}, f32[1,256]{1,0:T(1,128)}, f32[1,256,1024]{2,1,0:T(8,128)}, /*index=5*/f32[1,1024,256]{2,1,0:T(8,128)}) custom-call(s32[5]{0:T(128)S(1)} %stack.68.info, bf16[4,416,256]{2,1,0:T(8,128)(2,1)S(1)} %shard_map.160.zero_near, ...), custom_call_target="tpu_custom_call" | custom-call | flops 1100000000 | bytes 3400000 | tf_op jit(solution)/shard_map/pallas_call | solution.py:313
  (54 shorter events, 1.4 us)
Async XLA Ops:
  0.7 7.3 %copy-start.3 = (bf16[1,256,768]{2,1,0:T(8,128)(2,1)S(1)}, bf16[1,256,768]{2,1,0:T(8,128)(2,1)}, u32[]{:S(2)}) copy-start(bf16[1,256,768]{2,1,0:T(8,128)(2,1)} %param.13) | copy-start | bytes 1179652
  0.7 7.3 %copy-start.4 = (bf16[1,256,256]{2,1,0:T(8,128)(2,1)S(1)}, bf16[1,256,256]{2,1,0:T(8,128)(2,1)}, u32[]{:S(2)}) copy-start(bf16[1,256,256]{2,1,0:T(8,128)(2,1)} %param.14) | copy-start | bytes 393220
  0.7 9.2 %copy-start.1 = (bf16[1,256,1024]{2,1,0:T(8,128)(2,1)S(1)}, bf16[1,256,1024]{2,1,0:T(8,128)(2,1)}, u32[]{:S(2)}) copy-start(bf16[1,256,1024]{2,1,0:T(8,128)(2,1)} %param.16) | copy-start | bytes 1572868
  0.7 9.4 %copy-start.2 = (bf16[1,1024,256]{2,1,0:T(8,128)(2,1)S(1)}, bf16[1,1024,256]{2,1,0:T(8,128)(2,1)}, u32[]{:S(2)}) copy-start(bf16[1,1024,256]{2,1,0:T(8,128)(2,1)} %param.17) | copy-start | bytes 1572868
  2.3 5.8 %collective-permute-start.3 = (bf16[144,256]{1,0:T(8,128)(2,1)S(1)}, bf16[144,256]{1,0:T(8,128)(2,1)S(1)}, u32[]{:S(2)}, u32[]{:S(2)}) collective-permute-start(bf16[144,256]{1,0:T(8,128)(2,1)S(1)} %get-tuple-element.70.own0), channel_id=1, source_target_pairs={{0,16},{16,0},{1,17},{17,1},{2,18},{18,2},{3,19},{19,3},{4,20},{20... | collective-permute-start | bytes 221192 | tf_op jit(solution)/shard_map/ppermute | solution.py:1015
  2.8 7.4 %collective-permute-start = (bf16[128,256]{1,0:T(8,128)(2,1)S(1)}, bf16[128,256]{1,0:T(8,128)(2,1)S(1)}, u32[]{:S(2)}, u32[]{:S(2)}) collective-permute-start(bf16[128,256]{1,0:T(8,128)(2,1)S(1)} %get-tuple-element.71), channel_id=1, source_target_pairs={{0,4},{4,0},{8,12},{12,8},{1,5},{5,1},{9,13},{13,9},{2,6},{6,2},{1... | collective-permute-start | bytes 196616 | tf_op jit(solution)/shard_map/ppermute | solution.py:950
  5.5 7.7 %collective-permute-start.1 = (bf16[128,256]{1,0:T(8,128)(2,1)S(1)}, bf16[128,256]{1,0:T(8,128)(2,1)S(1)}, u32[]{:S(2)}, u32[]{:S(2)}) collective-permute-start(bf16[128,256]{1,0:T(8,128)(2,1)S(1)} %get-tuple-element.72), channel_id=1, source_target_pairs={{0,8},{4,12},{8,0},{12,4},{1,9},{5,13},{9,1},{13,5},{2,10},{6,14},... | collective-permute-start | bytes 196616 | tf_op jit(solution)/shard_map/ppermute | solution.py:950
  8.0 6.1 %collective-permute-start.2 = (bf16[128,256]{1,0:T(8,128)(2,1)S(1)}, bf16[128,256]{1,0:T(8,128)(2,1)S(1)}, u32[]{:S(2)}, u32[]{:S(2)}) collective-permute-start(bf16[128,256]{1,0:T(8,128)(2,1)S(1)} %get-tuple-element.73), channel_id=1, source_target_pairs={{0,12},{4,8},{8,4},{12,0},{1,13},{5,9},{9,5},{13,1},{2,14},{6,10},... | collective-permute-start | bytes 196616 | tf_op jit(solution)/shard_map/ppermute | solution.py:950
  8.1 6.1 %collective-permute-start.7 = (bf16[256,768]{1,0:T(8,128)(2,1)S(1)}, bf16[256,768]{1,0:T(8,128)(2,1)S(1)}, u32[]{:S(2)}, u32[]{:S(2)}) collective-permute-start(bf16[256,768]{1,0:T(8,128)(2,1)S(1)} %bitcast.95), channel_id=1, source_target_pairs={{0,16},{16,0},{1,17},{17,1},{2,18},{18,2},{3,19},{19,3},{4,20},{20... | collective-permute-start | bytes 1179656 | tf_op jit(solution)/shard_map/ppermute | solution.py:1017
  8.1 1.9 %collective-permute-start.8 = (bf16[256,256]{1,0:T(8,128)(2,1)S(1)}, bf16[256,256]{1,0:T(8,128)(2,1)S(1)}, u32[]{:S(2)}, u32[]{:S(2)}) collective-permute-start(bf16[256,256]{1,0:T(8,128)(2,1)S(1)} %bitcast.96), channel_id=1, source_target_pairs={{0,16},{16,0},{1,17},{17,1},{2,18},{18,2},{3,19},{19,3},{4,20},{20... | collective-permute-start | bytes 393224 | tf_op jit(solution)/shard_map/ppermute | solution.py:1017
  10.0 4.9 %collective-permute-start.9 = (bf16[256,1024]{1,0:T(8,128)(2,1)S(1)}, bf16[256,1024]{1,0:T(8,128)(2,1)S(1)}, u32[]{:S(2)}, u32[]{:S(2)}) collective-permute-start(bf16[256,1024]{1,0:T(8,128)(2,1)S(1)} %bitcast.93), channel_id=1, source_target_pairs={{0,16},{16,0},{1,17},{17,1},{2,18},{18,2},{3,19},{19,3},{4,20},{20... | collective-permute-start | bytes 1572872 | tf_op jit(solution)/shard_map/ppermute | solution.py:1017
  10.2 4.9 %collective-permute-start.10 = (bf16[1024,256]{1,0:T(8,128)(2,1)S(1)}, bf16[1024,256]{1,0:T(8,128)(2,1)S(1)}, u32[]{:S(2)}, u32[]{:S(2)}) collective-permute-start(bf16[1024,256]{1,0:T(8,128)(2,1)S(1)} %bitcast.94), channel_id=1, source_target_pairs={{0,16},{16,0},{1,17},{17,1},{2,18},{18,2},{3,19},{19,3},{4,20},{20... | collective-permute-start | bytes 1572872 | tf_op jit(solution)/shard_map/ppermute | solution.py:1017
  13.2 2.1 %collective-permute-start.4 = (bf16[128,256]{1,0:T(8,128)(2,1)S(1)}, bf16[128,256]{1,0:T(8,128)(2,1)S(1)}, u32[]{:S(2)}, u32[]{:S(2)}) collective-permute-start(bf16[128,256]{1,0:T(8,128)(2,1)S(1)} %collective-permute-done.own1), channel_id=1, source_target_pairs={{0,16},{16,0},{1,17},{17,1},{2,18},{18,2},{3,19},{19,3},{4,20},{20... | collective-permute-start | bytes 196616 | tf_op jit(solution)/shard_map/ppermute | solution.py:1015
  14.2 1.3 %collective-permute-start.5 = (bf16[128,256]{1,0:T(8,128)(2,1)S(1)}, bf16[128,256]{1,0:T(8,128)(2,1)S(1)}, u32[]{:S(2)}, u32[]{:S(2)}) collective-permute-start(bf16[128,256]{1,0:T(8,128)(2,1)S(1)} %collective-permute-done.1.own2), channel_id=1, source_target_pairs={{0,16},{16,0},{1,17},{17,1},{2,18},{18,2},{3,19},{19,3},{4,20},{20... | collective-permute-start | bytes 196616 | tf_op jit(solution)/shard_map/ppermute | solution.py:1015
  14.2 1.4 %collective-permute-start.6 = (bf16[128,256]{1,0:T(8,128)(2,1)S(1)}, bf16[128,256]{1,0:T(8,128)(2,1)S(1)}, u32[]{:S(2)}, u32[]{:S(2)}) collective-permute-start(bf16[128,256]{1,0:T(8,128)(2,1)S(1)} %collective-permute-done.2.own3), channel_id=1, source_target_pairs={{0,16},{16,0},{1,17},{17,1},{2,18},{18,2},{3,19},{19,3},{4,20},{20... | collective-permute-start | bytes 196616 | tf_op jit(solution)/shard_map/ppermute | solution.py:1015
  15.0 0.7 copy-start
  25.2 2.4 %collective-permute-start.11 = (bf16[4,416,256]{2,1,0:T(8,128)(2,1)S(1)}, bf16[4,416,256]{2,1,0:T(8,128)(2,1)S(1)}, u32[]{:S(2)}, u32[]{:S(2)}) collective-permute-start(bf16[4,416,256]{2,1,0:T(8,128)(2,1)S(1)} %slice_bitcast_fusion.1), channel_id=1, source_target_pairs={{0,16},{16,0},{1,17},{17,1},{2,18},{18,2},{3,19},{19,3},{4,20},{20... | collective-permute-start | bytes 2555912 | tf_op jit(solution)/shard_map/ppermute | solution.py:1114
  30.1 2.4 %collective-permute-start.19 = (bf16[4,416,256]{2,1,0:T(8,128)(2,1)S(1)}, bf16[4,416,256]{2,1,0:T(8,128)(2,1)S(1)}, u32[]{:S(2)}, u32[]{:S(2)}) collective-permute-start(bf16[4,416,256]{2,1,0:T(8,128)(2,1)S(1)} %slice_bitcast_fusion), channel_id=1, source_target_pairs={{0,16},{16,0},{1,17},{17,1},{2,18},{18,2},{3,19},{19,3},{4,20},{20... | collective-permute-start | bytes 2555912 | tf_op jit(solution)/shard_map/ppermute | solution.py:1166
  30.4 3.8 %collective-permute-start.15 = (bf16[832,256]{1,0:T(8,128)(2,1)S(1)}, bf16[832,256]{1,0:T(8,128)(2,1)S(1)}, u32[]{:S(2)}, u32[]{:S(2)}) collective-permute-start(bf16[832,256]{1,0:T(8,128)(2,1)S(1)} %get-tuple-element.113), channel_id=1, source_target_pairs={{0,16},{16,0},{1,17},{17,1},{2,18},{18,2},{3,19},{19,3},{4,20},{20... | collective-permute-start | bytes 1277960 | tf_op jit(solution)/shard_map/ppermute | solution.py:1157
  30.7 8.7 %collective-permute-start.12 = (bf16[2,416,256]{2,1,0:T(8,128)(2,1)S(1)}, bf16[2,416,256]{2,1,0:T(8,128)(2,1)S(1)}, u32[]{:S(2)}, u32[]{:S(2)}) collective-permute-start(bf16[2,416,256]{2,1,0:T(8,128)(2,1)S(1)} %bitcast_add_fusion), channel_id=1, source_target_pairs={{0,1},{1,0},{2,3},{3,2},{16,18},{17,19},{18,16},{19,17},{4,5},{5,4... | collective-permute-start | bytes 1277960 | tf_op jit(solution)/shard_map/ppermute | solution.py:955
  32.6 13.1 %collective-permute-start.20 = (bf16[2,416,256]{2,1,0:T(8,128)(2,1)S(1)}, bf16[2,416,256]{2,1,0:T(8,128)(2,1)S(1)}, u32[]{:S(2)}, u32[]{:S(2)}) collective-permute-start(bf16[2,416,256]{2,1,0:T(8,128)(2,1)S(1)} %slice_add_fusion), channel_id=1, source_target_pairs={{0,1},{1,0},{2,3},{3,2},{16,18},{17,19},{18,16},{19,17},{4,5},{5,4... | collective-permute-start | bytes 1277960 | tf_op jit(solution)/shard_map/ppermute | solution.py:955
  35.0 22.0 %collective-permute-start.16 = (bf16[256,256]{1,0:T(8,128)(2,1)S(1)}, bf16[256,256]{1,0:T(8,128)(2,1)S(1)}, u32[]{:S(2)}, u32[]{:S(2)}) collective-permute-start(bf16[256,256]{1,0:T(8,128)(2,1)S(1)} %get-tuple-element.115), channel_id=1, source_target_pairs={{0,4},{4,0},{8,12},{12,8},{1,5},{5,1},{9,13},{13,9},{2,6},{6,2},{1... | collective-permute-start | bytes 393224 | tf_op jit(solution)/shard_map/ppermute | solution.py:950
  36.3 20.7 %collective-permute-start.17 = (bf16[256,256]{1,0:T(8,128)(2,1)S(1)}, bf16[256,256]{1,0:T(8,128)(2,1)S(1)}, u32[]{:S(2)}, u32[]{:S(2)}) collective-permute-start(bf16[256,256]{1,0:T(8,128)(2,1)S(1)} %get-tuple-element.116), channel_id=1, source_target_pairs={{0,8},{4,12},{8,0},{12,4},{1,9},{5,13},{9,1},{13,5},{2,10},{6,14},... | collective-permute-start | bytes 393224 | tf_op jit(solution)/shard_map/ppermute | solution.py:950
  38.2 18.8 %collective-permute-start.18 = (bf16[256,256]{1,0:T(8,128)(2,1)S(1)}, bf16[256,256]{1,0:T(8,128)(2,1)S(1)}, u32[]{:S(2)}, u32[]{:S(2)}) collective-permute-start(bf16[256,256]{1,0:T(8,128)(2,1)S(1)} %get-tuple-element.117), channel_id=1, source_target_pairs={{0,12},{4,8},{8,4},{12,0},{1,13},{5,9},{9,5},{13,1},{2,14},{6,10},... | collective-permute-start | bytes 393224 | tf_op jit(solution)/shard_map/ppermute | solution.py:950
  39.5 8.1 %collective-permute-start.13 = (bf16[416,256]{1,0:T(8,128)(2,1)S(1)}, bf16[416,256]{1,0:T(8,128)(2,1)S(1)}, u32[]{:S(2)}, u32[]{:S(2)}) collective-permute-start(bf16[416,256]{1,0:T(8,128)(2,1)S(1)} %fusion.5), channel_id=1, source_target_pairs={{0,2},{1,3},{2,0},{3,1},{16,17},{17,16},{18,19},{19,18},{4,6},{5,7... | collective-permute-start | bytes 638984 | tf_op jit(solution)/shard_map/ppermute | solution.py:956
  45.7 5.9 %collective-permute-start.21 = (bf16[416,256]{1,0:T(8,128)(2,1)S(1)}, bf16[416,256]{1,0:T(8,128)(2,1)S(1)}, u32[]{:S(2)}, u32[]{:S(2)}) collective-permute-start(bf16[416,256]{1,0:T(8,128)(2,1)S(1)} %fusion), channel_id=1, source_target_pairs={{0,2},{1,3},{2,0},{3,1},{16,17},{17,16},{18,19},{19,18},{4,6},{5,7... | collective-permute-start | bytes 638984 | tf_op jit(solution)/shard_map/ppermute | solution.py:956
  47.6 9.3 %collective-permute-start.14 = (bf16[416,256]{1,0:T(8,128)(2,1)S(1)}, bf16[416,256]{1,0:T(8,128)(2,1)S(1)}, u32[]{:S(2)}, u32[]{:S(2)}) collective-permute-start(bf16[416,256]{1,0:T(8,128)(2,1)S(1)} %fusion.7), channel_id=1, source_target_pairs={{0,4},{4,0},{8,12},{12,8},{1,5},{5,1},{9,13},{13,9},{2,6},{6,2},{1... | collective-permute-start | bytes 638984 | tf_op jit(solution)/shard_map/ppermute | solution.py:950
  51.7 7.5 %collective-permute-start.22 = (bf16[416,256]{1,0:T(8,128)(2,1)S(1)}, bf16[416,256]{1,0:T(8,128)(2,1)S(1)}, u32[]{:S(2)}, u32[]{:S(2)}) collective-permute-start(bf16[416,256]{1,0:T(8,128)(2,1)S(1)} %fusion.3), channel_id=1, source_target_pairs={{0,4},{4,0},{8,12},{12,8},{1,5},{5,1},{9,13},{13,9},{2,6},{6,2},{1... | collective-permute-start | bytes 638984 | tf_op jit(solution)/shard_map/ppermute | solution.py:950
  57.0 8.9 %collective-permute-start.29 = (bf16[208,256]{1,0:T(8,128)(2,1)S(1)}, bf16[208,256]{1,0:T(8,128)(2,1)S(1)}, u32[]{:S(2)}, u32[]{:S(2)}) collective-permute-start(bf16[208,256]{1,0:T(8,128)(2,1)S(1)} %constant_dynamic-slice_fusion), channel_id=1, source_target_pairs={{0,8},{4,12},{8,0},{12,4},{1,9},{5,13},{9,1},{13,5},{2,10},{6,14},... | collective-permute-start | bytes 319496 | tf_op jit(solution)/shard_map/ppermute | solution.py:950
  59.2 7.8 %collective-permute-start.23 = (bf16[208,256]{1,0:T(8,128)(2,1)S(1)}, bf16[208,256]{1,0:T(8,128)(2,1)S(1)}, u32[]{:S(2)}, u32[]{:S(2)}) collective-permute-start(bf16[208,256]{1,0:T(8,128)(2,1)S(1)} %constant_dynamic-slice_fusion.1), channel_id=1, source_target_pairs={{0,8},{4,12},{8,0},{12,4},{1,9},{5,13},{9,1},{13,5},{2,10},{6,14},... | collective-permute-start | bytes 319496 | tf_op jit(solution)/shard_map/ppermute | solution.py:950
  66.0 4.9 %collective-permute-start.30 = (bf16[208,256]{1,0:T(8,128)(2,1)S(1)}, bf16[208,256]{1,0:T(8,128)(2,1)S(1)}, u32[]{:S(2)}, u32[]{:S(2)}) collective-permute-start(bf16[208,256]{1,0:T(8,128)(2,1)S(1)} %fusion.10), channel_id=1, source_target_pairs={{0,4},{4,0},{8,12},{12,8},{1,5},{5,1},{9,13},{13,9},{2,6},{6,2},{1... | collective-permute-start | bytes 319496 | tf_op jit(solution)/shard_map/ppermute | solution.py:950
  67.1 4.9 %collective-permute-start.24 = (bf16[208,256]{1,0:T(8,128)(2,1)S(1)}, bf16[208,256]{1,0:T(8,128)(2,1)S(1)}, u32[]{:S(2)}, u32[]{:S(2)}) collective-permute-start(bf16[208,256]{1,0:T(8,128)(2,1)S(1)} %fusion.11), channel_id=1, source_target_pairs={{0,4},{4,0},{8,12},{12,8},{1,5},{5,1},{9,13},{13,9},{2,6},{6,2},{1... | collective-permute-start | bytes 319496 | tf_op jit(solution)/shard_map/ppermute | solution.py:950
  70.9 8.3 %collective-permute-start.31 = (bf16[416,256]{1,0:T(8,128)(2,1)S(1)}, bf16[416,256]{1,0:T(8,128)(2,1)S(1)}, u32[]{:S(2)}, u32[]{:S(2)}) collective-permute-start(bf16[416,256]{1,0:T(8,128)(2,1)S(1)} %maximum_select_fusion.1.piece0), channel_id=1, source_target_pairs={{0,2},{1,3},{2,0},{3,1},{16,17},{17,16},{18,19},{19,18},{4,6},{5,7... | collective-permute-start | bytes 638984 | tf_op jit(solution)/shard_map/ppermute | solution.py:971
  72.1 11.7 %collective-permute-start.25 = (bf16[416,256]{1,0:T(8,128)(2,1)S(1)}, bf16[416,256]{1,0:T(8,128)(2,1)S(1)}, u32[]{:S(2)}, u32[]{:S(2)}) collective-permute-start(bf16[416,256]{1,0:T(8,128)(2,1)S(1)} %maximum_select_fusion.piece0), channel_id=1, source_target_pairs={{0,2},{1,3},{2,0},{3,1},{16,17},{17,16},{18,19},{19,18},{4,6},{5,7... | collective-permute-start | bytes 638984 | tf_op jit(solution)/shard_map/ppermute | solution.py:971
  73.2 11.8 %collective-permute-start.32 = (bf16[416,256]{1,0:T(8,128)(2,1)S(1)}, bf16[416,256]{1,0:T(8,128)(2,1)S(1)}, u32[]{:S(2)}, u32[]{:S(2)}) collective-permute-start(bf16[416,256]{1,0:T(8,128)(2,1)S(1)} %maximum_select_fusion.1.piece0), channel_id=1, source_target_pairs={{0,1},{1,0},{2,3},{3,2},{16,18},{17,19},{18,16},{19,17},{4,5},{5,4... | collective-permute-start | bytes 638984 | tf_op jit(solution)/shard_map/ppermute | solution.py:972
  79.2 5.8 %collective-permute-start.33 = (bf16[416,256]{1,0:T(8,128)(2,1)S(1)}, bf16[416,256]{1,0:T(8,128)(2,1)S(1)}, u32[]{:S(2)}, u32[]{:S(2)}) collective-permute-start(bf16[416,256]{1,0:T(8,128)(2,1)S(1)} %collective-permute-done.31.piece1), channel_id=1, source_target_pairs={{0,1},{1,0},{2,3},{3,2},{16,18},{17,19},{18,16},{19,17},{4,5},{5,4... | collective-permute-start | bytes 638984 | tf_op jit(solution)/shard_map/ppermute | solution.py:973
  80.4 6.9 %collective-permute-start.26 = (bf16[416,256]{1,0:T(8,128)(2,1)S(1)}, bf16[416,256]{1,0:T(8,128)(2,1)S(1)}, u32[]{:S(2)}, u32[]{:S(2)}) collective-permute-start(bf16[416,256]{1,0:T(8,128)(2,1)S(1)} %maximum_select_fusion.piece0), channel_id=1, source_target_pairs={{0,1},{1,0},{2,3},{3,2},{16,18},{17,19},{18,16},{19,17},{4,5},{5,4... | collective-permute-start | bytes 638984 | tf_op jit(solution)/shard_map/ppermute | solution.py:972
  83.8 5.8 %collective-permute-start.27 = (bf16[416,256]{1,0:T(8,128)(2,1)S(1)}, bf16[416,256]{1,0:T(8,128)(2,1)S(1)}, u32[]{:S(2)}, u32[]{:S(2)}) collective-permute-start(bf16[416,256]{1,0:T(8,128)(2,1)S(1)} %collective-permute-done.25.piece1), channel_id=1, source_target_pairs={{0,1},{1,0},{2,3},{3,2},{16,18},{17,19},{18,16},{19,17},{4,5},{5,4... | collective-permute-start | bytes 638984 | tf_op jit(solution)/shard_map/ppermute | solution.py:973
  85.7 7.2 %collective-permute-start.34 = (bf16[4,416,256]{2,1,0:T(8,128)(2,1)S(1)}, bf16[4,416,256]{2,1,0:T(8,128)(2,1)S(1)}, u32[]{:S(2)}, u32[]{:S(2)}) collective-permute-start(bf16[4,416,256]{2,1,0:T(8,128)(2,1)S(1)} %shard_map.161.one_near), channel_id=1, source_target_pairs={{0,16},{1,17},{2,18},{3,19},{4,20},{5,21},{6,22},{7,23},{8,24},{9,... | collective-permute-start | bytes 2555912 | tf_op jit(solution)/shard_map/ppermute | solution.py:1176
  90.2 4.3 %collective-permute-start.28 = (bf16[4,416,256]{2,1,0:T(8,128)(2,1)S(1)}, bf16[4,416,256]{2,1,0:T(8,128)(2,1)S(1)}, u32[]{:S(2)}, u32[]{:S(2)}) collective-permute-start(bf16[4,416,256]{2,1,0:T(8,128)(2,1)S(1)} %shard_map.160.zero_near), channel_id=1, source_target_pairs={{16,0},{17,1},{18,2},{19,3},{20,4},{21,5},{22,6},{23,7},{24,8},{25... | collective-permute-start | bytes 2555912 | tf_op jit(solution)/shard_map/ppermute | solution.py:1177

commit v3 on v2

--- a/solution.py
+++ b/solution.py
@@ -303,10 +303,10 @@
 BF = jnp.bfloat16
 F32 = jnp.float32
 MIB = 1024 * 1024
-GAIN_ROWS = 32
-
-
-def call(body, scalars, arrays, shapes, mib=24, micros=1.0, scratch=(), held=0):
+GAIN_ROWS = 16
+
+
+def call(body, scalars, arrays, shapes, mib=24, micros=1.0, scratch=(), held=0, out_held=()):
     in_specs = [pl.BlockSpec(memory_space=pltpu.SMEM)] * len(scalars)
     in_specs += [pl.BlockSpec(memory_space=pl.ANY)] * held
     in_specs += [pl.BlockSpec(memory_space=pltpu.VMEM)] * (len(arrays) - held)
@@ -314,7 +314,10 @@
         body,
         out_shape=tuple(jax.ShapeDtypeStruct(*shape) for shape in shapes),
         in_specs=in_specs,
-        out_specs=tuple(pl.BlockSpec(memory_space=pltpu.VMEM) for _ in shapes),
+        out_specs=tuple(
+            pl.BlockSpec(memory_space=pl.ANY if index in out_held else pltpu.VMEM)
+            for index in range(len(shapes))
+        ),
         scratch_shapes=list(scratch),
         compiler_params=pltpu.CompilerParams(vmem_limit_bytes=mib * MIB),
         cost_estimate=pl.CostEstimate(
@@ -327,24 +330,81 @@
     )
 
 
-SEC, ZED, REP, FLIP = 0, 1, 2, 3
+def my_section():
+    return lax.axis_index("section")
+
+
+def my_line():
+    return lax.axis_index("dp")
+
+
+def my_flip(core):
+    rep = lax.axis_index("rep")
+    low, high = rep & 1, rep >> 1
+    return 2 * low + high if core == 0 else 2 * high + low
 
 
 def rows_at(start, count):
     return pl.ds(pl.multiple_of(start, count), count)
 
 
-def pack_kernel(info, tokens, grads, gain_attn, gain_ffn, *rest):
-    *pieces, gains, sems, gain_sems = rest
+def segment_at(ends, position):
+    total = jnp.zeros(position.shape, jnp.int32)
+    for end in ends:
+        total = total + (position >= end).astype(jnp.int32)
+    return total
+
+
+def ends_of(lengths):
+    ends = []
+    so_far = jnp.int32(0)
+    for slot in range(lengths.shape[2]):
+        so_far = so_far + lengths[my_line(), lax.axis_index("rep"), slot]
+        ends.append(so_far)
+    return ends
+
+
+def write_masks(lengths, window_mask, strided_mask):
+    section = my_section()
+    rows, reach = window_mask.shape
+    half = rows // 4
+    block = 2 * half
+    ends = ends_of(lengths)
+    row = lax.broadcasted_iota(jnp.int32, (rows, reach), 0)
+    query_pos = block * (row // half) + section * half + (row & (half - 1))
+    key_pos = query_pos - (row & (half - 1)) - block
+    key_pos = key_pos + lax.broadcasted_iota(jnp.int32, (rows, reach), 1)
+    offset = query_pos - key_pos
+    segment = segment_at(ends, query_pos)
+    same = (segment == segment_at(ends, key_pos)) & (segment < len(ends)) & (key_pos >= 0)
+    allow = same & (offset >= 0) & (offset < STRIDE) | (offset == 0)
+    window_mask[...] = allow.astype(F32)
+
+    def place(axis):
+        index = lax.broadcasted_iota(jnp.int32, (rows, rows), axis)
+        return block * (index // half) + section * half + (index & (half - 1))
+
+    query_pos, key_pos = place(0), place(1)
+    offset = query_pos - key_pos
+    segment = segment_at(ends, query_pos)
+    same = (segment == segment_at(ends, key_pos)) & (segment < len(ends))
+    allow = same & (offset >= 0) & ((offset & (STRIDE - 1)) == 0) | (offset == 0)
+    strided_mask[...] = allow.astype(F32)
+
+
+def pack_kernel(tokens, grads, gain_attn, gain_ffn, lengths, *rest):
+    *pieces, window_mask, strided_mask, gains, lengths_held, sems, side_sems = rest
     block = tokens.shape[2]
     half = block // 2
-    rows = rows_at(info[SEC] * half, half)
-    copies = [
-        pltpu.make_async_copy(gain_attn, gains.at[0], gain_sems.at[0]),
-        pltpu.make_async_copy(gain_ffn, gains.at[1], gain_sems.at[1]),
+    rows = rows_at(my_section() * half, half)
+    side = [
+        pltpu.make_async_copy(lengths, lengths_held, side_sems.at[2]),
+        pltpu.make_async_copy(gain_attn, gains.at[0], side_sems.at[0]),
+        pltpu.make_async_copy(gain_ffn, gains.at[1], side_sems.at[1]),
     ]
+    copies = []
     for step, piece in enumerate(pieces):
-        micro = info[ZED] ^ step
+        micro = my_line() ^ step
         for part, source in enumerate((tokens, grads)):
             copies.append(
                 pltpu.make_async_copy(
@@ -353,10 +413,11 @@
                     sems.at[2 * step + part],
                 )
             )
-    for copy in copies:
+    for copy in (*side, *copies):
         copy.start()
-    for copy in copies:
+    for copy in side:
         copy.wait()
+    write_masks(lengths_held, window_mask, strided_mask)
     pieces[0][block:, :] = jnp.concatenate(
         [
             gains[0].astype(F32),
@@ -365,6 +426,8 @@
         ],
         axis=0,
     ).astype(BF)
+    for copy in copies:
+        copy.wait()
 
 
 def unit(values):
@@ -383,22 +446,6 @@
 
 def widened(column, width):
     return jnp.broadcast_to(column, (column.shape[0], width))
-
-
-def segment_at(ends, position):
-    total = jnp.zeros(position.shape, jnp.int32)
-    for end in ends:
-        total = total + (position >= end).astype(jnp.int32)
-    return total
-
-
-def ends_of(info, lengths):
-    ends = []
-    so_far = jnp.int32(0)
-    for slot in range(lengths.shape[2]):
-        so_far = so_far + lengths[info[ZED], info[REP], slot]
-        ends.append(so_far)
-    return ends
 
 
 def normalized_exp(scores):
@@ -438,8 +485,7 @@
 
 
 def zero_forward_kernel(
-    info,
-    lengths,
+    mask,
     own0,
     own1,
     own2,
@@ -464,7 +510,7 @@
     cotangent,
     *saved,
 ):
-    section = info[SEC]
+    section = my_section()
     reached, width = normal_all.shape
     half = line.shape[0] // 10
     block = 2 * half
@@ -475,7 +521,7 @@
     reach = block + half
     line[:block, :] = jnp.zeros((block, width), BF)
     for step, (near, far) in enumerate(((own0, far0), (own1, far1), (own2, far2), (own3, far3))):
-        spot = info[ZED] ^ step
+        spot = my_line() ^ step
         line[rows_at(spot * block + block, half), :] = near[:half, :]
         line[rows_at(spot * block + block + half - section * block, half), :] = far[:half, :]
         cotangent[rows_at(spot * half, half), :] = near[half:block, :]
@@ -489,15 +535,6 @@
         [normed[own_unit(spot, half), :] for spot in range(blocks)], axis=0
     )
     query[...] = product(normed_mine, w_qkv[0, :, :width]).astype(BF)
-    ends = ends_of(info, lengths)
-    row = lax.broadcasted_iota(jnp.int32, (rows, reach), 0)
-    query_pos = block * (row // half) + section * half + (row & (half - 1))
-    key_pos = query_pos - (row & (half - 1)) - block
-    key_pos = key_pos + lax.broadcasted_iota(jnp.int32, (rows, reach), 1)
-    offset = query_pos - key_pos
-    segment = segment_at(ends, query_pos)
-    same = (segment == segment_at(ends, key_pos)) & (segment < len(ends)) & (key_pos >= 0)
-    mask = same & (offset >= 0) & (offset < STRIDE) | (offset == 0)
     spots = [(slice(spot * half, (spot + 1) * half), key_units(spot, half)) for spot in range(blocks)]
     heads = [
         (slice(number * head, (number + 1) * head), slice(width + number * head, width + (number + 1) * head))
@@ -510,7 +547,7 @@
         )
         for columns, _ in heads
     ]
-    probs = [normalized_exp(jnp.where(mask, values * scale, NEG)) for values in scores]
+    probs = [normalized_exp(jnp.where(mask[...] > 0.5, values * scale, NEG)) for values in scores]
     attended = []
     for number, (_, value_columns) in enumerate(heads):
         probs_ref[number] = probs[number]
@@ -529,8 +566,7 @@
 
 
 def one_forward_kernel(
-    info,
-    lengths,
+    mask,
     hidden_ref,
     w_qkv,
     w_out,
@@ -545,7 +581,7 @@
     attended_ref,
     *saved,
 ):
-    section = info[SEC]
+    section = my_section()
     rows, width = hidden_ref.shape
     half = rows // 4
     block = 2 * half
@@ -558,17 +594,6 @@
     normed = (normal * gains[1, 0:1, :]).astype(BF)
     normed_ref[...] = normed
     packed[...] = product(normed, w_qkv[1]).astype(BF)
-    ends = ends_of(info, lengths)
-
-    def place(axis):
-        index = lax.broadcasted_iota(jnp.int32, (rows, rows), axis)
-        return block * (index // half) + section * half + (index & (half - 1))
-
-    query_pos, key_pos = place(0), place(1)
-    offset = query_pos - key_pos
-    segment = segment_at(ends, query_pos)
-    same = (segment == segment_at(ends, key_pos)) & (segment < len(ends))
-    mask = same & (offset >= 0) & ((offset & (STRIDE - 1)) == 0) | (offset == 0)
     heads = [
         tuple(
             slice(part * width + number * head, part * width + (number + 1) * head) for part in range(3)
@@ -576,7 +601,7 @@
         for number in range(HEADS)
     ]
     scores = [contract_cols(packed[:, near], packed[:, far]) for near, far, _ in heads]
-    probs = [normalized_exp(jnp.where(mask, values * scale, NEG)) for values in scores]
+    probs = [normalized_exp(jnp.where(mask[...] > 0.5, values * scale, NEG)) for values in scores]
     parts = []
     for number, (_, _, value_columns) in enumerate(heads):
         probs_ref[number] = probs[number]
@@ -586,11 +611,11 @@
     ffn_forward(hidden, attended, gains[1, 1:2, :], w_out[1], w_up.at[1], w_down.at[1], saved)
 
 
-def store_block(info, terms, number, value):
+def store_block(terms, number, value):
     width = value.shape[1]
     unit_rows = width // 2
     core, number = divmod(number, 6)
-    side, flip = info[SEC] ^ core, info[FLIP + core]
+    side, flip = my_section() ^ core, my_flip(core)
     value = value.astype(BF)
     for part in range(2):
         quarter, place = divmod(2 * number + part, 3)
@@ -599,7 +624,7 @@
         ]
 
 
-def store_gains(info, terms, attn_term, ffn_term):
+def store_gains(terms, attn_term, ffn_term):
     spare, width = terms.shape[2] - GAIN_ROWS, terms.shape[3]
     value = jnp.concatenate(
         [attn_term, ffn_term, jnp.zeros((GAIN_ROWS - 2, width), F32)], axis=0
@@ -628,17 +653,16 @@
     return grad_middle, contract_cols(grad_middle.astype(BF), w_out).astype(BF), gain_term
 
 
-def ffn_weight_grads(info, terms, grad_out, grad_middle, second, active, attended, grad_pre):
+def ffn_weight_grads(terms, grad_out, grad_middle, second, active, attended, grad_pre):
     width = grad_out.shape[1]
-    store_block(info, terms, 3, contract_rows(attended[...], grad_middle.astype(BF)))
+    store_block(terms, 3, contract_rows(attended[...], grad_middle.astype(BF)))
     for index in range(active.shape[1] // width):
         columns = slice(index * width, (index + 1) * width)
-        store_block(info, terms, 4 + index, contract_rows(second[...], grad_pre[:, columns]))
-        store_block(info, terms, 8 + index, contract_rows(active[:, columns], grad_out))
+        store_block(terms, 4 + index, contract_rows(second[...], grad_pre[:, columns]))
+        store_block(terms, 8 + index, contract_rows(active[:, columns], grad_out))
 
 
 def one_backward_kernel(
-    info,
     grad_ref,
     w_qkv,
     w_out,
@@ -666,7 +690,7 @@
         w_down.at[1],
         grad_pre,
     )
-    ffn_weight_grads(info, terms, grad_out, grad_middle, second, active, attended, grad_pre)
+    ffn_weight_grads(terms, grad_out, grad_middle, second, active, attended, grad_pre)
     heads = [
         tuple(
             slice(part * width + number * head, part * width + (number + 1) * head) for part in range(3)
@@ -692,9 +716,9 @@
         grad_block = jnp.concatenate(grad_parts[index], axis=1).astype(BF)
         term = contract_cols(grad_block, w_qkv[1, :, columns])
         grad_normed = term if grad_normed is None else grad_normed + term
-        store_block(info, terms, index, contract_rows(normed_ref[...], grad_block))
+        store_block(terms, index, contract_rows(normed_ref[...], grad_block))
     normal = normal_ref[...]
-    store_gains(info, terms, jnp.sum(grad_normed * normal, axis=0, keepdims=True), ffn_term)
+    store_gains(terms, jnp.sum(grad_normed * normal, axis=0, keepdims=True), ffn_term)
     grad_in[...] = (
         grad_middle + unit_back(grad_normed * gains[1, 0:1, :], normal, inverse_ref[:, 0:1])
     ).astype(BF)
@@ -729,7 +753,6 @@
 
 
 def zero_backward_kernel(
-    info,
     grad_ref,
     w_qkv,
     gains,
@@ -753,7 +776,7 @@
     swap,
     terms,
 ):
-    section = info[SEC]
+    section = my_section()
     rows, width = grad_ref.shape
     reached = normal_all.shape[0]
     half = rows // 4
@@ -774,7 +797,7 @@
 
     grad_middle = grad_middle_ref[...]
     grad_att = grad_att_ref[...]
-    ffn_weight_grads(info, terms, grad_out, grad_middle, second, active, attended, grad_pre)
+    ffn_weight_grads(terms, grad_out, grad_middle, second, active, attended, grad_pre)
     spots = [(slice(spot * half, (spot + 1) * half), key_units(spot, half)) for spot in range(blocks)]
     heads = [
         (slice(number * head, (number + 1) * head), slice(width + number * head, width + (number + 1) * head))
@@ -827,9 +850,9 @@
     normed_mine = jnp.concatenate(
         [normed[own_unit(spot, half), :] for spot in range(blocks)], axis=0
     )
-    store_block(info, terms, 0, contract_rows(normed_mine, grad_query))
-    store_block(info, terms, 1, contract_rows(normed, grad_keys))
-    store_block(info, terms, 2, contract_rows(normed, grad_values))
+    store_block(terms, 0, contract_rows(normed_mine, grad_query))
+    store_block(terms, 1, contract_rows(normed, grad_keys))
+    store_block(terms, 2, contract_rows(normed, grad_values))
     from_query = contract_cols(grad_query, w_qkv[0, :, :width])
     grad_line[:reached, :] = contract_cols(
         grad_keys, w_qkv[0, :, width : 2 * width]
@@ -838,7 +861,7 @@
         grad_line[own_unit(spot, half), :] += from_query[spot * half : (spot + 1) * half, :]
     grad_normed = grad_line[:reached, :]
     normal = normal_all[...]
-    store_gains(info, terms, jnp.sum(grad_normed * normal, axis=0, keepdims=True), ffn_term[...])
+    store_gains(terms, jnp.sum(grad_normed * normal, axis=0, keepdims=True), ffn_term[...])
     grad_line[:reached, :] = unit_back(grad_normed * gains[0, 0:1, :], normal, inverse_all[:, 0:1])
     for spot in range(blocks):
         grad_line[own_unit(spot, half), :] += grad_middle[spot * half : (spot + 1) * half, :]
@@ -853,15 +876,15 @@
         swap[rows:, :] = grad_line[:reached, :].astype(BF)
 
 
-def share_kernel(info, keep, one_near, zero_near, came, *pieces):
+def share_kernel(keep, one_near, zero_near, came, *pieces):
     rows = keep.shape[0]
     half = rows // 4
     block = 2 * half
-    section = info[SEC]
+    section = my_section()
     near_rows = rows_at(section * half, half)
     far_rows = rows_at(half - section * half, half)
     for step, piece in enumerate(pieces):
-        spot = info[ZED] ^ step
+        spot = my_line() ^ step
         mine = rows_at(spot * half, half)
         piece[near_rows, :] = keep[mine, :]
         piece[far_rows, :] = came[mine, :]
@@ -869,7 +892,7 @@
     @pl.when(section == 0)
     def _():
         for step, piece in enumerate(pieces):
-            base = (info[ZED] ^ step) * block
+            base = (my_line() ^ step) * block
             near, far = rows_at(base + block, block), rows_at(rows + base + half, half)
             far = pl.ds(far.start, block)
             piece[block:, :] = (zero_near[near, :] + came[far, :].astype(F32)).astype(BF)
@@ -877,59 +900,57 @@
     @pl.when(section == 1)
     def _():
         for step, piece in enumerate(pieces):
-            spot = info[ZED] ^ step
+            spot = my_line() ^ step
             piece[block : block + half, :] = came[rows_at(rows + spot * half, half), :]
             piece[block + half :, :] = one_near[rows_at(spot * half, half), :]
 
 
-def settle_kernel(info, piece0, piece1, piece2, piece3, results, input_grads):
+def settle_kernel(piece0, piece1, piece2, piece3, results, input_grads):
     block = piece0.shape[0] // 2
     for step, piece in enumerate((piece0, piece1, piece2, piece3)):
-        micro = info[ZED] ^ step
+        micro = my_line() ^ step
         results[0, micro, 0] = piece[:block, :]
         input_grads[0, micro, 0] = piece[block:, :]
 
 
-def collect_kernel(info, piece0, piece1, piece2, piece3, held):
-    for step, piece in enumerate((piece0, piece1, piece2, piece3)):
-        held[info[FLIP + info[SEC]] ^ step] = piece[...]
-
-
-def finish_kernel(info, zero_near, zero_far, one_near, one_far, *outs):
-    gain_attn, qkv, out, gain_ffn, up, down = outs
+def finish_kernel(zero_near, zero_far, one_near, one_far, *rest):
+    gain_attn, qkv, out, gain_ffn, up, down, qkv_held, out_held, up_held, down_held, sems = rest
     width = zero_near.shape[2]
     unit_rows = width // 2
+    targets = [(qkv_held, qkv, (slice(None), slice(n * width, (n + 1) * width))) for n in range(3)]
+    targets.append((out_held, out, (slice(None), slice(None))))
+    targets += [(up_held, up, (slice(None), slice(n * width, (n + 1) * width))) for n in range(4)]
+    targets += [(down_held, down, (slice(n * width, (n + 1) * width), slice(None))) for n in range(4)]
 
     def write(halves):
-        def units(number):
-            core, number = divmod(number, 6)
+        copies = []
+        for number, (held, target, (rows, columns)) in enumerate(targets):
+            core, place = divmod(number, 6)
+            start = rows.start or 0
             for part in range(2):
-                quarter, place = divmod(2 * number + part, 3)
-                yield part * unit_rows, halves[core][
-                    quarter, place * unit_rows : (place + 1) * unit_rows, :
-                ].astype(F32)
-
-        for number in range(12):
-            for row, value in units(number):
-                rows = slice(row, row + unit_rows)
-                if number < 3:
-                    qkv[0, rows, number * width : (number + 1) * width] = value
-                elif number == 3:
-                    out[0, rows, :] = value
-                elif number < 8:
-                    up[0, rows, (number - 4) * width : (number - 3) * width] = value
-                else:
-                    base = (number - 8) * width + row
-                    down[0, base : base + unit_rows, :] = value
-        spare = halves[0][0, zero_near.shape[1] - GAIN_ROWS :, :].astype(F32)
+                quarter, spot = divmod(2 * place + part, 3)
+                value = halves[core][
+                    my_flip(core) ^ quarter, spot * unit_rows : (spot + 1) * unit_rows, :
+                ]
+                first = start + part * unit_rows
+                held[first : first + unit_rows, columns] = value.astype(F32)
+            copies.append(
+                pltpu.make_async_copy(
+                    held.at[rows, columns], target.at[0, rows, columns], sems.at[number]
+                )
+            )
+            copies[-1].start()
+        spare = halves[0][my_flip(0), zero_near.shape[1] - GAIN_ROWS :, :].astype(F32)
         gain_attn[...] = spare[0:1, :]
         gain_ffn[...] = spare[1:2, :]
-
-    @pl.when(info[SEC] == 0)
+        for copy in copies:
+            copy.wait()
+
+    @pl.when(my_section() == 0)
     def _():
         write((zero_near, zero_far))
 
-    @pl.when(info[SEC] == 1)
+    @pl.when(my_section() == 1)
     def _():
         write((one_far, one_near))
 
@@ -950,14 +971,14 @@
     return lax.ppermute(value, "dp", [(z, z ^ step) for z in range(4)])
 
 
-def reduce_terms(info, terms, came, zed, along=()):
+def reduce_terms(terms, came, zed, along=()):
     bar = lax.optimization_barrier
     first = lax.ppermute(terms[0, 2:4] + came[2:4], PLANE, FIRST)
     second = lax.ppermute(terms[0, 1] + came[1] + first[1], PLANE, SECOND)
     total = bar(terms[0, 0] + came[0] + first[0] + second)
-    total = bar(total + along_line(total, 1))
     if along:
         total, *along = bar((total, *along))
+    total = bar(total + along_line(total, 1))
     half = total.shape[0] // 2
     odd = zed & 1
     mine = lax.dynamic_slice_in_dim(total, odd * half, half, 0)
@@ -968,11 +989,8 @@
             odd == 0, jnp.concatenate([mine, other]), jnp.concatenate([other, mine])
         )
     )
-    one = lax.ppermute(total, PLANE, SECOND)
-    two = lax.ppermute(total, PLANE, FIRST)
-    three = lax.ppermute(one, PLANE, FIRST)
-    shape = ((4, *total.shape), BF)
-    return call(collect_kernel, (info,), (total, one, two, three), (shape,), 8)[0], along
+    pair = jnp.stack([total, lax.ppermute(total, PLANE, SECOND)])
+    return pair, lax.ppermute(pair, PLANE, FIRST), along
 
 
 def lines(
@@ -988,9 +1006,6 @@
 ):
     section = lax.axis_index("section")
     zed = lax.axis_index("dp")
-    rep = lax.axis_index("rep")
-    low, high = rep & 1, rep >> 1
-    info = jnp.stack([section, zed, rep, 2 * low + high, 2 * high + low]).astype(jnp.int32)
     micro_count, _, block, width = block_input.shape
     hidden_units = up_proj.shape[2]
     half = block // 2
@@ -998,22 +1013,29 @@
     reached = rows + rows + half
     term_rows = 6 * width // 4 + GAIN_ROWS
 
-    packed = call(
+    *packed, window_mask, strided_mask = call(
         pack_kernel,
-        (info,),
-        (block_input, output_grad, attn_gain, ffn_gain),
-        (((block + 16, width), BF),) + (((block, width), BF),) * (micro_count - 1),
+        (),
+        (block_input, output_grad, attn_gain, ffn_gain, seq_lengths),
+        (
+            ((block + 16, width), BF),
+            *((((block, width), BF),) * (micro_count - 1)),
+            ((rows, reach), F32),
+            ((rows, rows), F32),
+        ),
         8,
         scratch=(
             pltpu.VMEM((2, 1, width), BF),
+            pltpu.SMEM(seq_lengths.shape, jnp.int32),
             pltpu.SemaphoreType.DMA((2 * micro_count,)),
-            pltpu.SemaphoreType.DMA((2,)),
-        ),
-        held=4,
+            pltpu.SemaphoreType.DMA((3,)),
+        ),
+        held=5,
     )
     near = [packed[0]] + [along_line(packed[step], step) for step in range(1, micro_count)]
     far = [lax.ppermute(piece, "section", SWAP) for piece in near]
     own = (qkv_proj[0], out_proj[0], up_proj[0], down_proj[0])
+    near[1], *own = lax.optimization_barrier((near[1], *own))
     swapped = [lax.ppermute(weight, "section", SWAP) for weight in own]
     weights = tuple(
         jnp.stack([jnp.where(section == 0, a, b), jnp.where(section == 0, b, a)])
@@ -1050,8 +1072,8 @@
         *saved_zero,
     ) = call(
         zero_forward_kernel,
-        (info, seq_lengths),
-        (*near, *far, *weights),
+        (),
+        (window_mask, *near, *far, *weights),
         (
             ((reached + half, width), BF),
             ((reached, width), F32),
@@ -1076,8 +1098,8 @@
         *saved_one,
     ) = call(
         one_forward_kernel,
-        (info, seq_lengths),
-        (result_zero, *weights),
+        (),
+        (strided_mask, result_zero, *weights),
         (
             ((rows, width), F32),
             ((rows, 128), F32),
@@ -1091,7 +1113,7 @@
     middle_one, mid_inverse_one, second_one, active_one, slope_one = saved_one
     grad_one, terms_one, _ = call(
         one_backward_kernel,
-        (info,),
+        (),
         (
             cotangent,
             *weights,
@@ -1125,10 +1147,9 @@
         ),
         micros=2.0,
     )
-    came_one, *zero_ffn = lax.optimization_barrier((came_one, *zero_ffn))
     result_keep, grad_line, swap, terms_zero = call(
         zero_backward_kernel,
-        (info,),
+        (),
         (
             grad_one,
             w_qkv,
@@ -1157,28 +1178,31 @@
     came = lax.ppermute(swap, "section", SWAP)
     shared = call(
         share_kernel,
-        (info,),
+        (),
         (result_keep, grad_one, grad_line, came),
         (((2 * block, width), BF),) * micro_count,
         8,
     )
     home = [shared[0]] + [along_line(shared[step], step) for step in range(1, micro_count)]
     came_zero = lax.ppermute(terms_zero[1], "section", SWAP)
-    one_near, home = reduce_terms(info, terms_one, came_one, zed, home)
+    one_pair, one_first, home = reduce_terms(terms_one, came_one, zed, home)
     results, input_grads = call(
         settle_kernel,
-        (info,),
+        (),
         home,
         (((1, micro_count, 1, block, width), BF),) * 2,
         8,
     )
-    zero_near, _ = reduce_terms(info, terms_zero, came_zero, zed)
-    one_far = lax.ppermute(one_near, "section", [(0, 1)])
-    zero_far = lax.ppermute(zero_near, "section", [(1, 0)])
+    zero_pair, zero_first, _ = reduce_terms(terms_zero, came_zero, zed)
+
+    def both_cores(parts, pairs):
+        near = jnp.concatenate(parts)
+        return near, jnp.concatenate([lax.ppermute(part, "section", pairs) for part in parts])
+
     sums = call(
         finish_kernel,
-        (info,),
-        (zero_near, zero_far, one_near, one_far),
+        (),
+        (*both_cores((zero_pair, zero_first), [(1, 0)]), *both_cores((one_pair, one_first), [(0, 1)])),
         (
             ((1, width), F32),
             ((1, width, 3 * width), F32),
@@ -1187,7 +1211,15 @@
             ((1, width, hidden_units), F32),
             ((1, hidden_units, width), F32),
         ),
-        16,
+        24,
+        scratch=(
+            pltpu.VMEM((width, 3 * width), F32),
+            pltpu.VMEM((width, width), F32),
+            pltpu.VMEM((width, hidden_units), F32),
+            pltpu.VMEM((hidden_units, width), F32),
+            pltpu.SemaphoreType.DMA((12,)),
+        ),
+        out_held=(1, 2, 4, 5),
     )
     return (results, input_grads, *sums)
 

time: 97.2 us -> 90.4 us (0.930)
  Pallas kernels: 19.9 us -> 13.9 us
  waiting for transfers between devices: 40.2 us -> 36.6 us
  starting transfers between devices: 34.3 us -> 37 us
    pallas_call x11 -> x9, Pallas kernels: 19.9 us -> 13.9 us  [call(): pl.pallas_call(body, out_shape=tuple((jax.ShapeDtypeStruct(*shape) for sh...]
    ppermute x12, starting transfers between devices: 16.6 us -> 19.2 us  [along_line(): return lax.ppermute(value, 'dp', [(z, z ^ step) for z in range(4)])]
    ppermute x2, waiting for transfers between devices: 2.85 us -> 0.93 us  [reduce_terms(): second = lax.ppermute(terms[0, 1] + came[1] + first[1], PLANE, SECOND)]
    ppermute x1, waiting for transfers between devices: 1.35 us -> 0.01 us  [lines(): came_one = lax.ppermute(terms_one[1], 'section', SWAP)]
    ppermute x8, waiting for transfers between devices: 11.6 us -> 10.5 us  [the longest x2 7.29 us: reduce_terms(): pair = jnp.stack([total, lax.ppermute(total, PLANE, SECOND)])]
  transfers between devices with their start and end apart: 35 -> 35, of which waited for: 21 -> 21; matrix products, arithmetic and copies ran while one was open for 1% -> 2% of each run, Pallas kernels for 4% -> 4%
where the time goes in v3:
time: 90.4 us; the launch traced here: 90.2 us
  starting transfers between devices  37 us (41%)
  waiting for transfers between devices  36.6 us (40%)
  Pallas kernels  13.9 us (15%)
  other arithmetic  1.47 us (2%)
  between operations  1 us (1%)
    ppermute x12, starting transfers between devices, along_line(): return lax.ppermute(value, 'dp', [(z, z ^ step) for z in range(4)])  19.2 us
    ppermute x12, waiting for transfers between devices, along_line(): return lax.ppermute(value, 'dp', [(z, z ^ step) for z in range(4)])  17.9 us
    pallas_call x9, Pallas kernels, call(): pl.pallas_call(body, out_shape=tuple((jax.ShapeDtypeStruct(*shape) for sh...  13.9 us
    ppermute x2, waiting for transfers between devices, reduce_terms(): pair = jnp.stack([total, lax.ppermute(total, PLANE, SECOND)])  7.29 us
    ppermute x2, waiting for transfers between devices, reduce_terms(): first = lax.ppermute(terms[0, 2:4] + came[2:4], PLANE, FIRST)  5.21 us
    ppermute x4, starting transfers between devices, both_cores(): lax.ppermute(part, 'section', pairs)  5.18 us
    ppermute x2, starting transfers between devices, reduce_terms(): second = lax.ppermute(terms[0, 1] + came[1] + first[1], PLANE, SECOND)  3.17 us
    ppermute x2, starting transfers between devices, reduce_terms(): first = lax.ppermute(terms[0, 2:4] + came[2:4], PLANE, FIRST)  3.11 us
  transfers between devices with their start and end apart: 35, of which 21 were waited for; matrix products, arithmetic and copies ran while one was open for 2% of the time, Pallas kernels for 4%

profile of v3, /device:TPU:0, one launch (start us, length us, event | category | flops | bytes accessed | tf_op | source)
XLA Modules:
  0.0 90.2 jit_solution(2409573641832251743)
XLA Ops:
  0.7 1.5 %shard_map.152 = (bf16[144,256]{1,0:T(8,128)(2,1)S(1)}, bf16[128,256]{1,0:T(8,128)(2,1)S(1)}, bf16[128,256]{1,0:T(8,128)(2,1)S(1)}, bf16[128,256]{1,0:T(8,128)(2...) custom-call(bf16[4,1,128,256]{3,2,1,0:T(8,128)(2,1)} %tokens.1, bf16[4,1,128,256]{3,2,1,0:T(8,128)(2,1)} %grads.1, ...), custom_call_target="tpu_custom_call" | custom-call | flops 1100000000 | bytes 3400000 | tf_op jit(solution)/shard_map/pallas_call | solution.py:313
  2.2 0.5 collective-permute-start.3
  2.7 2.6 %collective-permute-start = (bf16[128,256]{1,0:T(8,128)(2,1)S(1)}, bf16[128,256]{1,0:T(8,128)(2,1)S(1)}, u32[]{:S(2)}, u32[]{:S(2)}) collective-permute-start(bf16[128,256]{1,0:T(8,128)(2,1)S(1)} %get-tuple-element.74), channel_id=1, source_target_pairs={{0,4},{4,0},{8,12},{12,8},{1,5},{5,1},{9,13},{13,9},{2,6},{6,2},{1... | collective-permute-start | bytes 196616 | tf_op jit(solution)/shard_map/ppermute | solution.py:971
  5.3 2.6 %collective-permute-start.1 = (bf16[128,256]{1,0:T(8,128)(2,1)S(1)}, bf16[128,256]{1,0:T(8,128)(2,1)S(1)}, u32[]{:S(2)}, u32[]{:S(2)}) collective-permute-start(bf16[128,256]{1,0:T(8,128)(2,1)S(1)} %get-tuple-element.76), channel_id=1, source_target_pairs={{0,8},{4,12},{8,0},{12,4},{1,9},{5,13},{9,1},{13,5},{2,10},{6,14},... | collective-permute-start | bytes 196616 | tf_op jit(solution)/shard_map/ppermute | solution.py:971
  7.9 0.1 collective-permute-done.own1
  8.0 0.5 collective-permute-start.8
  8.5 0.1 collective-permute-start.7
  8.6 1.5 %collective-permute-done.8 = bf16[256,256]{1,0:T(8,128)(2,1)S(1)} collective-permute-done((bf16[256,256]{1,0:T(8,128)(2,1)S(1)}, bf16[256,256]{1,0:T(8,128)(2,1)S(1)}, u32[]{:S(2)}, u32[]{:S(2)}) %collective-permute-start.8) | collective-permute-done | bytes 131104 | tf_op jit(solution)/shard_map/ppermute | solution.py:1039
  10.1 0.1 collective-permute-start.9
  10.3 2.7 %collective-permute-done.1.own2 = bf16[128,256]{1,0:T(8,128)(2,1)S(1)} collective-permute-done((bf16[128,256]{1,0:T(8,128)(2,1)S(1)}, bf16[128,256]{1,0:T(8,128)(2,1)S(1)}, u32[]{:S(2)}, u32[]{:S(2)}) %collective-permute-start.1) | collective-permute-done | bytes 65568 | tf_op jit(solution)/shard_map/ppermute | solution.py:971
  13.0 1.0 %collective-permute-done.2.own3 = bf16[128,256]{1,0:T(8,128)(2,1)S(1)} collective-permute-done((bf16[128,256]{1,0:T(8,128)(2,1)S(1)}, bf16[128,256]{1,0:T(8,128)(2,1)S(1)}, u32[]{:S(2)}, u32[]{:S(2)}) %collective-permute-start.2) | collective-permute-done | bytes 65568 | tf_op jit(solution)/shard_map/ppermute | solution.py:971
  14.0 0.5 collective-permute-start.6
  14.6 0.1 pad_maximum_fusion.6.w_qkv
  14.7 0.1 select_bitcast_fusion.1
  14.8 0.1 pad_maximum_fusion.1.w_down
  15.0 0.1 pad_maximum_fusion.w_up
  15.1 0.2 collective-permute-done.5.far2
  15.3 0.2 collective-permute-done.6.far3
  15.4 2.2 %shard_map.153 = (bf16[640,256]{1,0:T(8,128)(2,1)}, f32[576,256]{1,0:T(8,128)S(1)}, f32[576,128]{1,0:T(8,128)S(1)}, bf16[576,256]{1,0:T(8,128)(2,1)S(1)}, bf16[2...) custom-call(f32[256,192]{1,0:T(8,128)S(1)} %get-tuple-element.72.mas, ...), custom_call_target="tpu_custom_call" | custom-call | flops 1100000000 | bytes 3400000 | tf_op jit(solution)/shard_map/pallas_call | solution.py:313
  17.7 1.8 %shard_map.154 = (f32[256,256]{1,0:T(8,128)S(1)}, f32[256,128]{1,0:T(8,128)S(1)}, bf16[256,256]{1,0:T(8,128)(2,1)S(1)}, bf16[256,768]{1,0:T(8,128)(2,1)S(1)}, f3...) custom-call(f32[256,256]{1,0:T(8,128)S(1)} %get-tuple-element.83.mas, ...), custom_call_target="tpu_custom_call" | custom-call | flops 1100000000 | bytes 3400000 | tf_op jit(solution)/shard_map/pallas_call | solution.py:313
  19.5 2.4 %shard_map.155 = (bf16[256,256]{1,0:T(8,128)(2,1)S(1)}, bf16[2,4,400,256]{3,2,1,0:T(8,128)(2,1)S(1)}, bf16[256,1024]{1,0:T(8,128)(2,1)}) custom-call(bf16[256,256]{1,0:T(8,128)(2,1)S(1)} %get-tuple-element.82.grad_ref, bf16[2,256,768]{2,1,0:T(8,128)(2,1)S(1)} %pad_maximum_fusion.6.w_qkv, bf16[2,256,256]{2,1,0:T(8,128)(2,1)S(1)} %pad_maximum_fusion.9.w_out, ...), custom_call_target="tpu_custom_call" | custom-call | flops 3300000000 | bytes 10200000 | tf_op jit(solution)/shard_map/pallas_call | solution.py:313
  22.0 0.4 collective-permute-start.11
  22.4 0.8 shard_map.156
  23.2 1.9 %shard_map.157 = (bf16[256,256]{1,0:T(8,128)(2,1)S(1)}, f32[640,256]{1,0:T(8,128)S(1)}, bf16[832,256]{1,0:T(8,128)(2,1)S(1)}, bf16[2,4,400,256]{3,2,1,0:T(8,128)(2,1)S(1)}) custom-call(bf16[256,256]{1,0:T(8,128)(2,1)S(1)} %get-tuple-element.97.grad_ref.one_near, bf16[2,256,768]{2,1,0:T(8,128)(2,1)S(1)} %pad_maximum_fusion.6.w_qkv, ...), custom_call_target="tpu_custom_call" | custom-call | flops 4400000000 | bytes 13600000 | tf_op jit(solution)/shard_map/pallas_call | solution.py:313
  25.2 0.2 collective-permute-start.18
  25.4 0.4 collective-permute-start.14
  25.8 1.6 %collective-permute-start.12 = (bf16[2,400,256]{2,1,0:T(8,128)(2,1)S(1)}, bf16[2,400,256]{2,1,0:T(8,128)(2,1)S(1)}, u32[]{:S(2)}, u32[]{:S(2)}) collective-permute-start(bf16[2,400,256]{2,1,0:T(8,128)(2,1)S(1)} %slice_add_fusion.1), channel_id=1, source_target_pairs={{0,1},{1,0},{2,3},{3,2},{16,18},{17,19},{18,16},{19,17},{4,5},{5,4... | collective-permute-start | bytes 1228808 | tf_op jit(solution)/shard_map/ppermute | solution.py:976
  27.4 0.2 collective-permute-done.18
  27.6 1.6 %collective-permute-start.19 = (bf16[2,400,256]{2,1,0:T(8,128)(2,1)S(1)}, bf16[2,400,256]{2,1,0:T(8,128)(2,1)S(1)}, u32[]{:S(2)}, u32[]{:S(2)}) collective-permute-start(bf16[2,400,256]{2,1,0:T(8,128)(2,1)S(1)} %slice_add_fusion), channel_id=1, source_target_pairs={{0,1},{1,0},{2,3},{3,2},{16,18},{17,19},{18,16},{19,17},{4,5},{5,4... | collective-permute-start | bytes 1228808 | tf_op jit(solution)/shard_map/ppermute | solution.py:976
  29.3 1.3 %collective-permute-start.15 = (bf16[256,256]{1,0:T(8,128)(2,1)S(1)}, bf16[256,256]{1,0:T(8,128)(2,1)S(1)}, u32[]{:S(2)}, u32[]{:S(2)}) collective-permute-start(bf16[256,256]{1,0:T(8,128)(2,1)S(1)} %get-tuple-element.119), channel_id=1, source_target_pairs={{0,4},{4,0},{8,12},{12,8},{1,5},{5,1},{9,13},{13,9},{2,6},{6,2},{1... | collective-permute-start | bytes 393224 | tf_op jit(solution)/shard_map/ppermute | solution.py:971
  30.6 1.8 %collective-permute-start.16 = (bf16[256,256]{1,0:T(8,128)(2,1)S(1)}, bf16[256,256]{1,0:T(8,128)(2,1)S(1)}, u32[]{:S(2)}, u32[]{:S(2)}) collective-permute-start(bf16[256,256]{1,0:T(8,128)(2,1)S(1)} %get-tuple-element.120), channel_id=1, source_target_pairs={{0,8},{4,12},{8,0},{12,4},{1,9},{5,13},{9,1},{13,5},{2,10},{6,14},... | collective-permute-start | bytes 393224 | tf_op jit(solution)/shard_map/ppermute | solution.py:971
  32.4 1.3 %collective-permute-start.17 = (bf16[256,256]{1,0:T(8,128)(2,1)S(1)}, bf16[256,256]{1,0:T(8,128)(2,1)S(1)}, u32[]{:S(2)}, u32[]{:S(2)}) collective-permute-start(bf16[256,256]{1,0:T(8,128)(2,1)S(1)} %get-tuple-element.121), channel_id=1, source_target_pairs={{0,12},{4,8},{8,4},{12,0},{1,13},{5,9},{9,5},{13,1},{2,14},{6,10},... | collective-permute-start | bytes 393224 | tf_op jit(solution)/shard_map/ppermute | solution.py:971
  33.7 0.1 collective-permute-done.12
  33.9 1.6 %collective-permute-start.13 = (bf16[400,256]{1,0:T(8,128)(2,1)S(1)}, bf16[400,256]{1,0:T(8,128)(2,1)S(1)}, u32[]{:S(2)}, u32[]{:S(2)}) collective-permute-start(bf16[400,256]{1,0:T(8,128)(2,1)S(1)} %fusion.5), channel_id=1, source_target_pairs={{0,2},{1,3},{2,0},{3,1},{16,17},{17,16},{18,19},{19,18},{4,6},{5,7... | collective-permute-start | bytes 614408 | tf_op jit(solution)/shard_map/ppermute | solution.py:977
  35.5 5.1 %collective-permute-done.19 = bf16[2,400,256]{2,1,0:T(8,128)(2,1)S(1)} collective-permute-done((bf16[2,400,256]{2,1,0:T(8,128)(2,1)S(1)}, bf16[2,400,256]{2,1,0:T(8,128)(2,1)S(1)}, u32[]{:S(2)}, u32[]{:S(2)}) %collective-permute-start.19) | collective-permute-done | bytes 409632 | tf_op jit(solution)/shard_map/ppermute | solution.py:976
  40.6 1.6 %collective-permute-start.20 = (bf16[400,256]{1,0:T(8,128)(2,1)S(1)}, bf16[400,256]{1,0:T(8,128)(2,1)S(1)}, u32[]{:S(2)}, u32[]{:S(2)}) collective-permute-start(bf16[400,256]{1,0:T(8,128)(2,1)S(1)} %fusion), channel_id=1, source_target_pairs={{0,2},{1,3},{2,0},{3,1},{16,17},{17,16},{18,19},{19,18},{4,6},{5,7... | collective-permute-start | bytes 614408 | tf_op jit(solution)/shard_map/ppermute | solution.py:977
  42.2 1.3 %collective-permute-done.16.piece2 = bf16[256,256]{1,0:T(8,128)(2,1)S(1)} collective-permute-done((bf16[256,256]{1,0:T(8,128)(2,1)S(1)}, bf16[256,256]{1,0:T(8,128)(2,1)S(1)}, u32[]{:S(2)}, u32[]{:S(2)}) %collective-permute-start.16) | collective-permute-done | bytes 131104 | tf_op jit(solution)/shard_map/ppermute | solution.py:971
  43.5 2.0 %collective-permute-start.28 = (bf16[400,256]{1,0:T(8,128)(2,1)S(1)}, bf16[400,256]{1,0:T(8,128)(2,1)S(1)}, u32[]{:S(2)}, u32[]{:S(2)}) collective-permute-start(bf16[400,256]{1,0:T(8,128)(2,1)S(1)} %fusion.8), channel_id=1, source_target_pairs={{0,4},{4,0},{8,12},{12,8},{1,5},{5,1},{9,13},{13,9},{2,6},{6,2},{1... | collective-permute-start | bytes 614408 | tf_op jit(solution)/shard_map/ppermute | solution.py:971
  45.5 0.9 %collective-permute-done.20 = bf16[400,256]{1,0:T(8,128)(2,1)S(1)} collective-permute-done((bf16[400,256]{1,0:T(8,128)(2,1)S(1)}, bf16[400,256]{1,0:T(8,128)(2,1)S(1)}, u32[]{:S(2)}, u32[]{:S(2)}) %collective-permute-start.20) | collective-permute-done | bytes 204832 | tf_op jit(solution)/shard_map/ppermute | solution.py:977
  46.5 1.2 %collective-permute-start.21 = (bf16[400,256]{1,0:T(8,128)(2,1)S(1)}, bf16[400,256]{1,0:T(8,128)(2,1)S(1)}, u32[]{:S(2)}, u32[]{:S(2)}) collective-permute-start(bf16[400,256]{1,0:T(8,128)(2,1)S(1)} %fusion.3), channel_id=1, source_target_pairs={{0,4},{4,0},{8,12},{12,8},{1,5},{5,1},{9,13},{13,9},{2,6},{6,2},{1... | collective-permute-start | bytes 614408 | tf_op jit(solution)/shard_map/ppermute | solution.py:971
  47.7 3.8 %collective-permute-done.28 = bf16[400,256]{1,0:T(8,128)(2,1)S(1)} collective-permute-done((bf16[400,256]{1,0:T(8,128)(2,1)S(1)}, bf16[400,256]{1,0:T(8,128)(2,1)S(1)}, u32[]{:S(2)}, u32[]{:S(2)}) %collective-permute-start.28) | collective-permute-done | bytes 204832 | tf_op jit(solution)/shard_map/ppermute | solution.py:971
  51.6 2.9 %collective-permute-start.29 = (bf16[200,256]{1,0:T(8,128)(2,1)S(1)}, bf16[200,256]{1,0:T(8,128)(2,1)S(1)}, u32[]{:S(2)}, u32[]{:S(2)}) collective-permute-start(bf16[200,256]{1,0:T(8,128)(2,1)S(1)} %constant_dynamic-slice_fusion), channel_id=1, source_target_pairs={{0,8},{4,12},{8,0},{12,4},{1,9},{5,13},{9,1},{13,5},{2,10},{6,14},... | collective-permute-start | bytes 307208 | tf_op jit(solution)/shard_map/ppermute | solution.py:971
  54.5 0.4 collective-permute-done.21
  55.0 3.2 %collective-permute-start.22 = (bf16[200,256]{1,0:T(8,128)(2,1)S(1)}, bf16[200,256]{1,0:T(8,128)(2,1)S(1)}, u32[]{:S(2)}, u32[]{:S(2)}) collective-permute-start(bf16[200,256]{1,0:T(8,128)(2,1)S(1)} %constant_dynamic-slice_fusion.1), channel_id=1, source_target_pairs={{0,8},{4,12},{8,0},{12,4},{1,9},{5,13},{9,1},{13,5},{2,10},{6,14},... | collective-permute-start | bytes 307208 | tf_op jit(solution)/shard_map/ppermute | solution.py:971
  58.3 2.1 %collective-permute-done.29 = bf16[200,256]{1,0:T(8,128)(2,1)S(1)} collective-permute-done((bf16[200,256]{1,0:T(8,128)(2,1)S(1)}, bf16[200,256]{1,0:T(8,128)(2,1)S(1)}, u32[]{:S(2)}, u32[]{:S(2)}) %collective-permute-start.29) | collective-permute-done | bytes 102432 | tf_op jit(solution)/shard_map/ppermute | solution.py:971
  60.5 2.4 %collective-permute-done.22 = bf16[200,256]{1,0:T(8,128)(2,1)S(1)} collective-permute-done((bf16[200,256]{1,0:T(8,128)(2,1)S(1)}, bf16[200,256]{1,0:T(8,128)(2,1)S(1)}, u32[]{:S(2)}, u32[]{:S(2)}) %collective-permute-start.22) | collective-permute-done | bytes 102432 | tf_op jit(solution)/shard_map/ppermute | solution.py:971
  63.0 2.4 %collective-permute-done.30 = bf16[200,256]{1,0:T(8,128)(2,1)S(1)} collective-permute-done((bf16[200,256]{1,0:T(8,128)(2,1)S(1)}, bf16[200,256]{1,0:T(8,128)(2,1)S(1)}, u32[]{:S(2)}, u32[]{:S(2)}) %collective-permute-start.30) | collective-permute-done | bytes 102432 | tf_op jit(solution)/shard_map/ppermute | solution.py:971
  65.5 0.5 collective-permute-start.31
  66.1 1.6 %collective-permute-done.23 = bf16[200,256]{1,0:T(8,128)(2,1)S(1)} collective-permute-done((bf16[200,256]{1,0:T(8,128)(2,1)S(1)}, bf16[200,256]{1,0:T(8,128)(2,1)S(1)}, u32[]{:S(2)}, u32[]{:S(2)}) %collective-permute-start.23) | collective-permute-done | bytes 102432 | tf_op jit(solution)/shard_map/ppermute | solution.py:971
  67.8 0.5 collective-permute-start.24
  68.3 3.2 %collective-permute-done.31 = bf16[400,256]{1,0:T(8,128)(2,1)S(1)} collective-permute-done((bf16[400,256]{1,0:T(8,128)(2,1)S(1)}, bf16[400,256]{1,0:T(8,128)(2,1)S(1)}, u32[]{:S(2)}, u32[]{:S(2)}) %collective-permute-start.31) | collective-permute-done | bytes 204832 | tf_op jit(solution)/shard_map/ppermute | solution.py:992
  71.5 0.2 collective-permute-start.32
  71.7 4.1 %collective-permute-done.24 = bf16[400,256]{1,0:T(8,128)(2,1)S(1)} collective-permute-done((bf16[400,256]{1,0:T(8,128)(2,1)S(1)}, bf16[400,256]{1,0:T(8,128)(2,1)S(1)}, u32[]{:S(2)}, u32[]{:S(2)}) %collective-permute-start.24) | collective-permute-done | bytes 204832 | tf_op jit(solution)/shard_map/ppermute | solution.py:992
  75.9 2.3 %collective-permute-start.25 = (bf16[2,400,256]{2,1,0:T(8,128)(2,1)S(1)}, bf16[2,400,256]{2,1,0:T(8,128)(2,1)S(1)}, u32[]{:S(2)}, u32[]{:S(2)}) collective-permute-start(bf16[2,400,256]{2,1,0:T(8,128)(2,1)S(1)} %pad_maximum_fusion.7), channel_id=1, source_target_pairs={{0,1},{1,0},{2,3},{3,2},{16,18},{17,19},{18,16},{19,17},{4,5},{5,4... | collective-permute-start | bytes 1228808 | tf_op jit(solution)/shard_map/ppermute | solution.py:993
  78.2 1.3 %collective-permute-start.33 = (bf16[2,400,256]{2,1,0:T(8,128)(2,1)S(1)}, bf16[2,400,256]{2,1,0:T(8,128)(2,1)S(1)}, u32[]{:S(2)}, u32[]{:S(2)}) collective-permute-start(bf16[2,400,256]{2,1,0:T(8,128)(2,1)S(1)} %pad_maximum_fusion.8), channel_id=1, source_target_pairs={{0,16},{1,17},{2,18},{3,19},{4,20},{5,21},{6,22},{7,23},{8,24},{9,... | collective-permute-start | bytes 1228808 | tf_op jit(solution)/shard_map/ppermute | solution.py:1200
  79.5 1.3 %collective-permute-start.34 = (bf16[2,400,256]{2,1,0:T(8,128)(2,1)S(1)}, bf16[2,400,256]{2,1,0:T(8,128)(2,1)S(1)}, u32[]{:S(2)}, u32[]{:S(2)}) collective-permute-start(bf16[2,400,256]{2,1,0:T(8,128)(2,1)S(1)} %collective-permute-done.32), channel_id=1, source_target_pairs={{0,16},{1,17},{2,18},{3,19},{4,20},{5,21},{6,22},{7,23},{8,24},{9,... | collective-permute-start | bytes 1228808 | tf_op jit(solution)/shard_map/ppermute | solution.py:1200
  80.8 1.3 %collective-permute-start.26 = (bf16[2,400,256]{2,1,0:T(8,128)(2,1)S(1)}, bf16[2,400,256]{2,1,0:T(8,128)(2,1)S(1)}, u32[]{:S(2)}, u32[]{:S(2)}) collective-permute-start(bf16[2,400,256]{2,1,0:T(8,128)(2,1)S(1)} %pad_maximum_fusion.7), channel_id=1, source_target_pairs={{16,0},{17,1},{18,2},{19,3},{20,4},{21,5},{22,6},{23,7},{24,8},{25... | collective-permute-start | bytes 1228808 | tf_op jit(solution)/shard_map/ppermute | solution.py:1200
  82.1 2.0 %collective-permute-done.25 = bf16[2,400,256]{2,1,0:T(8,128)(2,1)S(1)} collective-permute-done((bf16[2,400,256]{2,1,0:T(8,128)(2,1)S(1)}, bf16[2,400,256]{2,1,0:T(8,128)(2,1)S(1)}, u32[]{:S(2)}, u32[]{:S(2)}) %collective-permute-start.25) | collective-permute-done | bytes 409632 | tf_op jit(solution)/shard_map/ppermute | solution.py:993
  84.1 1.3 %collective-permute-start.27 = (bf16[2,400,256]{2,1,0:T(8,128)(2,1)S(1)}, bf16[2,400,256]{2,1,0:T(8,128)(2,1)S(1)}, u32[]{:S(2)}, u32[]{:S(2)}) collective-permute-start(bf16[2,400,256]{2,1,0:T(8,128)(2,1)S(1)} %collective-permute-done.25), channel_id=1, source_target_pairs={{16,0},{17,1},{18,2},{19,3},{20,4},{21,5},{22,6},{23,7},{24,8},{25... | collective-permute-start | bytes 1228808 | tf_op jit(solution)/shard_map/ppermute | solution.py:1200
  85.4 0.8 shard_map.159
  86.2 0.1 pad_maximum_fusion.4.one_near
  86.3 0.1 pad_maximum_fusion.2.zero_near
  86.5 1.2 %collective-permute-done.27 = bf16[2,400,256]{2,1,0:T(8,128)(2,1)S(1)} collective-permute-done((bf16[2,400,256]{2,1,0:T(8,128)(2,1)S(1)}, bf16[2,400,256]{2,1,0:T(8,128)(2,1)S(1)}, u32[]{:S(2)}, u32[]{:S(2)}) %collective-permute-start.27) | collective-permute-done | bytes 409632 | tf_op jit(solution)/shard_map/ppermute | solution.py:1200
  87.8 2.4 %shard_map.160 = (f32[1,256]{1,0:T(1,128)}, f32[1,256,768]{2,1,0:T(8,128)}, f32[1,256,256]{2,1,0:T(8,128)}, f32[1,256]{1,0:T(1,128)}, f32[1,256,1024]{2,1,0:T(8,128)}, /*index=5*/f32[1,1024,256]{2,1,0:T(8,128)}) custom-call(bf16[4,400,256]{2,1,0:T(8,128)(2,1)S(1)} %pad_maximum_fusion.2.zero_near, bf16[4,400,256]{2,1,0:T(8,128)(2,1)S(1)} %pad_maximum_fusion.3.zero_far, ...), custom_call_target="tpu_custom_call" | custom-call | flops 1100000000 | bytes 3400000 | tf_op jit(solution)/shard_map/pallas_call | solution.py:313
  (55 shorter events, 1.4 us)
Async XLA Ops:
  0.6 7.9 %copy-start.2 = (bf16[1,256,768]{2,1,0:T(8,128)(2,1)S(1)}, bf16[1,256,768]{2,1,0:T(8,128)(2,1)}, u32[]{:S(2)}) copy-start(bf16[1,256,768]{2,1,0:T(8,128)(2,1)} %param.13) | copy-start | bytes 1179652
  0.6 7.4 %copy-start.3 = (bf16[1,256,256]{2,1,0:T(8,128)(2,1)S(1)}, bf16[1,256,256]{2,1,0:T(8,128)(2,1)}, u32[]{:S(2)}) copy-start(bf16[1,256,256]{2,1,0:T(8,128)(2,1)} %param.14) | copy-start | bytes 393220
  0.7 9.5 %copy-start.1 = (bf16[1,256,1024]{2,1,0:T(8,128)(2,1)S(1)}, bf16[1,256,1024]{2,1,0:T(8,128)(2,1)}, u32[]{:S(2)}) copy-start(bf16[1,256,1024]{2,1,0:T(8,128)(2,1)} %param.16) | copy-start | bytes 1572868
  0.7 7.3 %copy-start = (bf16[1,1024,256]{2,1,0:T(8,128)(2,1)S(1)}, bf16[1,1024,256]{2,1,0:T(8,128)(2,1)}, u32[]{:S(2)}) copy-start(bf16[1,1024,256]{2,1,0:T(8,128)(2,1)} %param.17) | copy-start | bytes 1572868
  2.2 6.4 %collective-permute-start.3 = (bf16[144,256]{1,0:T(8,128)(2,1)S(1)}, bf16[144,256]{1,0:T(8,128)(2,1)S(1)}, u32[]{:S(2)}, u32[]{:S(2)}) collective-permute-start(bf16[144,256]{1,0:T(8,128)(2,1)S(1)} %get-tuple-element.73.own0), channel_id=1, source_target_pairs={{0,16},{16,0},{1,17},{17,1},{2,18},{18,2},{3,19},{19,3},{4,20},{20... | collective-permute-start | bytes 221192 | tf_op jit(solution)/shard_map/ppermute | solution.py:1036
  2.7 5.3 %collective-permute-start = (bf16[128,256]{1,0:T(8,128)(2,1)S(1)}, bf16[128,256]{1,0:T(8,128)(2,1)S(1)}, u32[]{:S(2)}, u32[]{:S(2)}) collective-permute-start(bf16[128,256]{1,0:T(8,128)(2,1)S(1)} %get-tuple-element.74), channel_id=1, source_target_pairs={{0,4},{4,0},{8,12},{12,8},{1,5},{5,1},{9,13},{13,9},{2,6},{6,2},{1... | collective-permute-start | bytes 196616 | tf_op jit(solution)/shard_map/ppermute | solution.py:971
  5.3 7.7 %collective-permute-start.1 = (bf16[128,256]{1,0:T(8,128)(2,1)S(1)}, bf16[128,256]{1,0:T(8,128)(2,1)S(1)}, u32[]{:S(2)}, u32[]{:S(2)}) collective-permute-start(bf16[128,256]{1,0:T(8,128)(2,1)S(1)} %get-tuple-element.76), channel_id=1, source_target_pairs={{0,8},{4,12},{8,0},{12,4},{1,9},{5,13},{9,1},{13,5},{2,10},{6,14},... | collective-permute-start | bytes 196616 | tf_op jit(solution)/shard_map/ppermute | solution.py:971
  7.9 6.1 %collective-permute-start.2 = (bf16[128,256]{1,0:T(8,128)(2,1)S(1)}, bf16[128,256]{1,0:T(8,128)(2,1)S(1)}, u32[]{:S(2)}, u32[]{:S(2)}) collective-permute-start(bf16[128,256]{1,0:T(8,128)(2,1)S(1)} %get-tuple-element.77), channel_id=1, source_target_pairs={{0,12},{4,8},{8,4},{12,0},{1,13},{5,9},{9,5},{13,1},{2,14},{6,10},... | collective-permute-start | bytes 196616 | tf_op jit(solution)/shard_map/ppermute | solution.py:971
  8.0 6.7 %collective-permute-start.10 = (bf16[1024,256]{1,0:T(8,128)(2,1)S(1)}, bf16[1024,256]{1,0:T(8,128)(2,1)S(1)}, u32[]{:S(2)}, u32[]{:S(2)}) collective-permute-start(bf16[1024,256]{1,0:T(8,128)(2,1)S(1)} %bitcast.96), channel_id=1, source_target_pairs={{0,16},{16,0},{1,17},{17,1},{2,18},{18,2},{3,19},{19,3},{4,20},{20... | collective-permute-start | bytes 1572872 | tf_op jit(solution)/shard_map/ppermute | solution.py:1039
  8.0 2.1 %collective-permute-start.8 = (bf16[256,256]{1,0:T(8,128)(2,1)S(1)}, bf16[256,256]{1,0:T(8,128)(2,1)S(1)}, u32[]{:S(2)}, u32[]{:S(2)}) collective-permute-start(bf16[256,256]{1,0:T(8,128)(2,1)S(1)} %bitcast.102), channel_id=1, source_target_pairs={{0,16},{16,0},{1,17},{17,1},{2,18},{18,2},{3,19},{19,3},{4,20},{20... | collective-permute-start | bytes 393224 | tf_op jit(solution)/shard_map/ppermute | solution.py:1039
  8.5 5.5 %collective-permute-start.7 = (bf16[256,768]{1,0:T(8,128)(2,1)S(1)}, bf16[256,768]{1,0:T(8,128)(2,1)S(1)}, u32[]{:S(2)}, u32[]{:S(2)}) collective-permute-start(bf16[256,768]{1,0:T(8,128)(2,1)S(1)} %bitcast.100), channel_id=1, source_target_pairs={{0,16},{16,0},{1,17},{17,1},{2,18},{18,2},{3,19},{19,3},{4,20},{20... | collective-permute-start | bytes 1179656 | tf_op jit(solution)/shard_map/ppermute | solution.py:1039
  10.1 4.8 %collective-permute-start.9 = (bf16[256,1024]{1,0:T(8,128)(2,1)S(1)}, bf16[256,1024]{1,0:T(8,128)(2,1)S(1)}, u32[]{:S(2)}, u32[]{:S(2)}) collective-permute-start(bf16[256,1024]{1,0:T(8,128)(2,1)S(1)} %bitcast.98), channel_id=1, source_target_pairs={{0,16},{16,0},{1,17},{17,1},{2,18},{18,2},{3,19},{19,3},{4,20},{20... | collective-permute-start | bytes 1572872 | tf_op jit(solution)/shard_map/ppermute | solution.py:1039
  13.0 2.1 %collective-permute-start.4 = (bf16[128,256]{1,0:T(8,128)(2,1)S(1)}, bf16[128,256]{1,0:T(8,128)(2,1)S(1)}, u32[]{:S(2)}, u32[]{:S(2)}) collective-permute-start(bf16[128,256]{1,0:T(8,128)(2,1)S(1)} %collective-permute-done.own1), channel_id=1, source_target_pairs={{0,16},{16,0},{1,17},{17,1},{2,18},{18,2},{3,19},{19,3},{4,20},{20... | collective-permute-start | bytes 196616 | tf_op jit(solution)/shard_map/ppermute | solution.py:1036
  14.0 1.3 %collective-permute-start.5 = (bf16[128,256]{1,0:T(8,128)(2,1)S(1)}, bf16[128,256]{1,0:T(8,128)(2,1)S(1)}, u32[]{:S(2)}, u32[]{:S(2)}) collective-permute-start(bf16[128,256]{1,0:T(8,128)(2,1)S(1)} %collective-permute-done.1.own2), channel_id=1, source_target_pairs={{0,16},{16,0},{1,17},{17,1},{2,18},{18,2},{3,19},{19,3},{4,20},{20... | collective-permute-start | bytes 196616 | tf_op jit(solution)/shard_map/ppermute | solution.py:1036
  14.0 1.4 %collective-permute-start.6 = (bf16[128,256]{1,0:T(8,128)(2,1)S(1)}, bf16[128,256]{1,0:T(8,128)(2,1)S(1)}, u32[]{:S(2)}, u32[]{:S(2)}) collective-permute-start(bf16[128,256]{1,0:T(8,128)(2,1)S(1)} %collective-permute-done.2.own3), channel_id=1, source_target_pairs={{0,16},{16,0},{1,17},{17,1},{2,18},{18,2},{3,19},{19,3},{4,20},{20... | collective-permute-start | bytes 196616 | tf_op jit(solution)/shard_map/ppermute | solution.py:1036
  22.0 3.8 %collective-permute-start.11 = (bf16[4,400,256]{2,1,0:T(8,128)(2,1)S(1)}, bf16[4,400,256]{2,1,0:T(8,128)(2,1)S(1)}, u32[]{:S(2)}, u32[]{:S(2)}) collective-permute-start(bf16[4,400,256]{2,1,0:T(8,128)(2,1)S(1)} %slice_bitcast_fusion.1), channel_id=1, source_target_pairs={{0,16},{16,0},{1,17},{17,1},{2,18},{18,2},{3,19},{19,3},{4,20},{20... | collective-permute-start | bytes 2457608 | tf_op jit(solution)/shard_map/ppermute | solution.py:1136
  25.2 2.4 %collective-permute-start.18 = (bf16[4,400,256]{2,1,0:T(8,128)(2,1)S(1)}, bf16[4,400,256]{2,1,0:T(8,128)(2,1)S(1)}, u32[]{:S(2)}, u32[]{:S(2)}) collective-permute-start(bf16[4,400,256]{2,1,0:T(8,128)(2,1)S(1)} %slice_bitcast_fusion), channel_id=1, source_target_pairs={{0,16},{16,0},{1,17},{17,1},{2,18},{18,2},{3,19},{19,3},{4,20},{20... | collective-permute-start | bytes 2457608 | tf_op jit(solution)/shard_map/ppermute | solution.py:1187
  25.4 3.8 %collective-permute-start.14 = (bf16[832,256]{1,0:T(8,128)(2,1)S(1)}, bf16[832,256]{1,0:T(8,128)(2,1)S(1)}, u32[]{:S(2)}, u32[]{:S(2)}) collective-permute-start(bf16[832,256]{1,0:T(8,128)(2,1)S(1)} %get-tuple-element.117), channel_id=1, source_target_pairs={{0,16},{16,0},{1,17},{17,1},{2,18},{18,2},{3,19},{19,3},{4,20},{20... | collective-permute-start | bytes 1277960 | tf_op jit(solution)/shard_map/ppermute | solution.py:1178
  25.8 8.0 %collective-permute-start.12 = (bf16[2,400,256]{2,1,0:T(8,128)(2,1)S(1)}, bf16[2,400,256]{2,1,0:T(8,128)(2,1)S(1)}, u32[]{:S(2)}, u32[]{:S(2)}) collective-permute-start(bf16[2,400,256]{2,1,0:T(8,128)(2,1)S(1)} %slice_add_fusion.1), channel_id=1, source_target_pairs={{0,1},{1,0},{2,3},{3,2},{16,18},{17,19},{18,16},{19,17},{4,5},{5,4... | collective-permute-start | bytes 1228808 | tf_op jit(solution)/shard_map/ppermute | solution.py:976
  27.6 12.9 %collective-permute-start.19 = (bf16[2,400,256]{2,1,0:T(8,128)(2,1)S(1)}, bf16[2,400,256]{2,1,0:T(8,128)(2,1)S(1)}, u32[]{:S(2)}, u32[]{:S(2)}) collective-permute-start(bf16[2,400,256]{2,1,0:T(8,128)(2,1)S(1)} %slice_add_fusion), channel_id=1, source_target_pairs={{0,1},{1,0},{2,3},{3,2},{16,18},{17,19},{18,16},{19,17},{4,5},{5,4... | collective-permute-start | bytes 1228808 | tf_op jit(solution)/shard_map/ppermute | solution.py:976
  29.3 13.0 %collective-permute-start.15 = (bf16[256,256]{1,0:T(8,128)(2,1)S(1)}, bf16[256,256]{1,0:T(8,128)(2,1)S(1)}, u32[]{:S(2)}, u32[]{:S(2)}) collective-permute-start(bf16[256,256]{1,0:T(8,128)(2,1)S(1)} %get-tuple-element.119), channel_id=1, source_target_pairs={{0,4},{4,0},{8,12},{12,8},{1,5},{5,1},{9,13},{13,9},{2,6},{6,2},{1... | collective-permute-start | bytes 393224 | tf_op jit(solution)/shard_map/ppermute | solution.py:971
  30.6 12.9 %collective-permute-start.16 = (bf16[256,256]{1,0:T(8,128)(2,1)S(1)}, bf16[256,256]{1,0:T(8,128)(2,1)S(1)}, u32[]{:S(2)}, u32[]{:S(2)}) collective-permute-start(bf16[256,256]{1,0:T(8,128)(2,1)S(1)} %get-tuple-element.120), channel_id=1, source_target_pairs={{0,8},{4,12},{8,0},{12,4},{1,9},{5,13},{9,1},{13,5},{2,10},{6,14},... | collective-permute-start | bytes 393224 | tf_op jit(solution)/shard_map/ppermute | solution.py:971
  32.4 11.1 %collective-permute-start.17 = (bf16[256,256]{1,0:T(8,128)(2,1)S(1)}, bf16[256,256]{1,0:T(8,128)(2,1)S(1)}, u32[]{:S(2)}, u32[]{:S(2)}) collective-permute-start(bf16[256,256]{1,0:T(8,128)(2,1)S(1)} %get-tuple-element.121), channel_id=1, source_target_pairs={{0,12},{4,8},{8,4},{12,0},{1,13},{5,9},{9,5},{13,1},{2,14},{6,10},... | collective-permute-start | bytes 393224 | tf_op jit(solution)/shard_map/ppermute | solution.py:971
  33.9 8.3 %collective-permute-start.13 = (bf16[400,256]{1,0:T(8,128)(2,1)S(1)}, bf16[400,256]{1,0:T(8,128)(2,1)S(1)}, u32[]{:S(2)}, u32[]{:S(2)}) collective-permute-start(bf16[400,256]{1,0:T(8,128)(2,1)S(1)} %fusion.5), channel_id=1, source_target_pairs={{0,2},{1,3},{2,0},{3,1},{16,17},{17,16},{18,19},{19,18},{4,6},{5,7... | collective-permute-start | bytes 614408 | tf_op jit(solution)/shard_map/ppermute | solution.py:977
  40.6 5.8 %collective-permute-start.20 = (bf16[400,256]{1,0:T(8,128)(2,1)S(1)}, bf16[400,256]{1,0:T(8,128)(2,1)S(1)}, u32[]{:S(2)}, u32[]{:S(2)}) collective-permute-start(bf16[400,256]{1,0:T(8,128)(2,1)S(1)} %fusion), channel_id=1, source_target_pairs={{0,2},{1,3},{2,0},{3,1},{16,17},{17,16},{18,19},{19,18},{4,6},{5,7... | collective-permute-start | bytes 614408 | tf_op jit(solution)/shard_map/ppermute | solution.py:977
  43.5 8.0 %collective-permute-start.28 = (bf16[400,256]{1,0:T(8,128)(2,1)S(1)}, bf16[400,256]{1,0:T(8,128)(2,1)S(1)}, u32[]{:S(2)}, u32[]{:S(2)}) collective-permute-start(bf16[400,256]{1,0:T(8,128)(2,1)S(1)} %fusion.8), channel_id=1, source_target_pairs={{0,4},{4,0},{8,12},{12,8},{1,5},{5,1},{9,13},{13,9},{2,6},{6,2},{1... | collective-permute-start | bytes 614408 | tf_op jit(solution)/shard_map/ppermute | solution.py:971
  46.5 8.5 %collective-permute-start.21 = (bf16[400,256]{1,0:T(8,128)(2,1)S(1)}, bf16[400,256]{1,0:T(8,128)(2,1)S(1)}, u32[]{:S(2)}, u32[]{:S(2)}) collective-permute-start(bf16[400,256]{1,0:T(8,128)(2,1)S(1)} %fusion.3), channel_id=1, source_target_pairs={{0,4},{4,0},{8,12},{12,8},{1,5},{5,1},{9,13},{13,9},{2,6},{6,2},{1... | collective-permute-start | bytes 614408 | tf_op jit(solution)/shard_map/ppermute | solution.py:971
  51.6 8.8 %collective-permute-start.29 = (bf16[200,256]{1,0:T(8,128)(2,1)S(1)}, bf16[200,256]{1,0:T(8,128)(2,1)S(1)}, u32[]{:S(2)}, u32[]{:S(2)}) collective-permute-start(bf16[200,256]{1,0:T(8,128)(2,1)S(1)} %constant_dynamic-slice_fusion), channel_id=1, source_target_pairs={{0,8},{4,12},{8,0},{12,4},{1,9},{5,13},{9,1},{13,5},{2,10},{6,14},... | collective-permute-start | bytes 307208 | tf_op jit(solution)/shard_map/ppermute | solution.py:971
  55.0 7.9 %collective-permute-start.22 = (bf16[200,256]{1,0:T(8,128)(2,1)S(1)}, bf16[200,256]{1,0:T(8,128)(2,1)S(1)}, u32[]{:S(2)}, u32[]{:S(2)}) collective-permute-start(bf16[200,256]{1,0:T(8,128)(2,1)S(1)} %constant_dynamic-slice_fusion.1), channel_id=1, source_target_pairs={{0,8},{4,12},{8,0},{12,4},{1,9},{5,13},{9,1},{13,5},{2,10},{6,14},... | collective-permute-start | bytes 307208 | tf_op jit(solution)/shard_map/ppermute | solution.py:971
  60.5 5.0 %collective-permute-start.30 = (bf16[200,256]{1,0:T(8,128)(2,1)S(1)}, bf16[200,256]{1,0:T(8,128)(2,1)S(1)}, u32[]{:S(2)}, u32[]{:S(2)}) collective-permute-start(bf16[200,256]{1,0:T(8,128)(2,1)S(1)} %fusion.12), channel_id=1, source_target_pairs={{0,4},{4,0},{8,12},{12,8},{1,5},{5,1},{9,13},{13,9},{2,6},{6,2},{1... | collective-permute-start | bytes 307208 | tf_op jit(solution)/shard_map/ppermute | solution.py:971
  63.0 4.7 %collective-permute-start.23 = (bf16[200,256]{1,0:T(8,128)(2,1)S(1)}, bf16[200,256]{1,0:T(8,128)(2,1)S(1)}, u32[]{:S(2)}, u32[]{:S(2)}) collective-permute-start(bf16[200,256]{1,0:T(8,128)(2,1)S(1)} %fusion.13), channel_id=1, source_target_pairs={{0,4},{4,0},{8,12},{12,8},{1,5},{5,1},{9,13},{13,9},{2,6},{6,2},{1... | collective-permute-start | bytes 307208 | tf_op jit(solution)/shard_map/ppermute | solution.py:971
  65.5 5.9 %collective-permute-start.31 = (bf16[400,256]{1,0:T(8,128)(2,1)S(1)}, bf16[400,256]{1,0:T(8,128)(2,1)S(1)}, u32[]{:S(2)}, u32[]{:S(2)}) collective-permute-start(bf16[400,256]{1,0:T(8,128)(2,1)S(1)} %maximum_select_fusion.1), channel_id=1, source_target_pairs={{0,2},{1,3},{2,0},{3,1},{16,17},{17,16},{18,19},{19,18},{4,6},{5,7... | collective-permute-start | bytes 614408 | tf_op jit(solution)/shard_map/ppermute | solution.py:992
  67.8 8.1 %collective-permute-start.24 = (bf16[400,256]{1,0:T(8,128)(2,1)S(1)}, bf16[400,256]{1,0:T(8,128)(2,1)S(1)}, u32[]{:S(2)}, u32[]{:S(2)}) collective-permute-start(bf16[400,256]{1,0:T(8,128)(2,1)S(1)} %maximum_select_fusion), channel_id=1, source_target_pairs={{0,2},{1,3},{2,0},{3,1},{16,17},{17,16},{18,19},{19,18},{4,6},{5,7... | collective-permute-start | bytes 614408 | tf_op jit(solution)/shard_map/ppermute | solution.py:992
  71.5 8.0 %collective-permute-start.32 = (bf16[2,400,256]{2,1,0:T(8,128)(2,1)S(1)}, bf16[2,400,256]{2,1,0:T(8,128)(2,1)S(1)}, u32[]{:S(2)}, u32[]{:S(2)}) collective-permute-start(bf16[2,400,256]{2,1,0:T(8,128)(2,1)S(1)} %pad_maximum_fusion.8), channel_id=1, source_target_pairs={{0,1},{1,0},{2,3},{3,2},{16,18},{17,19},{18,16},{19,17},{4,5},{5,4... | collective-permute-start | bytes 1228808 | tf_op jit(solution)/shard_map/ppermute | solution.py:993
  75.9 8.2 %collective-permute-start.25 = (bf16[2,400,256]{2,1,0:T(8,128)(2,1)S(1)}, bf16[2,400,256]{2,1,0:T(8,128)(2,1)S(1)}, u32[]{:S(2)}, u32[]{:S(2)}) collective-permute-start(bf16[2,400,256]{2,1,0:T(8,128)(2,1)S(1)} %pad_maximum_fusion.7), channel_id=1, source_target_pairs={{0,1},{1,0},{2,3},{3,2},{16,18},{17,19},{18,16},{19,17},{4,5},{5,4... | collective-permute-start | bytes 1228808 | tf_op jit(solution)/shard_map/ppermute | solution.py:993
  78.2 8.2 %collective-permute-start.33 = (bf16[2,400,256]{2,1,0:T(8,128)(2,1)S(1)}, bf16[2,400,256]{2,1,0:T(8,128)(2,1)S(1)}, u32[]{:S(2)}, u32[]{:S(2)}) collective-permute-start(bf16[2,400,256]{2,1,0:T(8,128)(2,1)S(1)} %pad_maximum_fusion.8), channel_id=1, source_target_pairs={{0,16},{1,17},{2,18},{3,19},{4,20},{5,21},{6,22},{7,23},{8,24},{9,... | collective-permute-start | bytes 1228808 | tf_op jit(solution)/shard_map/ppermute | solution.py:1200
  79.5 6.9 %collective-permute-start.34 = (bf16[2,400,256]{2,1,0:T(8,128)(2,1)S(1)}, bf16[2,400,256]{2,1,0:T(8,128)(2,1)S(1)}, u32[]{:S(2)}, u32[]{:S(2)}) collective-permute-start(bf16[2,400,256]{2,1,0:T(8,128)(2,1)S(1)} %collective-permute-done.32), channel_id=1, source_target_pairs={{0,16},{1,17},{2,18},{3,19},{4,20},{5,21},{6,22},{7,23},{8,24},{9,... | collective-permute-start | bytes 1228808 | tf_op jit(solution)/shard_map/ppermute | solution.py:1200
  80.8 5.7 %collective-permute-start.26 = (bf16[2,400,256]{2,1,0:T(8,128)(2,1)S(1)}, bf16[2,400,256]{2,1,0:T(8,128)(2,1)S(1)}, u32[]{:S(2)}, u32[]{:S(2)}) collective-permute-start(bf16[2,400,256]{2,1,0:T(8,128)(2,1)S(1)} %pad_maximum_fusion.7), channel_id=1, source_target_pairs={{16,0},{17,1},{18,2},{19,3},{20,4},{21,5},{22,6},{23,7},{24,8},{25... | collective-permute-start | bytes 1228808 | tf_op jit(solution)/shard_map/ppermute | solution.py:1200
  84.1 3.6 %collective-permute-start.27 = (bf16[2,400,256]{2,1,0:T(8,128)(2,1)S(1)}, bf16[2,400,256]{2,1,0:T(8,128)(2,1)S(1)}, u32[]{:S(2)}, u32[]{:S(2)}) collective-permute-start(bf16[2,400,256]{2,1,0:T(8,128)(2,1)S(1)} %collective-permute-done.25), channel_id=1, source_target_pairs={{16,0},{17,1},{18,2},{19,3},{20,4},{21,5},{22,6},{23,7},{24,8},{25... | collective-permute-start | bytes 1228808 | tf_op jit(solution)/shard_map/ppermute | solution.py:1200

commit v4 on v3

--- a/solution.py
+++ b/solution.py
@@ -306,7 +306,11 @@
 GAIN_ROWS = 16
 
 
-def call(body, scalars, arrays, shapes, mib=24, micros=1.0, scratch=(), held=0, out_held=()):
+def in_hbm(array):
+    return pltpu.with_memory_space_constraint(array, pltpu.HBM)
+
+
+def call(body, scalars, arrays, shapes, mib=24, micros=1.0, scratch=(), held=0, out_held=(), aliases=None):
     in_specs = [pl.BlockSpec(memory_space=pltpu.SMEM)] * len(scalars)
     in_specs += [pl.BlockSpec(memory_space=pl.ANY)] * held
     in_specs += [pl.BlockSpec(memory_space=pltpu.VMEM)] * (len(arrays) - held)
@@ -319,13 +323,14 @@
             for index in range(len(shapes))
         ),
         scratch_shapes=list(scratch),
+        input_output_aliases=aliases or {},
         compiler_params=pltpu.CompilerParams(vmem_limit_bytes=mib * MIB),
         cost_estimate=pl.CostEstimate(
             flops=int(micros * 1.1e9), bytes_accessed=int(micros * 3.4e6), transcendentals=0
         ),
     )(
         *scalars,
-        *(pltpu.with_memory_space_constraint(array, pltpu.HBM) for array in arrays[:held]),
+        *(array if aliases else in_hbm(array) for array in arrays[:held]),
         *arrays[held:],
     )
 
@@ -913,46 +918,52 @@
         input_grads[0, micro, 0] = piece[block:, :]
 
 
-def finish_kernel(zero_near, zero_far, one_near, one_far, *rest):
-    gain_attn, qkv, out, gain_ffn, up, down, qkv_held, out_held, up_held, down_held, sems = rest
-    width = zero_near.shape[2]
+def write_half(core, terms, targets, held, sems):
+    width = terms.shape[2]
     unit_rows = width // 2
-    targets = [(qkv_held, qkv, (slice(None), slice(n * width, (n + 1) * width))) for n in range(3)]
-    targets.append((out_held, out, (slice(None), slice(None))))
-    targets += [(up_held, up, (slice(None), slice(n * width, (n + 1) * width))) for n in range(4)]
-    targets += [(down_held, down, (slice(n * width, (n + 1) * width), slice(None))) for n in range(4)]
-
-    def write(halves):
-        copies = []
-        for number, (held, target, (rows, columns)) in enumerate(targets):
-            core, place = divmod(number, 6)
-            start = rows.start or 0
-            for part in range(2):
-                quarter, spot = divmod(2 * place + part, 3)
-                value = halves[core][
-                    my_flip(core) ^ quarter, spot * unit_rows : (spot + 1) * unit_rows, :
-                ]
-                first = start + part * unit_rows
-                held[first : first + unit_rows, columns] = value.astype(F32)
-            copies.append(
-                pltpu.make_async_copy(
-                    held.at[rows, columns], target.at[0, rows, columns], sems.at[number]
-                )
+    copies = []
+    for place in range(6):
+        number = 6 * core + place
+        for part in range(2):
+            quarter, spot = divmod(2 * place + part, 3)
+            value = terms[my_flip(core) ^ quarter, spot * unit_rows : (spot + 1) * unit_rows, :]
+            held[place, part * unit_rows : (part + 1) * unit_rows, :] = value.astype(F32)
+        which = 0 if number < 3 else 1 if number == 3 else 2 if number < 8 else 3
+        first = (number, 0, number - 4, number - 8)[which] * width
+        rows = pl.ds(first if which == 3 else 0, width)
+        columns = pl.ds(0 if which in (1, 3) else first, width)
+        copies.append(
+            pltpu.make_async_copy(
+                held.at[place], targets[which].at[0, rows, columns], sems.at[place]
             )
-            copies[-1].start()
-        spare = halves[0][my_flip(0), zero_near.shape[1] - GAIN_ROWS :, :].astype(F32)
-        gain_attn[...] = spare[0:1, :]
-        gain_ffn[...] = spare[1:2, :]
-        for copy in copies:
-            copy.wait()
-
-    @pl.when(my_section() == 0)
-    def _():
-        write((zero_near, zero_far))
-
-    @pl.when(my_section() == 1)
-    def _():
-        write((one_far, one_near))
+        )
+        copies[-1].start()
+    for copy in copies:
+        copy.wait()
+
+
+def by_section(body):
+    for core in range(2):
+        pl.when(my_section() == core)(partial(body, core))
+
+
+def near_kernel(zero, one, gain_attn, qkv, out, gain_ffn, up, down, held, sems):
+    spare = zero.shape[1] - GAIN_ROWS
+
+    def body(core):
+        terms = (zero, one)[core]
+        gains = terms[0, spare:, :].astype(F32)
+        gain_attn[...] = gains[0:1, :]
+        gain_ffn[...] = gains[1:2, :]
+        write_half(core, terms, (qkv, out, up, down), held, sems)
+
+    by_section(body)
+
+
+def far_kernel(qkv_in, out_in, up_in, down_in, zero, one, qkv, out, up, down, held, sems):
+    by_section(
+        lambda core: write_half(1 - core, (zero, one)[core], (qkv, out, up, down), held, sems)
+    )
 
 
 SWAP = [(0, 1), (1, 0)]
@@ -971,14 +982,15 @@
     return lax.ppermute(value, "dp", [(z, z ^ step) for z in range(4)])
 
 
-def reduce_terms(terms, came, zed, along=()):
+def reduce_terms(terms, came, zed, home, before, between=None):
     bar = lax.optimization_barrier
     first = lax.ppermute(terms[0, 2:4] + came[2:4], PLANE, FIRST)
     second = lax.ppermute(terms[0, 1] + came[1] + first[1], PLANE, SECOND)
     total = bar(terms[0, 0] + came[0] + first[0] + second)
-    if along:
-        total, *along = bar((total, *along))
+    total, home[before] = bar((total, home[before]))
     total = bar(total + along_line(total, 1))
+    if between is not None:
+        total, home[between] = bar((total, home[between]))
     half = total.shape[0] // 2
     odd = zed & 1
     mine = lax.dynamic_slice_in_dim(total, odd * half, half, 0)
@@ -990,7 +1002,7 @@
         )
     )
     pair = jnp.stack([total, lax.ppermute(total, PLANE, SECOND)])
-    return pair, lax.ppermute(pair, PLANE, FIRST), along
+    return pair, lax.ppermute(pair, PLANE, FIRST)
 
 
 def lines(
@@ -1185,7 +1197,8 @@
     )
     home = [shared[0]] + [along_line(shared[step], step) for step in range(1, micro_count)]
     came_zero = lax.ppermute(terms_zero[1], "section", SWAP)
-    one_pair, one_first, home = reduce_terms(terms_one, came_one, zed, home)
+    one_pair, one_first = reduce_terms(terms_one, came_one, zed, home, 1, 3)
+    zero_pair, zero_first = reduce_terms(terms_zero, came_zero, zed, home, 2)
     results, input_grads = call(
         settle_kernel,
         (),
@@ -1193,35 +1206,50 @@
         (((1, micro_count, 1, block, width), BF),) * 2,
         8,
     )
-    zero_pair, zero_first, _ = reduce_terms(terms_zero, came_zero, zed)
-
-    def both_cores(parts, pairs):
+
+    def both_cores(parts):
         near = jnp.concatenate(parts)
-        return near, jnp.concatenate([lax.ppermute(part, "section", pairs) for part in parts])
-
-    sums = call(
-        finish_kernel,
+        return near, jnp.concatenate([lax.ppermute(part, "section", SWAP) for part in parts])
+
+    zero_near, zero_far = both_cores((zero_pair, zero_first))
+    one_near, one_far = both_cores((one_pair, one_first))
+    sums = (
+        ((1, width, 3 * width), F32),
+        ((1, width, width), F32),
+        ((1, width, hidden_units), F32),
+        ((1, hidden_units, width), F32),
+    )
+    held = (pltpu.VMEM((6, width, width), F32), pltpu.SemaphoreType.DMA((6,)))
+    gain_attn_sum, qkv_half, out_half, gain_ffn_sum, up_half, down_half = call(
+        near_kernel,
         (),
-        (*both_cores((zero_pair, zero_first), [(1, 0)]), *both_cores((one_pair, one_first), [(0, 1)])),
-        (
-            ((1, width), F32),
-            ((1, width, 3 * width), F32),
-            ((1, width, width), F32),
-            ((1, width), F32),
-            ((1, width, hidden_units), F32),
-            ((1, hidden_units, width), F32),
-        ),
-        24,
-        scratch=(
-            pltpu.VMEM((width, 3 * width), F32),
-            pltpu.VMEM((width, width), F32),
-            pltpu.VMEM((width, hidden_units), F32),
-            pltpu.VMEM((hidden_units, width), F32),
-            pltpu.SemaphoreType.DMA((12,)),
-        ),
+        (zero_near, one_near),
+        (((1, width), F32), *sums[:2], ((1, width), F32), *sums[2:]),
+        16,
+        scratch=held,
         out_held=(1, 2, 4, 5),
     )
-    return (results, input_grads, *sums)
+    qkv_sum, out_sum, up_sum, down_sum = call(
+        far_kernel,
+        (),
+        (qkv_half, out_half, up_half, down_half, zero_far, one_far),
+        sums,
+        16,
+        scratch=held,
+        held=4,
+        out_held=(0, 1, 2, 3),
+        aliases={0: 0, 1: 1, 2: 2, 3: 3},
+    )
+    return (
+        results,
+        input_grads,
+        gain_attn_sum,
+        qkv_sum,
+        out_sum,
+        gain_ffn_sum,
+        up_sum,
+        down_sum,
+    )
 
 
 def local(*arrays):

time: 90.4 us -> 86.8 us (0.960)
  starting transfers between devices: 37 us -> 29 us
  waiting for transfers between devices: 36.6 us -> 39.4 us
    ppermute x12, starting transfers between devices: 19.2 us -> 14.6 us  [along_line(): return lax.ppermute(value, 'dp', [(z, z ^ step) for z in range(4)])]
    ppermute x6, starting transfers between devices: 7.69 us -> 3.58 us  [the longest x2 3.07 us: reduce_terms(): return (pair, lax.ppermute(pair, PLANE, FIRST))]
    ppermute x2, waiting for transfers between devices: 0.93 us -> 2.86 us  [reduce_terms(): second = lax.ppermute(terms[0, 1] + came[1] + first[1], PLANE, SECOND)]
    ppermute x6, waiting for transfers between devices: 3.23 us -> 5.11 us  [the longest x2 5.1 us: reduce_terms(): return (pair, lax.ppermute(pair, PLANE, FIRST))]
    ppermute x2, waiting for transfers between devices: 7.29 us -> 5.87 us  [reduce_terms(): pair = jnp.stack([total, lax.ppermute(total, PLANE, SECOND)])]
    pallas_call x9 -> x10, Pallas kernels: 13.9 us -> 14.7 us  [call(): pl.pallas_call(body, out_shape=tuple((jax.ShapeDtypeStruct(*shape) for sh...]
  transfers between devices with their start and end apart: 35 -> 35, of which waited for: 21 -> 20; matrix products, arithmetic and copies ran while one was open for 2% -> 2% of each run, Pallas kernels for 4% -> 6%
where the time goes in v4:
time: 86.8 us; the launch traced here: 86 us
  waiting for transfers between devices  39.4 us (45%)
  starting transfers between devices  29 us (33%)
  Pallas kernels  14.7 us (17%)
  other arithmetic  1.47 us (2%)
  between operations  1.17 us (1%)
    ppermute x12, waiting for transfers between devices, along_line(): return lax.ppermute(value, 'dp', [(z, z ^ step) for z in range(4)])  17.7 us
    pallas_call x10, Pallas kernels, call(): pl.pallas_call(body, out_shape=tuple((jax.ShapeDtypeStruct(*shape) for sh...  14.7 us
    ppermute x12, starting transfers between devices, along_line(): return lax.ppermute(value, 'dp', [(z, z ^ step) for z in range(4)])  14.6 us
    ppermute x2, waiting for transfers between devices, reduce_terms(): pair = jnp.stack([total, lax.ppermute(total, PLANE, SECOND)])  5.87 us
    ppermute x2, waiting for transfers between devices, reduce_terms(): first = lax.ppermute(terms[0, 2:4] + came[2:4], PLANE, FIRST)  5.79 us
    ppermute x2, waiting for transfers between devices, reduce_terms(): return (pair, lax.ppermute(pair, PLANE, FIRST))  5.1 us
    ppermute x2, starting transfers between devices, reduce_terms(): second = lax.ppermute(terms[0, 1] + came[1] + first[1], PLANE, SECOND)  3.12 us
    ppermute x2, starting transfers between devices, reduce_terms(): first = lax.ppermute(terms[0, 2:4] + came[2:4], PLANE, FIRST)  3.07 us
  transfers between devices with their start and end apart: 35, of which 20 were waited for; matrix products, arithmetic and copies ran while one was open for 2% of the time, Pallas kernels for 6%

profile of v4, /device:TPU:0, one launch (start us, length us, event | category | flops | bytes accessed | tf_op | source)
XLA Modules:
  0.0 86.0 jit_solution(1540809376616240638)
XLA Ops:
  0.7 1.5 %shard_map.152 = (bf16[144,256]{1,0:T(8,128)(2,1)S(1)}, bf16[128,256]{1,0:T(8,128)(2,1)S(1)}, bf16[128,256]{1,0:T(8,128)(2,1)S(1)}, bf16[128,256]{1,0:T(8,128)(2...) custom-call(bf16[4,1,128,256]{3,2,1,0:T(8,128)(2,1)} %tokens.1, bf16[4,1,128,256]{3,2,1,0:T(8,128)(2,1)} %grads.1, ...), custom_call_target="tpu_custom_call" | custom-call | flops 1100000000 | bytes 3400000 | tf_op jit(solution)/shard_map/pallas_call | solution.py:317
  2.2 0.5 collective-permute-start.3
  2.7 2.6 %collective-permute-start = (bf16[128,256]{1,0:T(8,128)(2,1)S(1)}, bf16[128,256]{1,0:T(8,128)(2,1)S(1)}, u32[]{:S(2)}, u32[]{:S(2)}) collective-permute-start(bf16[128,256]{1,0:T(8,128)(2,1)S(1)} %get-tuple-element.79), channel_id=1, source_target_pairs={{0,4},{4,0},{8,12},{12,8},{1,5},{5,1},{9,13},{13,9},{2,6},{6,2},{1... | collective-permute-start | bytes 196616 | tf_op jit(solution)/shard_map/ppermute | solution.py:982
  5.3 2.6 %collective-permute-start.1 = (bf16[128,256]{1,0:T(8,128)(2,1)S(1)}, bf16[128,256]{1,0:T(8,128)(2,1)S(1)}, u32[]{:S(2)}, u32[]{:S(2)}) collective-permute-start(bf16[128,256]{1,0:T(8,128)(2,1)S(1)} %get-tuple-element.81), channel_id=1, source_target_pairs={{0,8},{4,12},{8,0},{12,4},{1,9},{5,13},{9,1},{13,5},{2,10},{6,14},... | collective-permute-start | bytes 196616 | tf_op jit(solution)/shard_map/ppermute | solution.py:982
  7.9 0.1 collective-permute-done.own1
  8.0 0.5 collective-permute-start.8
  8.5 0.1 collective-permute-start.7
  8.6 1.5 %collective-permute-done.8 = bf16[256,256]{1,0:T(8,128)(2,1)S(1)} collective-permute-done((bf16[256,256]{1,0:T(8,128)(2,1)S(1)}, bf16[256,256]{1,0:T(8,128)(2,1)S(1)}, u32[]{:S(2)}, u32[]{:S(2)}) %collective-permute-start.8) | collective-permute-done | bytes 131104 | tf_op jit(solution)/shard_map/ppermute | solution.py:1051
  10.1 0.1 collective-permute-start.9
  10.3 2.7 %collective-permute-done.1.own2 = bf16[128,256]{1,0:T(8,128)(2,1)S(1)} collective-permute-done((bf16[128,256]{1,0:T(8,128)(2,1)S(1)}, bf16[128,256]{1,0:T(8,128)(2,1)S(1)}, u32[]{:S(2)}, u32[]{:S(2)}) %collective-permute-start.1) | collective-permute-done | bytes 65568 | tf_op jit(solution)/shard_map/ppermute | solution.py:982
  13.0 1.0 %collective-permute-done.2.own3 = bf16[128,256]{1,0:T(8,128)(2,1)S(1)} collective-permute-done((bf16[128,256]{1,0:T(8,128)(2,1)S(1)}, bf16[128,256]{1,0:T(8,128)(2,1)S(1)}, u32[]{:S(2)}, u32[]{:S(2)}) %collective-permute-start.2) | collective-permute-done | bytes 65568 | tf_op jit(solution)/shard_map/ppermute | solution.py:982
  14.0 0.5 collective-permute-start.6
  14.6 0.1 pad_maximum_fusion.6.w_qkv
  14.7 0.1 select_bitcast_fusion.1
  14.8 0.1 pad_maximum_fusion.1.w_down
  14.9 0.1 select_bitcast_fusion.3
  15.0 0.1 pad_maximum_fusion.w_up
  15.1 0.2 collective-permute-done.5.far2
  15.3 0.2 collective-permute-done.6.far3
  15.4 2.2 %shard_map.153 = (bf16[640,256]{1,0:T(8,128)(2,1)}, f32[576,256]{1,0:T(8,128)S(1)}, f32[576,128]{1,0:T(8,128)S(1)}, bf16[576,256]{1,0:T(8,128)(2,1)S(1)}, bf16[2...) custom-call(f32[256,192]{1,0:T(8,128)S(1)} %get-tuple-element.77.mas, ...), custom_call_target="tpu_custom_call" | custom-call | flops 1100000000 | bytes 3400000 | tf_op jit(solution)/shard_map/pallas_call | solution.py:317
  17.7 1.8 %shard_map.154 = (f32[256,256]{1,0:T(8,128)S(1)}, f32[256,128]{1,0:T(8,128)S(1)}, bf16[256,256]{1,0:T(8,128)(2,1)S(1)}, bf16[256,768]{1,0:T(8,128)(2,1)S(1)}, f3...) custom-call(f32[256,256]{1,0:T(8,128)S(1)} %get-tuple-element.88.mas, ...), custom_call_target="tpu_custom_call" | custom-call | flops 1100000000 | bytes 3400000 | tf_op jit(solution)/shard_map/pallas_call | solution.py:317
  19.5 2.5 %shard_map.155 = (bf16[256,256]{1,0:T(8,128)(2,1)S(1)}, bf16[2,4,400,256]{3,2,1,0:T(8,128)(2,1)S(1)}, bf16[256,1024]{1,0:T(8,128)(2,1)}) custom-call(bf16[256,256]{1,0:T(8,128)(2,1)S(1)} %get-tuple-element.87.grad_ref, bf16[2,256,768]{2,1,0:T(8,128)(2,1)S(1)} %pad_maximum_fusion.6.w_qkv, bf16[2,256,256]{2,1,0:T(8,128)(2,1)S(1)} %pad_maximum_fusion.9.w_out, ...), custom_call_target="tpu_custom_call" | custom-call | flops 3300000000 | bytes 10200000 | tf_op jit(solution)/shard_map/pallas_call | solution.py:317
  22.0 0.4 collective-permute-start.12
  22.4 0.8 shard_map.156
  23.2 1.9 %shard_map.157 = (bf16[256,256]{1,0:T(8,128)(2,1)S(1)}, f32[640,256]{1,0:T(8,128)S(1)}, bf16[832,256]{1,0:T(8,128)(2,1)S(1)}, bf16[2,4,400,256]{3,2,1,0:T(8,128)(2,1)S(1)}) custom-call(bf16[256,256]{1,0:T(8,128)(2,1)S(1)} %get-tuple-element.101.grad_ref.one_near, bf16[2,256,768]{2,1,0:T(8,128)(2,1)S(1)} %pad_maximum_fusion.6.w_qkv, ...), custom_call_target="tpu_custom_call" | custom-call | flops 4400000000 | bytes 13600000 | tf_op jit(solution)/shard_map/pallas_call | solution.py:317
  25.2 0.2 collective-permute-start.16
  25.4 0.3 collective-permute-start.11
  25.8 1.5 %collective-permute-start.13 = (bf16[2,400,256]{2,1,0:T(8,128)(2,1)S(1)}, bf16[2,400,256]{2,1,0:T(8,128)(2,1)S(1)}, u32[]{:S(2)}, u32[]{:S(2)}) collective-permute-start(bf16[2,400,256]{2,1,0:T(8,128)(2,1)S(1)} %slice_add_fusion.1), channel_id=1, source_target_pairs={{0,1},{1,0},{2,3},{3,2},{16,18},{17,19},{18,16},{19,17},{4,5},{5,4... | collective-permute-start | bytes 1228808 | tf_op jit(solution)/shard_map/ppermute | solution.py:987
  27.4 0.2 collective-permute-done.16
  27.6 1.5 %collective-permute-start.17 = (bf16[2,400,256]{2,1,0:T(8,128)(2,1)S(1)}, bf16[2,400,256]{2,1,0:T(8,128)(2,1)S(1)}, u32[]{:S(2)}, u32[]{:S(2)}) collective-permute-start(bf16[2,400,256]{2,1,0:T(8,128)(2,1)S(1)} %slice_add_fusion), channel_id=1, source_target_pairs={{0,1},{1,0},{2,3},{3,2},{16,18},{17,19},{18,16},{19,17},{4,5},{5,4... | collective-permute-start | bytes 1228808 | tf_op jit(solution)/shard_map/ppermute | solution.py:987
  29.2 0.2 shard_map.158
  29.4 1.3 %collective-permute-start.15 = (bf16[256,256]{1,0:T(8,128)(2,1)S(1)}, bf16[256,256]{1,0:T(8,128)(2,1)S(1)}, u32[]{:S(2)}, u32[]{:S(2)}) collective-permute-start(bf16[256,256]{1,0:T(8,128)(2,1)S(1)} %get-tuple-element.124), channel_id=1, source_target_pairs={{0,4},{4,0},{8,12},{12,8},{1,5},{5,1},{9,13},{13,9},{2,6},{6,2},{1... | collective-permute-start | bytes 393224 | tf_op jit(solution)/shard_map/ppermute | solution.py:982
  30.7 2.4 %collective-permute-start.21 = (bf16[256,256]{1,0:T(8,128)(2,1)S(1)}, bf16[256,256]{1,0:T(8,128)(2,1)S(1)}, u32[]{:S(2)}, u32[]{:S(2)}) collective-permute-start(bf16[256,256]{1,0:T(8,128)(2,1)S(1)} %get-tuple-element.130), channel_id=1, source_target_pairs={{0,12},{4,8},{8,4},{12,0},{1,13},{5,9},{9,5},{13,1},{2,14},{6,10},... | collective-permute-start | bytes 393224 | tf_op jit(solution)/shard_map/ppermute | solution.py:982
  33.1 0.7 collective-permute-done.13
  33.9 1.6 %collective-permute-start.14 = (bf16[400,256]{1,0:T(8,128)(2,1)S(1)}, bf16[400,256]{1,0:T(8,128)(2,1)S(1)}, u32[]{:S(2)}, u32[]{:S(2)}) collective-permute-start(bf16[400,256]{1,0:T(8,128)(2,1)S(1)} %fusion.5), channel_id=1, source_target_pairs={{0,2},{1,3},{2,0},{3,1},{16,17},{17,16},{18,19},{19,18},{4,6},{5,7... | collective-permute-start | bytes 614408 | tf_op jit(solution)/shard_map/ppermute | solution.py:988
  35.4 5.1 %collective-permute-done.17 = bf16[2,400,256]{2,1,0:T(8,128)(2,1)S(1)} collective-permute-done((bf16[2,400,256]{2,1,0:T(8,128)(2,1)S(1)}, bf16[2,400,256]{2,1,0:T(8,128)(2,1)S(1)}, u32[]{:S(2)}, u32[]{:S(2)}) %collective-permute-start.17) | collective-permute-done | bytes 409632 | tf_op jit(solution)/shard_map/ppermute | solution.py:987
  40.6 1.6 %collective-permute-start.18 = (bf16[400,256]{1,0:T(8,128)(2,1)S(1)}, bf16[400,256]{1,0:T(8,128)(2,1)S(1)}, u32[]{:S(2)}, u32[]{:S(2)}) collective-permute-start(bf16[400,256]{1,0:T(8,128)(2,1)S(1)} %fusion), channel_id=1, source_target_pairs={{0,2},{1,3},{2,0},{3,1},{16,17},{17,16},{18,19},{19,18},{4,6},{5,7... | collective-permute-start | bytes 614408 | tf_op jit(solution)/shard_map/ppermute | solution.py:988
  42.2 1.3 %collective-permute-start.20 = (bf16[400,256]{1,0:T(8,128)(2,1)S(1)}, bf16[400,256]{1,0:T(8,128)(2,1)S(1)}, u32[]{:S(2)}, u32[]{:S(2)}) collective-permute-start(bf16[400,256]{1,0:T(8,128)(2,1)S(1)} %fusion.8), channel_id=1, source_target_pairs={{0,4},{4,0},{8,12},{12,8},{1,5},{5,1},{9,13},{13,9},{2,6},{6,2},{1... | collective-permute-start | bytes 614408 | tf_op jit(solution)/shard_map/ppermute | solution.py:982
  43.5 2.9 %collective-permute-done.18 = bf16[400,256]{1,0:T(8,128)(2,1)S(1)} collective-permute-done((bf16[400,256]{1,0:T(8,128)(2,1)S(1)}, bf16[400,256]{1,0:T(8,128)(2,1)S(1)}, u32[]{:S(2)}, u32[]{:S(2)}) %collective-permute-start.18) | collective-permute-done | bytes 204832 | tf_op jit(solution)/shard_map/ppermute | solution.py:988
  46.4 1.3 %collective-permute-start.22 = (bf16[400,256]{1,0:T(8,128)(2,1)S(1)}, bf16[400,256]{1,0:T(8,128)(2,1)S(1)}, u32[]{:S(2)}, u32[]{:S(2)}) collective-permute-start(bf16[400,256]{1,0:T(8,128)(2,1)S(1)} %fusion.3), channel_id=1, source_target_pairs={{0,4},{4,0},{8,12},{12,8},{1,5},{5,1},{9,13},{13,9},{2,6},{6,2},{1... | collective-permute-start | bytes 614408 | tf_op jit(solution)/shard_map/ppermute | solution.py:982
  47.8 2.5 %collective-permute-done.20 = bf16[400,256]{1,0:T(8,128)(2,1)S(1)} collective-permute-done((bf16[400,256]{1,0:T(8,128)(2,1)S(1)}, bf16[400,256]{1,0:T(8,128)(2,1)S(1)}, u32[]{:S(2)}, u32[]{:S(2)}) %collective-permute-start.20) | collective-permute-done | bytes 204832 | tf_op jit(solution)/shard_map/ppermute | solution.py:982
  50.3 1.7 %collective-permute-start.27 = (bf16[200,256]{1,0:T(8,128)(2,1)S(1)}, bf16[200,256]{1,0:T(8,128)(2,1)S(1)}, u32[]{:S(2)}, u32[]{:S(2)}) collective-permute-start(bf16[200,256]{1,0:T(8,128)(2,1)S(1)} %constant_dynamic-slice_fusion), channel_id=1, source_target_pairs={{0,8},{4,12},{8,0},{12,4},{1,9},{5,13},{9,1},{13,5},{2,10},{6,14},... | collective-permute-start | bytes 307208 | tf_op jit(solution)/shard_map/ppermute | solution.py:982
  52.0 2.3 %collective-permute-done.22 = bf16[400,256]{1,0:T(8,128)(2,1)S(1)} collective-permute-done((bf16[400,256]{1,0:T(8,128)(2,1)S(1)}, bf16[400,256]{1,0:T(8,128)(2,1)S(1)}, u32[]{:S(2)}, u32[]{:S(2)}) %collective-permute-start.22) | collective-permute-done | bytes 204832 | tf_op jit(solution)/shard_map/ppermute | solution.py:982
  54.4 1.1 %collective-permute-start.23 = (bf16[200,256]{1,0:T(8,128)(2,1)S(1)}, bf16[200,256]{1,0:T(8,128)(2,1)S(1)}, u32[]{:S(2)}, u32[]{:S(2)}) collective-permute-start(bf16[200,256]{1,0:T(8,128)(2,1)S(1)} %constant_dynamic-slice_fusion.1), channel_id=1, source_target_pairs={{0,8},{4,12},{8,0},{12,4},{1,9},{5,13},{9,1},{13,5},{2,10},{6,14},... | collective-permute-start | bytes 307208 | tf_op jit(solution)/shard_map/ppermute | solution.py:982
  55.6 3.1 %collective-permute-done.27 = bf16[200,256]{1,0:T(8,128)(2,1)S(1)} collective-permute-done((bf16[200,256]{1,0:T(8,128)(2,1)S(1)}, bf16[200,256]{1,0:T(8,128)(2,1)S(1)}, u32[]{:S(2)}, u32[]{:S(2)}) %collective-permute-start.27) | collective-permute-done | bytes 102432 | tf_op jit(solution)/shard_map/ppermute | solution.py:982
  58.7 2.7 %collective-permute-done.23 = bf16[200,256]{1,0:T(8,128)(2,1)S(1)} collective-permute-done((bf16[200,256]{1,0:T(8,128)(2,1)S(1)}, bf16[200,256]{1,0:T(8,128)(2,1)S(1)}, u32[]{:S(2)}, u32[]{:S(2)}) %collective-permute-start.23) | collective-permute-done | bytes 102432 | tf_op jit(solution)/shard_map/ppermute | solution.py:982
  61.6 1.8 %collective-permute-done.28 = bf16[200,256]{1,0:T(8,128)(2,1)S(1)} collective-permute-done((bf16[200,256]{1,0:T(8,128)(2,1)S(1)}, bf16[200,256]{1,0:T(8,128)(2,1)S(1)}, u32[]{:S(2)}, u32[]{:S(2)}) %collective-permute-start.28) | collective-permute-done | bytes 102432 | tf_op jit(solution)/shard_map/ppermute | solution.py:982
  63.5 1.3 %collective-permute-start.29 = (bf16[400,256]{1,0:T(8,128)(2,1)S(1)}, bf16[400,256]{1,0:T(8,128)(2,1)S(1)}, u32[]{:S(2)}, u32[]{:S(2)}) collective-permute-start(bf16[400,256]{1,0:T(8,128)(2,1)S(1)} %maximum_select_fusion.1), channel_id=1, source_target_pairs={{0,2},{1,3},{2,0},{3,1},{16,17},{17,16},{18,19},{19,18},{4,6},{5,7... | collective-permute-start | bytes 614408 | tf_op jit(solution)/shard_map/ppermute | solution.py:1004
  64.8 1.5 %collective-permute-done.24 = bf16[200,256]{1,0:T(8,128)(2,1)S(1)} collective-permute-done((bf16[200,256]{1,0:T(8,128)(2,1)S(1)}, bf16[200,256]{1,0:T(8,128)(2,1)S(1)}, u32[]{:S(2)}, u32[]{:S(2)}) %collective-permute-start.24) | collective-permute-done | bytes 102432 | tf_op jit(solution)/shard_map/ppermute | solution.py:982
  66.3 0.6 collective-permute-start.25
  66.9 2.8 %collective-permute-done.29 = bf16[400,256]{1,0:T(8,128)(2,1)S(1)} collective-permute-done((bf16[400,256]{1,0:T(8,128)(2,1)S(1)}, bf16[400,256]{1,0:T(8,128)(2,1)S(1)}, u32[]{:S(2)}, u32[]{:S(2)}) %collective-permute-start.29) | collective-permute-done | bytes 204832 | tf_op jit(solution)/shard_map/ppermute | solution.py:1004
  69.8 1.5 %collective-permute-start.30 = (bf16[2,400,256]{2,1,0:T(8,128)(2,1)S(1)}, bf16[2,400,256]{2,1,0:T(8,128)(2,1)S(1)}, u32[]{:S(2)}, u32[]{:S(2)}) collective-permute-start(bf16[2,400,256]{2,1,0:T(8,128)(2,1)S(1)} %pad_maximum_fusion.8), channel_id=1, source_target_pairs={{0,1},{1,0},{2,3},{3,2},{16,18},{17,19},{18,16},{19,17},{4,5},{5,4... | collective-permute-start | bytes 1228808 | tf_op jit(solution)/shard_map/ppermute | solution.py:1005
  71.3 3.0 %collective-permute-done.25 = bf16[400,256]{1,0:T(8,128)(2,1)S(1)} collective-permute-done((bf16[400,256]{1,0:T(8,128)(2,1)S(1)}, bf16[400,256]{1,0:T(8,128)(2,1)S(1)}, u32[]{:S(2)}, u32[]{:S(2)}) %collective-permute-start.25) | collective-permute-done | bytes 204832 | tf_op jit(solution)/shard_map/ppermute | solution.py:1004
  74.4 1.6 %collective-permute-start.26 = (bf16[2,400,256]{2,1,0:T(8,128)(2,1)S(1)}, bf16[2,400,256]{2,1,0:T(8,128)(2,1)S(1)}, u32[]{:S(2)}, u32[]{:S(2)}) collective-permute-start(bf16[2,400,256]{2,1,0:T(8,128)(2,1)S(1)} %pad_maximum_fusion.7), channel_id=1, source_target_pairs={{0,1},{1,0},{2,3},{3,2},{16,18},{17,19},{18,16},{19,17},{4,5},{5,4... | collective-permute-start | bytes 1228808 | tf_op jit(solution)/shard_map/ppermute | solution.py:1005
  76.0 1.9 %collective-permute-done.30 = bf16[2,400,256]{2,1,0:T(8,128)(2,1)S(1)} collective-permute-done((bf16[2,400,256]{2,1,0:T(8,128)(2,1)S(1)}, bf16[2,400,256]{2,1,0:T(8,128)(2,1)S(1)}, u32[]{:S(2)}, u32[]{:S(2)}) %collective-permute-start.30) | collective-permute-done | bytes 409632 | tf_op jit(solution)/shard_map/ppermute | solution.py:1005
  77.8 0.8 shard_map.159
  78.7 0.5 collective-permute-start.31
  79.2 3.2 %collective-permute-done.26 = bf16[2,400,256]{2,1,0:T(8,128)(2,1)S(1)} collective-permute-done((bf16[2,400,256]{2,1,0:T(8,128)(2,1)S(1)}, bf16[2,400,256]{2,1,0:T(8,128)(2,1)S(1)}, u32[]{:S(2)}, u32[]{:S(2)}) %collective-permute-start.26) | collective-permute-done | bytes 409632 | tf_op jit(solution)/shard_map/ppermute | solution.py:1005
  82.4 0.1 pad_maximum_fusion.3.one
  82.5 0.1 pad_maximum_fusion.2.zero
  82.6 1.8 %shard_map.160 = (f32[1,256]{1,0:T(1,128)}, f32[1,256,768]{2,1,0:T(8,128)}, f32[1,256,256]{2,1,0:T(8,128)}, f32[1,256]{1,0:T(1,128)}, f32[1,256,1024]{2,1,0:T(8,128)}, /*index=5*/f32[1,1024,256]{2,1,0:T(8,128)}) custom-call(bf16[4,400,256]{2,1,0:T(8,128)(2,1)S(1)} %pad_maximum_fusion.2.zero, bf16[4,400,256]{2,1,0:T(8,128)(2,1)S(1)} %pad_maximum_fusion.3.one), custom_call_target="tpu_custom_call" | custom-call | flops 1100000000 | bytes 3400000 | tf_op jit(solution)/shard_map/pallas_call | solution.py:317
  84.4 0.1 pad_maximum_fusion.5.one
  84.5 0.1 pad_maximum_fusion.4.zero
  84.6 1.2 %shard_map.161 = (f32[1,256,768]{2,1,0:T(8,128)}, f32[1,256,256]{2,1,0:T(8,128)}, f32[1,256,1024]{2,1,0:T(8,128)}, f32[1,1024,256]{2,1,0:T(8,128)}) custom-call(f32[1,256,768]{2,1,0:T(8,128)} %get-tuple-element.137.qkv_in, f32[1,256,256]{2,1,0:T(8,128)} %get-tuple-element.138.out_in, ...), custom_call_target="tpu_custom_call", output_to_operand_aliasing={{0}: (0, {}), {1}: (1, {}), {2}: (2, {}), {3}: (3, {})} | custom-call | flops 1100000000 | bytes 3400000 | tf_op jit(solution)/shard_map/pallas_call | solution.py:317
  (56 shorter events, 1.1 us)
Async XLA Ops:
  0.6 7.9 %copy-start.2 = (bf16[1,256,768]{2,1,0:T(8,128)(2,1)S(1)}, bf16[1,256,768]{2,1,0:T(8,128)(2,1)}, u32[]{:S(2)}) copy-start(bf16[1,256,768]{2,1,0:T(8,128)(2,1)} %param.13) | copy-start | bytes 1179652
  0.6 7.4 %copy-start.3 = (bf16[1,256,256]{2,1,0:T(8,128)(2,1)S(1)}, bf16[1,256,256]{2,1,0:T(8,128)(2,1)}, u32[]{:S(2)}) copy-start(bf16[1,256,256]{2,1,0:T(8,128)(2,1)} %param.14) | copy-start | bytes 393220
  0.7 9.5 %copy-start.1 = (bf16[1,256,1024]{2,1,0:T(8,128)(2,1)S(1)}, bf16[1,256,1024]{2,1,0:T(8,128)(2,1)}, u32[]{:S(2)}) copy-start(bf16[1,256,1024]{2,1,0:T(8,128)(2,1)} %param.16) | copy-start | bytes 1572868
  0.7 7.3 %copy-start = (bf16[1,1024,256]{2,1,0:T(8,128)(2,1)S(1)}, bf16[1,1024,256]{2,1,0:T(8,128)(2,1)}, u32[]{:S(2)}) copy-start(bf16[1,1024,256]{2,1,0:T(8,128)(2,1)} %param.17) | copy-start | bytes 1572868
  2.2 6.4 %collective-permute-start.3 = (bf16[144,256]{1,0:T(8,128)(2,1)S(1)}, bf16[144,256]{1,0:T(8,128)(2,1)S(1)}, u32[]{:S(2)}, u32[]{:S(2)}) collective-permute-start(bf16[144,256]{1,0:T(8,128)(2,1)S(1)} %get-tuple-element.78.own0), channel_id=1, source_target_pairs={{0,16},{16,0},{1,17},{17,1},{2,18},{18,2},{3,19},{19,3},{4,20},{20... | collective-permute-start | bytes 221192 | tf_op jit(solution)/shard_map/ppermute | solution.py:1048
  2.7 5.3 %collective-permute-start = (bf16[128,256]{1,0:T(8,128)(2,1)S(1)}, bf16[128,256]{1,0:T(8,128)(2,1)S(1)}, u32[]{:S(2)}, u32[]{:S(2)}) collective-permute-start(bf16[128,256]{1,0:T(8,128)(2,1)S(1)} %get-tuple-element.79), channel_id=1, source_target_pairs={{0,4},{4,0},{8,12},{12,8},{1,5},{5,1},{9,13},{13,9},{2,6},{6,2},{1... | collective-permute-start | bytes 196616 | tf_op jit(solution)/shard_map/ppermute | solution.py:982
  5.3 7.7 %collective-permute-start.1 = (bf16[128,256]{1,0:T(8,128)(2,1)S(1)}, bf16[128,256]{1,0:T(8,128)(2,1)S(1)}, u32[]{:S(2)}, u32[]{:S(2)}) collective-permute-start(bf16[128,256]{1,0:T(8,128)(2,1)S(1)} %get-tuple-element.81), channel_id=1, source_target_pairs={{0,8},{4,12},{8,0},{12,4},{1,9},{5,13},{9,1},{13,5},{2,10},{6,14},... | collective-permute-start | bytes 196616 | tf_op jit(solution)/shard_map/ppermute | solution.py:982
  7.9 6.1 %collective-permute-start.2 = (bf16[128,256]{1,0:T(8,128)(2,1)S(1)}, bf16[128,256]{1,0:T(8,128)(2,1)S(1)}, u32[]{:S(2)}, u32[]{:S(2)}) collective-permute-start(bf16[128,256]{1,0:T(8,128)(2,1)S(1)} %get-tuple-element.82), channel_id=1, source_target_pairs={{0,12},{4,8},{8,4},{12,0},{1,13},{5,9},{9,5},{13,1},{2,14},{6,10},... | collective-permute-start | bytes 196616 | tf_op jit(solution)/shard_map/ppermute | solution.py:982
  8.0 6.7 %collective-permute-start.10 = (bf16[1024,256]{1,0:T(8,128)(2,1)S(1)}, bf16[1024,256]{1,0:T(8,128)(2,1)S(1)}, u32[]{:S(2)}, u32[]{:S(2)}) collective-permute-start(bf16[1024,256]{1,0:T(8,128)(2,1)S(1)} %bitcast.96), channel_id=1, source_target_pairs={{0,16},{16,0},{1,17},{17,1},{2,18},{18,2},{3,19},{19,3},{4,20},{20... | collective-permute-start | bytes 1572872 | tf_op jit(solution)/shard_map/ppermute | solution.py:1051
  8.0 2.1 %collective-permute-start.8 = (bf16[256,256]{1,0:T(8,128)(2,1)S(1)}, bf16[256,256]{1,0:T(8,128)(2,1)S(1)}, u32[]{:S(2)}, u32[]{:S(2)}) collective-permute-start(bf16[256,256]{1,0:T(8,128)(2,1)S(1)} %bitcast.102), channel_id=1, source_target_pairs={{0,16},{16,0},{1,17},{17,1},{2,18},{18,2},{3,19},{19,3},{4,20},{20... | collective-permute-start | bytes 393224 | tf_op jit(solution)/shard_map/ppermute | solution.py:1051
  8.5 5.5 %collective-permute-start.7 = (bf16[256,768]{1,0:T(8,128)(2,1)S(1)}, bf16[256,768]{1,0:T(8,128)(2,1)S(1)}, u32[]{:S(2)}, u32[]{:S(2)}) collective-permute-start(bf16[256,768]{1,0:T(8,128)(2,1)S(1)} %bitcast.100), channel_id=1, source_target_pairs={{0,16},{16,0},{1,17},{17,1},{2,18},{18,2},{3,19},{19,3},{4,20},{20... | collective-permute-start | bytes 1179656 | tf_op jit(solution)/shard_map/ppermute | solution.py:1051
  10.1 4.8 %collective-permute-start.9 = (bf16[256,1024]{1,0:T(8,128)(2,1)S(1)}, bf16[256,1024]{1,0:T(8,128)(2,1)S(1)}, u32[]{:S(2)}, u32[]{:S(2)}) collective-permute-start(bf16[256,1024]{1,0:T(8,128)(2,1)S(1)} %bitcast.98), channel_id=1, source_target_pairs={{0,16},{16,0},{1,17},{17,1},{2,18},{18,2},{3,19},{19,3},{4,20},{20... | collective-permute-start | bytes 1572872 | tf_op jit(solution)/shard_map/ppermute | solution.py:1051
  13.0 2.1 %collective-permute-start.4 = (bf16[128,256]{1,0:T(8,128)(2,1)S(1)}, bf16[128,256]{1,0:T(8,128)(2,1)S(1)}, u32[]{:S(2)}, u32[]{:S(2)}) collective-permute-start(bf16[128,256]{1,0:T(8,128)(2,1)S(1)} %collective-permute-done.own1), channel_id=1, source_target_pairs={{0,16},{16,0},{1,17},{17,1},{2,18},{18,2},{3,19},{19,3},{4,20},{20... | collective-permute-start | bytes 196616 | tf_op jit(solution)/shard_map/ppermute | solution.py:1048
  14.0 1.3 %collective-permute-start.5 = (bf16[128,256]{1,0:T(8,128)(2,1)S(1)}, bf16[128,256]{1,0:T(8,128)(2,1)S(1)}, u32[]{:S(2)}, u32[]{:S(2)}) collective-permute-start(bf16[128,256]{1,0:T(8,128)(2,1)S(1)} %collective-permute-done.1.own2), channel_id=1, source_target_pairs={{0,16},{16,0},{1,17},{17,1},{2,18},{18,2},{3,19},{19,3},{4,20},{20... | collective-permute-start | bytes 196616 | tf_op jit(solution)/shard_map/ppermute | solution.py:1048
  14.0 1.4 %collective-permute-start.6 = (bf16[128,256]{1,0:T(8,128)(2,1)S(1)}, bf16[128,256]{1,0:T(8,128)(2,1)S(1)}, u32[]{:S(2)}, u32[]{:S(2)}) collective-permute-start(bf16[128,256]{1,0:T(8,128)(2,1)S(1)} %collective-permute-done.2.own3), channel_id=1, source_target_pairs={{0,16},{16,0},{1,17},{17,1},{2,18},{18,2},{3,19},{19,3},{4,20},{20... | collective-permute-start | bytes 196616 | tf_op jit(solution)/shard_map/ppermute | solution.py:1048
  22.0 3.7 %collective-permute-start.12 = (bf16[4,400,256]{2,1,0:T(8,128)(2,1)S(1)}, bf16[4,400,256]{2,1,0:T(8,128)(2,1)S(1)}, u32[]{:S(2)}, u32[]{:S(2)}) collective-permute-start(bf16[4,400,256]{2,1,0:T(8,128)(2,1)S(1)} %slice_bitcast_fusion.1), channel_id=1, source_target_pairs={{0,16},{16,0},{1,17},{17,1},{2,18},{18,2},{3,19},{19,3},{4,20},{20... | collective-permute-start | bytes 2457608 | tf_op jit(solution)/shard_map/ppermute | solution.py:1148
  25.2 2.4 %collective-permute-start.16 = (bf16[4,400,256]{2,1,0:T(8,128)(2,1)S(1)}, bf16[4,400,256]{2,1,0:T(8,128)(2,1)S(1)}, u32[]{:S(2)}, u32[]{:S(2)}) collective-permute-start(bf16[4,400,256]{2,1,0:T(8,128)(2,1)S(1)} %slice_bitcast_fusion), channel_id=1, source_target_pairs={{0,16},{16,0},{1,17},{17,1},{2,18},{18,2},{3,19},{19,3},{4,20},{20... | collective-permute-start | bytes 2457608 | tf_op jit(solution)/shard_map/ppermute | solution.py:1199
  25.4 3.7 %collective-permute-start.11 = (bf16[832,256]{1,0:T(8,128)(2,1)S(1)}, bf16[832,256]{1,0:T(8,128)(2,1)S(1)}, u32[]{:S(2)}, u32[]{:S(2)}) collective-permute-start(bf16[832,256]{1,0:T(8,128)(2,1)S(1)} %get-tuple-element.121), channel_id=1, source_target_pairs={{0,16},{16,0},{1,17},{17,1},{2,18},{18,2},{3,19},{19,3},{4,20},{20... | collective-permute-start | bytes 1277960 | tf_op jit(solution)/shard_map/ppermute | solution.py:1190
  25.8 8.0 %collective-permute-start.13 = (bf16[2,400,256]{2,1,0:T(8,128)(2,1)S(1)}, bf16[2,400,256]{2,1,0:T(8,128)(2,1)S(1)}, u32[]{:S(2)}, u32[]{:S(2)}) collective-permute-start(bf16[2,400,256]{2,1,0:T(8,128)(2,1)S(1)} %slice_add_fusion.1), channel_id=1, source_target_pairs={{0,1},{1,0},{2,3},{3,2},{16,18},{17,19},{18,16},{19,17},{4,5},{5,4... | collective-permute-start | bytes 1228808 | tf_op jit(solution)/shard_map/ppermute | solution.py:987
  27.6 12.9 %collective-permute-start.17 = (bf16[2,400,256]{2,1,0:T(8,128)(2,1)S(1)}, bf16[2,400,256]{2,1,0:T(8,128)(2,1)S(1)}, u32[]{:S(2)}, u32[]{:S(2)}) collective-permute-start(bf16[2,400,256]{2,1,0:T(8,128)(2,1)S(1)} %slice_add_fusion), channel_id=1, source_target_pairs={{0,1},{1,0},{2,3},{3,2},{16,18},{17,19},{18,16},{19,17},{4,5},{5,4... | collective-permute-start | bytes 1228808 | tf_op jit(solution)/shard_map/ppermute | solution.py:987
  29.4 12.7 %collective-permute-start.15 = (bf16[256,256]{1,0:T(8,128)(2,1)S(1)}, bf16[256,256]{1,0:T(8,128)(2,1)S(1)}, u32[]{:S(2)}, u32[]{:S(2)}) collective-permute-start(bf16[256,256]{1,0:T(8,128)(2,1)S(1)} %get-tuple-element.124), channel_id=1, source_target_pairs={{0,4},{4,0},{8,12},{12,8},{1,5},{5,1},{9,13},{13,9},{2,6},{6,2},{1... | collective-permute-start | bytes 393224 | tf_op jit(solution)/shard_map/ppermute | solution.py:982
  30.7 19.6 %collective-permute-start.21 = (bf16[256,256]{1,0:T(8,128)(2,1)S(1)}, bf16[256,256]{1,0:T(8,128)(2,1)S(1)}, u32[]{:S(2)}, u32[]{:S(2)}) collective-permute-start(bf16[256,256]{1,0:T(8,128)(2,1)S(1)} %get-tuple-element.130), channel_id=1, source_target_pairs={{0,12},{4,8},{8,4},{12,0},{1,13},{5,9},{9,5},{13,1},{2,14},{6,10},... | collective-permute-start | bytes 393224 | tf_op jit(solution)/shard_map/ppermute | solution.py:982
  33.1 13.3 %collective-permute-start.19 = (bf16[256,256]{1,0:T(8,128)(2,1)S(1)}, bf16[256,256]{1,0:T(8,128)(2,1)S(1)}, u32[]{:S(2)}, u32[]{:S(2)}) collective-permute-start(bf16[256,256]{1,0:T(8,128)(2,1)S(1)} %get-tuple-element.127), channel_id=1, source_target_pairs={{0,8},{4,12},{8,0},{12,4},{1,9},{5,13},{9,1},{13,5},{2,10},{6,14},... | collective-permute-start | bytes 393224 | tf_op jit(solution)/shard_map/ppermute | solution.py:982
  33.9 8.2 %collective-permute-start.14 = (bf16[400,256]{1,0:T(8,128)(2,1)S(1)}, bf16[400,256]{1,0:T(8,128)(2,1)S(1)}, u32[]{:S(2)}, u32[]{:S(2)}) collective-permute-start(bf16[400,256]{1,0:T(8,128)(2,1)S(1)} %fusion.5), channel_id=1, source_target_pairs={{0,2},{1,3},{2,0},{3,1},{16,17},{17,16},{18,19},{19,18},{4,6},{5,7... | collective-permute-start | bytes 614408 | tf_op jit(solution)/shard_map/ppermute | solution.py:988
  40.6 5.8 %collective-permute-start.18 = (bf16[400,256]{1,0:T(8,128)(2,1)S(1)}, bf16[400,256]{1,0:T(8,128)(2,1)S(1)}, u32[]{:S(2)}, u32[]{:S(2)}) collective-permute-start(bf16[400,256]{1,0:T(8,128)(2,1)S(1)} %fusion), channel_id=1, source_target_pairs={{0,2},{1,3},{2,0},{3,1},{16,17},{17,16},{18,19},{19,18},{4,6},{5,7... | collective-permute-start | bytes 614408 | tf_op jit(solution)/shard_map/ppermute | solution.py:988
  42.2 8.1 %collective-permute-start.20 = (bf16[400,256]{1,0:T(8,128)(2,1)S(1)}, bf16[400,256]{1,0:T(8,128)(2,1)S(1)}, u32[]{:S(2)}, u32[]{:S(2)}) collective-permute-start(bf16[400,256]{1,0:T(8,128)(2,1)S(1)} %fusion.8), channel_id=1, source_target_pairs={{0,4},{4,0},{8,12},{12,8},{1,5},{5,1},{9,13},{13,9},{2,6},{6,2},{1... | collective-permute-start | bytes 614408 | tf_op jit(solution)/shard_map/ppermute | solution.py:982
  46.4 7.9 %collective-permute-start.22 = (bf16[400,256]{1,0:T(8,128)(2,1)S(1)}, bf16[400,256]{1,0:T(8,128)(2,1)S(1)}, u32[]{:S(2)}, u32[]{:S(2)}) collective-permute-start(bf16[400,256]{1,0:T(8,128)(2,1)S(1)} %fusion.3), channel_id=1, source_target_pairs={{0,4},{4,0},{8,12},{12,8},{1,5},{5,1},{9,13},{13,9},{2,6},{6,2},{1... | collective-permute-start | bytes 614408 | tf_op jit(solution)/shard_map/ppermute | solution.py:982
  50.3 8.3 %collective-permute-start.27 = (bf16[200,256]{1,0:T(8,128)(2,1)S(1)}, bf16[200,256]{1,0:T(8,128)(2,1)S(1)}, u32[]{:S(2)}, u32[]{:S(2)}) collective-permute-start(bf16[200,256]{1,0:T(8,128)(2,1)S(1)} %constant_dynamic-slice_fusion), channel_id=1, source_target_pairs={{0,8},{4,12},{8,0},{12,4},{1,9},{5,13},{9,1},{13,5},{2,10},{6,14},... | collective-permute-start | bytes 307208 | tf_op jit(solution)/shard_map/ppermute | solution.py:982
  54.4 7.0 %collective-permute-start.23 = (bf16[200,256]{1,0:T(8,128)(2,1)S(1)}, bf16[200,256]{1,0:T(8,128)(2,1)S(1)}, u32[]{:S(2)}, u32[]{:S(2)}) collective-permute-start(bf16[200,256]{1,0:T(8,128)(2,1)S(1)} %constant_dynamic-slice_fusion.1), channel_id=1, source_target_pairs={{0,8},{4,12},{8,0},{12,4},{1,9},{5,13},{9,1},{13,5},{2,10},{6,14},... | collective-permute-start | bytes 307208 | tf_op jit(solution)/shard_map/ppermute | solution.py:982
  58.7 4.7 %collective-permute-start.28 = (bf16[200,256]{1,0:T(8,128)(2,1)S(1)}, bf16[200,256]{1,0:T(8,128)(2,1)S(1)}, u32[]{:S(2)}, u32[]{:S(2)}) collective-permute-start(bf16[200,256]{1,0:T(8,128)(2,1)S(1)} %fusion.12), channel_id=1, source_target_pairs={{0,4},{4,0},{8,12},{12,8},{1,5},{5,1},{9,13},{13,9},{2,6},{6,2},{1... | collective-permute-start | bytes 307208 | tf_op jit(solution)/shard_map/ppermute | solution.py:982
  61.5 4.7 %collective-permute-start.24 = (bf16[200,256]{1,0:T(8,128)(2,1)S(1)}, bf16[200,256]{1,0:T(8,128)(2,1)S(1)}, u32[]{:S(2)}, u32[]{:S(2)}) collective-permute-start(bf16[200,256]{1,0:T(8,128)(2,1)S(1)} %fusion.13), channel_id=1, source_target_pairs={{0,4},{4,0},{8,12},{12,8},{1,5},{5,1},{9,13},{13,9},{2,6},{6,2},{1... | collective-permute-start | bytes 307208 | tf_op jit(solution)/shard_map/ppermute | solution.py:982
  63.5 6.3 %collective-permute-start.29 = (bf16[400,256]{1,0:T(8,128)(2,1)S(1)}, bf16[400,256]{1,0:T(8,128)(2,1)S(1)}, u32[]{:S(2)}, u32[]{:S(2)}) collective-permute-start(bf16[400,256]{1,0:T(8,128)(2,1)S(1)} %maximum_select_fusion.1), channel_id=1, source_target_pairs={{0,2},{1,3},{2,0},{3,1},{16,17},{17,16},{18,19},{19,18},{4,6},{5,7... | collective-permute-start | bytes 614408 | tf_op jit(solution)/shard_map/ppermute | solution.py:1004
  66.3 8.0 %collective-permute-start.25 = (bf16[400,256]{1,0:T(8,128)(2,1)S(1)}, bf16[400,256]{1,0:T(8,128)(2,1)S(1)}, u32[]{:S(2)}, u32[]{:S(2)}) collective-permute-start(bf16[400,256]{1,0:T(8,128)(2,1)S(1)} %maximum_select_fusion), channel_id=1, source_target_pairs={{0,2},{1,3},{2,0},{3,1},{16,17},{17,16},{18,19},{19,18},{4,6},{5,7... | collective-permute-start | bytes 614408 | tf_op jit(solution)/shard_map/ppermute | solution.py:1004
  69.8 8.0 %collective-permute-start.30 = (bf16[2,400,256]{2,1,0:T(8,128)(2,1)S(1)}, bf16[2,400,256]{2,1,0:T(8,128)(2,1)S(1)}, u32[]{:S(2)}, u32[]{:S(2)}) collective-permute-start(bf16[2,400,256]{2,1,0:T(8,128)(2,1)S(1)} %pad_maximum_fusion.8), channel_id=1, source_target_pairs={{0,1},{1,0},{2,3},{3,2},{16,18},{17,19},{18,16},{19,17},{4,5},{5,4... | collective-permute-start | bytes 1228808 | tf_op jit(solution)/shard_map/ppermute | solution.py:1005
  74.4 8.0 %collective-permute-start.26 = (bf16[2,400,256]{2,1,0:T(8,128)(2,1)S(1)}, bf16[2,400,256]{2,1,0:T(8,128)(2,1)S(1)}, u32[]{:S(2)}, u32[]{:S(2)}) collective-permute-start(bf16[2,400,256]{2,1,0:T(8,128)(2,1)S(1)} %pad_maximum_fusion.7), channel_id=1, source_target_pairs={{0,1},{1,0},{2,3},{3,2},{16,18},{17,19},{18,16},{19,17},{4,5},{5,4... | collective-permute-start | bytes 1228808 | tf_op jit(solution)/shard_map/ppermute | solution.py:1005
  76.0 8.4 %collective-permute-start.33 = (bf16[2,400,256]{2,1,0:T(8,128)(2,1)S(1)}, bf16[2,400,256]{2,1,0:T(8,128)(2,1)S(1)}, u32[]{:S(2)}, u32[]{:S(2)}) collective-permute-start(bf16[2,400,256]{2,1,0:T(8,128)(2,1)S(1)} %pad_maximum_fusion.8), channel_id=1, source_target_pairs={{0,16},{16,0},{1,17},{17,1},{2,18},{18,2},{3,19},{19,3},{4,20},{20... | collective-permute-start | bytes 1228808 | tf_op jit(solution)/shard_map/ppermute | solution.py:1212
  77.8 6.6 %collective-permute-start.34 = (bf16[2,400,256]{2,1,0:T(8,128)(2,1)S(1)}, bf16[2,400,256]{2,1,0:T(8,128)(2,1)S(1)}, u32[]{:S(2)}, u32[]{:S(2)}) collective-permute-start(bf16[2,400,256]{2,1,0:T(8,128)(2,1)S(1)} %collective-permute-done.30), channel_id=1, source_target_pairs={{0,16},{16,0},{1,17},{17,1},{2,18},{18,2},{3,19},{19,3},{4,20},{20... | collective-permute-start | bytes 1228808 | tf_op jit(solution)/shard_map/ppermute | solution.py:1212
  78.7 5.8 %collective-permute-start.31 = (bf16[2,400,256]{2,1,0:T(8,128)(2,1)S(1)}, bf16[2,400,256]{2,1,0:T(8,128)(2,1)S(1)}, u32[]{:S(2)}, u32[]{:S(2)}) collective-permute-start(bf16[2,400,256]{2,1,0:T(8,128)(2,1)S(1)} %pad_maximum_fusion.7), channel_id=1, source_target_pairs={{0,16},{16,0},{1,17},{17,1},{2,18},{18,2},{3,19},{19,3},{4,20},{20... | collective-permute-start | bytes 1228808 | tf_op jit(solution)/shard_map/ppermute | solution.py:1212
  82.4 2.1 %collective-permute-start.32 = (bf16[2,400,256]{2,1,0:T(8,128)(2,1)S(1)}, bf16[2,400,256]{2,1,0:T(8,128)(2,1)S(1)}, u32[]{:S(2)}, u32[]{:S(2)}) collective-permute-start(bf16[2,400,256]{2,1,0:T(8,128)(2,1)S(1)} %collective-permute-done.26), channel_id=1, source_target_pairs={{0,16},{16,0},{1,17},{17,1},{2,18},{18,2},{3,19},{19,3},{4,20},{20... | collective-permute-start | bytes 1228808 | tf_op jit(solution)/shard_map/ppermute | solution.py:1212

commit v5 on v4

--- a/solution.py
+++ b/solution.py
@@ -310,7 +310,7 @@
     return pltpu.with_memory_space_constraint(array, pltpu.HBM)
 
 
-def call(body, scalars, arrays, shapes, mib=24, micros=1.0, scratch=(), held=0, out_held=(), aliases=None):
+def call(body, scalars, arrays, shapes, mib=16, micros=1.0, scratch=(), held=0, out_held=(), aliases=None):
     in_specs = [pl.BlockSpec(memory_space=pltpu.SMEM)] * len(scalars)
     in_specs += [pl.BlockSpec(memory_space=pl.ANY)] * held
     in_specs += [pl.BlockSpec(memory_space=pltpu.VMEM)] * (len(arrays) - held)
@@ -375,24 +375,28 @@
     half = rows // 4
     block = 2 * half
     ends = ends_of(lengths)
-    row = lax.broadcasted_iota(jnp.int32, (rows, reach), 0)
-    query_pos = block * (row // half) + section * half + (row & (half - 1))
-    key_pos = query_pos - (row & (half - 1)) - block
-    key_pos = key_pos + lax.broadcasted_iota(jnp.int32, (rows, reach), 1)
-    offset = query_pos - key_pos
-    segment = segment_at(ends, query_pos)
-    same = (segment == segment_at(ends, key_pos)) & (segment < len(ends)) & (key_pos >= 0)
-    allow = same & (offset >= 0) & (offset < STRIDE) | (offset == 0)
-    window_mask[...] = allow.astype(F32)
+    slots = len(ends)
+    query_index = lax.broadcasted_iota(jnp.int32, (half, 1), 0)
+    key_index = lax.broadcasted_iota(jnp.int32, (1, reach), 1)
+    offset = block + query_index - key_index
+    near = (offset >= 0) & (offset < STRIDE)
+    for spot in range(4):
+        first = block * spot + section * half
+        key_pos = first - block + key_index
+        query_segment = segment_at(ends, first + query_index)
+        key_segment = jnp.where(key_pos >= 0, segment_at(ends, key_pos), slots)
+        same = (query_segment == key_segment) & (query_segment < slots)
+        window_mask[spot * half : (spot + 1) * half, :] = (same & near | (offset == 0)).astype(F32)
 
     def place(axis):
-        index = lax.broadcasted_iota(jnp.int32, (rows, rows), axis)
+        shape = (rows, 1) if axis == 0 else (1, rows)
+        index = lax.broadcasted_iota(jnp.int32, shape, axis)
         return block * (index // half) + section * half + (index & (half - 1))
 
     query_pos, key_pos = place(0), place(1)
     offset = query_pos - key_pos
     segment = segment_at(ends, query_pos)
-    same = (segment == segment_at(ends, key_pos)) & (segment < len(ends))
+    same = (segment == segment_at(ends, key_pos)) & (segment < slots)
     allow = same & (offset >= 0) & ((offset & (STRIDE - 1)) == 0) | (offset == 0)
     strided_mask[...] = allow.astype(F32)
 
@@ -729,6 +733,43 @@
     ).astype(BF)
 
 
+def one_kernel(mask, hidden_ref, cotangent, *rest):
+    weights, rest = rest[:5], rest[5:]
+    result_one, grad_one, terms, *held = rest
+    normal, inverse, normed, packed, probs, attended = held[:6]
+    middle, mid_inverse, second, active, slope, grad_pre = held[6:]
+    one_forward_kernel(
+        mask,
+        hidden_ref,
+        *weights,
+        *held[:6],
+        result_one,
+        middle,
+        mid_inverse,
+        second,
+        active,
+        slope,
+    )
+    one_backward_kernel(
+        cotangent,
+        *weights,
+        normal,
+        inverse,
+        normed,
+        packed,
+        probs,
+        middle,
+        mid_inverse,
+        second,
+        active,
+        slope,
+        attended,
+        grad_one,
+        terms,
+        grad_pre,
+    )
+
+
 def zero_ffn_kernel(
     grad_ref,
     w_out,
@@ -881,6 +922,39 @@
         swap[rows:, :] = grad_line[:reached, :].astype(BF)
 
 
+def zero_both_kernel(
+    grad_ref,
+    w_qkv,
+    w_out,
+    w_up,
+    w_down,
+    gains,
+    middle_unit,
+    middle_inverse,
+    slope,
+    *rest,
+):
+    *rest, grad_middle, grad_att, grad_pre, gain_term = rest
+    zero_ffn_kernel(
+        grad_ref,
+        w_out,
+        w_up,
+        w_down,
+        gains,
+        middle_unit,
+        middle_inverse,
+        slope,
+        grad_middle,
+        grad_att,
+        grad_pre,
+        gain_term,
+    )
+    inputs, outputs = rest[:-4], rest[-4:]
+    zero_backward_kernel(
+        grad_ref, w_qkv, gains, *inputs, grad_middle, grad_att, grad_pre, gain_term, *outputs
+    )
+
+
 def share_kernel(keep, one_near, zero_near, came, *pieces):
     rows = keep.shape[0]
     half = rows // 4
@@ -1099,73 +1173,34 @@
             *ffn_saved,
         ),
     )
-    (
-        normal_one,
-        inverse_one,
-        normed_one,
-        packed_one,
-        probs_one,
-        attended_one,
-        result_one,
-        *saved_one,
-    ) = call(
-        one_forward_kernel,
+    result_one, grad_one, terms_one = call(
+        one_kernel,
         (),
-        (strided_mask, result_zero, *weights),
-        (
-            ((rows, width), F32),
-            ((rows, 128), F32),
-            ((rows, width), BF),
-            ((rows, 3 * width), BF),
-            ((HEADS, rows, rows), F32),
-            ((rows, width), BF),
-            *ffn_saved,
+        (strided_mask, result_zero, cotangent, *weights),
+        (((rows, width), BF), ((rows, width), BF), ((2, 4, term_rows, width), BF)),
+        micros=4.0,
+        scratch=(
+            pltpu.VMEM((rows, width), F32),
+            pltpu.VMEM((rows, 128), F32),
+            pltpu.VMEM((rows, width), BF),
+            pltpu.VMEM((rows, 3 * width), BF),
+            pltpu.VMEM((HEADS, rows, rows), F32),
+            pltpu.VMEM((rows, width), BF),
+            *(pltpu.VMEM(*shape) for shape in ffn_saved[1:]),
+            pltpu.VMEM((rows, hidden_units), BF),
         ),
-    )
-    middle_one, mid_inverse_one, second_one, active_one, slope_one = saved_one
-    grad_one, terms_one, _ = call(
-        one_backward_kernel,
-        (),
-        (
-            cotangent,
-            *weights,
-            normal_one,
-            inverse_one,
-            normed_one,
-            packed_one,
-            probs_one,
-            middle_one,
-            mid_inverse_one,
-            second_one,
-            active_one,
-            slope_one,
-            attended_one,
-        ),
-        (((rows, width), BF), ((2, 4, term_rows, width), BF), ((rows, hidden_units), BF)),
-        micros=3.0,
     )
     middle_zero, mid_inverse_zero, second_zero, active_zero, slope_zero = saved_zero
     came_one = lax.ppermute(terms_one[1], "section", SWAP)
-    w_qkv, w_out, w_up, w_down, gains = weights
-    zero_ffn = call(
-        zero_ffn_kernel,
-        (),
-        (grad_one, w_out, w_up, w_down, gains, middle_zero, mid_inverse_zero, slope_zero),
-        (
-            ((rows, width), F32),
-            ((rows, width), BF),
-            ((rows, hidden_units), BF),
-            ((1, width), F32),
-        ),
-        micros=2.0,
-    )
     result_keep, grad_line, swap, terms_zero = call(
-        zero_backward_kernel,
+        zero_both_kernel,
         (),
         (
             grad_one,
-            w_qkv,
-            gains,
+            *weights,
+            middle_zero,
+            mid_inverse_zero,
+            slope_zero,
             normal_all,
             inverse_all,
             normed_all,
@@ -1177,7 +1212,6 @@
             second_zero,
             active_zero,
             attended_zero,
-            *zero_ffn,
         ),
         (
             ((rows, width), BF),
@@ -1186,6 +1220,12 @@
             ((2, 4, term_rows, width), BF),
         ),
         micros=4.0,
+        scratch=(
+            pltpu.VMEM((rows, width), F32),
+            pltpu.VMEM((rows, width), BF),
+            pltpu.VMEM((rows, hidden_units), BF),
+            pltpu.VMEM((1, width), F32),
+        ),
     )
     came = lax.ppermute(swap, "section", SWAP)
     shared = call(

time: 86.8 us -> 86.1 us (level)
  Pallas kernels: 14.7 us -> 13.6 us
    pallas_call x10 -> x8, Pallas kernels: 14.7 us -> 13.6 us  [call(): pl.pallas_call(body, out_shape=tuple((jax.ShapeDtypeStruct(*shape) for sh...]
where the time goes in v5:
time: 86.1 us; the launch traced here: 84.9 us
  waiting for transfers between devices  39.6 us (46%)
  starting transfers between devices  28.9 us (34%)
  Pallas kernels  13.6 us (16%)
  other arithmetic  1.47 us (2%)
  between operations  1.16 us (1%)
    ppermute x12, waiting for transfers between devices, along_line(): return lax.ppermute(value, 'dp', [(z, z ^ step) for z in range(4)])  18 us
    ppermute x12, starting transfers between devices, along_line(): return lax.ppermute(value, 'dp', [(z, z ^ step) for z in range(4)])  14.4 us
    pallas_call x8, Pallas kernels, call(): pl.pallas_call(body, out_shape=tuple((jax.ShapeDtypeStruct(*shape) for sh...  13.6 us
    ppermute x2, waiting for transfers between devices, reduce_terms(): pair = jnp.stack([total, lax.ppermute(total, PLANE, SECOND)])  5.85 us
    ppermute x2, waiting for transfers between devices, reduce_terms(): first = lax.ppermute(terms[0, 2:4] + came[2:4], PLANE, FIRST)  5.74 us
    ppermute x2, waiting for transfers between devices, reduce_terms(): return (pair, lax.ppermute(pair, PLANE, FIRST))  5.1 us
    ppermute x2, starting transfers between devices, reduce_terms(): second = lax.ppermute(terms[0, 1] + came[1] + first[1], PLANE, SECOND)  3.19 us
    ppermute x2, starting transfers between devices, reduce_terms(): first = lax.ppermute(terms[0, 2:4] + came[2:4], PLANE, FIRST)  3.15 us
  transfers between devices with their start and end apart: 35, of which 20 were waited for; matrix products, arithmetic and copies ran while one was open for 2% of the time, Pallas kernels for 6%

profile of v5, /device:TPU:0, one launch (start us, length us, event | category | flops | bytes accessed | tf_op | source)
XLA Modules:
  0.0 84.9 jit_solution(10441330940586877428)
XLA Ops:
  0.7 1.3 %shard_map.152 = (bf16[144,256]{1,0:T(8,128)(2,1)S(1)}, bf16[128,256]{1,0:T(8,128)(2,1)S(1)}, bf16[128,256]{1,0:T(8,128)(2,1)S(1)}, bf16[128,256]{1,0:T(8,128)(2...) custom-call(bf16[4,1,128,256]{3,2,1,0:T(8,128)(2,1)} %tokens.1, bf16[4,1,128,256]{3,2,1,0:T(8,128)(2,1)} %grads.1, ...), custom_call_target="tpu_custom_call" | custom-call | flops 1100000000 | bytes 3400000 | tf_op jit(solution)/shard_map/pallas_call | solution.py:317
  2.0 0.5 collective-permute-start.3
  2.5 2.6 %collective-permute-start = (bf16[128,256]{1,0:T(8,128)(2,1)S(1)}, bf16[128,256]{1,0:T(8,128)(2,1)S(1)}, u32[]{:S(2)}, u32[]{:S(2)}) collective-permute-start(bf16[128,256]{1,0:T(8,128)(2,1)S(1)} %get-tuple-element.65), channel_id=1, source_target_pairs={{0,4},{4,0},{8,12},{12,8},{1,5},{5,1},{9,13},{13,9},{2,6},{6,2},{1... | collective-permute-start | bytes 196616 | tf_op jit(solution)/shard_map/ppermute | solution.py:1056
  5.2 2.6 %collective-permute-start.1 = (bf16[128,256]{1,0:T(8,128)(2,1)S(1)}, bf16[128,256]{1,0:T(8,128)(2,1)S(1)}, u32[]{:S(2)}, u32[]{:S(2)}) collective-permute-start(bf16[128,256]{1,0:T(8,128)(2,1)S(1)} %get-tuple-element.67), channel_id=1, source_target_pairs={{0,8},{4,12},{8,0},{12,4},{1,9},{5,13},{9,1},{13,5},{2,10},{6,14},... | collective-permute-start | bytes 196616 | tf_op jit(solution)/shard_map/ppermute | solution.py:1056
  7.8 0.1 collective-permute-done.own1
  7.9 0.5 collective-permute-start.8
  8.4 0.1 collective-permute-start.7
  8.5 1.5 %collective-permute-done.8 = bf16[256,256]{1,0:T(8,128)(2,1)S(1)} collective-permute-done((bf16[256,256]{1,0:T(8,128)(2,1)S(1)}, bf16[256,256]{1,0:T(8,128)(2,1)S(1)}, u32[]{:S(2)}, u32[]{:S(2)}) %collective-permute-start.8) | collective-permute-done | bytes 131104 | tf_op jit(solution)/shard_map/ppermute | solution.py:1125
  10.0 0.1 collective-permute-start.9
  10.2 2.7 %collective-permute-done.1.own2 = bf16[128,256]{1,0:T(8,128)(2,1)S(1)} collective-permute-done((bf16[128,256]{1,0:T(8,128)(2,1)S(1)}, bf16[128,256]{1,0:T(8,128)(2,1)S(1)}, u32[]{:S(2)}, u32[]{:S(2)}) %collective-permute-start.1) | collective-permute-done | bytes 65568 | tf_op jit(solution)/shard_map/ppermute | solution.py:1056
  12.9 1.0 %collective-permute-done.2.own3 = bf16[128,256]{1,0:T(8,128)(2,1)S(1)} collective-permute-done((bf16[128,256]{1,0:T(8,128)(2,1)S(1)}, bf16[128,256]{1,0:T(8,128)(2,1)S(1)}, u32[]{:S(2)}, u32[]{:S(2)}) %collective-permute-start.2) | collective-permute-done | bytes 65568 | tf_op jit(solution)/shard_map/ppermute | solution.py:1056
  13.9 0.5 collective-permute-start.6
  14.5 0.1 pad_maximum_fusion.6.w_qkv.rest_0_
  14.5 0.1 select_bitcast_fusion.1
  14.6 0.1 pad_maximum_fusion.1.w_down.rest_3_
  14.7 0.1 select_bitcast_fusion.3
  14.8 0.1 pad_maximum_fusion.w_up.rest_2_
  14.9 0.2 collective-permute-done.5.far2
  15.1 0.2 collective-permute-done.6.far3
  15.3 2.2 %shard_map.153 = (bf16[640,256]{1,0:T(8,128)(2,1)}, f32[576,256]{1,0:T(8,128)S(1)}, f32[576,128]{1,0:T(8,128)S(1)}, bf16[576,256]{1,0:T(8,128)(2,1)S(1)}, bf16[2...) custom-call(f32[256,192]{1,0:T(8,128)S(1)} %get-tuple-element.63.mas, ...), custom_call_target="tpu_custom_call" | custom-call | flops 1100000000 | bytes 3400000 | tf_op jit(solution)/shard_map/pallas_call | solution.py:317
  17.5 3.4 %shard_map.154 = (bf16[256,256]{1,0:T(8,128)(2,1)S(1)}, bf16[256,256]{1,0:T(8,128)(2,1)S(1)}, bf16[2,4,400,256]{3,2,1,0:T(8,128)(2,1)S(1)}) custom-call(f32[256,256]{1,0:T(8,128)S(1)} %get-tuple-element.62.mask, bf16[256,256]{1,0:T(8,128)(2,1)S(1)} %get-tuple-element.73.hidden_ref.rest_6_, bf16[256,256]{1,0:T(8,128)(2,1)S(1)} %get-tuple-element.74.cotangent, ...), custom_call_target="tpu_custom_call" | custom-call | flops 4400000000 | bytes 13600000 | tf_op jit(solution)/shard_map/pallas_call | solution.py:317
  21.0 0.4 collective-permute-start.12
  21.4 2.6 %shard_map.155 = (bf16[256,256]{1,0:T(8,128)(2,1)S(1)}, f32[640,256]{1,0:T(8,128)S(1)}, bf16[832,256]{1,0:T(8,128)(2,1)S(1)}, bf16[2,4,400,256]{3,2,1,0:T(8,128)(2,1)S(1)}) custom-call(bf16[256,256]{1,0:T(8,128)(2,1)S(1)} %get-tuple-element.75.grad_ref.one_near, bf16[2,256,768]{2,1,0:T(8,128)(2,1)S(1)} %pad_maximum_fusion.6.w_qkv.rest_0_, ...), custom_call_target="tpu_custom_call" | custom-call | flops 4400000000 | bytes 13600000 | tf_op jit(solution)/shard_map/pallas_call | solution.py:317
  24.1 0.3 collective-permute-start.16
  24.3 0.3 collective-permute-start.11
  24.7 1.6 %collective-permute-start.13 = (bf16[2,400,256]{2,1,0:T(8,128)(2,1)S(1)}, bf16[2,400,256]{2,1,0:T(8,128)(2,1)S(1)}, u32[]{:S(2)}, u32[]{:S(2)}) collective-permute-start(bf16[2,400,256]{2,1,0:T(8,128)(2,1)S(1)} %slice_add_fusion.1), channel_id=1, source_target_pairs={{0,1},{1,0},{2,3},{3,2},{16,18},{17,19},{18,16},{19,17},{4,5},{5,4... | collective-permute-start | bytes 1228808 | tf_op jit(solution)/shard_map/ppermute | solution.py:1061
  26.3 0.2 collective-permute-done.16
  26.5 1.6 %collective-permute-start.17 = (bf16[2,400,256]{2,1,0:T(8,128)(2,1)S(1)}, bf16[2,400,256]{2,1,0:T(8,128)(2,1)S(1)}, u32[]{:S(2)}, u32[]{:S(2)}) collective-permute-start(bf16[2,400,256]{2,1,0:T(8,128)(2,1)S(1)} %slice_add_fusion), channel_id=1, source_target_pairs={{0,1},{1,0},{2,3},{3,2},{16,18},{17,19},{18,16},{19,17},{4,5},{5,4... | collective-permute-start | bytes 1228808 | tf_op jit(solution)/shard_map/ppermute | solution.py:1061
  28.1 0.2 shard_map.156
  28.3 1.3 %collective-permute-start.15 = (bf16[256,256]{1,0:T(8,128)(2,1)S(1)}, bf16[256,256]{1,0:T(8,128)(2,1)S(1)}, u32[]{:S(2)}, u32[]{:S(2)}) collective-permute-start(bf16[256,256]{1,0:T(8,128)(2,1)S(1)} %get-tuple-element.94), channel_id=1, source_target_pairs={{0,4},{4,0},{8,12},{12,8},{1,5},{5,1},{9,13},{13,9},{2,6},{6,2},{1... | collective-permute-start | bytes 393224 | tf_op jit(solution)/shard_map/ppermute | solution.py:1056
  29.6 2.4 %collective-permute-start.21 = (bf16[256,256]{1,0:T(8,128)(2,1)S(1)}, bf16[256,256]{1,0:T(8,128)(2,1)S(1)}, u32[]{:S(2)}, u32[]{:S(2)}) collective-permute-start(bf16[256,256]{1,0:T(8,128)(2,1)S(1)} %get-tuple-element.100), channel_id=1, source_target_pairs={{0,12},{4,8},{8,4},{12,0},{1,13},{5,9},{9,5},{13,1},{2,14},{6,10},... | collective-permute-start | bytes 393224 | tf_op jit(solution)/shard_map/ppermute | solution.py:1056
  32.0 0.7 collective-permute-done.13
  32.7 1.6 %collective-permute-start.14 = (bf16[400,256]{1,0:T(8,128)(2,1)S(1)}, bf16[400,256]{1,0:T(8,128)(2,1)S(1)}, u32[]{:S(2)}, u32[]{:S(2)}) collective-permute-start(bf16[400,256]{1,0:T(8,128)(2,1)S(1)} %fusion.5), channel_id=1, source_target_pairs={{0,2},{1,3},{2,0},{3,1},{16,17},{17,16},{18,19},{19,18},{4,6},{5,7... | collective-permute-start | bytes 614408 | tf_op jit(solution)/shard_map/ppermute | solution.py:1062
  34.3 5.0 %collective-permute-done.17 = bf16[2,400,256]{2,1,0:T(8,128)(2,1)S(1)} collective-permute-done((bf16[2,400,256]{2,1,0:T(8,128)(2,1)S(1)}, bf16[2,400,256]{2,1,0:T(8,128)(2,1)S(1)}, u32[]{:S(2)}, u32[]{:S(2)}) %collective-permute-start.17) | collective-permute-done | bytes 409632 | tf_op jit(solution)/shard_map/ppermute | solution.py:1061
  39.4 1.6 %collective-permute-start.18 = (bf16[400,256]{1,0:T(8,128)(2,1)S(1)}, bf16[400,256]{1,0:T(8,128)(2,1)S(1)}, u32[]{:S(2)}, u32[]{:S(2)}) collective-permute-start(bf16[400,256]{1,0:T(8,128)(2,1)S(1)} %fusion), channel_id=1, source_target_pairs={{0,2},{1,3},{2,0},{3,1},{16,17},{17,16},{18,19},{19,18},{4,6},{5,7... | collective-permute-start | bytes 614408 | tf_op jit(solution)/shard_map/ppermute | solution.py:1062
  41.1 1.3 %collective-permute-start.20 = (bf16[400,256]{1,0:T(8,128)(2,1)S(1)}, bf16[400,256]{1,0:T(8,128)(2,1)S(1)}, u32[]{:S(2)}, u32[]{:S(2)}) collective-permute-start(bf16[400,256]{1,0:T(8,128)(2,1)S(1)} %fusion.8), channel_id=1, source_target_pairs={{0,4},{4,0},{8,12},{12,8},{1,5},{5,1},{9,13},{13,9},{2,6},{6,2},{1... | collective-permute-start | bytes 614408 | tf_op jit(solution)/shard_map/ppermute | solution.py:1056
  42.3 2.9 %collective-permute-done.18 = bf16[400,256]{1,0:T(8,128)(2,1)S(1)} collective-permute-done((bf16[400,256]{1,0:T(8,128)(2,1)S(1)}, bf16[400,256]{1,0:T(8,128)(2,1)S(1)}, u32[]{:S(2)}, u32[]{:S(2)}) %collective-permute-start.18) | collective-permute-done | bytes 204832 | tf_op jit(solution)/shard_map/ppermute | solution.py:1062
  45.3 1.3 %collective-permute-start.22 = (bf16[400,256]{1,0:T(8,128)(2,1)S(1)}, bf16[400,256]{1,0:T(8,128)(2,1)S(1)}, u32[]{:S(2)}, u32[]{:S(2)}) collective-permute-start(bf16[400,256]{1,0:T(8,128)(2,1)S(1)} %fusion.3), channel_id=1, source_target_pairs={{0,4},{4,0},{8,12},{12,8},{1,5},{5,1},{9,13},{13,9},{2,6},{6,2},{1... | collective-permute-start | bytes 614408 | tf_op jit(solution)/shard_map/ppermute | solution.py:1056
  46.6 2.6 %collective-permute-done.20 = bf16[400,256]{1,0:T(8,128)(2,1)S(1)} collective-permute-done((bf16[400,256]{1,0:T(8,128)(2,1)S(1)}, bf16[400,256]{1,0:T(8,128)(2,1)S(1)}, u32[]{:S(2)}, u32[]{:S(2)}) %collective-permute-start.20) | collective-permute-done | bytes 204832 | tf_op jit(solution)/shard_map/ppermute | solution.py:1056
  49.2 1.7 %collective-permute-start.27 = (bf16[200,256]{1,0:T(8,128)(2,1)S(1)}, bf16[200,256]{1,0:T(8,128)(2,1)S(1)}, u32[]{:S(2)}, u32[]{:S(2)}) collective-permute-start(bf16[200,256]{1,0:T(8,128)(2,1)S(1)} %constant_dynamic-slice_fusion), channel_id=1, source_target_pairs={{0,8},{4,12},{8,0},{12,4},{1,9},{5,13},{9,1},{13,5},{2,10},{6,14},... | collective-permute-start | bytes 307208 | tf_op jit(solution)/shard_map/ppermute | solution.py:1056
  50.9 2.3 %collective-permute-done.22 = bf16[400,256]{1,0:T(8,128)(2,1)S(1)} collective-permute-done((bf16[400,256]{1,0:T(8,128)(2,1)S(1)}, bf16[400,256]{1,0:T(8,128)(2,1)S(1)}, u32[]{:S(2)}, u32[]{:S(2)}) %collective-permute-start.22) | collective-permute-done | bytes 204832 | tf_op jit(solution)/shard_map/ppermute | solution.py:1056
  53.3 1.1 %collective-permute-start.23 = (bf16[200,256]{1,0:T(8,128)(2,1)S(1)}, bf16[200,256]{1,0:T(8,128)(2,1)S(1)}, u32[]{:S(2)}, u32[]{:S(2)}) collective-permute-start(bf16[200,256]{1,0:T(8,128)(2,1)S(1)} %constant_dynamic-slice_fusion.1), channel_id=1, source_target_pairs={{0,8},{4,12},{8,0},{12,4},{1,9},{5,13},{9,1},{13,5},{2,10},{6,14},... | collective-permute-start | bytes 307208 | tf_op jit(solution)/shard_map/ppermute | solution.py:1056
  54.4 3.2 %collective-permute-done.27 = bf16[200,256]{1,0:T(8,128)(2,1)S(1)} collective-permute-done((bf16[200,256]{1,0:T(8,128)(2,1)S(1)}, bf16[200,256]{1,0:T(8,128)(2,1)S(1)}, u32[]{:S(2)}, u32[]{:S(2)}) %collective-permute-start.27) | collective-permute-done | bytes 102432 | tf_op jit(solution)/shard_map/ppermute | solution.py:1056
  57.6 0.1 collective-permute-start.28
  57.7 2.7 %collective-permute-done.23 = bf16[200,256]{1,0:T(8,128)(2,1)S(1)} collective-permute-done((bf16[200,256]{1,0:T(8,128)(2,1)S(1)}, bf16[200,256]{1,0:T(8,128)(2,1)S(1)}, u32[]{:S(2)}, u32[]{:S(2)}) %collective-permute-start.23) | collective-permute-done | bytes 102432 | tf_op jit(solution)/shard_map/ppermute | solution.py:1056
  60.4 0.1 collective-permute-start.24
  60.5 1.8 %collective-permute-done.28 = bf16[200,256]{1,0:T(8,128)(2,1)S(1)} collective-permute-done((bf16[200,256]{1,0:T(8,128)(2,1)S(1)}, bf16[200,256]{1,0:T(8,128)(2,1)S(1)}, u32[]{:S(2)}, u32[]{:S(2)}) %collective-permute-start.28) | collective-permute-done | bytes 102432 | tf_op jit(solution)/shard_map/ppermute | solution.py:1056
  62.4 1.2 %collective-permute-start.29 = (bf16[400,256]{1,0:T(8,128)(2,1)S(1)}, bf16[400,256]{1,0:T(8,128)(2,1)S(1)}, u32[]{:S(2)}, u32[]{:S(2)}) collective-permute-start(bf16[400,256]{1,0:T(8,128)(2,1)S(1)} %maximum_select_fusion.1), channel_id=1, source_target_pairs={{0,2},{1,3},{2,0},{3,1},{16,17},{17,16},{18,19},{19,18},{4,6},{5,7... | collective-permute-start | bytes 614408 | tf_op jit(solution)/shard_map/ppermute | solution.py:1078
  63.6 1.5 %collective-permute-done.24 = bf16[200,256]{1,0:T(8,128)(2,1)S(1)} collective-permute-done((bf16[200,256]{1,0:T(8,128)(2,1)S(1)}, bf16[200,256]{1,0:T(8,128)(2,1)S(1)}, u32[]{:S(2)}, u32[]{:S(2)}) %collective-permute-start.24) | collective-permute-done | bytes 102432 | tf_op jit(solution)/shard_map/ppermute | solution.py:1056
  65.2 0.6 collective-permute-start.25
  65.8 2.9 %collective-permute-done.29 = bf16[400,256]{1,0:T(8,128)(2,1)S(1)} collective-permute-done((bf16[400,256]{1,0:T(8,128)(2,1)S(1)}, bf16[400,256]{1,0:T(8,128)(2,1)S(1)}, u32[]{:S(2)}, u32[]{:S(2)}) %collective-permute-start.29) | collective-permute-done | bytes 204832 | tf_op jit(solution)/shard_map/ppermute | solution.py:1078
  68.8 1.5 %collective-permute-start.30 = (bf16[2,400,256]{2,1,0:T(8,128)(2,1)S(1)}, bf16[2,400,256]{2,1,0:T(8,128)(2,1)S(1)}, u32[]{:S(2)}, u32[]{:S(2)}) collective-permute-start(bf16[2,400,256]{2,1,0:T(8,128)(2,1)S(1)} %pad_maximum_fusion.8), channel_id=1, source_target_pairs={{0,1},{1,0},{2,3},{3,2},{16,18},{17,19},{18,16},{19,17},{4,5},{5,4... | collective-permute-start | bytes 1228808 | tf_op jit(solution)/shard_map/ppermute | solution.py:1079
  70.3 2.9 %collective-permute-done.25 = bf16[400,256]{1,0:T(8,128)(2,1)S(1)} collective-permute-done((bf16[400,256]{1,0:T(8,128)(2,1)S(1)}, bf16[400,256]{1,0:T(8,128)(2,1)S(1)}, u32[]{:S(2)}, u32[]{:S(2)}) %collective-permute-start.25) | collective-permute-done | bytes 204832 | tf_op jit(solution)/shard_map/ppermute | solution.py:1078
  73.3 1.6 %collective-permute-start.26 = (bf16[2,400,256]{2,1,0:T(8,128)(2,1)S(1)}, bf16[2,400,256]{2,1,0:T(8,128)(2,1)S(1)}, u32[]{:S(2)}, u32[]{:S(2)}) collective-permute-start(bf16[2,400,256]{2,1,0:T(8,128)(2,1)S(1)} %pad_maximum_fusion.7), channel_id=1, source_target_pairs={{0,1},{1,0},{2,3},{3,2},{16,18},{17,19},{18,16},{19,17},{4,5},{5,4... | collective-permute-start | bytes 1228808 | tf_op jit(solution)/shard_map/ppermute | solution.py:1079
  74.9 1.9 %collective-permute-done.30 = bf16[2,400,256]{2,1,0:T(8,128)(2,1)S(1)} collective-permute-done((bf16[2,400,256]{2,1,0:T(8,128)(2,1)S(1)}, bf16[2,400,256]{2,1,0:T(8,128)(2,1)S(1)}, u32[]{:S(2)}, u32[]{:S(2)}) %collective-permute-start.30) | collective-permute-done | bytes 409632 | tf_op jit(solution)/shard_map/ppermute | solution.py:1079
  76.8 0.8 shard_map.157
  77.6 0.5 collective-permute-start.31
  78.1 3.2 %collective-permute-done.26 = bf16[2,400,256]{2,1,0:T(8,128)(2,1)S(1)} collective-permute-done((bf16[2,400,256]{2,1,0:T(8,128)(2,1)S(1)}, bf16[2,400,256]{2,1,0:T(8,128)(2,1)S(1)}, u32[]{:S(2)}, u32[]{:S(2)}) %collective-permute-start.26) | collective-permute-done | bytes 409632 | tf_op jit(solution)/shard_map/ppermute | solution.py:1079
  81.3 0.1 pad_maximum_fusion.3.one
  81.4 0.1 pad_maximum_fusion.2.zero
  81.5 1.8 %shard_map.158 = (f32[1,256]{1,0:T(1,128)}, f32[1,256,768]{2,1,0:T(8,128)}, f32[1,256,256]{2,1,0:T(8,128)}, f32[1,256]{1,0:T(1,128)}, f32[1,256,1024]{2,1,0:T(8,128)}, /*index=5*/f32[1,1024,256]{2,1,0:T(8,128)}) custom-call(bf16[4,400,256]{2,1,0:T(8,128)(2,1)S(1)} %pad_maximum_fusion.2.zero, bf16[4,400,256]{2,1,0:T(8,128)(2,1)S(1)} %pad_maximum_fusion.3.one), custom_call_target="tpu_custom_call" | custom-call | flops 1100000000 | bytes 3400000 | tf_op jit(solution)/shard_map/pallas_call | solution.py:317
  83.3 0.1 pad_maximum_fusion.5.one
  83.4 0.1 pad_maximum_fusion.4.zero
  83.5 1.2 %shard_map.159 = (f32[1,256,768]{2,1,0:T(8,128)}, f32[1,256,256]{2,1,0:T(8,128)}, f32[1,256,1024]{2,1,0:T(8,128)}, f32[1,1024,256]{2,1,0:T(8,128)}) custom-call(f32[1,256,768]{2,1,0:T(8,128)} %get-tuple-element.107.qkv_in, f32[1,256,256]{2,1,0:T(8,128)} %get-tuple-element.108.out_in, ...), custom_call_target="tpu_custom_call", output_to_operand_aliasing={{0}: (0, {}), {1}: (1, {}), {2}: (2, {}), {3}: (3, {})} | custom-call | flops 1100000000 | bytes 3400000 | tf_op jit(solution)/shard_map/pallas_call | solution.py:317
  (54 shorter events, 1.0 us)
Async XLA Ops:
  0.6 7.7 %copy-start.2 = (bf16[1,256,768]{2,1,0:T(8,128)(2,1)S(1)}, bf16[1,256,768]{2,1,0:T(8,128)(2,1)}, u32[]{:S(2)}) copy-start(bf16[1,256,768]{2,1,0:T(8,128)(2,1)} %param.13) | copy-start | bytes 1179652
  0.6 7.2 %copy-start.3 = (bf16[1,256,256]{2,1,0:T(8,128)(2,1)S(1)}, bf16[1,256,256]{2,1,0:T(8,128)(2,1)}, u32[]{:S(2)}) copy-start(bf16[1,256,256]{2,1,0:T(8,128)(2,1)} %param.14) | copy-start | bytes 393220
  0.7 9.3 %copy-start.1 = (bf16[1,256,1024]{2,1,0:T(8,128)(2,1)S(1)}, bf16[1,256,1024]{2,1,0:T(8,128)(2,1)}, u32[]{:S(2)}) copy-start(bf16[1,256,1024]{2,1,0:T(8,128)(2,1)} %param.16) | copy-start | bytes 1572868
  0.7 7.2 %copy-start = (bf16[1,1024,256]{2,1,0:T(8,128)(2,1)S(1)}, bf16[1,1024,256]{2,1,0:T(8,128)(2,1)}, u32[]{:S(2)}) copy-start(bf16[1,1024,256]{2,1,0:T(8,128)(2,1)} %param.17) | copy-start | bytes 1572868
  2.0 6.4 %collective-permute-start.3 = (bf16[144,256]{1,0:T(8,128)(2,1)S(1)}, bf16[144,256]{1,0:T(8,128)(2,1)S(1)}, u32[]{:S(2)}, u32[]{:S(2)}) collective-permute-start(bf16[144,256]{1,0:T(8,128)(2,1)S(1)} %get-tuple-element.64.own0), channel_id=1, source_target_pairs={{0,16},{16,0},{1,17},{17,1},{2,18},{18,2},{3,19},{19,3},{4,20},{20... | collective-permute-start | bytes 221192 | tf_op jit(solution)/shard_map/ppermute | solution.py:1122
  2.5 5.3 %collective-permute-start = (bf16[128,256]{1,0:T(8,128)(2,1)S(1)}, bf16[128,256]{1,0:T(8,128)(2,1)S(1)}, u32[]{:S(2)}, u32[]{:S(2)}) collective-permute-start(bf16[128,256]{1,0:T(8,128)(2,1)S(1)} %get-tuple-element.65), channel_id=1, source_target_pairs={{0,4},{4,0},{8,12},{12,8},{1,5},{5,1},{9,13},{13,9},{2,6},{6,2},{1... | collective-permute-start | bytes 196616 | tf_op jit(solution)/shard_map/ppermute | solution.py:1056
  5.2 7.7 %collective-permute-start.1 = (bf16[128,256]{1,0:T(8,128)(2,1)S(1)}, bf16[128,256]{1,0:T(8,128)(2,1)S(1)}, u32[]{:S(2)}, u32[]{:S(2)}) collective-permute-start(bf16[128,256]{1,0:T(8,128)(2,1)S(1)} %get-tuple-element.67), channel_id=1, source_target_pairs={{0,8},{4,12},{8,0},{12,4},{1,9},{5,13},{9,1},{13,5},{2,10},{6,14},... | collective-permute-start | bytes 196616 | tf_op jit(solution)/shard_map/ppermute | solution.py:1056
  7.8 6.1 %collective-permute-start.2 = (bf16[128,256]{1,0:T(8,128)(2,1)S(1)}, bf16[128,256]{1,0:T(8,128)(2,1)S(1)}, u32[]{:S(2)}, u32[]{:S(2)}) collective-permute-start(bf16[128,256]{1,0:T(8,128)(2,1)S(1)} %get-tuple-element.68), channel_id=1, source_target_pairs={{0,12},{4,8},{8,4},{12,0},{1,13},{5,9},{9,5},{13,1},{2,14},{6,10},... | collective-permute-start | bytes 196616 | tf_op jit(solution)/shard_map/ppermute | solution.py:1056
  7.9 6.7 %collective-permute-start.10 = (bf16[1024,256]{1,0:T(8,128)(2,1)S(1)}, bf16[1024,256]{1,0:T(8,128)(2,1)S(1)}, u32[]{:S(2)}, u32[]{:S(2)}) collective-permute-start(bf16[1024,256]{1,0:T(8,128)(2,1)S(1)} %bitcast.96), channel_id=1, source_target_pairs={{0,16},{16,0},{1,17},{17,1},{2,18},{18,2},{3,19},{19,3},{4,20},{20... | collective-permute-start | bytes 1572872 | tf_op jit(solution)/shard_map/ppermute | solution.py:1125
  7.9 2.1 %collective-permute-start.8 = (bf16[256,256]{1,0:T(8,128)(2,1)S(1)}, bf16[256,256]{1,0:T(8,128)(2,1)S(1)}, u32[]{:S(2)}, u32[]{:S(2)}) collective-permute-start(bf16[256,256]{1,0:T(8,128)(2,1)S(1)} %bitcast.102), channel_id=1, source_target_pairs={{0,16},{16,0},{1,17},{17,1},{2,18},{18,2},{3,19},{19,3},{4,20},{20... | collective-permute-start | bytes 393224 | tf_op jit(solution)/shard_map/ppermute | solution.py:1125
  8.4 5.5 %collective-permute-start.7 = (bf16[256,768]{1,0:T(8,128)(2,1)S(1)}, bf16[256,768]{1,0:T(8,128)(2,1)S(1)}, u32[]{:S(2)}, u32[]{:S(2)}) collective-permute-start(bf16[256,768]{1,0:T(8,128)(2,1)S(1)} %bitcast.100), channel_id=1, source_target_pairs={{0,16},{16,0},{1,17},{17,1},{2,18},{18,2},{3,19},{19,3},{4,20},{20... | collective-permute-start | bytes 1179656 | tf_op jit(solution)/shard_map/ppermute | solution.py:1125
  10.0 4.8 %collective-permute-start.9 = (bf16[256,1024]{1,0:T(8,128)(2,1)S(1)}, bf16[256,1024]{1,0:T(8,128)(2,1)S(1)}, u32[]{:S(2)}, u32[]{:S(2)}) collective-permute-start(bf16[256,1024]{1,0:T(8,128)(2,1)S(1)} %bitcast.98), channel_id=1, source_target_pairs={{0,16},{16,0},{1,17},{17,1},{2,18},{18,2},{3,19},{19,3},{4,20},{20... | collective-permute-start | bytes 1572872 | tf_op jit(solution)/shard_map/ppermute | solution.py:1125
  12.9 2.1 %collective-permute-start.4 = (bf16[128,256]{1,0:T(8,128)(2,1)S(1)}, bf16[128,256]{1,0:T(8,128)(2,1)S(1)}, u32[]{:S(2)}, u32[]{:S(2)}) collective-permute-start(bf16[128,256]{1,0:T(8,128)(2,1)S(1)} %collective-permute-done.own1), channel_id=1, source_target_pairs={{0,16},{16,0},{1,17},{17,1},{2,18},{18,2},{3,19},{19,3},{4,20},{20... | collective-permute-start | bytes 196616 | tf_op jit(solution)/shard_map/ppermute | solution.py:1122
  13.9 1.3 %collective-permute-start.5 = (bf16[128,256]{1,0:T(8,128)(2,1)S(1)}, bf16[128,256]{1,0:T(8,128)(2,1)S(1)}, u32[]{:S(2)}, u32[]{:S(2)}) collective-permute-start(bf16[128,256]{1,0:T(8,128)(2,1)S(1)} %collective-permute-done.1.own2), channel_id=1, source_target_pairs={{0,16},{16,0},{1,17},{17,1},{2,18},{18,2},{3,19},{19,3},{4,20},{20... | collective-permute-start | bytes 196616 | tf_op jit(solution)/shard_map/ppermute | solution.py:1122
  13.9 1.4 %collective-permute-start.6 = (bf16[128,256]{1,0:T(8,128)(2,1)S(1)}, bf16[128,256]{1,0:T(8,128)(2,1)S(1)}, u32[]{:S(2)}, u32[]{:S(2)}) collective-permute-start(bf16[128,256]{1,0:T(8,128)(2,1)S(1)} %collective-permute-done.2.own3), channel_id=1, source_target_pairs={{0,16},{16,0},{1,17},{17,1},{2,18},{18,2},{3,19},{19,3},{4,20},{20... | collective-permute-start | bytes 196616 | tf_op jit(solution)/shard_map/ppermute | solution.py:1122
  21.0 3.6 %collective-permute-start.12 = (bf16[4,400,256]{2,1,0:T(8,128)(2,1)S(1)}, bf16[4,400,256]{2,1,0:T(8,128)(2,1)S(1)}, u32[]{:S(2)}, u32[]{:S(2)}) collective-permute-start(bf16[4,400,256]{2,1,0:T(8,128)(2,1)S(1)} %slice_bitcast_fusion.1), channel_id=1, source_target_pairs={{0,16},{16,0},{1,17},{17,1},{2,18},{18,2},{3,19},{19,3},{4,20},{20... | collective-permute-start | bytes 2457608 | tf_op jit(solution)/shard_map/ppermute | solution.py:1194
  24.1 2.4 %collective-permute-start.16 = (bf16[4,400,256]{2,1,0:T(8,128)(2,1)S(1)}, bf16[4,400,256]{2,1,0:T(8,128)(2,1)S(1)}, u32[]{:S(2)}, u32[]{:S(2)}) collective-permute-start(bf16[4,400,256]{2,1,0:T(8,128)(2,1)S(1)} %slice_bitcast_fusion), channel_id=1, source_target_pairs={{0,16},{16,0},{1,17},{17,1},{2,18},{18,2},{3,19},{19,3},{4,20},{20... | collective-permute-start | bytes 2457608 | tf_op jit(solution)/shard_map/ppermute | solution.py:1239
  24.3 3.8 %collective-permute-start.11 = (bf16[832,256]{1,0:T(8,128)(2,1)S(1)}, bf16[832,256]{1,0:T(8,128)(2,1)S(1)}, u32[]{:S(2)}, u32[]{:S(2)}) collective-permute-start(bf16[832,256]{1,0:T(8,128)(2,1)S(1)} %get-tuple-element.91), channel_id=1, source_target_pairs={{0,16},{16,0},{1,17},{17,1},{2,18},{18,2},{3,19},{19,3},{4,20},{20... | collective-permute-start | bytes 1277960 | tf_op jit(solution)/shard_map/ppermute | solution.py:1230
  24.7 8.0 %collective-permute-start.13 = (bf16[2,400,256]{2,1,0:T(8,128)(2,1)S(1)}, bf16[2,400,256]{2,1,0:T(8,128)(2,1)S(1)}, u32[]{:S(2)}, u32[]{:S(2)}) collective-permute-start(bf16[2,400,256]{2,1,0:T(8,128)(2,1)S(1)} %slice_add_fusion.1), channel_id=1, source_target_pairs={{0,1},{1,0},{2,3},{3,2},{16,18},{17,19},{18,16},{19,17},{4,5},{5,4... | collective-permute-start | bytes 1228808 | tf_op jit(solution)/shard_map/ppermute | solution.py:1061
  26.5 12.9 %collective-permute-start.17 = (bf16[2,400,256]{2,1,0:T(8,128)(2,1)S(1)}, bf16[2,400,256]{2,1,0:T(8,128)(2,1)S(1)}, u32[]{:S(2)}, u32[]{:S(2)}) collective-permute-start(bf16[2,400,256]{2,1,0:T(8,128)(2,1)S(1)} %slice_add_fusion), channel_id=1, source_target_pairs={{0,1},{1,0},{2,3},{3,2},{16,18},{17,19},{18,16},{19,17},{4,5},{5,4... | collective-permute-start | bytes 1228808 | tf_op jit(solution)/shard_map/ppermute | solution.py:1061
  28.3 12.7 %collective-permute-start.15 = (bf16[256,256]{1,0:T(8,128)(2,1)S(1)}, bf16[256,256]{1,0:T(8,128)(2,1)S(1)}, u32[]{:S(2)}, u32[]{:S(2)}) collective-permute-start(bf16[256,256]{1,0:T(8,128)(2,1)S(1)} %get-tuple-element.94), channel_id=1, source_target_pairs={{0,4},{4,0},{8,12},{12,8},{1,5},{5,1},{9,13},{13,9},{2,6},{6,2},{1... | collective-permute-start | bytes 393224 | tf_op jit(solution)/shard_map/ppermute | solution.py:1056
  29.6 19.6 %collective-permute-start.21 = (bf16[256,256]{1,0:T(8,128)(2,1)S(1)}, bf16[256,256]{1,0:T(8,128)(2,1)S(1)}, u32[]{:S(2)}, u32[]{:S(2)}) collective-permute-start(bf16[256,256]{1,0:T(8,128)(2,1)S(1)} %get-tuple-element.100), channel_id=1, source_target_pairs={{0,12},{4,8},{8,4},{12,0},{1,13},{5,9},{9,5},{13,1},{2,14},{6,10},... | collective-permute-start | bytes 393224 | tf_op jit(solution)/shard_map/ppermute | solution.py:1056
  32.0 13.3 %collective-permute-start.19 = (bf16[256,256]{1,0:T(8,128)(2,1)S(1)}, bf16[256,256]{1,0:T(8,128)(2,1)S(1)}, u32[]{:S(2)}, u32[]{:S(2)}) collective-permute-start(bf16[256,256]{1,0:T(8,128)(2,1)S(1)} %get-tuple-element.97), channel_id=1, source_target_pairs={{0,8},{4,12},{8,0},{12,4},{1,9},{5,13},{9,1},{13,5},{2,10},{6,14},... | collective-permute-start | bytes 393224 | tf_op jit(solution)/shard_map/ppermute | solution.py:1056
  32.7 8.3 %collective-permute-start.14 = (bf16[400,256]{1,0:T(8,128)(2,1)S(1)}, bf16[400,256]{1,0:T(8,128)(2,1)S(1)}, u32[]{:S(2)}, u32[]{:S(2)}) collective-permute-start(bf16[400,256]{1,0:T(8,128)(2,1)S(1)} %fusion.5), channel_id=1, source_target_pairs={{0,2},{1,3},{2,0},{3,1},{16,17},{17,16},{18,19},{19,18},{4,6},{5,7... | collective-permute-start | bytes 614408 | tf_op jit(solution)/shard_map/ppermute | solution.py:1062
  39.4 5.8 %collective-permute-start.18 = (bf16[400,256]{1,0:T(8,128)(2,1)S(1)}, bf16[400,256]{1,0:T(8,128)(2,1)S(1)}, u32[]{:S(2)}, u32[]{:S(2)}) collective-permute-start(bf16[400,256]{1,0:T(8,128)(2,1)S(1)} %fusion), channel_id=1, source_target_pairs={{0,2},{1,3},{2,0},{3,1},{16,17},{17,16},{18,19},{19,18},{4,6},{5,7... | collective-permute-start | bytes 614408 | tf_op jit(solution)/shard_map/ppermute | solution.py:1062
  41.1 8.1 %collective-permute-start.20 = (bf16[400,256]{1,0:T(8,128)(2,1)S(1)}, bf16[400,256]{1,0:T(8,128)(2,1)S(1)}, u32[]{:S(2)}, u32[]{:S(2)}) collective-permute-start(bf16[400,256]{1,0:T(8,128)(2,1)S(1)} %fusion.8), channel_id=1, source_target_pairs={{0,4},{4,0},{8,12},{12,8},{1,5},{5,1},{9,13},{13,9},{2,6},{6,2},{1... | collective-permute-start | bytes 614408 | tf_op jit(solution)/shard_map/ppermute | solution.py:1056
  45.3 8.0 %collective-permute-start.22 = (bf16[400,256]{1,0:T(8,128)(2,1)S(1)}, bf16[400,256]{1,0:T(8,128)(2,1)S(1)}, u32[]{:S(2)}, u32[]{:S(2)}) collective-permute-start(bf16[400,256]{1,0:T(8,128)(2,1)S(1)} %fusion.3), channel_id=1, source_target_pairs={{0,4},{4,0},{8,12},{12,8},{1,5},{5,1},{9,13},{13,9},{2,6},{6,2},{1... | collective-permute-start | bytes 614408 | tf_op jit(solution)/shard_map/ppermute | solution.py:1056
  49.2 8.3 %collective-permute-start.27 = (bf16[200,256]{1,0:T(8,128)(2,1)S(1)}, bf16[200,256]{1,0:T(8,128)(2,1)S(1)}, u32[]{:S(2)}, u32[]{:S(2)}) collective-permute-start(bf16[200,256]{1,0:T(8,128)(2,1)S(1)} %constant_dynamic-slice_fusion), channel_id=1, source_target_pairs={{0,8},{4,12},{8,0},{12,4},{1,9},{5,13},{9,1},{13,5},{2,10},{6,14},... | collective-permute-start | bytes 307208 | tf_op jit(solution)/shard_map/ppermute | solution.py:1056
  53.3 7.1 %collective-permute-start.23 = (bf16[200,256]{1,0:T(8,128)(2,1)S(1)}, bf16[200,256]{1,0:T(8,128)(2,1)S(1)}, u32[]{:S(2)}, u32[]{:S(2)}) collective-permute-start(bf16[200,256]{1,0:T(8,128)(2,1)S(1)} %constant_dynamic-slice_fusion.1), channel_id=1, source_target_pairs={{0,8},{4,12},{8,0},{12,4},{1,9},{5,13},{9,1},{13,5},{2,10},{6,14},... | collective-permute-start | bytes 307208 | tf_op jit(solution)/shard_map/ppermute | solution.py:1056
  57.6 4.7 %collective-permute-start.28 = (bf16[200,256]{1,0:T(8,128)(2,1)S(1)}, bf16[200,256]{1,0:T(8,128)(2,1)S(1)}, u32[]{:S(2)}, u32[]{:S(2)}) collective-permute-start(bf16[200,256]{1,0:T(8,128)(2,1)S(1)} %fusion.12), channel_id=1, source_target_pairs={{0,4},{4,0},{8,12},{12,8},{1,5},{5,1},{9,13},{13,9},{2,6},{6,2},{1... | collective-permute-start | bytes 307208 | tf_op jit(solution)/shard_map/ppermute | solution.py:1056
  60.4 4.7 %collective-permute-start.24 = (bf16[200,256]{1,0:T(8,128)(2,1)S(1)}, bf16[200,256]{1,0:T(8,128)(2,1)S(1)}, u32[]{:S(2)}, u32[]{:S(2)}) collective-permute-start(bf16[200,256]{1,0:T(8,128)(2,1)S(1)} %fusion.13), channel_id=1, source_target_pairs={{0,4},{4,0},{8,12},{12,8},{1,5},{5,1},{9,13},{13,9},{2,6},{6,2},{1... | collective-permute-start | bytes 307208 | tf_op jit(solution)/shard_map/ppermute | solution.py:1056
  62.4 6.3 %collective-permute-start.29 = (bf16[400,256]{1,0:T(8,128)(2,1)S(1)}, bf16[400,256]{1,0:T(8,128)(2,1)S(1)}, u32[]{:S(2)}, u32[]{:S(2)}) collective-permute-start(bf16[400,256]{1,0:T(8,128)(2,1)S(1)} %maximum_select_fusion.1), channel_id=1, source_target_pairs={{0,2},{1,3},{2,0},{3,1},{16,17},{17,16},{18,19},{19,18},{4,6},{5,7... | collective-permute-start | bytes 614408 | tf_op jit(solution)/shard_map/ppermute | solution.py:1078
  65.2 8.0 %collective-permute-start.25 = (bf16[400,256]{1,0:T(8,128)(2,1)S(1)}, bf16[400,256]{1,0:T(8,128)(2,1)S(1)}, u32[]{:S(2)}, u32[]{:S(2)}) collective-permute-start(bf16[400,256]{1,0:T(8,128)(2,1)S(1)} %maximum_select_fusion), channel_id=1, source_target_pairs={{0,2},{1,3},{2,0},{3,1},{16,17},{17,16},{18,19},{19,18},{4,6},{5,7... | collective-permute-start | bytes 614408 | tf_op jit(solution)/shard_map/ppermute | solution.py:1078
  68.8 8.0 %collective-permute-start.30 = (bf16[2,400,256]{2,1,0:T(8,128)(2,1)S(1)}, bf16[2,400,256]{2,1,0:T(8,128)(2,1)S(1)}, u32[]{:S(2)}, u32[]{:S(2)}) collective-permute-start(bf16[2,400,256]{2,1,0:T(8,128)(2,1)S(1)} %pad_maximum_fusion.8), channel_id=1, source_target_pairs={{0,1},{1,0},{2,3},{3,2},{16,18},{17,19},{18,16},{19,17},{4,5},{5,4... | collective-permute-start | bytes 1228808 | tf_op jit(solution)/shard_map/ppermute | solution.py:1079
  73.3 8.0 %collective-permute-start.26 = (bf16[2,400,256]{2,1,0:T(8,128)(2,1)S(1)}, bf16[2,400,256]{2,1,0:T(8,128)(2,1)S(1)}, u32[]{:S(2)}, u32[]{:S(2)}) collective-permute-start(bf16[2,400,256]{2,1,0:T(8,128)(2,1)S(1)} %pad_maximum_fusion.7), channel_id=1, source_target_pairs={{0,1},{1,0},{2,3},{3,2},{16,18},{17,19},{18,16},{19,17},{4,5},{5,4... | collective-permute-start | bytes 1228808 | tf_op jit(solution)/shard_map/ppermute | solution.py:1079
  74.9 8.4 %collective-permute-start.33 = (bf16[2,400,256]{2,1,0:T(8,128)(2,1)S(1)}, bf16[2,400,256]{2,1,0:T(8,128)(2,1)S(1)}, u32[]{:S(2)}, u32[]{:S(2)}) collective-permute-start(bf16[2,400,256]{2,1,0:T(8,128)(2,1)S(1)} %pad_maximum_fusion.8), channel_id=1, source_target_pairs={{0,16},{16,0},{1,17},{17,1},{2,18},{18,2},{3,19},{19,3},{4,20},{20... | collective-permute-start | bytes 1228808 | tf_op jit(solution)/shard_map/ppermute | solution.py:1252
  76.8 6.5 %collective-permute-start.34 = (bf16[2,400,256]{2,1,0:T(8,128)(2,1)S(1)}, bf16[2,400,256]{2,1,0:T(8,128)(2,1)S(1)}, u32[]{:S(2)}, u32[]{:S(2)}) collective-permute-start(bf16[2,400,256]{2,1,0:T(8,128)(2,1)S(1)} %collective-permute-done.30), channel_id=1, source_target_pairs={{0,16},{16,0},{1,17},{17,1},{2,18},{18,2},{3,19},{19,3},{4,20},{20... | collective-permute-start | bytes 1228808 | tf_op jit(solution)/shard_map/ppermute | solution.py:1252
  77.6 5.8 %collective-permute-start.31 = (bf16[2,400,256]{2,1,0:T(8,128)(2,1)S(1)}, bf16[2,400,256]{2,1,0:T(8,128)(2,1)S(1)}, u32[]{:S(2)}, u32[]{:S(2)}) collective-permute-start(bf16[2,400,256]{2,1,0:T(8,128)(2,1)S(1)} %pad_maximum_fusion.7), channel_id=1, source_target_pairs={{0,16},{16,0},{1,17},{17,1},{2,18},{18,2},{3,19},{19,3},{4,20},{20... | collective-permute-start | bytes 1228808 | tf_op jit(solution)/shard_map/ppermute | solution.py:1252
  81.3 2.1 %collective-permute-start.32 = (bf16[2,400,256]{2,1,0:T(8,128)(2,1)S(1)}, bf16[2,400,256]{2,1,0:T(8,128)(2,1)S(1)}, u32[]{:S(2)}, u32[]{:S(2)}) collective-permute-start(bf16[2,400,256]{2,1,0:T(8,128)(2,1)S(1)} %collective-permute-done.26), channel_id=1, source_target_pairs={{0,16},{16,0},{1,17},{17,1},{2,18},{18,2},{3,19},{19,3},{4,20},{20... | collective-permute-start | bytes 1228808 | tf_op jit(solution)/shard_map/ppermute | solution.py:1252

commit v6 on v5

--- a/solution.py
+++ b/solution.py
@@ -735,7 +735,7 @@
 
 def one_kernel(mask, hidden_ref, cotangent, *rest):
     weights, rest = rest[:5], rest[5:]
-    result_one, grad_one, terms, *held = rest
+    result_one, grad_one, keep, send, *held, terms = rest
     normal, inverse, normed, packed, probs, attended = held[:6]
     middle, mid_inverse, second, active, slope, grad_pre = held[6:]
     one_forward_kernel(
@@ -768,6 +768,8 @@
         terms,
         grad_pre,
     )
+    keep[...] = terms[0]
+    send[...] = terms[1]
 
 
 def zero_ffn_kernel(
@@ -934,7 +936,7 @@
     slope,
     *rest,
 ):
-    *rest, grad_middle, grad_att, grad_pre, gain_term = rest
+    *rest, grad_middle, grad_att, grad_pre, gain_term, terms = rest
     zero_ffn_kernel(
         grad_ref,
         w_out,
@@ -949,10 +951,12 @@
         grad_pre,
         gain_term,
     )
-    inputs, outputs = rest[:-4], rest[-4:]
+    inputs, outputs, (keep, send) = rest[:-5], rest[-5:-2], rest[-2:]
     zero_backward_kernel(
-        grad_ref, w_qkv, gains, *inputs, grad_middle, grad_att, grad_pre, gain_term, *outputs
-    )
+        grad_ref, w_qkv, gains, *inputs, grad_middle, grad_att, grad_pre, gain_term, *outputs, terms
+    )
+    keep[...] = terms[0]
+    send[...] = terms[1]
 
 
 def share_kernel(keep, one_near, zero_near, came, *pieces):
@@ -1056,25 +1060,16 @@
     return lax.ppermute(value, "dp", [(z, z ^ step) for z in range(4)])
 
 
-def reduce_terms(terms, came, zed, home, before, between=None):
+def reduce_terms(keep, came, home, steps, before, between=None):
     bar = lax.optimization_barrier
-    first = lax.ppermute(terms[0, 2:4] + came[2:4], PLANE, FIRST)
-    second = lax.ppermute(terms[0, 1] + came[1] + first[1], PLANE, SECOND)
-    total = bar(terms[0, 0] + came[0] + first[0] + second)
+    first = lax.ppermute(keep[2:4] + came[2:4], PLANE, FIRST)
+    second = lax.ppermute(keep[1] + came[1] + first[1], PLANE, SECOND)
+    total = bar(keep[0] + came[0] + first[0] + second)
     total, home[before] = bar((total, home[before]))
-    total = bar(total + along_line(total, 1))
+    total = bar(total + along_line(total, steps[0]))
     if between is not None:
         total, home[between] = bar((total, home[between]))
-    half = total.shape[0] // 2
-    odd = zed & 1
-    mine = lax.dynamic_slice_in_dim(total, odd * half, half, 0)
-    mine = bar(mine + along_line(mine, 2))
-    other = along_line(mine, 1)
-    total = bar(
-        jnp.where(
-            odd == 0, jnp.concatenate([mine, other]), jnp.concatenate([other, mine])
-        )
-    )
+    total = bar(total + along_line(total, steps[1]))
     pair = jnp.stack([total, lax.ppermute(total, PLANE, SECOND)])
     return pair, lax.ppermute(pair, PLANE, FIRST)
 
@@ -1091,7 +1086,6 @@
     down_proj,
 ):
     section = lax.axis_index("section")
-    zed = lax.axis_index("dp")
     micro_count, _, block, width = block_input.shape
     hidden_units = up_proj.shape[2]
     half = block // 2
@@ -1173,11 +1167,11 @@
             *ffn_saved,
         ),
     )
-    result_one, grad_one, terms_one = call(
+    result_one, grad_one, keep_one, send_one = call(
         one_kernel,
         (),
         (strided_mask, result_zero, cotangent, *weights),
-        (((rows, width), BF), ((rows, width), BF), ((2, 4, term_rows, width), BF)),
+        (((rows, width), BF), ((rows, width), BF), *(((4, term_rows, width), BF),) * 2),
         micros=4.0,
         scratch=(
             pltpu.VMEM((rows, width), F32),
@@ -1188,11 +1182,12 @@
             pltpu.VMEM((rows, width), BF),
             *(pltpu.VMEM(*shape) for shape in ffn_saved[1:]),
             pltpu.VMEM((rows, hidden_units), BF),
+            pltpu.VMEM((2, 4, term_rows, width), BF),
         ),
     )
     middle_zero, mid_inverse_zero, second_zero, active_zero, slope_zero = saved_zero
-    came_one = lax.ppermute(terms_one[1], "section", SWAP)
-    result_keep, grad_line, swap, terms_zero = call(
+    came_one = lax.ppermute(send_one, "section", SWAP)
+    result_keep, grad_line, swap, keep_zero, send_zero = call(
         zero_both_kernel,
         (),
         (
@@ -1217,7 +1212,7 @@
             ((rows, width), BF),
             ((reached + half, width), F32),
             ((rows + reached, width), BF),
-            ((2, 4, term_rows, width), BF),
+            *(((4, term_rows, width), BF),) * 2,
         ),
         micros=4.0,
         scratch=(
@@ -1225,6 +1220,7 @@
             pltpu.VMEM((rows, width), BF),
             pltpu.VMEM((rows, hidden_units), BF),
             pltpu.VMEM((1, width), F32),
+            pltpu.VMEM((2, 4, term_rows, width), BF),
         ),
     )
     came = lax.ppermute(swap, "section", SWAP)
@@ -1236,9 +1232,9 @@
         8,
     )
     home = [shared[0]] + [along_line(shared[step], step) for step in range(1, micro_count)]
-    came_zero = lax.ppermute(terms_zero[1], "section", SWAP)
-    one_pair, one_first = reduce_terms(terms_one, came_one, zed, home, 1, 3)
-    zero_pair, zero_first = reduce_terms(terms_zero, came_zero, zed, home, 2)
+    came_zero = lax.ppermute(send_zero, "section", SWAP)
+    one_pair, one_first = reduce_terms(keep_one, came_one, home, (2, 1), 3, 2)
+    zero_pair, zero_first = reduce_terms(keep_zero, came_zero, home, (1, 2), 1)
     results, input_grads = call(
         settle_kernel,
         (),

time: 86.1 us -> 84 us (0.976); the launches traced: 84.9 us -> 83.8 us
  waiting for transfers between devices: 39.6 us -> 36.6 us
  starting transfers between devices: 28.9 us -> 31.2 us
    ppermute x6, waiting for transfers between devices: 8.84 us -> 7.3 us  [the longest x2 5.13 us: reduce_terms(): first = lax.ppermute(keep[2:4] + came[2:4], PLANE, FIRST)]
    ppermute x2, starting transfers between devices: 1.77 us -> 3.23 us  [reduce_terms(): pair = jnp.stack([total, lax.ppermute(total, PLANE, SECOND)])]
    ppermute x2, waiting for transfers between devices: 5.85 us -> 4.62 us  [reduce_terms(): pair = jnp.stack([total, lax.ppermute(total, PLANE, SECOND)])]
    ppermute x12 -> x10, starting transfers between devices: 14.4 us -> 15.3 us  [along_line(): return lax.ppermute(value, 'dp', [(z, z ^ step) for z in range(4)])]
    ppermute x12 -> x10, waiting for transfers between devices: 18 us -> 17.7 us  [along_line(): return lax.ppermute(value, 'dp', [(z, z ^ step) for z in range(4)])]
  transfers between devices with their start and end apart: 35 -> 33, of which waited for: 20 -> 18; matrix products, arithmetic and copies ran while one was open for 2% -> 2% of each run, Pallas kernels for 6% -> 6%
where the time goes in v6:
time: 84 us; the launch traced here: 83.8 us
  waiting for transfers between devices  36.6 us (44%)
  starting transfers between devices  31.2 us (37%)
  Pallas kernels  13.6 us (16%)
  other arithmetic  1.39 us (2%)
  between operations  0.96 us (1%)
    ppermute x10, waiting for transfers between devices, along_line(): return lax.ppermute(value, 'dp', [(z, z ^ step) for z in range(4)])  17.7 us
    ppermute x10, starting transfers between devices, along_line(): return lax.ppermute(value, 'dp', [(z, z ^ step) for z in range(4)])  15.3 us
    pallas_call x8, Pallas kernels, call(): pl.pallas_call(body, out_shape=tuple((jax.ShapeDtypeStruct(*shape) for sh...  13.6 us
    ppermute x2, waiting for transfers between devices, reduce_terms(): return (pair, lax.ppermute(pair, PLANE, FIRST))  5.13 us
    ppermute x2, waiting for transfers between devices, reduce_terms(): first = lax.ppermute(keep[2:4] + came[2:4], PLANE, FIRST)  5.13 us
    ppermute x2, waiting for transfers between devices, reduce_terms(): pair = jnp.stack([total, lax.ppermute(total, PLANE, SECOND)])  4.62 us
    ppermute x2, starting transfers between devices, reduce_terms(): pair = jnp.stack([total, lax.ppermute(total, PLANE, SECOND)])  3.23 us
    ppermute x2, starting transfers between devices, reduce_terms(): second = lax.ppermute(keep[1] + came[1] + first[1], PLANE, SECOND)  3.22 us
  transfers between devices with their start and end apart: 33, of which 18 were waited for; matrix products, arithmetic and copies ran while one was open for 2% of the time, Pallas kernels for 6%

profile of v6, /device:TPU:0, one launch (start us, length us, event | category | flops | bytes accessed | tf_op | source)
XLA Modules:
  0.0 83.8 jit_solution(1540364717479586815)
XLA Ops:
  0.7 1.3 %shard_map.152 = (bf16[144,256]{1,0:T(8,128)(2,1)S(1)}, bf16[128,256]{1,0:T(8,128)(2,1)S(1)}, bf16[128,256]{1,0:T(8,128)(2,1)S(1)}, bf16[128,256]{1,0:T(8,128)(2...) custom-call(bf16[4,1,128,256]{3,2,1,0:T(8,128)(2,1)} %tokens.1, bf16[4,1,128,256]{3,2,1,0:T(8,128)(2,1)} %grads.1, ...), custom_call_target="tpu_custom_call" | custom-call | flops 1100000000 | bytes 3400000 | tf_op jit(solution)/shard_map/pallas_call | solution.py:317
  2.0 0.5 collective-permute-start.3
  2.5 2.6 %collective-permute-start = (bf16[128,256]{1,0:T(8,128)(2,1)S(1)}, bf16[128,256]{1,0:T(8,128)(2,1)S(1)}, u32[]{:S(2)}, u32[]{:S(2)}) collective-permute-start(bf16[128,256]{1,0:T(8,128)(2,1)S(1)} %get-tuple-element.67), channel_id=1, source_target_pairs={{0,4},{4,0},{8,12},{12,8},{1,5},{5,1},{9,13},{13,9},{2,6},{6,2},{1... | collective-permute-start | bytes 196616 | tf_op jit(solution)/shard_map/ppermute | solution.py:1060
  5.2 2.6 %collective-permute-start.1 = (bf16[128,256]{1,0:T(8,128)(2,1)S(1)}, bf16[128,256]{1,0:T(8,128)(2,1)S(1)}, u32[]{:S(2)}, u32[]{:S(2)}) collective-permute-start(bf16[128,256]{1,0:T(8,128)(2,1)S(1)} %get-tuple-element.69), channel_id=1, source_target_pairs={{0,8},{4,12},{8,0},{12,4},{1,9},{5,13},{9,1},{13,5},{2,10},{6,14},... | collective-permute-start | bytes 196616 | tf_op jit(solution)/shard_map/ppermute | solution.py:1060
  7.8 0.1 collective-permute-done.own1
  7.9 0.5 collective-permute-start.8
  8.4 0.1 collective-permute-start.7
  8.5 1.5 %collective-permute-done.8 = bf16[256,256]{1,0:T(8,128)(2,1)S(1)} collective-permute-done((bf16[256,256]{1,0:T(8,128)(2,1)S(1)}, bf16[256,256]{1,0:T(8,128)(2,1)S(1)}, u32[]{:S(2)}, u32[]{:S(2)}) %collective-permute-start.8) | collective-permute-done | bytes 131104 | tf_op jit(solution)/shard_map/ppermute | solution.py:1119
  10.0 0.1 collective-permute-start.9
  10.2 2.7 %collective-permute-done.1.own2 = bf16[128,256]{1,0:T(8,128)(2,1)S(1)} collective-permute-done((bf16[128,256]{1,0:T(8,128)(2,1)S(1)}, bf16[128,256]{1,0:T(8,128)(2,1)S(1)}, u32[]{:S(2)}, u32[]{:S(2)}) %collective-permute-start.1) | collective-permute-done | bytes 65568 | tf_op jit(solution)/shard_map/ppermute | solution.py:1060
  12.9 1.0 %collective-permute-done.2.own3 = bf16[128,256]{1,0:T(8,128)(2,1)S(1)} collective-permute-done((bf16[128,256]{1,0:T(8,128)(2,1)S(1)}, bf16[128,256]{1,0:T(8,128)(2,1)S(1)}, u32[]{:S(2)}, u32[]{:S(2)}) %collective-permute-start.2) | collective-permute-done | bytes 65568 | tf_op jit(solution)/shard_map/ppermute | solution.py:1060
  13.9 0.5 collective-permute-start.6
  14.4 0.1 select_bitcast_fusion.5
  14.5 0.1 pad_maximum_fusion.6.w_qkv.rest_0_
  14.5 0.1 select_bitcast_fusion.1
  14.6 0.1 pad_maximum_fusion.1.w_down.rest_3_
  14.7 0.1 select_bitcast_fusion.3
  14.8 0.1 pad_maximum_fusion.w_up.rest_2_
  14.9 0.2 collective-permute-done.5.far2
  15.1 0.2 collective-permute-done.6.far3
  15.3 2.2 %shard_map.153 = (bf16[640,256]{1,0:T(8,128)(2,1)}, f32[576,256]{1,0:T(8,128)S(1)}, f32[576,128]{1,0:T(8,128)S(1)}, bf16[576,256]{1,0:T(8,128)(2,1)S(1)}, bf16[2...) custom-call(f32[256,192]{1,0:T(8,128)S(1)} %get-tuple-element.65.mas, ...), custom_call_target="tpu_custom_call" | custom-call | flops 1100000000 | bytes 3400000 | tf_op jit(solution)/shard_map/pallas_call | solution.py:317
  17.5 3.5 %shard_map.154 = (bf16[256,256]{1,0:T(8,128)(2,1)S(1)}, bf16[256,256]{1,0:T(8,128)(2,1)S(1)}, bf16[4,400,256]{2,1,0:T(8,128)(2,1)S(1)}, bf16[4,400,256]{2,1,0:T(8,128)(2,1)S(1)}) custom-call(f32[256,256]{1,0:T(8,128)S(1)} %get-tuple-element.64.mask, bf16[256,256]{1,0:T(8,128)(2,1)S(1)} %get-tuple-element.75.hidden_ref.rest_6_, ...), custom_call_target="tpu_custom_call" | custom-call | flops 4400000000 | bytes 13600000 | tf_op jit(solution)/shard_map/pallas_call | solution.py:317
  21.0 0.4 collective-permute-start.16
  21.4 2.7 %shard_map.155 = (bf16[256,256]{1,0:T(8,128)(2,1)S(1)}, f32[640,256]{1,0:T(8,128)S(1)}, bf16[832,256]{1,0:T(8,128)(2,1)S(1)}, bf16[4,400,256]{2,1,0:T(8,128)(2,1)S(1)}, bf16[4,400,256]{2,1,0:T(8,128)(2,1)S(1)}) custom-call(bf16[256,256]{1,0:T(8,128)(2,1)S(1)} %get-tuple-element.77.grad_ref.one_near, ...), custom_call_target="tpu_custom_call" | custom-call | flops 4400000000 | bytes 13600000 | tf_op jit(solution)/shard_map/pallas_call | solution.py:317
  24.1 0.3 collective-permute-start.12
  24.4 0.3 collective-permute-start.11
  24.7 1.6 %collective-permute-start.17 = (bf16[2,400,256]{2,1,0:T(8,128)(2,1)S(1)}, bf16[2,400,256]{2,1,0:T(8,128)(2,1)S(1)}, u32[]{:S(2)}, u32[]{:S(2)}) collective-permute-start(bf16[2,400,256]{2,1,0:T(8,128)(2,1)S(1)} %slice_add_fusion), channel_id=1, source_target_pairs={{0,1},{1,0},{2,3},{3,2},{16,18},{17,19},{18,16},{19,17},{4,5},{5,4... | collective-permute-start | bytes 1228808 | tf_op jit(solution)/shard_map/ppermute | solution.py:1065
  26.3 0.2 collective-permute-done.12
  26.6 1.6 %collective-permute-start.13 = (bf16[2,400,256]{2,1,0:T(8,128)(2,1)S(1)}, bf16[2,400,256]{2,1,0:T(8,128)(2,1)S(1)}, u32[]{:S(2)}, u32[]{:S(2)}) collective-permute-start(bf16[2,400,256]{2,1,0:T(8,128)(2,1)S(1)} %slice_add_fusion.1), channel_id=1, source_target_pairs={{0,1},{1,0},{2,3},{3,2},{16,18},{17,19},{18,16},{19,17},{4,5},{5,4... | collective-permute-start | bytes 1228808 | tf_op jit(solution)/shard_map/ppermute | solution.py:1065
  28.1 0.1 shard_map.156
  28.2 2.6 %collective-permute-start.19 = (bf16[256,256]{1,0:T(8,128)(2,1)S(1)}, bf16[256,256]{1,0:T(8,128)(2,1)S(1)}, u32[]{:S(2)}, u32[]{:S(2)}) collective-permute-start(bf16[256,256]{1,0:T(8,128)(2,1)S(1)} %get-tuple-element.101), channel_id=1, source_target_pairs={{0,12},{4,8},{8,4},{12,0},{1,13},{5,9},{9,5},{13,1},{2,14},{6,10},... | collective-permute-start | bytes 393224 | tf_op jit(solution)/shard_map/ppermute | solution.py:1060
  30.8 0.1 collective-permute-start.21
  30.9 1.7 %collective-permute-start.15 = (bf16[256,256]{1,0:T(8,128)(2,1)S(1)}, bf16[256,256]{1,0:T(8,128)(2,1)S(1)}, u32[]{:S(2)}, u32[]{:S(2)}) collective-permute-start(bf16[256,256]{1,0:T(8,128)(2,1)S(1)} %get-tuple-element.97), channel_id=1, source_target_pairs={{0,4},{4,0},{8,12},{12,8},{1,5},{5,1},{9,13},{13,9},{2,6},{6,2},{1... | collective-permute-start | bytes 393224 | tf_op jit(solution)/shard_map/ppermute | solution.py:1060
  32.7 0.1 collective-permute-done.17
  32.8 1.6 %collective-permute-start.18 = (bf16[400,256]{1,0:T(8,128)(2,1)S(1)}, bf16[400,256]{1,0:T(8,128)(2,1)S(1)}, u32[]{:S(2)}, u32[]{:S(2)}) collective-permute-start(bf16[400,256]{1,0:T(8,128)(2,1)S(1)} %fusion), channel_id=1, source_target_pairs={{0,2},{1,3},{2,0},{3,1},{16,17},{17,16},{18,19},{19,18},{4,6},{5,7... | collective-permute-start | bytes 614408 | tf_op jit(solution)/shard_map/ppermute | solution.py:1066
  34.4 5.0 %collective-permute-done.13 = bf16[2,400,256]{2,1,0:T(8,128)(2,1)S(1)} collective-permute-done((bf16[2,400,256]{2,1,0:T(8,128)(2,1)S(1)}, bf16[2,400,256]{2,1,0:T(8,128)(2,1)S(1)}, u32[]{:S(2)}, u32[]{:S(2)}) %collective-permute-start.13) | collective-permute-done | bytes 409632 | tf_op jit(solution)/shard_map/ppermute | solution.py:1065
  39.5 1.6 %collective-permute-start.14 = (bf16[400,256]{1,0:T(8,128)(2,1)S(1)}, bf16[400,256]{1,0:T(8,128)(2,1)S(1)}, u32[]{:S(2)}, u32[]{:S(2)}) collective-permute-start(bf16[400,256]{1,0:T(8,128)(2,1)S(1)} %fusion.3), channel_id=1, source_target_pairs={{0,2},{1,3},{2,0},{3,1},{16,17},{17,16},{18,19},{19,18},{4,6},{5,7... | collective-permute-start | bytes 614408 | tf_op jit(solution)/shard_map/ppermute | solution.py:1066
  41.1 2.2 %collective-permute-start.20 = (bf16[400,256]{1,0:T(8,128)(2,1)S(1)}, bf16[400,256]{1,0:T(8,128)(2,1)S(1)}, u32[]{:S(2)}, u32[]{:S(2)}) collective-permute-start(bf16[400,256]{1,0:T(8,128)(2,1)S(1)} %fusion.2), channel_id=1, source_target_pairs={{0,8},{4,12},{8,0},{12,4},{1,9},{5,13},{9,1},{13,5},{2,10},{6,14},... | collective-permute-start | bytes 614408 | tf_op jit(solution)/shard_map/ppermute | solution.py:1060
  43.3 2.0 %collective-permute-done.14 = bf16[400,256]{1,0:T(8,128)(2,1)S(1)} collective-permute-done((bf16[400,256]{1,0:T(8,128)(2,1)S(1)}, bf16[400,256]{1,0:T(8,128)(2,1)S(1)}, u32[]{:S(2)}, u32[]{:S(2)}) %collective-permute-start.14) | collective-permute-done | bytes 204832 | tf_op jit(solution)/shard_map/ppermute | solution.py:1066
  45.3 1.3 %collective-permute-start.22 = (bf16[400,256]{1,0:T(8,128)(2,1)S(1)}, bf16[400,256]{1,0:T(8,128)(2,1)S(1)}, u32[]{:S(2)}, u32[]{:S(2)}) collective-permute-start(bf16[400,256]{1,0:T(8,128)(2,1)S(1)} %fusion.5), channel_id=1, source_target_pairs={{0,4},{4,0},{8,12},{12,8},{1,5},{5,1},{9,13},{13,9},{2,6},{6,2},{1... | collective-permute-start | bytes 614408 | tf_op jit(solution)/shard_map/ppermute | solution.py:1060
  46.6 5.2 %collective-permute-done.20 = bf16[400,256]{1,0:T(8,128)(2,1)S(1)} collective-permute-done((bf16[400,256]{1,0:T(8,128)(2,1)S(1)}, bf16[400,256]{1,0:T(8,128)(2,1)S(1)}, u32[]{:S(2)}, u32[]{:S(2)}) %collective-permute-start.20) | collective-permute-done | bytes 204832 | tf_op jit(solution)/shard_map/ppermute | solution.py:1060
  51.9 0.1 add.80
  51.9 0.1 collective-permute-start.26
  52.0 1.1 %collective-permute-done.22 = bf16[400,256]{1,0:T(8,128)(2,1)S(1)} collective-permute-done((bf16[400,256]{1,0:T(8,128)(2,1)S(1)}, bf16[400,256]{1,0:T(8,128)(2,1)S(1)}, u32[]{:S(2)}, u32[]{:S(2)}) %collective-permute-start.22) | collective-permute-done | bytes 204832 | tf_op jit(solution)/shard_map/ppermute | solution.py:1060
  53.1 2.1 %collective-permute-start.23 = (bf16[400,256]{1,0:T(8,128)(2,1)S(1)}, bf16[400,256]{1,0:T(8,128)(2,1)S(1)}, u32[]{:S(2)}, u32[]{:S(2)}) collective-permute-start(bf16[400,256]{1,0:T(8,128)(2,1)S(1)} %add.81), channel_id=1, source_target_pairs={{0,8},{4,12},{8,0},{12,4},{1,9},{5,13},{9,1},{13,5},{2,10},{6,14},... | collective-permute-start | bytes 614408 | tf_op jit(solution)/shard_map/ppermute | solution.py:1060
  55.2 6.7 %collective-permute-done.26 = bf16[400,256]{1,0:T(8,128)(2,1)S(1)} collective-permute-done((bf16[400,256]{1,0:T(8,128)(2,1)S(1)}, bf16[400,256]{1,0:T(8,128)(2,1)S(1)}, u32[]{:S(2)}, u32[]{:S(2)}) %collective-permute-start.26) | collective-permute-done | bytes 204832 | tf_op jit(solution)/shard_map/ppermute | solution.py:1060
  61.9 1.3 %collective-permute-start.27 = (bf16[400,256]{1,0:T(8,128)(2,1)S(1)}, bf16[400,256]{1,0:T(8,128)(2,1)S(1)}, u32[]{:S(2)}, u32[]{:S(2)}) collective-permute-start(bf16[400,256]{1,0:T(8,128)(2,1)S(1)} %add.83), channel_id=1, source_target_pairs={{0,2},{1,3},{2,0},{3,1},{16,17},{17,16},{18,19},{19,18},{4,6},{5,7... | collective-permute-start | bytes 614408 | tf_op jit(solution)/shard_map/ppermute | solution.py:1073
  63.3 0.9 %collective-permute-done.23 = bf16[400,256]{1,0:T(8,128)(2,1)S(1)} collective-permute-done((bf16[400,256]{1,0:T(8,128)(2,1)S(1)}, bf16[400,256]{1,0:T(8,128)(2,1)S(1)}, u32[]{:S(2)}, u32[]{:S(2)}) %collective-permute-start.23) | collective-permute-done | bytes 204832 | tf_op jit(solution)/shard_map/ppermute | solution.py:1060
  64.2 0.1 add.82
  64.3 1.9 %collective-permute-start.24 = (bf16[400,256]{1,0:T(8,128)(2,1)S(1)}, bf16[400,256]{1,0:T(8,128)(2,1)S(1)}, u32[]{:S(2)}, u32[]{:S(2)}) collective-permute-start(bf16[400,256]{1,0:T(8,128)(2,1)S(1)} %add.82), channel_id=1, source_target_pairs={{0,2},{1,3},{2,0},{3,1},{16,17},{17,16},{18,19},{19,18},{4,6},{5,7... | collective-permute-start | bytes 614408 | tf_op jit(solution)/shard_map/ppermute | solution.py:1073
  66.2 1.7 %collective-permute-done.27 = bf16[400,256]{1,0:T(8,128)(2,1)S(1)} collective-permute-done((bf16[400,256]{1,0:T(8,128)(2,1)S(1)}, bf16[400,256]{1,0:T(8,128)(2,1)S(1)}, u32[]{:S(2)}, u32[]{:S(2)}) %collective-permute-start.27) | collective-permute-done | bytes 204832 | tf_op jit(solution)/shard_map/ppermute | solution.py:1073
  67.9 1.5 %collective-permute-start.28 = (bf16[2,400,256]{2,1,0:T(8,128)(2,1)S(1)}, bf16[2,400,256]{2,1,0:T(8,128)(2,1)S(1)}, u32[]{:S(2)}, u32[]{:S(2)}) collective-permute-start(bf16[2,400,256]{2,1,0:T(8,128)(2,1)S(1)} %pad_maximum_fusion.8), channel_id=1, source_target_pairs={{0,1},{1,0},{2,3},{3,2},{16,18},{17,19},{18,16},{19,17},{4,5},{5,4... | collective-permute-start | bytes 1228808 | tf_op jit(solution)/shard_map/ppermute | solution.py:1074
  69.4 2.9 %collective-permute-done.24 = bf16[400,256]{1,0:T(8,128)(2,1)S(1)} collective-permute-done((bf16[400,256]{1,0:T(8,128)(2,1)S(1)}, bf16[400,256]{1,0:T(8,128)(2,1)S(1)}, u32[]{:S(2)}, u32[]{:S(2)}) %collective-permute-start.24) | collective-permute-done | bytes 204832 | tf_op jit(solution)/shard_map/ppermute | solution.py:1073
  72.3 1.5 %collective-permute-start.25 = (bf16[2,400,256]{2,1,0:T(8,128)(2,1)S(1)}, bf16[2,400,256]{2,1,0:T(8,128)(2,1)S(1)}, u32[]{:S(2)}, u32[]{:S(2)}) collective-permute-start(bf16[2,400,256]{2,1,0:T(8,128)(2,1)S(1)} %pad_maximum_fusion.7), channel_id=1, source_target_pairs={{0,1},{1,0},{2,3},{3,2},{16,18},{17,19},{18,16},{19,17},{4,5},{5,4... | collective-permute-start | bytes 1228808 | tf_op jit(solution)/shard_map/ppermute | solution.py:1074
  73.9 2.0 %collective-permute-done.28 = bf16[2,400,256]{2,1,0:T(8,128)(2,1)S(1)} collective-permute-done((bf16[2,400,256]{2,1,0:T(8,128)(2,1)S(1)}, bf16[2,400,256]{2,1,0:T(8,128)(2,1)S(1)}, u32[]{:S(2)}, u32[]{:S(2)}) %collective-permute-start.28) | collective-permute-done | bytes 409632 | tf_op jit(solution)/shard_map/ppermute | solution.py:1074
  75.9 0.8 shard_map.157
  76.8 0.5 collective-permute-start.29
  77.3 3.1 %collective-permute-done.25 = bf16[2,400,256]{2,1,0:T(8,128)(2,1)S(1)} collective-permute-done((bf16[2,400,256]{2,1,0:T(8,128)(2,1)S(1)}, bf16[2,400,256]{2,1,0:T(8,128)(2,1)S(1)}, u32[]{:S(2)}, u32[]{:S(2)}) %collective-permute-start.25) | collective-permute-done | bytes 409632 | tf_op jit(solution)/shard_map/ppermute | solution.py:1074
  80.4 0.1 pad_maximum_fusion.3.one
  80.5 0.1 pad_maximum_fusion.2.zero
  80.5 1.8 %shard_map.158 = (f32[1,256]{1,0:T(1,128)}, f32[1,256,768]{2,1,0:T(8,128)}, f32[1,256,256]{2,1,0:T(8,128)}, f32[1,256]{1,0:T(1,128)}, f32[1,256,1024]{2,1,0:T(8,128)}, /*index=5*/f32[1,1024,256]{2,1,0:T(8,128)}) custom-call(bf16[4,400,256]{2,1,0:T(8,128)(2,1)S(1)} %pad_maximum_fusion.2.zero, bf16[4,400,256]{2,1,0:T(8,128)(2,1)S(1)} %pad_maximum_fusion.3.one), custom_call_target="tpu_custom_call" | custom-call | flops 1100000000 | bytes 3400000 | tf_op jit(solution)/shard_map/pallas_call | solution.py:317
  82.4 0.1 pad_maximum_fusion.5.one
  82.5 0.1 pad_maximum_fusion.4.zero
  82.5 1.2 %shard_map.159 = (f32[1,256,768]{2,1,0:T(8,128)}, f32[1,256,256]{2,1,0:T(8,128)}, f32[1,256,1024]{2,1,0:T(8,128)}, f32[1,1024,256]{2,1,0:T(8,128)}) custom-call(f32[1,256,768]{2,1,0:T(8,128)} %get-tuple-element.111.qkv_in, f32[1,256,256]{2,1,0:T(8,128)} %get-tuple-element.112.out_in, ...), custom_call_target="tpu_custom_call", output_to_operand_aliasing={{0}: (0, {}), {1}: (1, {}), {2}: (2, {}), {3}: (3, {})} | custom-call | flops 1100000000 | bytes 3400000 | tf_op jit(solution)/shard_map/pallas_call | solution.py:317
  (44 shorter events, 0.6 us)
Async XLA Ops:
  0.6 7.7 %copy-start.2 = (bf16[1,256,768]{2,1,0:T(8,128)(2,1)S(1)}, bf16[1,256,768]{2,1,0:T(8,128)(2,1)}, u32[]{:S(2)}) copy-start(bf16[1,256,768]{2,1,0:T(8,128)(2,1)} %param.13) | copy-start | bytes 1179652
  0.6 7.2 %copy-start.3 = (bf16[1,256,256]{2,1,0:T(8,128)(2,1)S(1)}, bf16[1,256,256]{2,1,0:T(8,128)(2,1)}, u32[]{:S(2)}) copy-start(bf16[1,256,256]{2,1,0:T(8,128)(2,1)} %param.14) | copy-start | bytes 393220
  0.7 9.3 %copy-start.1 = (bf16[1,256,1024]{2,1,0:T(8,128)(2,1)S(1)}, bf16[1,256,1024]{2,1,0:T(8,128)(2,1)}, u32[]{:S(2)}) copy-start(bf16[1,256,1024]{2,1,0:T(8,128)(2,1)} %param.16) | copy-start | bytes 1572868
  0.7 7.2 %copy-start = (bf16[1,1024,256]{2,1,0:T(8,128)(2,1)S(1)}, bf16[1,1024,256]{2,1,0:T(8,128)(2,1)}, u32[]{:S(2)}) copy-start(bf16[1,1024,256]{2,1,0:T(8,128)(2,1)} %param.17) | copy-start | bytes 1572868
  2.0 6.4 %collective-permute-start.3 = (bf16[144,256]{1,0:T(8,128)(2,1)S(1)}, bf16[144,256]{1,0:T(8,128)(2,1)S(1)}, u32[]{:S(2)}, u32[]{:S(2)}) collective-permute-start(bf16[144,256]{1,0:T(8,128)(2,1)S(1)} %get-tuple-element.66.own0), channel_id=1, source_target_pairs={{0,16},{16,0},{1,17},{17,1},{2,18},{18,2},{3,19},{19,3},{4,20},{20... | collective-permute-start | bytes 221192 | tf_op jit(solution)/shard_map/ppermute | solution.py:1116
  2.5 5.3 %collective-permute-start = (bf16[128,256]{1,0:T(8,128)(2,1)S(1)}, bf16[128,256]{1,0:T(8,128)(2,1)S(1)}, u32[]{:S(2)}, u32[]{:S(2)}) collective-permute-start(bf16[128,256]{1,0:T(8,128)(2,1)S(1)} %get-tuple-element.67), channel_id=1, source_target_pairs={{0,4},{4,0},{8,12},{12,8},{1,5},{5,1},{9,13},{13,9},{2,6},{6,2},{1... | collective-permute-start | bytes 196616 | tf_op jit(solution)/shard_map/ppermute | solution.py:1060
  5.2 7.7 %collective-permute-start.1 = (bf16[128,256]{1,0:T(8,128)(2,1)S(1)}, bf16[128,256]{1,0:T(8,128)(2,1)S(1)}, u32[]{:S(2)}, u32[]{:S(2)}) collective-permute-start(bf16[128,256]{1,0:T(8,128)(2,1)S(1)} %get-tuple-element.69), channel_id=1, source_target_pairs={{0,8},{4,12},{8,0},{12,4},{1,9},{5,13},{9,1},{13,5},{2,10},{6,14},... | collective-permute-start | bytes 196616 | tf_op jit(solution)/shard_map/ppermute | solution.py:1060
  7.8 6.1 %collective-permute-start.2 = (bf16[128,256]{1,0:T(8,128)(2,1)S(1)}, bf16[128,256]{1,0:T(8,128)(2,1)S(1)}, u32[]{:S(2)}, u32[]{:S(2)}) collective-permute-start(bf16[128,256]{1,0:T(8,128)(2,1)S(1)} %get-tuple-element.70), channel_id=1, source_target_pairs={{0,12},{4,8},{8,4},{12,0},{1,13},{5,9},{9,5},{13,1},{2,14},{6,10},... | collective-permute-start | bytes 196616 | tf_op jit(solution)/shard_map/ppermute | solution.py:1060
  7.9 6.7 %collective-permute-start.10 = (bf16[1024,256]{1,0:T(8,128)(2,1)S(1)}, bf16[1024,256]{1,0:T(8,128)(2,1)S(1)}, u32[]{:S(2)}, u32[]{:S(2)}) collective-permute-start(bf16[1024,256]{1,0:T(8,128)(2,1)S(1)} %bitcast.48), channel_id=1, source_target_pairs={{0,16},{16,0},{1,17},{17,1},{2,18},{18,2},{3,19},{19,3},{4,20},{20... | collective-permute-start | bytes 1572872 | tf_op jit(solution)/shard_map/ppermute | solution.py:1119
  7.9 2.1 %collective-permute-start.8 = (bf16[256,256]{1,0:T(8,128)(2,1)S(1)}, bf16[256,256]{1,0:T(8,128)(2,1)S(1)}, u32[]{:S(2)}, u32[]{:S(2)}) collective-permute-start(bf16[256,256]{1,0:T(8,128)(2,1)S(1)} %bitcast.54), channel_id=1, source_target_pairs={{0,16},{16,0},{1,17},{17,1},{2,18},{18,2},{3,19},{19,3},{4,20},{20... | collective-permute-start | bytes 393224 | tf_op jit(solution)/shard_map/ppermute | solution.py:1119
  8.4 5.5 %collective-permute-start.7 = (bf16[256,768]{1,0:T(8,128)(2,1)S(1)}, bf16[256,768]{1,0:T(8,128)(2,1)S(1)}, u32[]{:S(2)}, u32[]{:S(2)}) collective-permute-start(bf16[256,768]{1,0:T(8,128)(2,1)S(1)} %bitcast.52), channel_id=1, source_target_pairs={{0,16},{16,0},{1,17},{17,1},{2,18},{18,2},{3,19},{19,3},{4,20},{20... | collective-permute-start | bytes 1179656 | tf_op jit(solution)/shard_map/ppermute | solution.py:1119
  10.0 4.8 %collective-permute-start.9 = (bf16[256,1024]{1,0:T(8,128)(2,1)S(1)}, bf16[256,1024]{1,0:T(8,128)(2,1)S(1)}, u32[]{:S(2)}, u32[]{:S(2)}) collective-permute-start(bf16[256,1024]{1,0:T(8,128)(2,1)S(1)} %bitcast.50), channel_id=1, source_target_pairs={{0,16},{16,0},{1,17},{17,1},{2,18},{18,2},{3,19},{19,3},{4,20},{20... | collective-permute-start | bytes 1572872 | tf_op jit(solution)/shard_map/ppermute | solution.py:1119
  12.9 2.1 %collective-permute-start.4 = (bf16[128,256]{1,0:T(8,128)(2,1)S(1)}, bf16[128,256]{1,0:T(8,128)(2,1)S(1)}, u32[]{:S(2)}, u32[]{:S(2)}) collective-permute-start(bf16[128,256]{1,0:T(8,128)(2,1)S(1)} %collective-permute-done.own1), channel_id=1, source_target_pairs={{0,16},{16,0},{1,17},{17,1},{2,18},{18,2},{3,19},{19,3},{4,20},{20... | collective-permute-start | bytes 196616 | tf_op jit(solution)/shard_map/ppermute | solution.py:1116
  13.9 1.3 %collective-permute-start.5 = (bf16[128,256]{1,0:T(8,128)(2,1)S(1)}, bf16[128,256]{1,0:T(8,128)(2,1)S(1)}, u32[]{:S(2)}, u32[]{:S(2)}) collective-permute-start(bf16[128,256]{1,0:T(8,128)(2,1)S(1)} %collective-permute-done.1.own2), channel_id=1, source_target_pairs={{0,16},{16,0},{1,17},{17,1},{2,18},{18,2},{3,19},{19,3},{4,20},{20... | collective-permute-start | bytes 196616 | tf_op jit(solution)/shard_map/ppermute | solution.py:1116
  13.9 1.4 %collective-permute-start.6 = (bf16[128,256]{1,0:T(8,128)(2,1)S(1)}, bf16[128,256]{1,0:T(8,128)(2,1)S(1)}, u32[]{:S(2)}, u32[]{:S(2)}) collective-permute-start(bf16[128,256]{1,0:T(8,128)(2,1)S(1)} %collective-permute-done.2.own3), channel_id=1, source_target_pairs={{0,16},{16,0},{1,17},{17,1},{2,18},{18,2},{3,19},{19,3},{4,20},{20... | collective-permute-start | bytes 196616 | tf_op jit(solution)/shard_map/ppermute | solution.py:1116
  21.0 3.7 %collective-permute-start.16 = (bf16[4,400,256]{2,1,0:T(8,128)(2,1)S(1)}, bf16[4,400,256]{2,1,0:T(8,128)(2,1)S(1)}, u32[]{:S(2)}, u32[]{:S(2)}) collective-permute-start(bf16[4,400,256]{2,1,0:T(8,128)(2,1)S(1)} %get-tuple-element.100), channel_id=1, source_target_pairs={{0,16},{16,0},{1,17},{17,1},{2,18},{18,2},{3,19},{19,3},{4,20},{20... | collective-permute-start | bytes 2457608 | tf_op jit(solution)/shard_map/ppermute | solution.py:1189
  24.1 2.4 %collective-permute-start.12 = (bf16[4,400,256]{2,1,0:T(8,128)(2,1)S(1)}, bf16[4,400,256]{2,1,0:T(8,128)(2,1)S(1)}, u32[]{:S(2)}, u32[]{:S(2)}) collective-permute-start(bf16[4,400,256]{2,1,0:T(8,128)(2,1)S(1)} %get-tuple-element.96), channel_id=1, source_target_pairs={{0,16},{16,0},{1,17},{17,1},{2,18},{18,2},{3,19},{19,3},{4,20},{20... | collective-permute-start | bytes 2457608 | tf_op jit(solution)/shard_map/ppermute | solution.py:1235
  24.4 3.8 %collective-permute-start.11 = (bf16[832,256]{1,0:T(8,128)(2,1)S(1)}, bf16[832,256]{1,0:T(8,128)(2,1)S(1)}, u32[]{:S(2)}, u32[]{:S(2)}) collective-permute-start(bf16[832,256]{1,0:T(8,128)(2,1)S(1)} %get-tuple-element.93), channel_id=1, source_target_pairs={{0,16},{16,0},{1,17},{17,1},{2,18},{18,2},{3,19},{19,3},{4,20},{20... | collective-permute-start | bytes 1277960 | tf_op jit(solution)/shard_map/ppermute | solution.py:1226
  24.7 8.0 %collective-permute-start.17 = (bf16[2,400,256]{2,1,0:T(8,128)(2,1)S(1)}, bf16[2,400,256]{2,1,0:T(8,128)(2,1)S(1)}, u32[]{:S(2)}, u32[]{:S(2)}) collective-permute-start(bf16[2,400,256]{2,1,0:T(8,128)(2,1)S(1)} %slice_add_fusion), channel_id=1, source_target_pairs={{0,1},{1,0},{2,3},{3,2},{16,18},{17,19},{18,16},{19,17},{4,5},{5,4... | collective-permute-start | bytes 1228808 | tf_op jit(solution)/shard_map/ppermute | solution.py:1065
  26.6 12.9 %collective-permute-start.13 = (bf16[2,400,256]{2,1,0:T(8,128)(2,1)S(1)}, bf16[2,400,256]{2,1,0:T(8,128)(2,1)S(1)}, u32[]{:S(2)}, u32[]{:S(2)}) collective-permute-start(bf16[2,400,256]{2,1,0:T(8,128)(2,1)S(1)} %slice_add_fusion.1), channel_id=1, source_target_pairs={{0,1},{1,0},{2,3},{3,2},{16,18},{17,19},{18,16},{19,17},{4,5},{5,4... | collective-permute-start | bytes 1228808 | tf_op jit(solution)/shard_map/ppermute | solution.py:1065
  28.2 12.9 %collective-permute-start.19 = (bf16[256,256]{1,0:T(8,128)(2,1)S(1)}, bf16[256,256]{1,0:T(8,128)(2,1)S(1)}, u32[]{:S(2)}, u32[]{:S(2)}) collective-permute-start(bf16[256,256]{1,0:T(8,128)(2,1)S(1)} %get-tuple-element.101), channel_id=1, source_target_pairs={{0,12},{4,8},{8,4},{12,0},{1,13},{5,9},{9,5},{13,1},{2,14},{6,10},... | collective-permute-start | bytes 393224 | tf_op jit(solution)/shard_map/ppermute | solution.py:1060
  30.8 21.1 %collective-permute-start.21 = (bf16[256,256]{1,0:T(8,128)(2,1)S(1)}, bf16[256,256]{1,0:T(8,128)(2,1)S(1)}, u32[]{:S(2)}, u32[]{:S(2)}) collective-permute-start(bf16[256,256]{1,0:T(8,128)(2,1)S(1)} %get-tuple-element.103), channel_id=1, source_target_pairs={{0,8},{4,12},{8,0},{12,4},{1,9},{5,13},{9,1},{13,5},{2,10},{6,14},... | collective-permute-start | bytes 393224 | tf_op jit(solution)/shard_map/ppermute | solution.py:1060
  30.9 14.4 %collective-permute-start.15 = (bf16[256,256]{1,0:T(8,128)(2,1)S(1)}, bf16[256,256]{1,0:T(8,128)(2,1)S(1)}, u32[]{:S(2)}, u32[]{:S(2)}) collective-permute-start(bf16[256,256]{1,0:T(8,128)(2,1)S(1)} %get-tuple-element.97), channel_id=1, source_target_pairs={{0,4},{4,0},{8,12},{12,8},{1,5},{5,1},{9,13},{13,9},{2,6},{6,2},{1... | collective-permute-start | bytes 393224 | tf_op jit(solution)/shard_map/ppermute | solution.py:1060
  32.8 8.3 %collective-permute-start.18 = (bf16[400,256]{1,0:T(8,128)(2,1)S(1)}, bf16[400,256]{1,0:T(8,128)(2,1)S(1)}, u32[]{:S(2)}, u32[]{:S(2)}) collective-permute-start(bf16[400,256]{1,0:T(8,128)(2,1)S(1)} %fusion), channel_id=1, source_target_pairs={{0,2},{1,3},{2,0},{3,1},{16,17},{17,16},{18,19},{19,18},{4,6},{5,7... | collective-permute-start | bytes 614408 | tf_op jit(solution)/shard_map/ppermute | solution.py:1066
  39.5 5.8 %collective-permute-start.14 = (bf16[400,256]{1,0:T(8,128)(2,1)S(1)}, bf16[400,256]{1,0:T(8,128)(2,1)S(1)}, u32[]{:S(2)}, u32[]{:S(2)}) collective-permute-start(bf16[400,256]{1,0:T(8,128)(2,1)S(1)} %fusion.3), channel_id=1, source_target_pairs={{0,2},{1,3},{2,0},{3,1},{16,17},{17,16},{18,19},{19,18},{4,6},{5,7... | collective-permute-start | bytes 614408 | tf_op jit(solution)/shard_map/ppermute | solution.py:1066
  41.1 10.7 %collective-permute-start.20 = (bf16[400,256]{1,0:T(8,128)(2,1)S(1)}, bf16[400,256]{1,0:T(8,128)(2,1)S(1)}, u32[]{:S(2)}, u32[]{:S(2)}) collective-permute-start(bf16[400,256]{1,0:T(8,128)(2,1)S(1)} %fusion.2), channel_id=1, source_target_pairs={{0,8},{4,12},{8,0},{12,4},{1,9},{5,13},{9,1},{13,5},{2,10},{6,14},... | collective-permute-start | bytes 614408 | tf_op jit(solution)/shard_map/ppermute | solution.py:1060
  45.3 7.7 %collective-permute-start.22 = (bf16[400,256]{1,0:T(8,128)(2,1)S(1)}, bf16[400,256]{1,0:T(8,128)(2,1)S(1)}, u32[]{:S(2)}, u32[]{:S(2)}) collective-permute-start(bf16[400,256]{1,0:T(8,128)(2,1)S(1)} %fusion.5), channel_id=1, source_target_pairs={{0,4},{4,0},{8,12},{12,8},{1,5},{5,1},{9,13},{13,9},{2,6},{6,2},{1... | collective-permute-start | bytes 614408 | tf_op jit(solution)/shard_map/ppermute | solution.py:1060
  51.9 10.0 %collective-permute-start.26 = (bf16[400,256]{1,0:T(8,128)(2,1)S(1)}, bf16[400,256]{1,0:T(8,128)(2,1)S(1)}, u32[]{:S(2)}, u32[]{:S(2)}) collective-permute-start(bf16[400,256]{1,0:T(8,128)(2,1)S(1)} %add.80), channel_id=1, source_target_pairs={{0,4},{4,0},{8,12},{12,8},{1,5},{5,1},{9,13},{13,9},{2,6},{6,2},{1... | collective-permute-start | bytes 614408 | tf_op jit(solution)/shard_map/ppermute | solution.py:1060
  53.1 11.1 %collective-permute-start.23 = (bf16[400,256]{1,0:T(8,128)(2,1)S(1)}, bf16[400,256]{1,0:T(8,128)(2,1)S(1)}, u32[]{:S(2)}, u32[]{:S(2)}) collective-permute-start(bf16[400,256]{1,0:T(8,128)(2,1)S(1)} %add.81), channel_id=1, source_target_pairs={{0,8},{4,12},{8,0},{12,4},{1,9},{5,13},{9,1},{13,5},{2,10},{6,14},... | collective-permute-start | bytes 614408 | tf_op jit(solution)/shard_map/ppermute | solution.py:1060
  61.9 5.9 %collective-permute-start.27 = (bf16[400,256]{1,0:T(8,128)(2,1)S(1)}, bf16[400,256]{1,0:T(8,128)(2,1)S(1)}, u32[]{:S(2)}, u32[]{:S(2)}) collective-permute-start(bf16[400,256]{1,0:T(8,128)(2,1)S(1)} %add.83), channel_id=1, source_target_pairs={{0,2},{1,3},{2,0},{3,1},{16,17},{17,16},{18,19},{19,18},{4,6},{5,7... | collective-permute-start | bytes 614408 | tf_op jit(solution)/shard_map/ppermute | solution.py:1073
  64.3 8.0 %collective-permute-start.24 = (bf16[400,256]{1,0:T(8,128)(2,1)S(1)}, bf16[400,256]{1,0:T(8,128)(2,1)S(1)}, u32[]{:S(2)}, u32[]{:S(2)}) collective-permute-start(bf16[400,256]{1,0:T(8,128)(2,1)S(1)} %add.82), channel_id=1, source_target_pairs={{0,2},{1,3},{2,0},{3,1},{16,17},{17,16},{18,19},{19,18},{4,6},{5,7... | collective-permute-start | bytes 614408 | tf_op jit(solution)/shard_map/ppermute | solution.py:1073
  67.9 8.0 %collective-permute-start.28 = (bf16[2,400,256]{2,1,0:T(8,128)(2,1)S(1)}, bf16[2,400,256]{2,1,0:T(8,128)(2,1)S(1)}, u32[]{:S(2)}, u32[]{:S(2)}) collective-permute-start(bf16[2,400,256]{2,1,0:T(8,128)(2,1)S(1)} %pad_maximum_fusion.8), channel_id=1, source_target_pairs={{0,1},{1,0},{2,3},{3,2},{16,18},{17,19},{18,16},{19,17},{4,5},{5,4... | collective-permute-start | bytes 1228808 | tf_op jit(solution)/shard_map/ppermute | solution.py:1074
  72.3 8.0 %collective-permute-start.25 = (bf16[2,400,256]{2,1,0:T(8,128)(2,1)S(1)}, bf16[2,400,256]{2,1,0:T(8,128)(2,1)S(1)}, u32[]{:S(2)}, u32[]{:S(2)}) collective-permute-start(bf16[2,400,256]{2,1,0:T(8,128)(2,1)S(1)} %pad_maximum_fusion.7), channel_id=1, source_target_pairs={{0,1},{1,0},{2,3},{3,2},{16,18},{17,19},{18,16},{19,17},{4,5},{5,4... | collective-permute-start | bytes 1228808 | tf_op jit(solution)/shard_map/ppermute | solution.py:1074
  73.9 8.5 %collective-permute-start.31 = (bf16[2,400,256]{2,1,0:T(8,128)(2,1)S(1)}, bf16[2,400,256]{2,1,0:T(8,128)(2,1)S(1)}, u32[]{:S(2)}, u32[]{:S(2)}) collective-permute-start(bf16[2,400,256]{2,1,0:T(8,128)(2,1)S(1)} %pad_maximum_fusion.8), channel_id=1, source_target_pairs={{0,16},{16,0},{1,17},{17,1},{2,18},{18,2},{3,19},{19,3},{4,20},{20... | collective-permute-start | bytes 1228808 | tf_op jit(solution)/shard_map/ppermute | solution.py:1248
  75.9 6.4 %collective-permute-start.32 = (bf16[2,400,256]{2,1,0:T(8,128)(2,1)S(1)}, bf16[2,400,256]{2,1,0:T(8,128)(2,1)S(1)}, u32[]{:S(2)}, u32[]{:S(2)}) collective-permute-start(bf16[2,400,256]{2,1,0:T(8,128)(2,1)S(1)} %collective-permute-done.28), channel_id=1, source_target_pairs={{0,16},{16,0},{1,17},{17,1},{2,18},{18,2},{3,19},{19,3},{4,20},{20... | collective-permute-start | bytes 1228808 | tf_op jit(solution)/shard_map/ppermute | solution.py:1248
  76.8 5.7 %collective-permute-start.29 = (bf16[2,400,256]{2,1,0:T(8,128)(2,1)S(1)}, bf16[2,400,256]{2,1,0:T(8,128)(2,1)S(1)}, u32[]{:S(2)}, u32[]{:S(2)}) collective-permute-start(bf16[2,400,256]{2,1,0:T(8,128)(2,1)S(1)} %pad_maximum_fusion.7), channel_id=1, source_target_pairs={{0,16},{16,0},{1,17},{17,1},{2,18},{18,2},{3,19},{19,3},{4,20},{20... | collective-permute-start | bytes 1228808 | tf_op jit(solution)/shard_map/ppermute | solution.py:1248
  80.4 2.1 %collective-permute-start.30 = (bf16[2,400,256]{2,1,0:T(8,128)(2,1)S(1)}, bf16[2,400,256]{2,1,0:T(8,128)(2,1)S(1)}, u32[]{:S(2)}, u32[]{:S(2)}) collective-permute-start(bf16[2,400,256]{2,1,0:T(8,128)(2,1)S(1)} %collective-permute-done.25), channel_id=1, source_target_pairs={{0,16},{16,0},{1,17},{17,1},{2,18},{18,2},{3,19},{19,3},{4,20},{20... | collective-permute-start | bytes 1228808 | tf_op jit(solution)/shard_map/ppermute | solution.py:1248

commit v7 on v6

--- a/solution.py
+++ b/solution.py
@@ -1025,15 +1025,20 @@
         pl.when(my_section() == core)(partial(body, core))
 
 
-def near_kernel(zero, one, gain_attn, qkv, out, gain_ffn, up, down, held, sems):
+def near_kernel(zero, one, gain_attn, qkv, out, gain_ffn, up, down, held, sems, gains, gain_sems):
     spare = zero.shape[1] - GAIN_ROWS
 
     def body(core):
         terms = (zero, one)[core]
-        gains = terms[0, spare:, :].astype(F32)
-        gain_attn[...] = gains[0:1, :]
-        gain_ffn[...] = gains[1:2, :]
+        sums = terms[0, spare:, :].astype(F32)
+        copies = []
+        for index, target in enumerate((gain_attn, gain_ffn)):
+            gains[index] = sums[index : index + 1, :]
+            copies.append(pltpu.make_async_copy(gains.at[index], target, gain_sems.at[index]))
+            copies[-1].start()
         write_half(core, terms, (qkv, out, up, down), held, sems)
+        for copy in copies:
+            copy.wait()
 
     by_section(body)
 
@@ -1262,8 +1267,8 @@
         (zero_near, one_near),
         (((1, width), F32), *sums[:2], ((1, width), F32), *sums[2:]),
         16,
-        scratch=held,
-        out_held=(1, 2, 4, 5),
+        scratch=(*held, pltpu.VMEM((2, 1, width), F32), pltpu.SemaphoreType.DMA((2,))),
+        out_held=(0, 1, 2, 3, 4, 5),
     )
     qkv_sum, out_sum, up_sum, down_sum = call(
         far_kernel,

time: 84 us -> 83.6 us (level)
  transfers between devices with their start and end apart: 33 -> 33, of which waited for: 18 -> 19; matrix products, arithmetic and copies ran while one was open for 2% -> 2% of each run, Pallas kernels for 6% -> 6%
where the time goes in v7:
time: 83.6 us; the launch traced here: 83.4 us
  waiting for transfers between devices  36.8 us (44%)
  starting transfers between devices  31.2 us (37%)
  Pallas kernels  13.1 us (16%)
  other arithmetic  1.39 us (2%)
  between operations  0.95 us (1%)
    ppermute x10, waiting for transfers between devices, along_line(): return lax.ppermute(value, 'dp', [(z, z ^ step) for z in range(4)])  17.7 us
    ppermute x10, starting transfers between devices, along_line(): return lax.ppermute(value, 'dp', [(z, z ^ step) for z in range(4)])  15.3 us
    pallas_call x8, Pallas kernels, call(): pl.pallas_call(body, out_shape=tuple((jax.ShapeDtypeStruct(*shape) for sh...  13.1 us
    ppermute x2, waiting for transfers between devices, reduce_terms(): first = lax.ppermute(keep[2:4] + came[2:4], PLANE, FIRST)  5.13 us
    ppermute x2, waiting for transfers between devices, reduce_terms(): return (pair, lax.ppermute(pair, PLANE, FIRST))  5.13 us
    ppermute x2, waiting for transfers between devices, reduce_terms(): pair = jnp.stack([total, lax.ppermute(total, PLANE, SECOND)])  4.62 us
    ppermute x2, starting transfers between devices, reduce_terms(): pair = jnp.stack([total, lax.ppermute(total, PLANE, SECOND)])  3.24 us
    ppermute x2, starting transfers between devices, reduce_terms(): second = lax.ppermute(keep[1] + came[1] + first[1], PLANE, SECOND)  3.22 us
  transfers between devices with their start and end apart: 33, of which 19 were waited for; matrix products, arithmetic and copies ran while one was open for 2% of the time, Pallas kernels for 6%

profile of v7, /device:TPU:0, one launch (start us, length us, event | category | flops | bytes accessed | tf_op | source)
XLA Modules:
  0.0 83.4 jit_solution(11283460200813114155)
XLA Ops:
  0.7 1.3 %shard_map.152 = (bf16[144,256]{1,0:T(8,128)(2,1)S(1)}, bf16[128,256]{1,0:T(8,128)(2,1)S(1)}, bf16[128,256]{1,0:T(8,128)(2,1)S(1)}, bf16[128,256]{1,0:T(8,128)(2...) custom-call(bf16[4,1,128,256]{3,2,1,0:T(8,128)(2,1)} %tokens.1, bf16[4,1,128,256]{3,2,1,0:T(8,128)(2,1)} %grads.1, ...), custom_call_target="tpu_custom_call" | custom-call | flops 1100000000 | bytes 3400000 | tf_op jit(solution)/shard_map/pallas_call | solution.py:317
  2.0 0.5 collective-permute-start.3
  2.5 2.6 %collective-permute-start = (bf16[128,256]{1,0:T(8,128)(2,1)S(1)}, bf16[128,256]{1,0:T(8,128)(2,1)S(1)}, u32[]{:S(2)}, u32[]{:S(2)}) collective-permute-start(bf16[128,256]{1,0:T(8,128)(2,1)S(1)} %get-tuple-element.67), channel_id=1, source_target_pairs={{0,4},{4,0},{8,12},{12,8},{1,5},{5,1},{9,13},{13,9},{2,6},{6,2},{1... | collective-permute-start | bytes 196616 | tf_op jit(solution)/shard_map/ppermute | solution.py:1065
  5.2 2.6 %collective-permute-start.1 = (bf16[128,256]{1,0:T(8,128)(2,1)S(1)}, bf16[128,256]{1,0:T(8,128)(2,1)S(1)}, u32[]{:S(2)}, u32[]{:S(2)}) collective-permute-start(bf16[128,256]{1,0:T(8,128)(2,1)S(1)} %get-tuple-element.69), channel_id=1, source_target_pairs={{0,8},{4,12},{8,0},{12,4},{1,9},{5,13},{9,1},{13,5},{2,10},{6,14},... | collective-permute-start | bytes 196616 | tf_op jit(solution)/shard_map/ppermute | solution.py:1065
  7.8 0.1 collective-permute-done.own1
  7.9 0.5 collective-permute-start.8
  8.4 0.1 collective-permute-start.7
  8.5 1.5 %collective-permute-done.8 = bf16[256,256]{1,0:T(8,128)(2,1)S(1)} collective-permute-done((bf16[256,256]{1,0:T(8,128)(2,1)S(1)}, bf16[256,256]{1,0:T(8,128)(2,1)S(1)}, u32[]{:S(2)}, u32[]{:S(2)}) %collective-permute-start.8) | collective-permute-done | bytes 131104 | tf_op jit(solution)/shard_map/ppermute | solution.py:1124
  10.0 0.1 collective-permute-start.9
  10.2 2.7 %collective-permute-done.1.own2 = bf16[128,256]{1,0:T(8,128)(2,1)S(1)} collective-permute-done((bf16[128,256]{1,0:T(8,128)(2,1)S(1)}, bf16[128,256]{1,0:T(8,128)(2,1)S(1)}, u32[]{:S(2)}, u32[]{:S(2)}) %collective-permute-start.1) | collective-permute-done | bytes 65568 | tf_op jit(solution)/shard_map/ppermute | solution.py:1065
  12.9 1.0 %collective-permute-done.2.own3 = bf16[128,256]{1,0:T(8,128)(2,1)S(1)} collective-permute-done((bf16[128,256]{1,0:T(8,128)(2,1)S(1)}, bf16[128,256]{1,0:T(8,128)(2,1)S(1)}, u32[]{:S(2)}, u32[]{:S(2)}) %collective-permute-start.2) | collective-permute-done | bytes 65568 | tf_op jit(solution)/shard_map/ppermute | solution.py:1065
  13.9 0.5 collective-permute-start.6
  14.4 0.1 select_bitcast_fusion.5
  14.5 0.1 pad_maximum_fusion.6.w_qkv.rest_0_
  14.5 0.1 select_bitcast_fusion.1
  14.6 0.1 pad_maximum_fusion.1.w_down.rest_3_
  14.7 0.1 select_bitcast_fusion.3
  14.8 0.1 pad_maximum_fusion.w_up.rest_2_
  14.9 0.2 collective-permute-done.5.far2
  15.1 0.2 collective-permute-done.6.far3
  15.3 2.2 %shard_map.153 = (bf16[640,256]{1,0:T(8,128)(2,1)}, f32[576,256]{1,0:T(8,128)S(1)}, f32[576,128]{1,0:T(8,128)S(1)}, bf16[576,256]{1,0:T(8,128)(2,1)S(1)}, bf16[2...) custom-call(f32[256,192]{1,0:T(8,128)S(1)} %get-tuple-element.65.mas, ...), custom_call_target="tpu_custom_call" | custom-call | flops 1100000000 | bytes 3400000 | tf_op jit(solution)/shard_map/pallas_call | solution.py:317
  17.5 3.5 %shard_map.154 = (bf16[256,256]{1,0:T(8,128)(2,1)S(1)}, bf16[256,256]{1,0:T(8,128)(2,1)S(1)}, bf16[4,400,256]{2,1,0:T(8,128)(2,1)S(1)}, bf16[4,400,256]{2,1,0:T(8,128)(2,1)S(1)}) custom-call(f32[256,256]{1,0:T(8,128)S(1)} %get-tuple-element.64.mask, bf16[256,256]{1,0:T(8,128)(2,1)S(1)} %get-tuple-element.75.hidden_ref.rest_6_, ...), custom_call_target="tpu_custom_call" | custom-call | flops 4400000000 | bytes 13600000 | tf_op jit(solution)/shard_map/pallas_call | solution.py:317
  21.0 0.4 collective-permute-start.16
  21.4 2.7 %shard_map.155 = (bf16[256,256]{1,0:T(8,128)(2,1)S(1)}, f32[640,256]{1,0:T(8,128)S(1)}, bf16[832,256]{1,0:T(8,128)(2,1)S(1)}, bf16[4,400,256]{2,1,0:T(8,128)(2,1)S(1)}, bf16[4,400,256]{2,1,0:T(8,128)(2,1)S(1)}) custom-call(bf16[256,256]{1,0:T(8,128)(2,1)S(1)} %get-tuple-element.77.grad_ref.one_near, ...), custom_call_target="tpu_custom_call" | custom-call | flops 4400000000 | bytes 13600000 | tf_op jit(solution)/shard_map/pallas_call | solution.py:317
  24.1 0.3 collective-permute-start.12
  24.4 0.3 collective-permute-start.11
  24.7 1.6 %collective-permute-start.17 = (bf16[2,400,256]{2,1,0:T(8,128)(2,1)S(1)}, bf16[2,400,256]{2,1,0:T(8,128)(2,1)S(1)}, u32[]{:S(2)}, u32[]{:S(2)}) collective-permute-start(bf16[2,400,256]{2,1,0:T(8,128)(2,1)S(1)} %slice_add_fusion), channel_id=1, source_target_pairs={{0,1},{1,0},{2,3},{3,2},{16,18},{17,19},{18,16},{19,17},{4,5},{5,4... | collective-permute-start | bytes 1228808 | tf_op jit(solution)/shard_map/ppermute | solution.py:1070
  26.3 0.2 collective-permute-done.12
  26.6 1.6 %collective-permute-start.13 = (bf16[2,400,256]{2,1,0:T(8,128)(2,1)S(1)}, bf16[2,400,256]{2,1,0:T(8,128)(2,1)S(1)}, u32[]{:S(2)}, u32[]{:S(2)}) collective-permute-start(bf16[2,400,256]{2,1,0:T(8,128)(2,1)S(1)} %slice_add_fusion.1), channel_id=1, source_target_pairs={{0,1},{1,0},{2,3},{3,2},{16,18},{17,19},{18,16},{19,17},{4,5},{5,4... | collective-permute-start | bytes 1228808 | tf_op jit(solution)/shard_map/ppermute | solution.py:1070
  28.1 0.1 shard_map.156
  28.2 2.6 %collective-permute-start.19 = (bf16[256,256]{1,0:T(8,128)(2,1)S(1)}, bf16[256,256]{1,0:T(8,128)(2,1)S(1)}, u32[]{:S(2)}, u32[]{:S(2)}) collective-permute-start(bf16[256,256]{1,0:T(8,128)(2,1)S(1)} %get-tuple-element.101), channel_id=1, source_target_pairs={{0,12},{4,8},{8,4},{12,0},{1,13},{5,9},{9,5},{13,1},{2,14},{6,10},... | collective-permute-start | bytes 393224 | tf_op jit(solution)/shard_map/ppermute | solution.py:1065
  30.8 0.1 collective-permute-start.21
  30.9 1.7 %collective-permute-start.15 = (bf16[256,256]{1,0:T(8,128)(2,1)S(1)}, bf16[256,256]{1,0:T(8,128)(2,1)S(1)}, u32[]{:S(2)}, u32[]{:S(2)}) collective-permute-start(bf16[256,256]{1,0:T(8,128)(2,1)S(1)} %get-tuple-element.97), channel_id=1, source_target_pairs={{0,4},{4,0},{8,12},{12,8},{1,5},{5,1},{9,13},{13,9},{2,6},{6,2},{1... | collective-permute-start | bytes 393224 | tf_op jit(solution)/shard_map/ppermute | solution.py:1065
  32.7 0.1 collective-permute-done.17
  32.8 1.6 %collective-permute-start.18 = (bf16[400,256]{1,0:T(8,128)(2,1)S(1)}, bf16[400,256]{1,0:T(8,128)(2,1)S(1)}, u32[]{:S(2)}, u32[]{:S(2)}) collective-permute-start(bf16[400,256]{1,0:T(8,128)(2,1)S(1)} %fusion), channel_id=1, source_target_pairs={{0,2},{1,3},{2,0},{3,1},{16,17},{17,16},{18,19},{19,18},{4,6},{5,7... | collective-permute-start | bytes 614408 | tf_op jit(solution)/shard_map/ppermute | solution.py:1071
  34.4 5.0 %collective-permute-done.13 = bf16[2,400,256]{2,1,0:T(8,128)(2,1)S(1)} collective-permute-done((bf16[2,400,256]{2,1,0:T(8,128)(2,1)S(1)}, bf16[2,400,256]{2,1,0:T(8,128)(2,1)S(1)}, u32[]{:S(2)}, u32[]{:S(2)}) %collective-permute-start.13) | collective-permute-done | bytes 409632 | tf_op jit(solution)/shard_map/ppermute | solution.py:1070
  39.5 1.6 %collective-permute-start.14 = (bf16[400,256]{1,0:T(8,128)(2,1)S(1)}, bf16[400,256]{1,0:T(8,128)(2,1)S(1)}, u32[]{:S(2)}, u32[]{:S(2)}) collective-permute-start(bf16[400,256]{1,0:T(8,128)(2,1)S(1)} %fusion.3), channel_id=1, source_target_pairs={{0,2},{1,3},{2,0},{3,1},{16,17},{17,16},{18,19},{19,18},{4,6},{5,7... | collective-permute-start | bytes 614408 | tf_op jit(solution)/shard_map/ppermute | solution.py:1071
  41.1 2.2 %collective-permute-start.20 = (bf16[400,256]{1,0:T(8,128)(2,1)S(1)}, bf16[400,256]{1,0:T(8,128)(2,1)S(1)}, u32[]{:S(2)}, u32[]{:S(2)}) collective-permute-start(bf16[400,256]{1,0:T(8,128)(2,1)S(1)} %fusion.2), channel_id=1, source_target_pairs={{0,8},{4,12},{8,0},{12,4},{1,9},{5,13},{9,1},{13,5},{2,10},{6,14},... | collective-permute-start | bytes 614408 | tf_op jit(solution)/shard_map/ppermute | solution.py:1065
  43.3 2.0 %collective-permute-done.14 = bf16[400,256]{1,0:T(8,128)(2,1)S(1)} collective-permute-done((bf16[400,256]{1,0:T(8,128)(2,1)S(1)}, bf16[400,256]{1,0:T(8,128)(2,1)S(1)}, u32[]{:S(2)}, u32[]{:S(2)}) %collective-permute-start.14) | collective-permute-done | bytes 204832 | tf_op jit(solution)/shard_map/ppermute | solution.py:1071
  45.3 1.3 %collective-permute-start.22 = (bf16[400,256]{1,0:T(8,128)(2,1)S(1)}, bf16[400,256]{1,0:T(8,128)(2,1)S(1)}, u32[]{:S(2)}, u32[]{:S(2)}) collective-permute-start(bf16[400,256]{1,0:T(8,128)(2,1)S(1)} %fusion.5), channel_id=1, source_target_pairs={{0,4},{4,0},{8,12},{12,8},{1,5},{5,1},{9,13},{13,9},{2,6},{6,2},{1... | collective-permute-start | bytes 614408 | tf_op jit(solution)/shard_map/ppermute | solution.py:1065
  46.6 5.2 %collective-permute-done.20 = bf16[400,256]{1,0:T(8,128)(2,1)S(1)} collective-permute-done((bf16[400,256]{1,0:T(8,128)(2,1)S(1)}, bf16[400,256]{1,0:T(8,128)(2,1)S(1)}, u32[]{:S(2)}, u32[]{:S(2)}) %collective-permute-start.20) | collective-permute-done | bytes 204832 | tf_op jit(solution)/shard_map/ppermute | solution.py:1065
  51.9 0.1 collective-permute-start.26
  52.0 1.1 %collective-permute-done.22 = bf16[400,256]{1,0:T(8,128)(2,1)S(1)} collective-permute-done((bf16[400,256]{1,0:T(8,128)(2,1)S(1)}, bf16[400,256]{1,0:T(8,128)(2,1)S(1)}, u32[]{:S(2)}, u32[]{:S(2)}) %collective-permute-start.22) | collective-permute-done | bytes 204832 | tf_op jit(solution)/shard_map/ppermute | solution.py:1065
  53.1 2.1 %collective-permute-start.23 = (bf16[400,256]{1,0:T(8,128)(2,1)S(1)}, bf16[400,256]{1,0:T(8,128)(2,1)S(1)}, u32[]{:S(2)}, u32[]{:S(2)}) collective-permute-start(bf16[400,256]{1,0:T(8,128)(2,1)S(1)} %add.81), channel_id=1, source_target_pairs={{0,8},{4,12},{8,0},{12,4},{1,9},{5,13},{9,1},{13,5},{2,10},{6,14},... | collective-permute-start | bytes 614408 | tf_op jit(solution)/shard_map/ppermute | solution.py:1065
  55.2 6.7 %collective-permute-done.26 = bf16[400,256]{1,0:T(8,128)(2,1)S(1)} collective-permute-done((bf16[400,256]{1,0:T(8,128)(2,1)S(1)}, bf16[400,256]{1,0:T(8,128)(2,1)S(1)}, u32[]{:S(2)}, u32[]{:S(2)}) %collective-permute-start.26) | collective-permute-done | bytes 204832 | tf_op jit(solution)/shard_map/ppermute | solution.py:1065
  61.9 1.4 %collective-permute-start.27 = (bf16[400,256]{1,0:T(8,128)(2,1)S(1)}, bf16[400,256]{1,0:T(8,128)(2,1)S(1)}, u32[]{:S(2)}, u32[]{:S(2)}) collective-permute-start(bf16[400,256]{1,0:T(8,128)(2,1)S(1)} %add.83), channel_id=1, source_target_pairs={{0,2},{1,3},{2,0},{3,1},{16,17},{17,16},{18,19},{19,18},{4,6},{5,7... | collective-permute-start | bytes 614408 | tf_op jit(solution)/shard_map/ppermute | solution.py:1078
  63.3 0.9 %collective-permute-done.23 = bf16[400,256]{1,0:T(8,128)(2,1)S(1)} collective-permute-done((bf16[400,256]{1,0:T(8,128)(2,1)S(1)}, bf16[400,256]{1,0:T(8,128)(2,1)S(1)}, u32[]{:S(2)}, u32[]{:S(2)}) %collective-permute-start.23) | collective-permute-done | bytes 204832 | tf_op jit(solution)/shard_map/ppermute | solution.py:1065
  64.2 0.1 add.82
  64.3 1.9 %collective-permute-start.24 = (bf16[400,256]{1,0:T(8,128)(2,1)S(1)}, bf16[400,256]{1,0:T(8,128)(2,1)S(1)}, u32[]{:S(2)}, u32[]{:S(2)}) collective-permute-start(bf16[400,256]{1,0:T(8,128)(2,1)S(1)} %add.82), channel_id=1, source_target_pairs={{0,2},{1,3},{2,0},{3,1},{16,17},{17,16},{18,19},{19,18},{4,6},{5,7... | collective-permute-start | bytes 614408 | tf_op jit(solution)/shard_map/ppermute | solution.py:1078
  66.2 1.7 %collective-permute-done.27 = bf16[400,256]{1,0:T(8,128)(2,1)S(1)} collective-permute-done((bf16[400,256]{1,0:T(8,128)(2,1)S(1)}, bf16[400,256]{1,0:T(8,128)(2,1)S(1)}, u32[]{:S(2)}, u32[]{:S(2)}) %collective-permute-start.27) | collective-permute-done | bytes 204832 | tf_op jit(solution)/shard_map/ppermute | solution.py:1078
  67.9 1.5 %collective-permute-start.28 = (bf16[2,400,256]{2,1,0:T(8,128)(2,1)S(1)}, bf16[2,400,256]{2,1,0:T(8,128)(2,1)S(1)}, u32[]{:S(2)}, u32[]{:S(2)}) collective-permute-start(bf16[2,400,256]{2,1,0:T(8,128)(2,1)S(1)} %pad_maximum_fusion.8), channel_id=1, source_target_pairs={{0,1},{1,0},{2,3},{3,2},{16,18},{17,19},{18,16},{19,17},{4,5},{5,4... | collective-permute-start | bytes 1228808 | tf_op jit(solution)/shard_map/ppermute | solution.py:1079
  69.4 2.9 %collective-permute-done.24 = bf16[400,256]{1,0:T(8,128)(2,1)S(1)} collective-permute-done((bf16[400,256]{1,0:T(8,128)(2,1)S(1)}, bf16[400,256]{1,0:T(8,128)(2,1)S(1)}, u32[]{:S(2)}, u32[]{:S(2)}) %collective-permute-start.24) | collective-permute-done | bytes 204832 | tf_op jit(solution)/shard_map/ppermute | solution.py:1078
  72.3 1.5 %collective-permute-start.25 = (bf16[2,400,256]{2,1,0:T(8,128)(2,1)S(1)}, bf16[2,400,256]{2,1,0:T(8,128)(2,1)S(1)}, u32[]{:S(2)}, u32[]{:S(2)}) collective-permute-start(bf16[2,400,256]{2,1,0:T(8,128)(2,1)S(1)} %pad_maximum_fusion.7), channel_id=1, source_target_pairs={{0,1},{1,0},{2,3},{3,2},{16,18},{17,19},{18,16},{19,17},{4,5},{5,4... | collective-permute-start | bytes 1228808 | tf_op jit(solution)/shard_map/ppermute | solution.py:1079
  73.9 2.0 %collective-permute-done.28 = bf16[2,400,256]{2,1,0:T(8,128)(2,1)S(1)} collective-permute-done((bf16[2,400,256]{2,1,0:T(8,128)(2,1)S(1)}, bf16[2,400,256]{2,1,0:T(8,128)(2,1)S(1)}, u32[]{:S(2)}, u32[]{:S(2)}) %collective-permute-start.28) | collective-permute-done | bytes 409632 | tf_op jit(solution)/shard_map/ppermute | solution.py:1079
  75.9 0.8 shard_map.157
  76.8 0.5 collective-permute-start.29
  77.3 3.1 %collective-permute-done.25 = bf16[2,400,256]{2,1,0:T(8,128)(2,1)S(1)} collective-permute-done((bf16[2,400,256]{2,1,0:T(8,128)(2,1)S(1)}, bf16[2,400,256]{2,1,0:T(8,128)(2,1)S(1)}, u32[]{:S(2)}, u32[]{:S(2)}) %collective-permute-start.25) | collective-permute-done | bytes 409632 | tf_op jit(solution)/shard_map/ppermute | solution.py:1079
  80.4 0.1 pad_maximum_fusion.3.one
  80.5 0.1 pad_maximum_fusion.2.zero
  80.5 1.2 %shard_map.158 = (f32[1,256]{1,0:T(1,128)}, f32[1,256,768]{2,1,0:T(8,128)}, f32[1,256,256]{2,1,0:T(8,128)}, f32[1,256]{1,0:T(1,128)}, f32[1,256,1024]{2,1,0:T(8,128)}, /*index=5*/f32[1,1024,256]{2,1,0:T(8,128)}) custom-call(bf16[4,400,256]{2,1,0:T(8,128)(2,1)S(1)} %pad_maximum_fusion.2.zero, bf16[4,400,256]{2,1,0:T(8,128)(2,1)S(1)} %pad_maximum_fusion.3.one), custom_call_target="tpu_custom_call" | custom-call | flops 1100000000 | bytes 3400000 | tf_op jit(solution)/shard_map/pallas_call | solution.py:317
  81.8 0.1 pad_maximum_fusion.5.one
  81.9 0.2 collective-permute-done.30
  82.1 0.1 pad_maximum_fusion.4.zero
  82.2 1.2 %shard_map.159 = (f32[1,256,768]{2,1,0:T(8,128)}, f32[1,256,256]{2,1,0:T(8,128)}, f32[1,256,1024]{2,1,0:T(8,128)}, f32[1,1024,256]{2,1,0:T(8,128)}) custom-call(f32[1,256,768]{2,1,0:T(8,128)} %get-tuple-element.111.qkv_in, f32[1,256,256]{2,1,0:T(8,128)} %get-tuple-element.112.out_in, ...), custom_call_target="tpu_custom_call", output_to_operand_aliasing={{0}: (0, {}), {1}: (1, {}), {2}: (2, {}), {3}: (3, {})} | custom-call | flops 1100000000 | bytes 3400000 | tf_op jit(solution)/shard_map/pallas_call | solution.py:317
  (44 shorter events, 0.6 us)
Async XLA Ops:
  0.6 7.7 %copy-start.2 = (bf16[1,256,768]{2,1,0:T(8,128)(2,1)S(1)}, bf16[1,256,768]{2,1,0:T(8,128)(2,1)}, u32[]{:S(2)}) copy-start(bf16[1,256,768]{2,1,0:T(8,128)(2,1)} %param.13) | copy-start | bytes 1179652
  0.6 7.2 %copy-start.3 = (bf16[1,256,256]{2,1,0:T(8,128)(2,1)S(1)}, bf16[1,256,256]{2,1,0:T(8,128)(2,1)}, u32[]{:S(2)}) copy-start(bf16[1,256,256]{2,1,0:T(8,128)(2,1)} %param.14) | copy-start | bytes 393220
  0.7 9.3 %copy-start.1 = (bf16[1,256,1024]{2,1,0:T(8,128)(2,1)S(1)}, bf16[1,256,1024]{2,1,0:T(8,128)(2,1)}, u32[]{:S(2)}) copy-start(bf16[1,256,1024]{2,1,0:T(8,128)(2,1)} %param.16) | copy-start | bytes 1572868
  0.7 7.2 %copy-start = (bf16[1,1024,256]{2,1,0:T(8,128)(2,1)S(1)}, bf16[1,1024,256]{2,1,0:T(8,128)(2,1)}, u32[]{:S(2)}) copy-start(bf16[1,1024,256]{2,1,0:T(8,128)(2,1)} %param.17) | copy-start | bytes 1572868
  2.0 6.4 %collective-permute-start.3 = (bf16[144,256]{1,0:T(8,128)(2,1)S(1)}, bf16[144,256]{1,0:T(8,128)(2,1)S(1)}, u32[]{:S(2)}, u32[]{:S(2)}) collective-permute-start(bf16[144,256]{1,0:T(8,128)(2,1)S(1)} %get-tuple-element.66.own0), channel_id=1, source_target_pairs={{0,16},{16,0},{1,17},{17,1},{2,18},{18,2},{3,19},{19,3},{4,20},{20... | collective-permute-start | bytes 221192 | tf_op jit(solution)/shard_map/ppermute | solution.py:1121
  2.5 5.3 %collective-permute-start = (bf16[128,256]{1,0:T(8,128)(2,1)S(1)}, bf16[128,256]{1,0:T(8,128)(2,1)S(1)}, u32[]{:S(2)}, u32[]{:S(2)}) collective-permute-start(bf16[128,256]{1,0:T(8,128)(2,1)S(1)} %get-tuple-element.67), channel_id=1, source_target_pairs={{0,4},{4,0},{8,12},{12,8},{1,5},{5,1},{9,13},{13,9},{2,6},{6,2},{1... | collective-permute-start | bytes 196616 | tf_op jit(solution)/shard_map/ppermute | solution.py:1065
  5.2 7.7 %collective-permute-start.1 = (bf16[128,256]{1,0:T(8,128)(2,1)S(1)}, bf16[128,256]{1,0:T(8,128)(2,1)S(1)}, u32[]{:S(2)}, u32[]{:S(2)}) collective-permute-start(bf16[128,256]{1,0:T(8,128)(2,1)S(1)} %get-tuple-element.69), channel_id=1, source_target_pairs={{0,8},{4,12},{8,0},{12,4},{1,9},{5,13},{9,1},{13,5},{2,10},{6,14},... | collective-permute-start | bytes 196616 | tf_op jit(solution)/shard_map/ppermute | solution.py:1065
  7.8 6.1 %collective-permute-start.2 = (bf16[128,256]{1,0:T(8,128)(2,1)S(1)}, bf16[128,256]{1,0:T(8,128)(2,1)S(1)}, u32[]{:S(2)}, u32[]{:S(2)}) collective-permute-start(bf16[128,256]{1,0:T(8,128)(2,1)S(1)} %get-tuple-element.70), channel_id=1, source_target_pairs={{0,12},{4,8},{8,4},{12,0},{1,13},{5,9},{9,5},{13,1},{2,14},{6,10},... | collective-permute-start | bytes 196616 | tf_op jit(solution)/shard_map/ppermute | solution.py:1065
  7.9 6.7 %collective-permute-start.10 = (bf16[1024,256]{1,0:T(8,128)(2,1)S(1)}, bf16[1024,256]{1,0:T(8,128)(2,1)S(1)}, u32[]{:S(2)}, u32[]{:S(2)}) collective-permute-start(bf16[1024,256]{1,0:T(8,128)(2,1)S(1)} %bitcast.48), channel_id=1, source_target_pairs={{0,16},{16,0},{1,17},{17,1},{2,18},{18,2},{3,19},{19,3},{4,20},{20... | collective-permute-start | bytes 1572872 | tf_op jit(solution)/shard_map/ppermute | solution.py:1124
  7.9 2.1 %collective-permute-start.8 = (bf16[256,256]{1,0:T(8,128)(2,1)S(1)}, bf16[256,256]{1,0:T(8,128)(2,1)S(1)}, u32[]{:S(2)}, u32[]{:S(2)}) collective-permute-start(bf16[256,256]{1,0:T(8,128)(2,1)S(1)} %bitcast.54), channel_id=1, source_target_pairs={{0,16},{16,0},{1,17},{17,1},{2,18},{18,2},{3,19},{19,3},{4,20},{20... | collective-permute-start | bytes 393224 | tf_op jit(solution)/shard_map/ppermute | solution.py:1124
  8.4 5.5 %collective-permute-start.7 = (bf16[256,768]{1,0:T(8,128)(2,1)S(1)}, bf16[256,768]{1,0:T(8,128)(2,1)S(1)}, u32[]{:S(2)}, u32[]{:S(2)}) collective-permute-start(bf16[256,768]{1,0:T(8,128)(2,1)S(1)} %bitcast.52), channel_id=1, source_target_pairs={{0,16},{16,0},{1,17},{17,1},{2,18},{18,2},{3,19},{19,3},{4,20},{20... | collective-permute-start | bytes 1179656 | tf_op jit(solution)/shard_map/ppermute | solution.py:1124
  10.0 4.8 %collective-permute-start.9 = (bf16[256,1024]{1,0:T(8,128)(2,1)S(1)}, bf16[256,1024]{1,0:T(8,128)(2,1)S(1)}, u32[]{:S(2)}, u32[]{:S(2)}) collective-permute-start(bf16[256,1024]{1,0:T(8,128)(2,1)S(1)} %bitcast.50), channel_id=1, source_target_pairs={{0,16},{16,0},{1,17},{17,1},{2,18},{18,2},{3,19},{19,3},{4,20},{20... | collective-permute-start | bytes 1572872 | tf_op jit(solution)/shard_map/ppermute | solution.py:1124
  12.9 2.1 %collective-permute-start.4 = (bf16[128,256]{1,0:T(8,128)(2,1)S(1)}, bf16[128,256]{1,0:T(8,128)(2,1)S(1)}, u32[]{:S(2)}, u32[]{:S(2)}) collective-permute-start(bf16[128,256]{1,0:T(8,128)(2,1)S(1)} %collective-permute-done.own1), channel_id=1, source_target_pairs={{0,16},{16,0},{1,17},{17,1},{2,18},{18,2},{3,19},{19,3},{4,20},{20... | collective-permute-start | bytes 196616 | tf_op jit(solution)/shard_map/ppermute | solution.py:1121
  13.9 1.3 %collective-permute-start.5 = (bf16[128,256]{1,0:T(8,128)(2,1)S(1)}, bf16[128,256]{1,0:T(8,128)(2,1)S(1)}, u32[]{:S(2)}, u32[]{:S(2)}) collective-permute-start(bf16[128,256]{1,0:T(8,128)(2,1)S(1)} %collective-permute-done.1.own2), channel_id=1, source_target_pairs={{0,16},{16,0},{1,17},{17,1},{2,18},{18,2},{3,19},{19,3},{4,20},{20... | collective-permute-start | bytes 196616 | tf_op jit(solution)/shard_map/ppermute | solution.py:1121
  13.9 1.4 %collective-permute-start.6 = (bf16[128,256]{1,0:T(8,128)(2,1)S(1)}, bf16[128,256]{1,0:T(8,128)(2,1)S(1)}, u32[]{:S(2)}, u32[]{:S(2)}) collective-permute-start(bf16[128,256]{1,0:T(8,128)(2,1)S(1)} %collective-permute-done.2.own3), channel_id=1, source_target_pairs={{0,16},{16,0},{1,17},{17,1},{2,18},{18,2},{3,19},{19,3},{4,20},{20... | collective-permute-start | bytes 196616 | tf_op jit(solution)/shard_map/ppermute | solution.py:1121
  21.0 3.7 %collective-permute-start.16 = (bf16[4,400,256]{2,1,0:T(8,128)(2,1)S(1)}, bf16[4,400,256]{2,1,0:T(8,128)(2,1)S(1)}, u32[]{:S(2)}, u32[]{:S(2)}) collective-permute-start(bf16[4,400,256]{2,1,0:T(8,128)(2,1)S(1)} %get-tuple-element.100), channel_id=1, source_target_pairs={{0,16},{16,0},{1,17},{17,1},{2,18},{18,2},{3,19},{19,3},{4,20},{20... | collective-permute-start | bytes 2457608 | tf_op jit(solution)/shard_map/ppermute | solution.py:1194
  24.1 2.4 %collective-permute-start.12 = (bf16[4,400,256]{2,1,0:T(8,128)(2,1)S(1)}, bf16[4,400,256]{2,1,0:T(8,128)(2,1)S(1)}, u32[]{:S(2)}, u32[]{:S(2)}) collective-permute-start(bf16[4,400,256]{2,1,0:T(8,128)(2,1)S(1)} %get-tuple-element.96), channel_id=1, source_target_pairs={{0,16},{16,0},{1,17},{17,1},{2,18},{18,2},{3,19},{19,3},{4,20},{20... | collective-permute-start | bytes 2457608 | tf_op jit(solution)/shard_map/ppermute | solution.py:1240
  24.4 3.8 %collective-permute-start.11 = (bf16[832,256]{1,0:T(8,128)(2,1)S(1)}, bf16[832,256]{1,0:T(8,128)(2,1)S(1)}, u32[]{:S(2)}, u32[]{:S(2)}) collective-permute-start(bf16[832,256]{1,0:T(8,128)(2,1)S(1)} %get-tuple-element.93), channel_id=1, source_target_pairs={{0,16},{16,0},{1,17},{17,1},{2,18},{18,2},{3,19},{19,3},{4,20},{20... | collective-permute-start | bytes 1277960 | tf_op jit(solution)/shard_map/ppermute | solution.py:1231
  24.7 8.0 %collective-permute-start.17 = (bf16[2,400,256]{2,1,0:T(8,128)(2,1)S(1)}, bf16[2,400,256]{2,1,0:T(8,128)(2,1)S(1)}, u32[]{:S(2)}, u32[]{:S(2)}) collective-permute-start(bf16[2,400,256]{2,1,0:T(8,128)(2,1)S(1)} %slice_add_fusion), channel_id=1, source_target_pairs={{0,1},{1,0},{2,3},{3,2},{16,18},{17,19},{18,16},{19,17},{4,5},{5,4... | collective-permute-start | bytes 1228808 | tf_op jit(solution)/shard_map/ppermute | solution.py:1070
  26.6 12.9 %collective-permute-start.13 = (bf16[2,400,256]{2,1,0:T(8,128)(2,1)S(1)}, bf16[2,400,256]{2,1,0:T(8,128)(2,1)S(1)}, u32[]{:S(2)}, u32[]{:S(2)}) collective-permute-start(bf16[2,400,256]{2,1,0:T(8,128)(2,1)S(1)} %slice_add_fusion.1), channel_id=1, source_target_pairs={{0,1},{1,0},{2,3},{3,2},{16,18},{17,19},{18,16},{19,17},{4,5},{5,4... | collective-permute-start | bytes 1228808 | tf_op jit(solution)/shard_map/ppermute | solution.py:1070
  28.2 12.9 %collective-permute-start.19 = (bf16[256,256]{1,0:T(8,128)(2,1)S(1)}, bf16[256,256]{1,0:T(8,128)(2,1)S(1)}, u32[]{:S(2)}, u32[]{:S(2)}) collective-permute-start(bf16[256,256]{1,0:T(8,128)(2,1)S(1)} %get-tuple-element.101), channel_id=1, source_target_pairs={{0,12},{4,8},{8,4},{12,0},{1,13},{5,9},{9,5},{13,1},{2,14},{6,10},... | collective-permute-start | bytes 393224 | tf_op jit(solution)/shard_map/ppermute | solution.py:1065
  30.8 21.1 %collective-permute-start.21 = (bf16[256,256]{1,0:T(8,128)(2,1)S(1)}, bf16[256,256]{1,0:T(8,128)(2,1)S(1)}, u32[]{:S(2)}, u32[]{:S(2)}) collective-permute-start(bf16[256,256]{1,0:T(8,128)(2,1)S(1)} %get-tuple-element.103), channel_id=1, source_target_pairs={{0,8},{4,12},{8,0},{12,4},{1,9},{5,13},{9,1},{13,5},{2,10},{6,14},... | collective-permute-start | bytes 393224 | tf_op jit(solution)/shard_map/ppermute | solution.py:1065
  30.9 14.4 %collective-permute-start.15 = (bf16[256,256]{1,0:T(8,128)(2,1)S(1)}, bf16[256,256]{1,0:T(8,128)(2,1)S(1)}, u32[]{:S(2)}, u32[]{:S(2)}) collective-permute-start(bf16[256,256]{1,0:T(8,128)(2,1)S(1)} %get-tuple-element.97), channel_id=1, source_target_pairs={{0,4},{4,0},{8,12},{12,8},{1,5},{5,1},{9,13},{13,9},{2,6},{6,2},{1... | collective-permute-start | bytes 393224 | tf_op jit(solution)/shard_map/ppermute | solution.py:1065
  32.8 8.3 %collective-permute-start.18 = (bf16[400,256]{1,0:T(8,128)(2,1)S(1)}, bf16[400,256]{1,0:T(8,128)(2,1)S(1)}, u32[]{:S(2)}, u32[]{:S(2)}) collective-permute-start(bf16[400,256]{1,0:T(8,128)(2,1)S(1)} %fusion), channel_id=1, source_target_pairs={{0,2},{1,3},{2,0},{3,1},{16,17},{17,16},{18,19},{19,18},{4,6},{5,7... | collective-permute-start | bytes 614408 | tf_op jit(solution)/shard_map/ppermute | solution.py:1071
  39.5 5.8 %collective-permute-start.14 = (bf16[400,256]{1,0:T(8,128)(2,1)S(1)}, bf16[400,256]{1,0:T(8,128)(2,1)S(1)}, u32[]{:S(2)}, u32[]{:S(2)}) collective-permute-start(bf16[400,256]{1,0:T(8,128)(2,1)S(1)} %fusion.3), channel_id=1, source_target_pairs={{0,2},{1,3},{2,0},{3,1},{16,17},{17,16},{18,19},{19,18},{4,6},{5,7... | collective-permute-start | bytes 614408 | tf_op jit(solution)/shard_map/ppermute | solution.py:1071
  41.1 10.7 %collective-permute-start.20 = (bf16[400,256]{1,0:T(8,128)(2,1)S(1)}, bf16[400,256]{1,0:T(8,128)(2,1)S(1)}, u32[]{:S(2)}, u32[]{:S(2)}) collective-permute-start(bf16[400,256]{1,0:T(8,128)(2,1)S(1)} %fusion.2), channel_id=1, source_target_pairs={{0,8},{4,12},{8,0},{12,4},{1,9},{5,13},{9,1},{13,5},{2,10},{6,14},... | collective-permute-start | bytes 614408 | tf_op jit(solution)/shard_map/ppermute | solution.py:1065
  45.3 7.7 %collective-permute-start.22 = (bf16[400,256]{1,0:T(8,128)(2,1)S(1)}, bf16[400,256]{1,0:T(8,128)(2,1)S(1)}, u32[]{:S(2)}, u32[]{:S(2)}) collective-permute-start(bf16[400,256]{1,0:T(8,128)(2,1)S(1)} %fusion.5), channel_id=1, source_target_pairs={{0,4},{4,0},{8,12},{12,8},{1,5},{5,1},{9,13},{13,9},{2,6},{6,2},{1... | collective-permute-start | bytes 614408 | tf_op jit(solution)/shard_map/ppermute | solution.py:1065
  51.9 9.9 %collective-permute-start.26 = (bf16[400,256]{1,0:T(8,128)(2,1)S(1)}, bf16[400,256]{1,0:T(8,128)(2,1)S(1)}, u32[]{:S(2)}, u32[]{:S(2)}) collective-permute-start(bf16[400,256]{1,0:T(8,128)(2,1)S(1)} %add.80), channel_id=1, source_target_pairs={{0,4},{4,0},{8,12},{12,8},{1,5},{5,1},{9,13},{13,9},{2,6},{6,2},{1... | collective-permute-start | bytes 614408 | tf_op jit(solution)/shard_map/ppermute | solution.py:1065
  53.1 11.1 %collective-permute-start.23 = (bf16[400,256]{1,0:T(8,128)(2,1)S(1)}, bf16[400,256]{1,0:T(8,128)(2,1)S(1)}, u32[]{:S(2)}, u32[]{:S(2)}) collective-permute-start(bf16[400,256]{1,0:T(8,128)(2,1)S(1)} %add.81), channel_id=1, source_target_pairs={{0,8},{4,12},{8,0},{12,4},{1,9},{5,13},{9,1},{13,5},{2,10},{6,14},... | collective-permute-start | bytes 614408 | tf_op jit(solution)/shard_map/ppermute | solution.py:1065
  61.9 5.9 %collective-permute-start.27 = (bf16[400,256]{1,0:T(8,128)(2,1)S(1)}, bf16[400,256]{1,0:T(8,128)(2,1)S(1)}, u32[]{:S(2)}, u32[]{:S(2)}) collective-permute-start(bf16[400,256]{1,0:T(8,128)(2,1)S(1)} %add.83), channel_id=1, source_target_pairs={{0,2},{1,3},{2,0},{3,1},{16,17},{17,16},{18,19},{19,18},{4,6},{5,7... | collective-permute-start | bytes 614408 | tf_op jit(solution)/shard_map/ppermute | solution.py:1078
  64.3 8.0 %collective-permute-start.24 = (bf16[400,256]{1,0:T(8,128)(2,1)S(1)}, bf16[400,256]{1,0:T(8,128)(2,1)S(1)}, u32[]{:S(2)}, u32[]{:S(2)}) collective-permute-start(bf16[400,256]{1,0:T(8,128)(2,1)S(1)} %add.82), channel_id=1, source_target_pairs={{0,2},{1,3},{2,0},{3,1},{16,17},{17,16},{18,19},{19,18},{4,6},{5,7... | collective-permute-start | bytes 614408 | tf_op jit(solution)/shard_map/ppermute | solution.py:1078
  67.9 8.0 %collective-permute-start.28 = (bf16[2,400,256]{2,1,0:T(8,128)(2,1)S(1)}, bf16[2,400,256]{2,1,0:T(8,128)(2,1)S(1)}, u32[]{:S(2)}, u32[]{:S(2)}) collective-permute-start(bf16[2,400,256]{2,1,0:T(8,128)(2,1)S(1)} %pad_maximum_fusion.8), channel_id=1, source_target_pairs={{0,1},{1,0},{2,3},{3,2},{16,18},{17,19},{18,16},{19,17},{4,5},{5,4... | collective-permute-start | bytes 1228808 | tf_op jit(solution)/shard_map/ppermute | solution.py:1079
  72.3 8.0 %collective-permute-start.25 = (bf16[2,400,256]{2,1,0:T(8,128)(2,1)S(1)}, bf16[2,400,256]{2,1,0:T(8,128)(2,1)S(1)}, u32[]{:S(2)}, u32[]{:S(2)}) collective-permute-start(bf16[2,400,256]{2,1,0:T(8,128)(2,1)S(1)} %pad_maximum_fusion.7), channel_id=1, source_target_pairs={{0,1},{1,0},{2,3},{3,2},{16,18},{17,19},{18,16},{19,17},{4,5},{5,4... | collective-permute-start | bytes 1228808 | tf_op jit(solution)/shard_map/ppermute | solution.py:1079
  73.9 7.9 %collective-permute-start.31 = (bf16[2,400,256]{2,1,0:T(8,128)(2,1)S(1)}, bf16[2,400,256]{2,1,0:T(8,128)(2,1)S(1)}, u32[]{:S(2)}, u32[]{:S(2)}) collective-permute-start(bf16[2,400,256]{2,1,0:T(8,128)(2,1)S(1)} %pad_maximum_fusion.8), channel_id=1, source_target_pairs={{0,16},{16,0},{1,17},{17,1},{2,18},{18,2},{3,19},{19,3},{4,20},{20... | collective-permute-start | bytes 1228808 | tf_op jit(solution)/shard_map/ppermute | solution.py:1253
  75.9 5.9 %collective-permute-start.32 = (bf16[2,400,256]{2,1,0:T(8,128)(2,1)S(1)}, bf16[2,400,256]{2,1,0:T(8,128)(2,1)S(1)}, u32[]{:S(2)}, u32[]{:S(2)}) collective-permute-start(bf16[2,400,256]{2,1,0:T(8,128)(2,1)S(1)} %collective-permute-done.28), channel_id=1, source_target_pairs={{0,16},{16,0},{1,17},{17,1},{2,18},{18,2},{3,19},{19,3},{4,20},{20... | collective-permute-start | bytes 1228808 | tf_op jit(solution)/shard_map/ppermute | solution.py:1253
  76.8 5.1 %collective-permute-start.29 = (bf16[2,400,256]{2,1,0:T(8,128)(2,1)S(1)}, bf16[2,400,256]{2,1,0:T(8,128)(2,1)S(1)}, u32[]{:S(2)}, u32[]{:S(2)}) collective-permute-start(bf16[2,400,256]{2,1,0:T(8,128)(2,1)S(1)} %pad_maximum_fusion.7), channel_id=1, source_target_pairs={{0,16},{16,0},{1,17},{17,1},{2,18},{18,2},{3,19},{19,3},{4,20},{20... | collective-permute-start | bytes 1228808 | tf_op jit(solution)/shard_map/ppermute | solution.py:1253
  80.4 1.7 %collective-permute-start.30 = (bf16[2,400,256]{2,1,0:T(8,128)(2,1)S(1)}, bf16[2,400,256]{2,1,0:T(8,128)(2,1)S(1)}, u32[]{:S(2)}, u32[]{:S(2)}) collective-permute-start(bf16[2,400,256]{2,1,0:T(8,128)(2,1)S(1)} %collective-permute-done.25), channel_id=1, source_target_pairs={{0,16},{16,0},{1,17},{17,1},{2,18},{18,2},{3,19},{19,3},{4,20},{20... | collective-permute-start | bytes 1228808 | tf_op jit(solution)/shard_map/ppermute | solution.py:1253

commit v8 on v7

--- a/solution.py
+++ b/solution.py
@@ -1238,8 +1238,8 @@
     )
     home = [shared[0]] + [along_line(shared[step], step) for step in range(1, micro_count)]
     came_zero = lax.ppermute(send_zero, "section", SWAP)
+    zero_pair, zero_first = reduce_terms(keep_zero, came_zero, home, (1, 2), 1)
     one_pair, one_first = reduce_terms(keep_one, came_one, home, (2, 1), 3, 2)
-    zero_pair, zero_first = reduce_terms(keep_zero, came_zero, home, (1, 2), 1)
     results, input_grads = call(
         settle_kernel,
         (),

time: 83.6 us -> 83.6 us (level)
  no operation moved by 1% of the time
where the time goes in v8:
time: 83.6 us; the launch traced here: 83.4 us
  waiting for transfers between devices  36.8 us (44%)
  starting transfers between devices  31.2 us (37%)
  Pallas kernels  13.1 us (16%)
  other arithmetic  1.39 us (2%)
  between operations  0.95 us (1%)
    ppermute x10, waiting for transfers between devices, along_line(): return lax.ppermute(value, 'dp', [(z, z ^ step) for z in range(4)])  17.7 us
    ppermute x10, starting transfers between devices, along_line(): return lax.ppermute(value, 'dp', [(z, z ^ step) for z in range(4)])  15.3 us
    pallas_call x8, Pallas kernels, call(): pl.pallas_call(body, out_shape=tuple((jax.ShapeDtypeStruct(*shape) for sh...  13.1 us
    ppermute x2, waiting for transfers between devices, reduce_terms(): first = lax.ppermute(keep[2:4] + came[2:4], PLANE, FIRST)  5.13 us
    ppermute x2, waiting for transfers between devices, reduce_terms(): return (pair, lax.ppermute(pair, PLANE, FIRST))  5.13 us
    ppermute x2, waiting for transfers between devices, reduce_terms(): pair = jnp.stack([total, lax.ppermute(total, PLANE, SECOND)])  4.62 us
    ppermute x2, starting transfers between devices, reduce_terms(): pair = jnp.stack([total, lax.ppermute(total, PLANE, SECOND)])  3.24 us
    ppermute x2, starting transfers between devices, reduce_terms(): second = lax.ppermute(keep[1] + came[1] + first[1], PLANE, SECOND)  3.22 us
  transfers between devices with their start and end apart: 33, of which 19 were waited for; matrix products, arithmetic and copies ran while one was open for 2% of the time, Pallas kernels for 6%

profile of v8, /device:TPU:0, one launch (start us, length us, event | category | flops | bytes accessed | tf_op | source)
XLA Modules:
  0.0 83.4 jit_solution(11283460200813114155)
XLA Ops:
  0.7 1.3 %shard_map.152 = (bf16[144,256]{1,0:T(8,128)(2,1)S(1)}, bf16[128,256]{1,0:T(8,128)(2,1)S(1)}, bf16[128,256]{1,0:T(8,128)(2,1)S(1)}, bf16[128,256]{1,0:T(8,128)(2...) custom-call(bf16[4,1,128,256]{3,2,1,0:T(8,128)(2,1)} %tokens.1, bf16[4,1,128,256]{3,2,1,0:T(8,128)(2,1)} %grads.1, ...), custom_call_target="tpu_custom_call" | custom-call | flops 1100000000 | bytes 3400000 | tf_op jit(solution)/shard_map/pallas_call | solution.py:317
  2.0 0.5 collective-permute-start.3
  2.5 2.6 %collective-permute-start = (bf16[128,256]{1,0:T(8,128)(2,1)S(1)}, bf16[128,256]{1,0:T(8,128)(2,1)S(1)}, u32[]{:S(2)}, u32[]{:S(2)}) collective-permute-start(bf16[128,256]{1,0:T(8,128)(2,1)S(1)} %get-tuple-element.67), channel_id=1, source_target_pairs={{0,4},{4,0},{8,12},{12,8},{1,5},{5,1},{9,13},{13,9},{2,6},{6,2},{1... | collective-permute-start | bytes 196616 | tf_op jit(solution)/shard_map/ppermute | solution.py:1065
  5.2 2.6 %collective-permute-start.1 = (bf16[128,256]{1,0:T(8,128)(2,1)S(1)}, bf16[128,256]{1,0:T(8,128)(2,1)S(1)}, u32[]{:S(2)}, u32[]{:S(2)}) collective-permute-start(bf16[128,256]{1,0:T(8,128)(2,1)S(1)} %get-tuple-element.69), channel_id=1, source_target_pairs={{0,8},{4,12},{8,0},{12,4},{1,9},{5,13},{9,1},{13,5},{2,10},{6,14},... | collective-permute-start | bytes 196616 | tf_op jit(solution)/shard_map/ppermute | solution.py:1065
  7.8 0.1 collective-permute-done.own1
  7.9 0.5 collective-permute-start.8
  8.4 0.1 collective-permute-start.7
  8.5 1.5 %collective-permute-done.8 = bf16[256,256]{1,0:T(8,128)(2,1)S(1)} collective-permute-done((bf16[256,256]{1,0:T(8,128)(2,1)S(1)}, bf16[256,256]{1,0:T(8,128)(2,1)S(1)}, u32[]{:S(2)}, u32[]{:S(2)}) %collective-permute-start.8) | collective-permute-done | bytes 131104 | tf_op jit(solution)/shard_map/ppermute | solution.py:1124
  10.0 0.1 collective-permute-start.9
  10.2 2.7 %collective-permute-done.1.own2 = bf16[128,256]{1,0:T(8,128)(2,1)S(1)} collective-permute-done((bf16[128,256]{1,0:T(8,128)(2,1)S(1)}, bf16[128,256]{1,0:T(8,128)(2,1)S(1)}, u32[]{:S(2)}, u32[]{:S(2)}) %collective-permute-start.1) | collective-permute-done | bytes 65568 | tf_op jit(solution)/shard_map/ppermute | solution.py:1065
  12.9 1.0 %collective-permute-done.2.own3 = bf16[128,256]{1,0:T(8,128)(2,1)S(1)} collective-permute-done((bf16[128,256]{1,0:T(8,128)(2,1)S(1)}, bf16[128,256]{1,0:T(8,128)(2,1)S(1)}, u32[]{:S(2)}, u32[]{:S(2)}) %collective-permute-start.2) | collective-permute-done | bytes 65568 | tf_op jit(solution)/shard_map/ppermute | solution.py:1065
  13.9 0.5 collective-permute-start.6
  14.4 0.1 select_bitcast_fusion.5
  14.5 0.1 pad_maximum_fusion.6.w_qkv.rest_0_
  14.5 0.1 select_bitcast_fusion.1
  14.6 0.1 pad_maximum_fusion.1.w_down.rest_3_
  14.7 0.1 select_bitcast_fusion.3
  14.8 0.1 pad_maximum_fusion.w_up.rest_2_
  14.9 0.2 collective-permute-done.5.far2
  15.1 0.2 collective-permute-done.6.far3
  15.3 2.2 %shard_map.153 = (bf16[640,256]{1,0:T(8,128)(2,1)}, f32[576,256]{1,0:T(8,128)S(1)}, f32[576,128]{1,0:T(8,128)S(1)}, bf16[576,256]{1,0:T(8,128)(2,1)S(1)}, bf16[2...) custom-call(f32[256,192]{1,0:T(8,128)S(1)} %get-tuple-element.65.mas, ...), custom_call_target="tpu_custom_call" | custom-call | flops 1100000000 | bytes 3400000 | tf_op jit(solution)/shard_map/pallas_call | solution.py:317
  17.5 3.5 %shard_map.154 = (bf16[256,256]{1,0:T(8,128)(2,1)S(1)}, bf16[256,256]{1,0:T(8,128)(2,1)S(1)}, bf16[4,400,256]{2,1,0:T(8,128)(2,1)S(1)}, bf16[4,400,256]{2,1,0:T(8,128)(2,1)S(1)}) custom-call(f32[256,256]{1,0:T(8,128)S(1)} %get-tuple-element.64.mask, bf16[256,256]{1,0:T(8,128)(2,1)S(1)} %get-tuple-element.75.hidden_ref.rest_6_, ...), custom_call_target="tpu_custom_call" | custom-call | flops 4400000000 | bytes 13600000 | tf_op jit(solution)/shard_map/pallas_call | solution.py:317
  21.0 0.4 collective-permute-start.16
  21.4 2.7 %shard_map.155 = (bf16[256,256]{1,0:T(8,128)(2,1)S(1)}, f32[640,256]{1,0:T(8,128)S(1)}, bf16[832,256]{1,0:T(8,128)(2,1)S(1)}, bf16[4,400,256]{2,1,0:T(8,128)(2,1)S(1)}, bf16[4,400,256]{2,1,0:T(8,128)(2,1)S(1)}) custom-call(bf16[256,256]{1,0:T(8,128)(2,1)S(1)} %get-tuple-element.77.grad_ref.one_near, ...), custom_call_target="tpu_custom_call" | custom-call | flops 4400000000 | bytes 13600000 | tf_op jit(solution)/shard_map/pallas_call | solution.py:317
  24.1 0.3 collective-permute-start.12
  24.4 0.3 collective-permute-start.11
  24.7 1.6 %collective-permute-start.17 = (bf16[2,400,256]{2,1,0:T(8,128)(2,1)S(1)}, bf16[2,400,256]{2,1,0:T(8,128)(2,1)S(1)}, u32[]{:S(2)}, u32[]{:S(2)}) collective-permute-start(bf16[2,400,256]{2,1,0:T(8,128)(2,1)S(1)} %slice_add_fusion), channel_id=1, source_target_pairs={{0,1},{1,0},{2,3},{3,2},{16,18},{17,19},{18,16},{19,17},{4,5},{5,4... | collective-permute-start | bytes 1228808 | tf_op jit(solution)/shard_map/ppermute | solution.py:1070
  26.3 0.2 collective-permute-done.12
  26.6 1.6 %collective-permute-start.13 = (bf16[2,400,256]{2,1,0:T(8,128)(2,1)S(1)}, bf16[2,400,256]{2,1,0:T(8,128)(2,1)S(1)}, u32[]{:S(2)}, u32[]{:S(2)}) collective-permute-start(bf16[2,400,256]{2,1,0:T(8,128)(2,1)S(1)} %slice_add_fusion.1), channel_id=1, source_target_pairs={{0,1},{1,0},{2,3},{3,2},{16,18},{17,19},{18,16},{19,17},{4,5},{5,4... | collective-permute-start | bytes 1228808 | tf_op jit(solution)/shard_map/ppermute | solution.py:1070
  28.1 0.1 shard_map.156
  28.2 2.6 %collective-permute-start.19 = (bf16[256,256]{1,0:T(8,128)(2,1)S(1)}, bf16[256,256]{1,0:T(8,128)(2,1)S(1)}, u32[]{:S(2)}, u32[]{:S(2)}) collective-permute-start(bf16[256,256]{1,0:T(8,128)(2,1)S(1)} %get-tuple-element.101), channel_id=1, source_target_pairs={{0,12},{4,8},{8,4},{12,0},{1,13},{5,9},{9,5},{13,1},{2,14},{6,10},... | collective-permute-start | bytes 393224 | tf_op jit(solution)/shard_map/ppermute | solution.py:1065
  30.8 0.1 collective-permute-start.21
  30.9 1.7 %collective-permute-start.15 = (bf16[256,256]{1,0:T(8,128)(2,1)S(1)}, bf16[256,256]{1,0:T(8,128)(2,1)S(1)}, u32[]{:S(2)}, u32[]{:S(2)}) collective-permute-start(bf16[256,256]{1,0:T(8,128)(2,1)S(1)} %get-tuple-element.97), channel_id=1, source_target_pairs={{0,4},{4,0},{8,12},{12,8},{1,5},{5,1},{9,13},{13,9},{2,6},{6,2},{1... | collective-permute-start | bytes 393224 | tf_op jit(solution)/shard_map/ppermute | solution.py:1065
  32.7 0.1 collective-permute-done.17
  32.8 1.6 %collective-permute-start.18 = (bf16[400,256]{1,0:T(8,128)(2,1)S(1)}, bf16[400,256]{1,0:T(8,128)(2,1)S(1)}, u32[]{:S(2)}, u32[]{:S(2)}) collective-permute-start(bf16[400,256]{1,0:T(8,128)(2,1)S(1)} %fusion), channel_id=1, source_target_pairs={{0,2},{1,3},{2,0},{3,1},{16,17},{17,16},{18,19},{19,18},{4,6},{5,7... | collective-permute-start | bytes 614408 | tf_op jit(solution)/shard_map/ppermute | solution.py:1071
  34.4 5.0 %collective-permute-done.13 = bf16[2,400,256]{2,1,0:T(8,128)(2,1)S(1)} collective-permute-done((bf16[2,400,256]{2,1,0:T(8,128)(2,1)S(1)}, bf16[2,400,256]{2,1,0:T(8,128)(2,1)S(1)}, u32[]{:S(2)}, u32[]{:S(2)}) %collective-permute-start.13) | collective-permute-done | bytes 409632 | tf_op jit(solution)/shard_map/ppermute | solution.py:1070
  39.5 1.6 %collective-permute-start.14 = (bf16[400,256]{1,0:T(8,128)(2,1)S(1)}, bf16[400,256]{1,0:T(8,128)(2,1)S(1)}, u32[]{:S(2)}, u32[]{:S(2)}) collective-permute-start(bf16[400,256]{1,0:T(8,128)(2,1)S(1)} %fusion.3), channel_id=1, source_target_pairs={{0,2},{1,3},{2,0},{3,1},{16,17},{17,16},{18,19},{19,18},{4,6},{5,7... | collective-permute-start | bytes 614408 | tf_op jit(solution)/shard_map/ppermute | solution.py:1071
  41.1 2.2 %collective-permute-start.20 = (bf16[400,256]{1,0:T(8,128)(2,1)S(1)}, bf16[400,256]{1,0:T(8,128)(2,1)S(1)}, u32[]{:S(2)}, u32[]{:S(2)}) collective-permute-start(bf16[400,256]{1,0:T(8,128)(2,1)S(1)} %fusion.2), channel_id=1, source_target_pairs={{0,8},{4,12},{8,0},{12,4},{1,9},{5,13},{9,1},{13,5},{2,10},{6,14},... | collective-permute-start | bytes 614408 | tf_op jit(solution)/shard_map/ppermute | solution.py:1065
  43.3 2.0 %collective-permute-done.14 = bf16[400,256]{1,0:T(8,128)(2,1)S(1)} collective-permute-done((bf16[400,256]{1,0:T(8,128)(2,1)S(1)}, bf16[400,256]{1,0:T(8,128)(2,1)S(1)}, u32[]{:S(2)}, u32[]{:S(2)}) %collective-permute-start.14) | collective-permute-done | bytes 204832 | tf_op jit(solution)/shard_map/ppermute | solution.py:1071
  45.3 1.3 %collective-permute-start.22 = (bf16[400,256]{1,0:T(8,128)(2,1)S(1)}, bf16[400,256]{1,0:T(8,128)(2,1)S(1)}, u32[]{:S(2)}, u32[]{:S(2)}) collective-permute-start(bf16[400,256]{1,0:T(8,128)(2,1)S(1)} %fusion.5), channel_id=1, source_target_pairs={{0,4},{4,0},{8,12},{12,8},{1,5},{5,1},{9,13},{13,9},{2,6},{6,2},{1... | collective-permute-start | bytes 614408 | tf_op jit(solution)/shard_map/ppermute | solution.py:1065
  46.6 5.2 %collective-permute-done.20 = bf16[400,256]{1,0:T(8,128)(2,1)S(1)} collective-permute-done((bf16[400,256]{1,0:T(8,128)(2,1)S(1)}, bf16[400,256]{1,0:T(8,128)(2,1)S(1)}, u32[]{:S(2)}, u32[]{:S(2)}) %collective-permute-start.20) | collective-permute-done | bytes 204832 | tf_op jit(solution)/shard_map/ppermute | solution.py:1065
  51.9 0.1 collective-permute-start.26
  52.0 1.1 %collective-permute-done.22 = bf16[400,256]{1,0:T(8,128)(2,1)S(1)} collective-permute-done((bf16[400,256]{1,0:T(8,128)(2,1)S(1)}, bf16[400,256]{1,0:T(8,128)(2,1)S(1)}, u32[]{:S(2)}, u32[]{:S(2)}) %collective-permute-start.22) | collective-permute-done | bytes 204832 | tf_op jit(solution)/shard_map/ppermute | solution.py:1065
  53.1 2.1 %collective-permute-start.23 = (bf16[400,256]{1,0:T(8,128)(2,1)S(1)}, bf16[400,256]{1,0:T(8,128)(2,1)S(1)}, u32[]{:S(2)}, u32[]{:S(2)}) collective-permute-start(bf16[400,256]{1,0:T(8,128)(2,1)S(1)} %add.81), channel_id=1, source_target_pairs={{0,8},{4,12},{8,0},{12,4},{1,9},{5,13},{9,1},{13,5},{2,10},{6,14},... | collective-permute-start | bytes 614408 | tf_op jit(solution)/shard_map/ppermute | solution.py:1065
  55.2 6.7 %collective-permute-done.26 = bf16[400,256]{1,0:T(8,128)(2,1)S(1)} collective-permute-done((bf16[400,256]{1,0:T(8,128)(2,1)S(1)}, bf16[400,256]{1,0:T(8,128)(2,1)S(1)}, u32[]{:S(2)}, u32[]{:S(2)}) %collective-permute-start.26) | collective-permute-done | bytes 204832 | tf_op jit(solution)/shard_map/ppermute | solution.py:1065
  61.9 1.4 %collective-permute-start.27 = (bf16[400,256]{1,0:T(8,128)(2,1)S(1)}, bf16[400,256]{1,0:T(8,128)(2,1)S(1)}, u32[]{:S(2)}, u32[]{:S(2)}) collective-permute-start(bf16[400,256]{1,0:T(8,128)(2,1)S(1)} %add.83), channel_id=1, source_target_pairs={{0,2},{1,3},{2,0},{3,1},{16,17},{17,16},{18,19},{19,18},{4,6},{5,7... | collective-permute-start | bytes 614408 | tf_op jit(solution)/shard_map/ppermute | solution.py:1078
  63.3 0.9 %collective-permute-done.23 = bf16[400,256]{1,0:T(8,128)(2,1)S(1)} collective-permute-done((bf16[400,256]{1,0:T(8,128)(2,1)S(1)}, bf16[400,256]{1,0:T(8,128)(2,1)S(1)}, u32[]{:S(2)}, u32[]{:S(2)}) %collective-permute-start.23) | collective-permute-done | bytes 204832 | tf_op jit(solution)/shard_map/ppermute | solution.py:1065
  64.2 0.1 add.82
  64.3 1.9 %collective-permute-start.24 = (bf16[400,256]{1,0:T(8,128)(2,1)S(1)}, bf16[400,256]{1,0:T(8,128)(2,1)S(1)}, u32[]{:S(2)}, u32[]{:S(2)}) collective-permute-start(bf16[400,256]{1,0:T(8,128)(2,1)S(1)} %add.82), channel_id=1, source_target_pairs={{0,2},{1,3},{2,0},{3,1},{16,17},{17,16},{18,19},{19,18},{4,6},{5,7... | collective-permute-start | bytes 614408 | tf_op jit(solution)/shard_map/ppermute | solution.py:1078
  66.2 1.7 %collective-permute-done.27 = bf16[400,256]{1,0:T(8,128)(2,1)S(1)} collective-permute-done((bf16[400,256]{1,0:T(8,128)(2,1)S(1)}, bf16[400,256]{1,0:T(8,128)(2,1)S(1)}, u32[]{:S(2)}, u32[]{:S(2)}) %collective-permute-start.27) | collective-permute-done | bytes 204832 | tf_op jit(solution)/shard_map/ppermute | solution.py:1078
  67.9 1.5 %collective-permute-start.28 = (bf16[2,400,256]{2,1,0:T(8,128)(2,1)S(1)}, bf16[2,400,256]{2,1,0:T(8,128)(2,1)S(1)}, u32[]{:S(2)}, u32[]{:S(2)}) collective-permute-start(bf16[2,400,256]{2,1,0:T(8,128)(2,1)S(1)} %pad_maximum_fusion.8), channel_id=1, source_target_pairs={{0,1},{1,0},{2,3},{3,2},{16,18},{17,19},{18,16},{19,17},{4,5},{5,4... | collective-permute-start | bytes 1228808 | tf_op jit(solution)/shard_map/ppermute | solution.py:1079
  69.4 2.9 %collective-permute-done.24 = bf16[400,256]{1,0:T(8,128)(2,1)S(1)} collective-permute-done((bf16[400,256]{1,0:T(8,128)(2,1)S(1)}, bf16[400,256]{1,0:T(8,128)(2,1)S(1)}, u32[]{:S(2)}, u32[]{:S(2)}) %collective-permute-start.24) | collective-permute-done | bytes 204832 | tf_op jit(solution)/shard_map/ppermute | solution.py:1078
  72.3 1.5 %collective-permute-start.25 = (bf16[2,400,256]{2,1,0:T(8,128)(2,1)S(1)}, bf16[2,400,256]{2,1,0:T(8,128)(2,1)S(1)}, u32[]{:S(2)}, u32[]{:S(2)}) collective-permute-start(bf16[2,400,256]{2,1,0:T(8,128)(2,1)S(1)} %pad_maximum_fusion.7), channel_id=1, source_target_pairs={{0,1},{1,0},{2,3},{3,2},{16,18},{17,19},{18,16},{19,17},{4,5},{5,4... | collective-permute-start | bytes 1228808 | tf_op jit(solution)/shard_map/ppermute | solution.py:1079
  73.9 2.0 %collective-permute-done.28 = bf16[2,400,256]{2,1,0:T(8,128)(2,1)S(1)} collective-permute-done((bf16[2,400,256]{2,1,0:T(8,128)(2,1)S(1)}, bf16[2,400,256]{2,1,0:T(8,128)(2,1)S(1)}, u32[]{:S(2)}, u32[]{:S(2)}) %collective-permute-start.28) | collective-permute-done | bytes 409632 | tf_op jit(solution)/shard_map/ppermute | solution.py:1079
  75.9 0.8 shard_map.157
  76.8 0.5 collective-permute-start.29
  77.3 3.1 %collective-permute-done.25 = bf16[2,400,256]{2,1,0:T(8,128)(2,1)S(1)} collective-permute-done((bf16[2,400,256]{2,1,0:T(8,128)(2,1)S(1)}, bf16[2,400,256]{2,1,0:T(8,128)(2,1)S(1)}, u32[]{:S(2)}, u32[]{:S(2)}) %collective-permute-start.25) | collective-permute-done | bytes 409632 | tf_op jit(solution)/shard_map/ppermute | solution.py:1079
  80.4 0.1 pad_maximum_fusion.3.one
  80.5 0.1 pad_maximum_fusion.2.zero
  80.5 1.2 %shard_map.158 = (f32[1,256]{1,0:T(1,128)}, f32[1,256,768]{2,1,0:T(8,128)}, f32[1,256,256]{2,1,0:T(8,128)}, f32[1,256]{1,0:T(1,128)}, f32[1,256,1024]{2,1,0:T(8,128)}, /*index=5*/f32[1,1024,256]{2,1,0:T(8,128)}) custom-call(bf16[4,400,256]{2,1,0:T(8,128)(2,1)S(1)} %pad_maximum_fusion.2.zero, bf16[4,400,256]{2,1,0:T(8,128)(2,1)S(1)} %pad_maximum_fusion.3.one), custom_call_target="tpu_custom_call" | custom-call | flops 1100000000 | bytes 3400000 | tf_op jit(solution)/shard_map/pallas_call | solution.py:317
  81.8 0.1 pad_maximum_fusion.5.one
  81.9 0.2 collective-permute-done.30
  82.1 0.1 pad_maximum_fusion.4.zero
  82.2 1.2 %shard_map.159 = (f32[1,256,768]{2,1,0:T(8,128)}, f32[1,256,256]{2,1,0:T(8,128)}, f32[1,256,1024]{2,1,0:T(8,128)}, f32[1,1024,256]{2,1,0:T(8,128)}) custom-call(f32[1,256,768]{2,1,0:T(8,128)} %get-tuple-element.111.qkv_in, f32[1,256,256]{2,1,0:T(8,128)} %get-tuple-element.112.out_in, ...), custom_call_target="tpu_custom_call", output_to_operand_aliasing={{0}: (0, {}), {1}: (1, {}), {2}: (2, {}), {3}: (3, {})} | custom-call | flops 1100000000 | bytes 3400000 | tf_op jit(solution)/shard_map/pallas_call | solution.py:317
  (44 shorter events, 0.6 us)
Async XLA Ops:
  0.6 7.7 %copy-start.2 = (bf16[1,256,768]{2,1,0:T(8,128)(2,1)S(1)}, bf16[1,256,768]{2,1,0:T(8,128)(2,1)}, u32[]{:S(2)}) copy-start(bf16[1,256,768]{2,1,0:T(8,128)(2,1)} %param.13) | copy-start | bytes 1179652
  0.6 7.2 %copy-start.3 = (bf16[1,256,256]{2,1,0:T(8,128)(2,1)S(1)}, bf16[1,256,256]{2,1,0:T(8,128)(2,1)}, u32[]{:S(2)}) copy-start(bf16[1,256,256]{2,1,0:T(8,128)(2,1)} %param.14) | copy-start | bytes 393220
  0.7 9.3 %copy-start.1 = (bf16[1,256,1024]{2,1,0:T(8,128)(2,1)S(1)}, bf16[1,256,1024]{2,1,0:T(8,128)(2,1)}, u32[]{:S(2)}) copy-start(bf16[1,256,1024]{2,1,0:T(8,128)(2,1)} %param.16) | copy-start | bytes 1572868
  0.7 7.2 %copy-start = (bf16[1,1024,256]{2,1,0:T(8,128)(2,1)S(1)}, bf16[1,1024,256]{2,1,0:T(8,128)(2,1)}, u32[]{:S(2)}) copy-start(bf16[1,1024,256]{2,1,0:T(8,128)(2,1)} %param.17) | copy-start | bytes 1572868
  2.0 6.4 %collective-permute-start.3 = (bf16[144,256]{1,0:T(8,128)(2,1)S(1)}, bf16[144,256]{1,0:T(8,128)(2,1)S(1)}, u32[]{:S(2)}, u32[]{:S(2)}) collective-permute-start(bf16[144,256]{1,0:T(8,128)(2,1)S(1)} %get-tuple-element.66.own0), channel_id=1, source_target_pairs={{0,16},{16,0},{1,17},{17,1},{2,18},{18,2},{3,19},{19,3},{4,20},{20... | collective-permute-start | bytes 221192 | tf_op jit(solution)/shard_map/ppermute | solution.py:1121
  2.5 5.3 %collective-permute-start = (bf16[128,256]{1,0:T(8,128)(2,1)S(1)}, bf16[128,256]{1,0:T(8,128)(2,1)S(1)}, u32[]{:S(2)}, u32[]{:S(2)}) collective-permute-start(bf16[128,256]{1,0:T(8,128)(2,1)S(1)} %get-tuple-element.67), channel_id=1, source_target_pairs={{0,4},{4,0},{8,12},{12,8},{1,5},{5,1},{9,13},{13,9},{2,6},{6,2},{1... | collective-permute-start | bytes 196616 | tf_op jit(solution)/shard_map/ppermute | solution.py:1065
  5.2 7.7 %collective-permute-start.1 = (bf16[128,256]{1,0:T(8,128)(2,1)S(1)}, bf16[128,256]{1,0:T(8,128)(2,1)S(1)}, u32[]{:S(2)}, u32[]{:S(2)}) collective-permute-start(bf16[128,256]{1,0:T(8,128)(2,1)S(1)} %get-tuple-element.69), channel_id=1, source_target_pairs={{0,8},{4,12},{8,0},{12,4},{1,9},{5,13},{9,1},{13,5},{2,10},{6,14},... | collective-permute-start | bytes 196616 | tf_op jit(solution)/shard_map/ppermute | solution.py:1065
  7.8 6.1 %collective-permute-start.2 = (bf16[128,256]{1,0:T(8,128)(2,1)S(1)}, bf16[128,256]{1,0:T(8,128)(2,1)S(1)}, u32[]{:S(2)}, u32[]{:S(2)}) collective-permute-start(bf16[128,256]{1,0:T(8,128)(2,1)S(1)} %get-tuple-element.70), channel_id=1, source_target_pairs={{0,12},{4,8},{8,4},{12,0},{1,13},{5,9},{9,5},{13,1},{2,14},{6,10},... | collective-permute-start | bytes 196616 | tf_op jit(solution)/shard_map/ppermute | solution.py:1065
  7.9 6.7 %collective-permute-start.10 = (bf16[1024,256]{1,0:T(8,128)(2,1)S(1)}, bf16[1024,256]{1,0:T(8,128)(2,1)S(1)}, u32[]{:S(2)}, u32[]{:S(2)}) collective-permute-start(bf16[1024,256]{1,0:T(8,128)(2,1)S(1)} %bitcast.48), channel_id=1, source_target_pairs={{0,16},{16,0},{1,17},{17,1},{2,18},{18,2},{3,19},{19,3},{4,20},{20... | collective-permute-start | bytes 1572872 | tf_op jit(solution)/shard_map/ppermute | solution.py:1124
  7.9 2.1 %collective-permute-start.8 = (bf16[256,256]{1,0:T(8,128)(2,1)S(1)}, bf16[256,256]{1,0:T(8,128)(2,1)S(1)}, u32[]{:S(2)}, u32[]{:S(2)}) collective-permute-start(bf16[256,256]{1,0:T(8,128)(2,1)S(1)} %bitcast.54), channel_id=1, source_target_pairs={{0,16},{16,0},{1,17},{17,1},{2,18},{18,2},{3,19},{19,3},{4,20},{20... | collective-permute-start | bytes 393224 | tf_op jit(solution)/shard_map/ppermute | solution.py:1124
  8.4 5.5 %collective-permute-start.7 = (bf16[256,768]{1,0:T(8,128)(2,1)S(1)}, bf16[256,768]{1,0:T(8,128)(2,1)S(1)}, u32[]{:S(2)}, u32[]{:S(2)}) collective-permute-start(bf16[256,768]{1,0:T(8,128)(2,1)S(1)} %bitcast.52), channel_id=1, source_target_pairs={{0,16},{16,0},{1,17},{17,1},{2,18},{18,2},{3,19},{19,3},{4,20},{20... | collective-permute-start | bytes 1179656 | tf_op jit(solution)/shard_map/ppermute | solution.py:1124
  10.0 4.8 %collective-permute-start.9 = (bf16[256,1024]{1,0:T(8,128)(2,1)S(1)}, bf16[256,1024]{1,0:T(8,128)(2,1)S(1)}, u32[]{:S(2)}, u32[]{:S(2)}) collective-permute-start(bf16[256,1024]{1,0:T(8,128)(2,1)S(1)} %bitcast.50), channel_id=1, source_target_pairs={{0,16},{16,0},{1,17},{17,1},{2,18},{18,2},{3,19},{19,3},{4,20},{20... | collective-permute-start | bytes 1572872 | tf_op jit(solution)/shard_map/ppermute | solution.py:1124
  12.9 2.1 %collective-permute-start.4 = (bf16[128,256]{1,0:T(8,128)(2,1)S(1)}, bf16[128,256]{1,0:T(8,128)(2,1)S(1)}, u32[]{:S(2)}, u32[]{:S(2)}) collective-permute-start(bf16[128,256]{1,0:T(8,128)(2,1)S(1)} %collective-permute-done.own1), channel_id=1, source_target_pairs={{0,16},{16,0},{1,17},{17,1},{2,18},{18,2},{3,19},{19,3},{4,20},{20... | collective-permute-start | bytes 196616 | tf_op jit(solution)/shard_map/ppermute | solution.py:1121
  13.9 1.3 %collective-permute-start.5 = (bf16[128,256]{1,0:T(8,128)(2,1)S(1)}, bf16[128,256]{1,0:T(8,128)(2,1)S(1)}, u32[]{:S(2)}, u32[]{:S(2)}) collective-permute-start(bf16[128,256]{1,0:T(8,128)(2,1)S(1)} %collective-permute-done.1.own2), channel_id=1, source_target_pairs={{0,16},{16,0},{1,17},{17,1},{2,18},{18,2},{3,19},{19,3},{4,20},{20... | collective-permute-start | bytes 196616 | tf_op jit(solution)/shard_map/ppermute | solution.py:1121
  13.9 1.4 %collective-permute-start.6 = (bf16[128,256]{1,0:T(8,128)(2,1)S(1)}, bf16[128,256]{1,0:T(8,128)(2,1)S(1)}, u32[]{:S(2)}, u32[]{:S(2)}) collective-permute-start(bf16[128,256]{1,0:T(8,128)(2,1)S(1)} %collective-permute-done.2.own3), channel_id=1, source_target_pairs={{0,16},{16,0},{1,17},{17,1},{2,18},{18,2},{3,19},{19,3},{4,20},{20... | collective-permute-start | bytes 196616 | tf_op jit(solution)/shard_map/ppermute | solution.py:1121
  21.0 3.7 %collective-permute-start.16 = (bf16[4,400,256]{2,1,0:T(8,128)(2,1)S(1)}, bf16[4,400,256]{2,1,0:T(8,128)(2,1)S(1)}, u32[]{:S(2)}, u32[]{:S(2)}) collective-permute-start(bf16[4,400,256]{2,1,0:T(8,128)(2,1)S(1)} %get-tuple-element.100), channel_id=1, source_target_pairs={{0,16},{16,0},{1,17},{17,1},{2,18},{18,2},{3,19},{19,3},{4,20},{20... | collective-permute-start | bytes 2457608 | tf_op jit(solution)/shard_map/ppermute | solution.py:1194
  24.1 2.4 %collective-permute-start.12 = (bf16[4,400,256]{2,1,0:T(8,128)(2,1)S(1)}, bf16[4,400,256]{2,1,0:T(8,128)(2,1)S(1)}, u32[]{:S(2)}, u32[]{:S(2)}) collective-permute-start(bf16[4,400,256]{2,1,0:T(8,128)(2,1)S(1)} %get-tuple-element.96), channel_id=1, source_target_pairs={{0,16},{16,0},{1,17},{17,1},{2,18},{18,2},{3,19},{19,3},{4,20},{20... | collective-permute-start | bytes 2457608 | tf_op jit(solution)/shard_map/ppermute | solution.py:1240
  24.4 3.8 %collective-permute-start.11 = (bf16[832,256]{1,0:T(8,128)(2,1)S(1)}, bf16[832,256]{1,0:T(8,128)(2,1)S(1)}, u32[]{:S(2)}, u32[]{:S(2)}) collective-permute-start(bf16[832,256]{1,0:T(8,128)(2,1)S(1)} %get-tuple-element.93), channel_id=1, source_target_pairs={{0,16},{16,0},{1,17},{17,1},{2,18},{18,2},{3,19},{19,3},{4,20},{20... | collective-permute-start | bytes 1277960 | tf_op jit(solution)/shard_map/ppermute | solution.py:1231
  24.7 8.0 %collective-permute-start.17 = (bf16[2,400,256]{2,1,0:T(8,128)(2,1)S(1)}, bf16[2,400,256]{2,1,0:T(8,128)(2,1)S(1)}, u32[]{:S(2)}, u32[]{:S(2)}) collective-permute-start(bf16[2,400,256]{2,1,0:T(8,128)(2,1)S(1)} %slice_add_fusion), channel_id=1, source_target_pairs={{0,1},{1,0},{2,3},{3,2},{16,18},{17,19},{18,16},{19,17},{4,5},{5,4... | collective-permute-start | bytes 1228808 | tf_op jit(solution)/shard_map/ppermute | solution.py:1070
  26.6 12.9 %collective-permute-start.13 = (bf16[2,400,256]{2,1,0:T(8,128)(2,1)S(1)}, bf16[2,400,256]{2,1,0:T(8,128)(2,1)S(1)}, u32[]{:S(2)}, u32[]{:S(2)}) collective-permute-start(bf16[2,400,256]{2,1,0:T(8,128)(2,1)S(1)} %slice_add_fusion.1), channel_id=1, source_target_pairs={{0,1},{1,0},{2,3},{3,2},{16,18},{17,19},{18,16},{19,17},{4,5},{5,4... | collective-permute-start | bytes 1228808 | tf_op jit(solution)/shard_map/ppermute | solution.py:1070
  28.2 12.9 %collective-permute-start.19 = (bf16[256,256]{1,0:T(8,128)(2,1)S(1)}, bf16[256,256]{1,0:T(8,128)(2,1)S(1)}, u32[]{:S(2)}, u32[]{:S(2)}) collective-permute-start(bf16[256,256]{1,0:T(8,128)(2,1)S(1)} %get-tuple-element.101), channel_id=1, source_target_pairs={{0,12},{4,8},{8,4},{12,0},{1,13},{5,9},{9,5},{13,1},{2,14},{6,10},... | collective-permute-start | bytes 393224 | tf_op jit(solution)/shard_map/ppermute | solution.py:1065
  30.8 21.1 %collective-permute-start.21 = (bf16[256,256]{1,0:T(8,128)(2,1)S(1)}, bf16[256,256]{1,0:T(8,128)(2,1)S(1)}, u32[]{:S(2)}, u32[]{:S(2)}) collective-permute-start(bf16[256,256]{1,0:T(8,128)(2,1)S(1)} %get-tuple-element.103), channel_id=1, source_target_pairs={{0,8},{4,12},{8,0},{12,4},{1,9},{5,13},{9,1},{13,5},{2,10},{6,14},... | collective-permute-start | bytes 393224 | tf_op jit(solution)/shard_map/ppermute | solution.py:1065
  30.9 14.4 %collective-permute-start.15 = (bf16[256,256]{1,0:T(8,128)(2,1)S(1)}, bf16[256,256]{1,0:T(8,128)(2,1)S(1)}, u32[]{:S(2)}, u32[]{:S(2)}) collective-permute-start(bf16[256,256]{1,0:T(8,128)(2,1)S(1)} %get-tuple-element.97), channel_id=1, source_target_pairs={{0,4},{4,0},{8,12},{12,8},{1,5},{5,1},{9,13},{13,9},{2,6},{6,2},{1... | collective-permute-start | bytes 393224 | tf_op jit(solution)/shard_map/ppermute | solution.py:1065
  32.8 8.3 %collective-permute-start.18 = (bf16[400,256]{1,0:T(8,128)(2,1)S(1)}, bf16[400,256]{1,0:T(8,128)(2,1)S(1)}, u32[]{:S(2)}, u32[]{:S(2)}) collective-permute-start(bf16[400,256]{1,0:T(8,128)(2,1)S(1)} %fusion), channel_id=1, source_target_pairs={{0,2},{1,3},{2,0},{3,1},{16,17},{17,16},{18,19},{19,18},{4,6},{5,7... | collective-permute-start | bytes 614408 | tf_op jit(solution)/shard_map/ppermute | solution.py:1071
  39.5 5.8 %collective-permute-start.14 = (bf16[400,256]{1,0:T(8,128)(2,1)S(1)}, bf16[400,256]{1,0:T(8,128)(2,1)S(1)}, u32[]{:S(2)}, u32[]{:S(2)}) collective-permute-start(bf16[400,256]{1,0:T(8,128)(2,1)S(1)} %fusion.3), channel_id=1, source_target_pairs={{0,2},{1,3},{2,0},{3,1},{16,17},{17,16},{18,19},{19,18},{4,6},{5,7... | collective-permute-start | bytes 614408 | tf_op jit(solution)/shard_map/ppermute | solution.py:1071
  41.1 10.7 %collective-permute-start.20 = (bf16[400,256]{1,0:T(8,128)(2,1)S(1)}, bf16[400,256]{1,0:T(8,128)(2,1)S(1)}, u32[]{:S(2)}, u32[]{:S(2)}) collective-permute-start(bf16[400,256]{1,0:T(8,128)(2,1)S(1)} %fusion.2), channel_id=1, source_target_pairs={{0,8},{4,12},{8,0},{12,4},{1,9},{5,13},{9,1},{13,5},{2,10},{6,14},... | collective-permute-start | bytes 614408 | tf_op jit(solution)/shard_map/ppermute | solution.py:1065
  45.3 7.7 %collective-permute-start.22 = (bf16[400,256]{1,0:T(8,128)(2,1)S(1)}, bf16[400,256]{1,0:T(8,128)(2,1)S(1)}, u32[]{:S(2)}, u32[]{:S(2)}) collective-permute-start(bf16[400,256]{1,0:T(8,128)(2,1)S(1)} %fusion.5), channel_id=1, source_target_pairs={{0,4},{4,0},{8,12},{12,8},{1,5},{5,1},{9,13},{13,9},{2,6},{6,2},{1... | collective-permute-start | bytes 614408 | tf_op jit(solution)/shard_map/ppermute | solution.py:1065
  51.9 9.9 %collective-permute-start.26 = (bf16[400,256]{1,0:T(8,128)(2,1)S(1)}, bf16[400,256]{1,0:T(8,128)(2,1)S(1)}, u32[]{:S(2)}, u32[]{:S(2)}) collective-permute-start(bf16[400,256]{1,0:T(8,128)(2,1)S(1)} %add.80), channel_id=1, source_target_pairs={{0,4},{4,0},{8,12},{12,8},{1,5},{5,1},{9,13},{13,9},{2,6},{6,2},{1... | collective-permute-start | bytes 614408 | tf_op jit(solution)/shard_map/ppermute | solution.py:1065
  53.1 11.1 %collective-permute-start.23 = (bf16[400,256]{1,0:T(8,128)(2,1)S(1)}, bf16[400,256]{1,0:T(8,128)(2,1)S(1)}, u32[]{:S(2)}, u32[]{:S(2)}) collective-permute-start(bf16[400,256]{1,0:T(8,128)(2,1)S(1)} %add.81), channel_id=1, source_target_pairs={{0,8},{4,12},{8,0},{12,4},{1,9},{5,13},{9,1},{13,5},{2,10},{6,14},... | collective-permute-start | bytes 614408 | tf_op jit(solution)/shard_map/ppermute | solution.py:1065
  61.9 5.9 %collective-permute-start.27 = (bf16[400,256]{1,0:T(8,128)(2,1)S(1)}, bf16[400,256]{1,0:T(8,128)(2,1)S(1)}, u32[]{:S(2)}, u32[]{:S(2)}) collective-permute-start(bf16[400,256]{1,0:T(8,128)(2,1)S(1)} %add.83), channel_id=1, source_target_pairs={{0,2},{1,3},{2,0},{3,1},{16,17},{17,16},{18,19},{19,18},{4,6},{5,7... | collective-permute-start | bytes 614408 | tf_op jit(solution)/shard_map/ppermute | solution.py:1078
  64.3 8.0 %collective-permute-start.24 = (bf16[400,256]{1,0:T(8,128)(2,1)S(1)}, bf16[400,256]{1,0:T(8,128)(2,1)S(1)}, u32[]{:S(2)}, u32[]{:S(2)}) collective-permute-start(bf16[400,256]{1,0:T(8,128)(2,1)S(1)} %add.82), channel_id=1, source_target_pairs={{0,2},{1,3},{2,0},{3,1},{16,17},{17,16},{18,19},{19,18},{4,6},{5,7... | collective-permute-start | bytes 614408 | tf_op jit(solution)/shard_map/ppermute | solution.py:1078
  67.9 8.0 %collective-permute-start.28 = (bf16[2,400,256]{2,1,0:T(8,128)(2,1)S(1)}, bf16[2,400,256]{2,1,0:T(8,128)(2,1)S(1)}, u32[]{:S(2)}, u32[]{:S(2)}) collective-permute-start(bf16[2,400,256]{2,1,0:T(8,128)(2,1)S(1)} %pad_maximum_fusion.8), channel_id=1, source_target_pairs={{0,1},{1,0},{2,3},{3,2},{16,18},{17,19},{18,16},{19,17},{4,5},{5,4... | collective-permute-start | bytes 1228808 | tf_op jit(solution)/shard_map/ppermute | solution.py:1079
  72.3 8.0 %collective-permute-start.25 = (bf16[2,400,256]{2,1,0:T(8,128)(2,1)S(1)}, bf16[2,400,256]{2,1,0:T(8,128)(2,1)S(1)}, u32[]{:S(2)}, u32[]{:S(2)}) collective-permute-start(bf16[2,400,256]{2,1,0:T(8,128)(2,1)S(1)} %pad_maximum_fusion.7), channel_id=1, source_target_pairs={{0,1},{1,0},{2,3},{3,2},{16,18},{17,19},{18,16},{19,17},{4,5},{5,4... | collective-permute-start | bytes 1228808 | tf_op jit(solution)/shard_map/ppermute | solution.py:1079
  73.9 7.9 %collective-permute-start.31 = (bf16[2,400,256]{2,1,0:T(8,128)(2,1)S(1)}, bf16[2,400,256]{2,1,0:T(8,128)(2,1)S(1)}, u32[]{:S(2)}, u32[]{:S(2)}) collective-permute-start(bf16[2,400,256]{2,1,0:T(8,128)(2,1)S(1)} %pad_maximum_fusion.8), channel_id=1, source_target_pairs={{0,16},{16,0},{1,17},{17,1},{2,18},{18,2},{3,19},{19,3},{4,20},{20... | collective-permute-start | bytes 1228808 | tf_op jit(solution)/shard_map/ppermute | solution.py:1253
  75.9 5.9 %collective-permute-start.32 = (bf16[2,400,256]{2,1,0:T(8,128)(2,1)S(1)}, bf16[2,400,256]{2,1,0:T(8,128)(2,1)S(1)}, u32[]{:S(2)}, u32[]{:S(2)}) collective-permute-start(bf16[2,400,256]{2,1,0:T(8,128)(2,1)S(1)} %collective-permute-done.28), channel_id=1, source_target_pairs={{0,16},{16,0},{1,17},{17,1},{2,18},{18,2},{3,19},{19,3},{4,20},{20... | collective-permute-start | bytes 1228808 | tf_op jit(solution)/shard_map/ppermute | solution.py:1253
  76.8 5.1 %collective-permute-start.29 = (bf16[2,400,256]{2,1,0:T(8,128)(2,1)S(1)}, bf16[2,400,256]{2,1,0:T(8,128)(2,1)S(1)}, u32[]{:S(2)}, u32[]{:S(2)}) collective-permute-start(bf16[2,400,256]{2,1,0:T(8,128)(2,1)S(1)} %pad_maximum_fusion.7), channel_id=1, source_target_pairs={{0,16},{16,0},{1,17},{17,1},{2,18},{18,2},{3,19},{19,3},{4,20},{20... | collective-permute-start | bytes 1228808 | tf_op jit(solution)/shard_map/ppermute | solution.py:1253
  80.4 1.7 %collective-permute-start.30 = (bf16[2,400,256]{2,1,0:T(8,128)(2,1)S(1)}, bf16[2,400,256]{2,1,0:T(8,128)(2,1)S(1)}, u32[]{:S(2)}, u32[]{:S(2)}) collective-permute-start(bf16[2,400,256]{2,1,0:T(8,128)(2,1)S(1)} %collective-permute-done.25), channel_id=1, source_target_pairs={{0,16},{16,0},{1,17},{17,1},{2,18},{18,2},{3,19},{19,3},{4,20},{20... | collective-permute-start | bytes 1228808 | tf_op jit(solution)/shard_map/ppermute | solution.py:1253
